TPU v7x, 32 devices: a whole 2x2x4 slice. The times are simulated.
32 devices in a mesh: dp: 8 (over y, x, core), tensor: 4 (over z).
Axes of the slice: x: 2, y: 2, z: 4, core: 2. Of those that a mesh axis runs over, the one named last changes fastest.
Arguments:
- tokens: bfloat16 [2048, 4096], P(('dp', 'tensor')), may hold values from -110 to 110
- norm_gain: bfloat16 [4096], replicated, may hold values from 0.099609375 to 1.8984375
- query_weight: bfloat16 [4096, 4096], P('dp', 'tensor'), may hold values from -1 to 1
- kv_weight: bfloat16 [4096, 1024], P('dp', 'tensor'), may hold values from -1 to 1
- out_weight: bfloat16 [4096, 4096], P('tensor', 'dp'), may hold values from -0.09375 to 0.09375
- grad_out: bfloat16 [2048, 4096], P(('dp', 'tensor')), may hold values from -6 to 6
- doc_lengths: int32 [8, 4], P('dp'), may hold values from 1 to 128, 256 in all within a row
Outputs:
- input_grad: bfloat16 [2048, 4096], P(('dp', 'tensor'))
- query_weight_grad: float32 [4096, 4096], P('dp', 'tensor')
- kv_weight_grad: float32 [4096, 1024], P('dp', 'tensor')
Inputs may be any that keep to these rules, and one draw needn't show every extreme that they name: `doc_lengths`: each row sums to 256.
All inputs are finite; a program needn't handle non-finite values.
Results may differ from a plain program's by a relative error of at most 0.025.
Values may be sent and summed in bfloat16 or wider, within the bound.
No kernel may reach another device: no remote copies, remote signals or barrier semaphores. Data moves between devices by JAX's collectives and lax.ppermute only.
A program may use at most 64 MiB of HBM per device.

v0:
```python
import math

import jax
import jax.numpy as jnp
from jax import lax
from jax.sharding import PartitionSpec as P

KVH = 4
HD = 128


epsilon = 1e-05


def for_sending(value):

    def short(part):
        return part.astype(jnp.bfloat16) if part.dtype == jnp.float32 else part

    return jax.tree.map(short, value)


def partner_2(value, axis, bit):
    mask = 2**bit
    pairs = [(source, source ^ mask) for source in range(lax.axis_size(axis))]
    return lax.ppermute(value, axis, pairs)


def document_mask(lengths, length_total):
    ends = jnp.cumsum(lengths)
    positions = jnp.arange(length_total, dtype=jnp.int32)
    labels = jnp.sum((ends[None, :] <= positions[:, None]).astype(jnp.int32), axis=1)
    return (labels[:, None] == labels[None, :]) & (positions[None, :] <= positions[:, None])


def local(tokens, norm_gain, query_weight, kv_weight, out_weight, grad_out, doc_lengths):
    tensor_size = lax.axis_size("tensor")
    data_size = lax.axis_size("dp")
    tensor_index = lax.axis_index("tensor")
    sharers = tensor_size // KVH
    levels = sharers.bit_length() - 1
    contract_last = (((1,), (1,)), ((), ()))
    values32 = tokens.astype(jnp.float32)
    root_mean = jnp.sqrt(jnp.mean(values32 * values32, axis=-1) + epsilon)
    unit = values32 / root_mean[:, None]
    gain32 = norm_gain.astype(jnp.float32)
    normed_local = (unit * gain32).astype(jnp.bfloat16)
    normed = lax.all_gather(normed_local, "tensor", axis=0, tiled=True)
    seq_length = normed.shape[0]
    query_full = lax.all_gather(query_weight, "dp", axis=0, tiled=True)
    queries = jnp.dot(normed, query_full, preferred_element_type=jnp.float32).astype(jnp.bfloat16)
    kv_local = lax.all_gather(kv_weight, "dp", axis=0, tiled=True)
    head_weight = kv_local
    for bit_index in range(levels):
        partner = partner_2(for_sending(head_weight), "tensor", bit_index).astype(head_weight.dtype)
        joined_upper_half = tensor_index >> bit_index & 1 == 1
        head_weight = jnp.concatenate(
            [
                jnp.where(joined_upper_half, partner, head_weight),
                jnp.where(joined_upper_half, head_weight, partner),
            ],
            axis=1,
        )
    keyvals = jnp.dot(normed, head_weight, preferred_element_type=jnp.float32).astype(jnp.bfloat16)
    key_rows = keyvals[:, :HD]
    value_rows = keyvals[:, HD:]
    grad_full = lax.all_gather(grad_out, "tensor", axis=0, tiled=True)
    out_grad = lax.dot_general(
        grad_full,
        lax.all_gather(out_weight, "dp", axis=1, tiled=True),
        contract_last,
        preferred_element_type=jnp.float32,
    ).astype(jnp.bfloat16)
    local_heads = queries.shape[1] // HD
    query_heads = queries.reshape(seq_length, local_heads, HD)
    out_heads = out_grad.reshape(seq_length, local_heads, HD)
    allowed = document_mask(doc_lengths[0], seq_length)
    scores = jnp.einsum(
        "qhd,td->hqt", query_heads, key_rows, preferred_element_type=jnp.float32
    ) / math.sqrt(HD)
    scores = jnp.where(allowed[None, :, :], scores, -1e30)
    peak = jnp.max(scores, axis=-1, keepdims=True)
    expo = jnp.exp(scores - peak)
    probs = expo / jnp.sum(expo, axis=-1, keepdims=True)
    probs_low = probs.astype(jnp.bfloat16)
    prob_grad = jnp.einsum("qhd,td->hqt", out_heads, value_rows, preferred_element_type=jnp.float32)
    inner = jnp.sum(probs * prob_grad, axis=-1, keepdims=True)
    score_grad = (probs * (prob_grad - inner) / math.sqrt(HD)).astype(jnp.bfloat16)
    query_grad = jnp.einsum("hqt,td->qhd", score_grad, key_rows, preferred_element_type=jnp.float32)
    query_grad = query_grad.astype(jnp.bfloat16).reshape(seq_length, local_heads * HD)
    key_part = jnp.einsum(
        "hqt,qhd->td", score_grad, query_heads, preferred_element_type=jnp.float32
    )
    value_part = jnp.einsum("hqt,qhd->td", probs_low, out_heads, preferred_element_type=jnp.float32)
    kv_partial = jnp.concatenate([key_part, value_part], axis=1)
    for bit_index in reversed(range(levels)):
        half_cols = kv_partial.shape[1] // 2
        upper_half = tensor_index >> bit_index & 1 == 1
        lower_cols = kv_partial[:, :half_cols]
        higher_cols = kv_partial[:, half_cols:]
        kept = jnp.where(upper_half, higher_cols, lower_cols)
        handed = jnp.where(upper_half, lower_cols, higher_cols)
        kv_partial = kept + partner_2(handed.astype(jnp.bfloat16), "tensor", bit_index).astype(
            handed.dtype
        )
    kv_grad = kv_partial.astype(jnp.bfloat16)
    from_query = lax.dot_general(
        query_grad, query_full, contract_last, preferred_element_type=jnp.float32
    )
    from_kv = lax.dot_general(kv_grad, kv_local, contract_last, preferred_element_type=jnp.float32)
    normed_grad = lax.psum_scatter(
        (from_query + from_kv).astype(jnp.bfloat16), "tensor", scatter_dimension=0, tiled=True
    ).astype(jnp.float32)
    scaled = normed_grad * gain32
    correction = unit * jnp.mean(scaled * unit, axis=-1, keepdims=True)
    input_grad = (grad_out.astype(jnp.float32) + (scaled - correction) / root_mean[:, None]).astype(
        jnp.bfloat16
    )
    combined = jnp.concatenate([query_grad, kv_grad], axis=1)
    weight_grads = (
        lax.psum_scatter(
            lax.dot_general(
                normed, combined, (((0,), (0,)), ((), ())), preferred_element_type=jnp.float32
            ).astype(jnp.bfloat16),
            "dp",
            scatter_dimension=0,
            tiled=True,
        ).astype(jnp.float32)
        / data_size
    )
    query_width = query_weight.shape[1]
    return (input_grad, weight_grads[:, :query_width], weight_grads[:, query_width:])


def solution(mesh):
    placed = (
        P(("dp", "tensor"), None),
        P(),
        P("dp", "tensor"),
        P("dp", "tensor"),
        P("tensor", "dp"),
        P(("dp", "tensor"), None),
        P("dp", None),
    )
    return jax.shard_map(
        local,
        mesh=mesh,
        in_specs=placed,
        out_specs=(P(("dp", "tensor"), None), P("dp", "tensor"), P("dp", "tensor")),
        check_vma=False,
    )
```

profile of v0, /device:TPU:1, one launch (start us, length us, event | category | flops | bytes accessed | tf_op | source)
XLA Modules:
  0.0 418.3 jit_solution(2987131348847703610)
XLA Ops:
  7.2 1.2 fusion.9
  8.5 0.7 convert_element_type.54
  9.2 2.0 multiply_convert_fusion
  11.3 0.7 all-gather.8.cloned.1.call-update
  12.1 0.7 all-gather.12.cloned.1.call-update
  12.8 0.5 all-gather.14.cloned.1.call-update
  13.4 0.5 all-gather.10.cloned.1.call-update
  14.3 45.1 %all-gather.6.cloned.1.call-done = bf16[256,4096]{1,0:T(8,128)(2,1)} async-done(((bf16[64,4096]{1,0:T(8,128)(2,1)}), bf16[256,4096]{1,0:T(8,128)(2,1)}) %all-gather.6.cloned.1.call-update) | async-done | bytes 2097168 | tf_op jit(solution)/shard_map/all_gather | solution.py:48
  59.4 29.0 %all-gather.8.cloned.1.call-done = bf16[4096,256]{1,0:T(8,128)(2,1)} async-done(((bf16[512,256]{1,0:T(8,128)(2,1)}), bf16[4096,256]{1,0:T(8,128)(2,1)}) %all-gather.8.cloned.1.call-update) | async-done | bytes 2097168 | tf_op jit(solution)/shard_map/all_gather | solution.py:52
  88.4 2.9 convolution_convert_fusion.4
  91.3 44.2 %all-gather.12.cloned.1.call-done = bf16[256,4096]{1,0:T(8,128)(2,1)} async-done(((bf16[64,4096]{1,0:T(8,128)(2,1)}), bf16[256,4096]{1,0:T(8,128)(2,1)}) %all-gather.12.cloned.1.call-update) | async-done | bytes 2097168 | tf_op jit(solution)/shard_map/all_gather | solution.py:67
  135.5 56.9 %all-gather.14.cloned.1.call-done = bf16[1024,4096]{1,0:T(8,128)(2,1)} async-done(((bf16[1024,512]{1,0:T(8,128)(2,1)}), bf16[1024,4096]{1,0:T(8,128)(2,1)}) %all-gather.14.cloned.1.call-update) | async-done | bytes 8388624 | tf_op jit(solution)/shard_map/all_gather | solution.py:70
  192.4 6.4 %convolution_convert_fusion.2 = bf16[256,1024]{1,0:T(8,128)(2,1)S(1)} fusion(bf16[256,4096]{1,0:T(8,128)(2,1)} %all-gather.12.cloned.1.call-done, bf16[1024,4096]{1,0:T(8,128)(2,1)} %all-gather.14.cloned.1.call-done), kind=kOutput, calls=%fused_computation.17 | convolution fusion | flops 2147745792 | bytes 11010048 | tf_op jit(solution)/shard_map/dot_general | solution.py:68
  199.0 49.6 %all-gather.10.cloned.1.call-done = bf16[4096,1024]{1,0:T(8,128)(2,1)} async-done(((bf16[512,1024]{1,0:T(8,128)(2,1)}), bf16[4096,1024]{1,0:T(8,128)(2,1)}) %all-gather.10.cloned.1.call-update) | async-done | bytes 8388624 | tf_op jit(solution)/shard_map/all_gather | solution.py:50
  248.5 6.5 %convolution_convert_fusion.3 = bf16[256,1024]{1,0:T(8,128)(2,1)} fusion(bf16[256,4096]{1,0:T(8,128)(2,1)S(1)} %copy-done.1, bf16[4096,1024]{1,0:T(8,128)(2,1)} %all-gather.10.cloned.1.call-done), kind=kOutput, calls=%fused_computation.18 | convolution fusion | flops 2147745792 | bytes 11010048 | tf_op jit(solution)/shard_map/dot_general | solution.py:51
  255.0 1.2 copy.31
  256.3 1.7 fusion.26
  258.0 2.2 fusion.36
  260.2 2.1 fusion.8
  262.3 4.4 %fusion.7 = bf16[256,128]{0,1:T(8,128)(2,1)S(1)} fusion(bf16[256,8,128]{0,2,1:T(8,128)(2,1)S(1)} %bitcast.74, f32[256,256,8]{1,0,2:T(8,128)} %fusion.26, f32[8,256,256]{1,2,0:T(8,128)} %get-tuple-element.4, f32[8,256]{1,0:T(8,128)S(1)} %get-tuple-element.3), kind=kOutput, calls=%fused_computation.22 | convolution fusion | flops 137922816 | bytes 4792320 | tf_op jit(solution)/shard_map/hqt,qhd->td/dot_general | solution.py:91
  266.6 4.4 %convolution_convert_fusion.1 = bf16[128,8,256]{2,0,1:T(8,128)(2,1)S(1)} fusion(f32[256,256,8]{1,0,2:T(8,128)} %fusion.26, bf16[256,256]{1,0:T(8,128)(2,1)S(1)} %convolution_convert_fusion.4, f32[8,256,256]{1,2,0:T(8,128)} %get-tuple-element.4, f32[8,256]{1,0:T(8,128)S(1)} %get-tuple-element.3), kind=kOutput, calls=%fused_computation.16 | convolution fusion | flops 138152192 | bytes 8994816 | tf_op jit(solution)/shard_map/hqt,td->qhd/dot_general | solution.py:89
  271.1 5.9 %fusion.37 = f32[256,4096]{1,0:T(8,128)S(1)} fusion(bf16[256,1024]{0,1:T(8,128)(2,1)S(1)} %bitcast.71, bf16[4096,1024]{1,0:T(8,128)(2,1)} %all-gather.10.cloned.1.call-done), kind=kOutput, calls=%fused_computation.63 | convolution fusion | flops 2147483648 | bytes 13107200 | tf_op jit(solution)/shard_map/dot_general | solution.py:107
  277.0 2.1 fusion.2
  279.1 0.2 reduce-scatter.5.cloned.1.call-start
  279.3 5.6 %convolution_convert_fusion = bf16[4096,1280]{1,0:T(8,128)(2,1)} fusion(bf16[256,4096]{1,0:T(8,128)(2,1)S(1)} %copy-done.1, bf16[256,128]{0,1:T(8,128)(2,1)S(1)} %fusion.8, bf16[256,128]{0,1:T(8,128)(2,1)S(1)} %fusion.7, bf16[256,1024]{0,1:T(8,128)(2,1)S(1)} %bitcast.72), kind=kOutput, calls=%fused_computation.2 | convolution fusion | flops 2691563520 | bytes 13238272 | tf_op jit(solution)/shard_map/dot_general | solution.py:122
  285.0 37.6 %reduce-scatter.3.cloned.1.call-done = bf16[64,4096]{1,0:T(8,128)(2,1)} async-done(((bf16[256,4096]{1,0:T(8,128)(2,1)}), bf16[64,4096]{1,0:T(8,128)(2,1)}) %reduce-scatter.3.cloned.1.call-update) | async-done | bytes 524304 | tf_op jit(solution)/shard_map/reduce_scatter | solution.py:111
  322.6 1.4 multiply_reduce_fusion
  324.0 2.2 add_convert_fusion
  326.2 81.4 %reduce-scatter.5.cloned.1.call-done = bf16[512,1280]{1,0:T(8,128)(2,1)} async-done(((bf16[4096,1280]{1,0:T(8,128)(2,1)}), bf16[512,1280]{1,0:T(8,128)(2,1)}) %reduce-scatter.5.cloned.1.call-update) | async-done | bytes 1310736 | tf_op jit(solution)/shard_map/reduce_scatter | solution.py:121
  407.6 1.5 convert_multiply_fusion
  409.1 0.8 slice.19
  409.9 1.6 slice.18
  (25 shorter events, 0.9 us)
Async XLA Ops:
  7.2 52.3 %all-gather.6.cloned.1.call-start = ((), (), s32[]{:S(2)}) async-start(), calls=%async_computation.2 | async-start | bytes 2621440 | tf_op jit(solution)/shard_map/all_gather | solution.py:48
  9.2 4.8 %copy-start.4 = (s32[1,4]{1,0:T(1,128)S(1)}, s32[1,4]{1,0:T(1,128)}, u32[]{:S(2)}) copy-start(s32[1,4]{1,0:T(1,128)} %param.13) | copy-start | bytes 52
  11.3 77.1 %all-gather.8.cloned.1.call-start = ((), (), s32[]{:S(2)}) async-start(), calls=%async_computation.3 | async-start | bytes 2359296 | tf_op jit(solution)/shard_map/all_gather | solution.py:52
  12.0 123.5 %all-gather.12.cloned.1.call-start = ((), (), s32[]{:S(2)}) async-start(), calls=%async_computation.5 | async-start | bytes 2621440 | tf_op jit(solution)/shard_map/all_gather | solution.py:67
  12.7 179.6 %all-gather.14.cloned.1.call-start = ((), (), s32[]{:S(2)}) async-start(), calls=%async_computation.6 | async-start | bytes 9437184 | tf_op jit(solution)/shard_map/all_gather | solution.py:70
  13.3 235.2 %all-gather.10.cloned.1.call-start = ((), (), s32[]{:S(2)}) async-start(), calls=%async_computation.4 | async-start | bytes 9437184 | tf_op jit(solution)/shard_map/all_gather | solution.py:50
  13.9 308.6 %reduce-scatter.3.cloned.1.call-start = ((), (), s32[]{:S(2)}) async-start(), calls=%async_computation.7 | async-start | bytes 2621440 | tf_op jit(solution)/shard_map/reduce_scatter | solution.py:111
  91.3 157.2 %copy-start.1 = (bf16[256,4096]{1,0:T(8,128)(2,1)S(1)}, bf16[256,4096]{1,0:T(8,128)(2,1)}, u32[]{:S(2)}) copy-start(bf16[256,4096]{1,0:T(8,128)(2,1)} %all-gather.6.cloned.1.call-done) | copy-start | bytes 6291460
  271.0 5.9 %copy-start.3 = (bf16[4096,256]{1,0:T(8,128)(2,1)S(1)}, bf16[4096,256]{1,0:T(8,128)(2,1)}, u32[]{:S(2)}) copy-start(bf16[4096,256]{1,0:T(8,128)(2,1)} %all-gather.8.cloned.1.call-done) | copy-start | bytes 6291460
  279.1 128.4 %reduce-scatter.5.cloned.1.call-start = ((), (), s32[]{:S(2)}) async-start(), calls=%async_computation.8 | async-start | bytes 11796480 | tf_op jit(solution)/shard_map/reduce_scatter | solution.py:121
  284.9 37.6 %copy-start = (bf16[64,4096]{1,0:T(8,128)(2,1)S(1)}, bf16[64,4096]{1,0:T(8,128)(2,1)}, u32[]{:S(2)}) copy-start(bf16[64,4096]{1,0:T(8,128)(2,1)} %param.7) | copy-start | bytes 1572868
  284.9 39.0 %copy-start.2 = (bf16[64,4096]{1,0:T(8,128)(2,1)S(1)}, bf16[64,4096]{1,0:T(8,128)(2,1)}, u32[]{:S(2)}) copy-start(bf16[64,4096]{1,0:T(8,128)(2,1)} %param.12) | copy-start | bytes 1572868
Sparse Core Ops, SparseCore 0:
  11.4 48.0 all-gather.5
  61.3 27.0 all-gather.7
  90.0 45.5 all-gather.11
  137.2 55.0 all-gather.13
  194.1 54.3 all-gather.9
  279.2 43.2 reduce-scatter.2
  326.5 81.0 reduce-scatter.4
where the time goes:
time: 419 us; the launch traced here: 418 us
  waiting for transfers between devices  346 us (83%)
  matrix products  44.2 us (11%)
  between operations  14.3 us (3%)
  other arithmetic  9.46 us (2%)
    reduce_scatter x1, waiting for transfers between devices, local(): lax.psum_scatter(lax.dot_general(normed, combined, (((0,), (0,)), ((), ()...  81.4 us
    all_gather x1, waiting for transfers between devices, local(): lax.all_gather(out_weight, 'dp', axis=1, tiled=True)  56.9 us
    all_gather x1, waiting for transfers between devices, local(): query_full = lax.all_gather(query_weight, 'dp', axis=0, tiled=True)  49.6 us
    all_gather x1, waiting for transfers between devices, local(): normed = lax.all_gather(normed_local, 'tensor', axis=0, tiled=True)  45.1 us
    all_gather x1, waiting for transfers between devices, local(): grad_full = lax.all_gather(grad_out, 'tensor', axis=0, tiled=True)  44.2 us
    reduce_scatter x1, waiting for transfers between devices, local(): lax.psum_scatter((from_query + from_kv).astype(jnp.bfloat16), 'tensor', s...  37.6 us
    all_gather x1, waiting for transfers between devices, local(): kv_local = lax.all_gather(kv_weight, 'dp', axis=0, tiled=True)  29 us
  transfers between devices with their start and end apart: 7, of which 7 were waited for; matrix products, arithmetic and copies ran while one was open for 5% of the time, Pallas kernels for 0%

commit v1 on v0

v1 whole, which is shorter than its diff:
```python
import math

import jax
import jax.numpy as jnp
from jax import lax
from jax.sharding import PartitionSpec as P

KVH = 4
HD = 128

epsilon = 1e-05


def swap(value, axis, mask):
    pairs = [(source, source ^ mask) for source in range(lax.axis_size(axis))]
    return lax.ppermute(value, axis, pairs)


def gather_chips(value):
    chips = lax.axis_size("dp") // 2
    if chips != 4:
        return [value] + [swap(value, "dp", 2 * k) for k in range(1, chips)]
    half = value.shape[0] // 2
    near_x = swap(value, "dp", 2)
    near_y = swap(value, "dp", 4)
    far_top = swap(near_x[:half], "dp", 4)
    far_bottom = swap(near_y[half:], "dp", 2)
    return [value, near_x, near_y, jnp.concatenate([far_top, far_bottom], axis=0)]


def scatter_chips(blocks):
    chips = lax.axis_size("dp") // 2
    total = blocks[0].astype(jnp.float32)
    if chips != 4:
        for k in range(1, chips):
            total = total + swap(blocks[k], "dp", 2 * k).astype(jnp.float32)
        return total
    half = blocks[0].shape[0] // 2
    far_top = swap(blocks[3][:half], "dp", 4)
    far_bottom = swap(blocks[3][half:], "dp", 2)
    x_bottom = swap(blocks[1][half:], "dp", 2)
    y_top = swap(blocks[2][:half], "dp", 4)
    x_top = swap(blocks[1][:half] + far_top, "dp", 2)
    y_bottom = swap(blocks[2][half:] + far_bottom, "dp", 4)
    top = x_top.astype(jnp.float32) + y_top.astype(jnp.float32)
    bottom = x_bottom.astype(jnp.float32) + y_bottom.astype(jnp.float32)
    return total + jnp.concatenate([top, bottom], axis=0)


def gather_tensor(value):
    size = lax.axis_size("tensor")
    if size != 4:
        return [value] + [swap(value, "tensor", k) for k in range(1, size)]
    index = lax.axis_index("tensor")
    two = swap(value, "tensor", 2)
    one = swap(value, "tensor", 1)
    inner = lax.ppermute(value, "tensor", [(1, 2), (2, 1)])
    outer = lax.ppermute(two, "tensor", [(2, 3), (1, 0)])
    return [value, one, two, jnp.where((index == 1) | (index == 2), inner, outer)]


def scatter_tensor(blocks):
    size = lax.axis_size("tensor")
    total = blocks[0].astype(jnp.float32)
    if size != 4:
        for k in range(1, size):
            total = total + swap(blocks[k], "tensor", k).astype(jnp.float32)
        return total
    outer = lax.ppermute(blocks[3], "tensor", [(0, 1), (3, 2)])
    one = swap(blocks[1], "tensor", 1)
    inner = lax.ppermute(blocks[3], "tensor", [(1, 2), (2, 1)])
    two = swap(blocks[2] + outer, "tensor", 2)
    return total + one.astype(jnp.float32) + inner.astype(jnp.float32) + two.astype(jnp.float32)


def local(tokens, norm_gain, query_weight, kv_weight, out_weight, grad_out, doc_lengths):
    tensor_size = lax.axis_size("tensor")
    data_size = lax.axis_size("dp")
    tensor_index = lax.axis_index("tensor")
    data_index = lax.axis_index("dp")
    core, chip = data_index & 1, data_index >> 1
    chips = data_size // 2
    sharers = tensor_size // KVH
    levels = sharers.bit_length() - 1
    rows, width = tokens.shape
    block = width // data_size
    length = rows * tensor_size
    query_width = query_weight.shape[1]
    out_width = out_weight.shape[0]
    contract_last = (((1,), (1,)), ((), ()))

    def columns(value, which):
        starts = [((chip ^ k) * 2 + which) * block for k in range(chips)]
        return jnp.concatenate(
            [lax.dynamic_slice(value, (0, start), (value.shape[0], block)) for start in starts], axis=1
        )

    def share(value):
        handed = swap(columns(value, 1 - core), "dp", 1)
        return jnp.concatenate([columns(value, core), handed], axis=0)

    def all_rows(value):
        return jnp.stack(gather_tensor(share(value)), axis=0).reshape(2 * length, width // 2)

    def join(product):
        split = product.reshape(tensor_size, 2, rows, product.shape[1])
        handed = swap(split[:, 1].astype(jnp.bfloat16), "dp", 1)
        return (split[:, 0] + handed.astype(jnp.float32)).astype(jnp.bfloat16).reshape(length, -1)

    out_blocks = gather_chips(out_weight)
    joint_blocks = gather_chips(jnp.concatenate([query_weight, kv_weight], axis=1))

    grad_rows = all_rows(grad_out)
    values32 = tokens.astype(jnp.float32)
    root_mean = jnp.sqrt(jnp.mean(values32 * values32, axis=-1) + epsilon)
    unit = values32 / root_mean[:, None]
    gain32 = norm_gain.astype(jnp.float32)
    normed = all_rows((unit * gain32).astype(jnp.bfloat16))

    out_grad = join(
        lax.dot_general(
            grad_rows,
            jnp.concatenate(out_blocks, axis=1),
            contract_last,
            preferred_element_type=jnp.float32,
        )
    )
    joint_weight = jnp.concatenate(joint_blocks, axis=0)
    projected = join(jnp.dot(normed, joint_weight, preferred_element_type=jnp.float32))
    queries = projected[:, :query_width]
    keyvals = projected[:, query_width:]
    for bit_index in range(levels):
        partner = swap(keyvals, "tensor", 2**bit_index)
        upper = tensor_index >> bit_index & 1 == 1
        keyvals = jnp.concatenate(
            [jnp.where(upper, partner, keyvals), jnp.where(upper, keyvals, partner)], axis=1
        )
    key_rows = keyvals[:, :HD]
    value_rows = keyvals[:, HD:]

    order = jnp.arange(length, dtype=jnp.int32)
    positions = ((order // rows) ^ tensor_index) * rows + order % rows
    ends = jnp.cumsum(doc_lengths[0])
    labels = jnp.sum((ends[None, :] <= positions[:, None]).astype(jnp.int32), axis=1)
    allowed = (labels[:, None] == labels[None, :]) & (positions[None, :] <= positions[:, None])

    local_heads = query_width // HD
    query_heads = queries.reshape(length, local_heads, HD)
    out_heads = out_grad.reshape(length, local_heads, HD)
    scores = jnp.einsum(
        "qhd,td->hqt", query_heads, key_rows, preferred_element_type=jnp.float32
    ) / math.sqrt(HD)
    scores = jnp.where(allowed[None, :, :], scores, -1e30)
    peak = jnp.max(scores, axis=-1, keepdims=True)
    expo = jnp.exp(scores - peak)
    probs = expo / jnp.sum(expo, axis=-1, keepdims=True)
    probs_low = probs.astype(jnp.bfloat16)
    prob_grad = jnp.einsum("qhd,td->hqt", out_heads, value_rows, preferred_element_type=jnp.float32)
    inner = jnp.sum(probs * prob_grad, axis=-1, keepdims=True)
    score_grad = (probs * (prob_grad - inner) / math.sqrt(HD)).astype(jnp.bfloat16)
    query_grad = jnp.einsum("hqt,td->qhd", score_grad, key_rows, preferred_element_type=jnp.float32)
    query_grad = query_grad.astype(jnp.bfloat16).reshape(length, local_heads * HD)
    key_part = jnp.einsum(
        "hqt,qhd->td", score_grad, query_heads, preferred_element_type=jnp.float32
    )
    value_part = jnp.einsum("hqt,qhd->td", probs_low, out_heads, preferred_element_type=jnp.float32)
    kv_partial = jnp.concatenate([key_part, value_part], axis=1)
    for bit_index in reversed(range(levels)):
        half_cols = kv_partial.shape[1] // 2
        upper = tensor_index >> bit_index & 1 == 1
        lower_cols = kv_partial[:, :half_cols]
        higher_cols = kv_partial[:, half_cols:]
        kept = jnp.where(upper, higher_cols, lower_cols)
        handed = jnp.where(upper, lower_cols, higher_cols)
        kv_partial = kept + swap(handed.astype(jnp.bfloat16), "tensor", 2**bit_index).astype(
            jnp.float32
        )
    combined = jnp.concatenate([query_grad, kv_partial.astype(jnp.bfloat16)], axis=1)
    joint_width = combined.shape[1]
    other = swap(combined, "dp", 1)
    both = jnp.stack(
        [
            combined.reshape(tensor_size, rows, joint_width),
            other.reshape(tensor_size, rows, joint_width),
        ],
        axis=1,
    ).reshape(2 * length, joint_width)

    weight_terms = lax.dot_general(
        normed, both, (((0,), (0,)), ((), ())), preferred_element_type=jnp.float32
    ).astype(jnp.bfloat16)
    weight_grads = (
        scatter_chips([weight_terms[k * block : (k + 1) * block] for k in range(chips)]) / data_size
    )

    row_terms = lax.dot_general(
        both, joint_weight, contract_last, preferred_element_type=jnp.float32
    ).astype(jnp.bfloat16)
    normed_part = scatter_tensor(
        [row_terms[k * 2 * rows : (k + 1) * 2 * rows] for k in range(tensor_size)]
    )
    handed = swap(normed_part[rows:].astype(jnp.bfloat16), "dp", 1).astype(jnp.float32)
    relative = jnp.concatenate([normed_part[:rows], handed], axis=1)
    normed_grad = jnp.concatenate(
        [
            lax.dynamic_slice(
                relative,
                (0, (((b & 1) ^ core) * chips + ((b >> 1) ^ chip)) * block),
                (rows, block),
            )
            for b in range(data_size)
        ],
        axis=1,
    )
    scaled = normed_grad * gain32
    correction = unit * jnp.mean(scaled * unit, axis=-1, keepdims=True)
    input_grad = (grad_out.astype(jnp.float32) + (scaled - correction) / root_mean[:, None]).astype(
        jnp.bfloat16
    )
    return (input_grad, weight_grads[:, :query_width], weight_grads[:, query_width:])


def solution(mesh):
    placed = (
        P(("dp", "tensor"), None),
        P(),
        P("dp", "tensor"),
        P("dp", "tensor"),
        P("tensor", "dp"),
        P(("dp", "tensor"), None),
        P("dp", None),
    )
    return jax.shard_map(
        local,
        mesh=mesh,
        in_specs=placed,
        out_specs=(P(("dp", "tensor"), None), P("dp", "tensor"), P("dp", "tensor")),
        check_vma=False,
    )
```

time: 419 us -> 245 us (0.58)
  waiting for transfers between devices: 346 us -> 111 us
  starting transfers between devices: 0.45 us -> 57.9 us
  local copies, waits for them, and re-layouts: 3.87 us -> 20.3 us
  between operations: 14.3 us -> 1.46 us
  matrix products: 44.2 us -> 32.2 us
  other arithmetic: 9.46 us -> 20.3 us
    all_gather x5 -> x0, waiting for transfers between devices: 225 us -> none  [the longest x1 56.9 us: local(): lax.all_gather(out_weight, 'dp', axis=1, tiled=True)]
    reduce_scatter x2 -> x0, waiting for transfers between devices: 119 us -> none  [the longest x1 81.4 us: local(): lax.psum_scatter(lax.dot_general(normed, combined, (((0,), (0,)), ((), ()...]
    ppermute x0 -> x32, waiting for transfers between devices: none -> 111 us  [the longest x26 92.8 us: swap(): return lax.ppermute(value, axis, pairs)]
    ppermute x0 -> x32, starting transfers between devices: none -> 57.9 us  [the longest x26 51.2 us: swap(): return lax.ppermute(value, axis, pairs)]
    dot_general x6 -> x4, matrix products: 29.4 us -> 18.7 us  [the longest x1 5.7 us: local(): lax.dot_general(both, joint_weight, contract_last, preferred_element_type...]
    unnamed x10 -> x59, local copies, waits for them, and re-layouts: 0.02 us -> 8.9 us
    add x0 -> x6, other arithmetic: none -> 4.96 us  [the longest x1 1.87 us: scatter_chips(): x_top = swap(blocks[1][:half] + far_top, 'dp', 2)]
    slice x0 -> x10, local copies, waits for them, and re-layouts: none -> 4.24 us  [the longest x2 1.12 us: gather_chips(): far_bottom = swap(near_y[half:], 'dp', 2)]
  transfers between devices with their start and end apart: 7 -> 32, of which waited for: 7 -> 9; matrix products, arithmetic and copies ran while one was open for 5% -> 15% of each run, Pallas kernels for 0% -> 0%
where the time goes in v1:
time: 245 us; the launch traced here: 244 us
  waiting for transfers between devices  111 us (45%)
  starting transfers between devices  57.9 us (24%)
  matrix products  32.2 us (13%)
  other arithmetic  20.3 us (8%)
  local copies, waits for them, and re-layouts  20.3 us (8%)
    ppermute x26, waiting for transfers between devices, swap(): return lax.ppermute(value, axis, pairs)  92.8 us
    ppermute x26, starting transfers between devices, swap(): return lax.ppermute(value, axis, pairs)  51.2 us
    ppermute x2, waiting for transfers between devices, gather_tensor(): outer = lax.ppermute(two, 'tensor', [(2, 3), (1, 0)])  10.1 us
    unnamed x59, local copies, waits for them, and re-layouts  8.9 us
    ppermute x1, waiting for transfers between devices, scatter_tensor(): outer = lax.ppermute(blocks[3], 'tensor', [(0, 1), (3, 2)])  8.57 us
    dot_general x1, matrix products, local(): lax.dot_general(both, joint_weight, contract_last, preferred_element_type...  5.7 us
    dot_general x1, matrix products, local(): jnp.dot(normed, joint_weight, preferred_element_type=jnp.float32)  4.92 us
  transfers between devices with their start and end apart: 32, of which 9 were waited for; matrix products, arithmetic and copies ran while one was open for 15% of the time, Pallas kernels for 0%

profile of v1, /device:TPU:1, one launch (start us, length us, event | category | flops | bytes accessed | tf_op | source)
XLA Modules:
  0.0 243.7 jit_solution(9796039781809929253)
XLA Ops:
  5.4 2.7 %collective-permute-start.16 = (bf16[1024,512]{1,0:T(8,128)(2,1)}, bf16[1024,512]{1,0:T(8,128)(2,1)}, u32[]{:S(2)}, u32[]{:S(2)}) collective-permute-start(bf16[1024,512]{1,0:T(8,128)(2,1)} %param.11), channel_id=1, source_target_pairs={{0,16},{4,20},{8,24},{12,28},{16,0},{20,4},{24,8},{28,12},{1,17},{... | collective-permute-start | bytes 3145736 | tf_op jit(solution)/shard_map/ppermute | solution.py:16
  10.9 2.3 collective-permute-start.12
  13.2 1.7 constant_dynamic-update-slice_fusion.1
  17.1 19.7 %collective-permute-done.12 = bf16[128,2048]{1,0:T(8,128)(2,1)} collective-permute-done((bf16[128,2048]{1,0:T(8,128)(2,1)}, bf16[128,2048]{1,0:T(8,128)(2,1)}, u32[]{:S(2)}, u32[]{:S(2)}) %collective-permute-start.12) | collective-permute-done | bytes 524320 | tf_op jit(solution)/shard_map/ppermute | solution.py:16
  37.6 3.2 %collective-permute-start.2 = (bf16[128,2048]{1,0:T(8,128)(2,1)}, bf16[128,2048]{1,0:T(8,128)(2,1)}, u32[]{:S(2)}, u32[]{:S(2)}) collective-permute-start(bf16[128,2048]{1,0:T(8,128)(2,1)} %pad_maximum_fusion.3), channel_id=1, source_target_pairs={{0,2},{1,3},{2,0},{3,1},{4,6},{5,7},{6,4},{7,5},{8,10},{9,11},{10,... | collective-permute-start | bytes 1572872 | tf_op jit(solution)/shard_map/ppermute | solution.py:16
  44.3 19.8 %collective-permute-start.11 = (bf16[128,2048]{1,0:T(8,128)(2,1)}, bf16[128,2048]{1,0:T(8,128)(2,1)S(1)}, u32[]{:S(2)}, u32[]{:S(2)}) collective-permute-start(bf16[128,2048]{1,0:T(8,128)(2,1)} %pad_maximum_fusion.4), channel_id=1, source_target_pairs={{0,1},{1,0},{2,3},{3,2},{4,5},{5,4},{6,7},{7,6},{8,9},{9,8},{10,11... | collective-permute-start | bytes 1572872 | tf_op jit(solution)/shard_map/ppermute | solution.py:16
  64.0 11.1 %collective-permute-done.2 = bf16[128,2048]{1,0:T(8,128)(2,1)} collective-permute-done((bf16[128,2048]{1,0:T(8,128)(2,1)}, bf16[128,2048]{1,0:T(8,128)(2,1)}, u32[]{:S(2)}, u32[]{:S(2)}) %collective-permute-start.2) | collective-permute-done | bytes 524320 | tf_op jit(solution)/shard_map/ppermute | solution.py:16
  81.1 7.0 %collective-permute-start.1 = (bf16[128,2048]{1,0:T(8,128)(2,1)}, bf16[128,2048]{1,0:T(8,128)(2,1)S(1)}, u32[]{:S(2)}, u32[]{:S(2)}) collective-permute-start(bf16[128,2048]{1,0:T(8,128)(2,1)} %pad_maximum_fusion.3), channel_id=1, source_target_pairs={{0,1},{1,0},{2,3},{3,2},{4,5},{5,4},{6,7},{7,6},{8,9},{9,8},{10,11... | collective-permute-start | bytes 1572872 | tf_op jit(solution)/shard_map/ppermute | solution.py:16
  88.1 10.1 %collective-permute-done.4 = bf16[128,2048]{1,0:T(8,128)(2,1)S(1)} collective-permute-done((bf16[128,2048]{1,0:T(8,128)(2,1)}, bf16[128,2048]{1,0:T(8,128)(2,1)S(1)}, u32[]{:S(2)}, u32[]{:S(2)}) %collective-permute-start.4) | collective-permute-done | bytes 524320 | tf_op jit(solution)/shard_map/ppermute | solution.py:58
  98.7 4.9 %fusion.4 = f32[4,2,64,1024]{3,2,1,0:T(8,128)S(1)} fusion(bf16[512,512]{1,0:T(8,128)(2,1)S(1)} %collective-permute-done.18, bf16[512,512]{1,0:T(8,128)(2,1)S(1)} %collective-permute-done.17, bf16[1024,512]{1,0:T(8,128)(2,1)} %collective-permute-done.16, bf16[1024,512]{1,0:T(8,128)(2,1)} %collective-permute-done.15, bf16[1024,512]{1,0:T(8,128)(2,1)} %param.11, ...), kind=kOutput, calls=%fused_computation.6 | convolution fusion | flops 2171600896 | bytes 8388608 | tf_op jit(solution)/shard_map/dot_general | solution.py:121
  105.9 8.0 %collective-permute-done.7 = bf16[256,1280]{1,0:T(8,128)(2,1)S(1)} collective-permute-done((bf16[256,1280]{1,0:T(8,128)(2,1)S(1)}, bf16[256,1280]{1,0:T(8,128)(2,1)S(1)}, u32[]{:S(2)}, u32[]{:S(2)}) %collective-permute-start.7) | collective-permute-done | bytes 655392 | tf_op jit(solution)/shard_map/ppermute | solution.py:16
  114.0 4.9 %fusion.2 = f32[4,2,64,1280]{3,2,1,0:T(8,128)S(1)} fusion(bf16[2048,1280]{1,0:T(8,128)(2,1)S(1)} %constant_dynamic-update-slice_fusion.2, bf16[1,2,64,2048]{3,2,1,0:T(8,128)(2,1)S(1)} %bitcast.122, bf16[1,2,64,2048]{3,2,1,0:T(8,128)(2,1)} %bitcast.2, bf16[1,2,64,2048]{3,2,1,0:T(8,128)(2,1)S(1)} %bitcast.130, bf16[1,2,64,2048]{3,2,1,0:T(8,128)(2,1)} %bitcast), kind=kOutput, calls=%fused_computation.3 | convolution fusion | flops 2687500288 | bytes 9961472 | tf_op jit(solution)/shard_map/dot_general | solution.py:129
  119.0 1.5 copy-done.5
  121.4 1.8 collective-permute-start.9
  127.2 3.7 %fusion.82 = (f32[8,256]{1,0:T(8,128)}, f32[8,256,256]{1,2,0:T(8,128)}) fusion(pred[256,256]{0,1:T(8,128)(4,1)} %compare_and_fusion, bf16[256,8,128]{0,2,1:T(8,128)(2,1)} %bitcast.128, bf16[256,1280]{1,0:T(8,128)(2,1)S(1)} %bitcast.114), kind=kOutput, calls=%fused_computation.169 | convolution fusion | flops 136315136 | bytes 2760704 | tf_op jit(solution)/shard_map/sub | solution.py:155
  130.9 2.7 %fusion.35 = bf16[256,128]{1,0:T(8,128)(2,1)} fusion(bf16[256,8,128]{2,1,0:T(8,128)(2,1)S(1)} %bitcast.120, f32[8,256,256]{1,2,0:T(8,128)} %get-tuple-element.30, f32[8,256]{1,0:T(8,128)} %get-tuple-element.29), kind=kOutput, calls=%fused_computation.70 | convolution fusion | flops 135299072 | bytes 2695168 | tf_op jit(solution)/shard_map/hqt,qhd->td/dot_general | solution.py:166
  133.6 3.7 %fusion.34 = bf16[256,128]{1,0:T(8,128)(2,1)} fusion(bf16[256,8,128]{0,2,1:T(8,128)(2,1)} %bitcast.129, f32[256,256,8]{1,0,2:T(8,128)S(1)} %fusion.47, f32[8,256,256]{1,2,0:T(8,128)} %get-tuple-element.30, f32[8,256]{1,0:T(8,128)} %get-tuple-element.29), kind=kOutput, calls=%fused_computation.69 | convolution fusion | flops 137922816 | bytes 4792320 | tf_op jit(solution)/shard_map/hqt,qhd->td/dot_general | solution.py:163
  137.3 3.0 %convolution_convert_fusion.2 = bf16[128,8,256]{2,0,1:T(8,128)(2,1)S(1)} fusion(f32[256,256,8]{1,0,2:T(8,128)S(1)} %fusion.47, bf16[256,1280]{1,0:T(8,128)(2,1)S(1)} %bitcast.115, f32[8,256,256]{1,2,0:T(8,128)} %get-tuple-element.30, f32[8,256]{1,0:T(8,128)} %get-tuple-element.29), kind=kOutput, calls=%fused_computation.66 | convolution fusion | flops 138152192 | bytes 8994816 | tf_op jit(solution)/shard_map/hqt,td->qhd/dot_general | solution.py:161
  142.1 1.5 collective-permute-done.20
  143.9 5.7 %convolution_convert_fusion.1 = bf16[512,2048]{1,0:T(8,128)(2,1)S(1)} fusion(bf16[512,1280]{1,0:T(8,128)(2,1)S(1)} %bitcast.124, bf16[2048,1280]{1,0:T(8,128)(2,1)} %copy-done.21), kind=kOutput, calls=%fused_computation.15 | convolution fusion | flops 2685403136 | bytes 8650752 | tf_op jit(solution)/shard_map/dot_general | solution.py:196
  154.7 8.6 %collective-permute-done.23 = bf16[128,2048]{1,0:T(8,128)(2,1)S(1)} collective-permute-done((bf16[128,2048]{1,0:T(8,128)(2,1)}, bf16[128,2048]{1,0:T(8,128)(2,1)S(1)}, u32[]{:S(2)}, u32[]{:S(2)}) %collective-permute-start.23) | collective-permute-done | bytes 524320 | tf_op jit(solution)/shard_map/ppermute | solution.py:69
  164.3 1.9 collective-permute-start.24
  166.5 3.2 %convolution_convert_fusion = bf16[2048,1280]{1,0:T(8,128)(2,1)S(1)} fusion(bf16[512,2048]{1,0:T(8,128)(2,1)S(1)} %bitcast.116, bf16[512,1280]{1,0:T(8,128)(2,1)S(1)} %bitcast.125), kind=kOutput, calls=%fused_computation.2 | convolution fusion | flops 2686976000 | bytes 8650752 | tf_op jit(solution)/shard_map/dot_general | solution.py:189
  169.7 2.3 copy-done.1
  173.3 16.3 %collective-permute-done.24 = bf16[128,2048]{1,0:T(8,128)(2,1)} collective-permute-done((bf16[128,2048]{1,0:T(8,128)(2,1)}, bf16[128,2048]{1,0:T(8,128)(2,1)}, u32[]{:S(2)}, u32[]{:S(2)}) %collective-permute-start.24) | collective-permute-done | bytes 524320 | tf_op jit(solution)/shard_map/ppermute | solution.py:16
  189.6 1.7 convert_add_fusion.2
  191.3 1.7 collective-permute-start.25
  193.0 1.9 slice_add_fusion.1
  199.6 11.7 %collective-permute-done.30 = bf16[256,1280]{1,0:T(8,128)(2,1)S(1)} collective-permute-done((bf16[256,1280]{1,0:T(8,128)(2,1)S(1)}, bf16[256,1280]{1,0:T(8,128)(2,1)S(1)}, u32[]{:S(2)}, u32[]{:S(2)}) %collective-permute-start.30) | collective-permute-done | bytes 655392 | tf_op jit(solution)/shard_map/ppermute | solution.py:16
  214.9 24.5 %collective-permute-done.27 = bf16[256,1280]{1,0:T(8,128)(2,1)S(1)} collective-permute-done((bf16[256,1280]{1,0:T(8,128)(2,1)S(1)}, bf16[256,1280]{1,0:T(8,128)(2,1)S(1)}, u32[]{:S(2)}, u32[]{:S(2)}) %collective-permute-start.27) | collective-permute-done | bytes 655392 | tf_op jit(solution)/shard_map/ppermute | solution.py:16
  239.7 1.6 fusion.13
  241.3 1.6 slice.143
  (161 shorter events, 46.4 us)
Async XLA Ops:
  5.3 4.8 %collective-permute-start.10 = (bf16[64,2048]{1,0:T(8,128)(2,1)S(1)}, bf16[64,2048]{1,0:T(8,128)(2,1)S(1)}, u32[]{:S(2)}, u32[]{:S(2)}) collective-permute-start(bf16[64,2048]{1,0:T(8,128)(2,1)S(1)} %pad_maximum_fusion.6), channel_id=1, source_target_pairs={{0,4},{4,0},{8,12},{12,8},{16,20},{20,16},{24,28},{28,24},{1,5},{5... | collective-permute-start | bytes 786440 | tf_op jit(solution)/shard_map/ppermute | solution.py:16
  5.4 32.2 %collective-permute-start.16 = (bf16[1024,512]{1,0:T(8,128)(2,1)}, bf16[1024,512]{1,0:T(8,128)(2,1)}, u32[]{:S(2)}, u32[]{:S(2)}) collective-permute-start(bf16[1024,512]{1,0:T(8,128)(2,1)} %param.11), channel_id=1, source_target_pairs={{0,16},{4,20},{8,24},{12,28},{16,0},{20,4},{24,8},{28,12},{1,17},{... | collective-permute-start | bytes 3145736 | tf_op jit(solution)/shard_map/ppermute | solution.py:16
  8.1 32.7 %collective-permute-start.15 = (bf16[1024,512]{1,0:T(8,128)(2,1)}, bf16[1024,512]{1,0:T(8,128)(2,1)}, u32[]{:S(2)}, u32[]{:S(2)}) collective-permute-start(bf16[1024,512]{1,0:T(8,128)(2,1)} %param.11), channel_id=1, source_target_pairs={{0,8},{4,12},{8,0},{12,4},{16,24},{20,28},{24,16},{28,20},{1,9},{5... | collective-permute-start | bytes 3145736 | tf_op jit(solution)/shard_map/ppermute | solution.py:16
  9.3 6.7 %collective-permute-start = (bf16[64,2048]{1,0:T(8,128)(2,1)S(1)}, bf16[64,2048]{1,0:T(8,128)(2,1)S(1)}, u32[]{:S(2)}, u32[]{:S(2)}) collective-permute-start(bf16[64,2048]{1,0:T(8,128)(2,1)S(1)} %pad_maximum_fusion.5), channel_id=1, source_target_pairs={{0,4},{4,0},{8,12},{12,8},{16,20},{20,16},{24,28},{28,24},{1,5},{5... | collective-permute-start | bytes 786440 | tf_op jit(solution)/shard_map/ppermute | solution.py:16
  10.9 26.0 %collective-permute-start.12 = (bf16[128,2048]{1,0:T(8,128)(2,1)}, bf16[128,2048]{1,0:T(8,128)(2,1)}, u32[]{:S(2)}, u32[]{:S(2)}) collective-permute-start(bf16[128,2048]{1,0:T(8,128)(2,1)} %pad_maximum_fusion.4), channel_id=1, source_target_pairs={{0,2},{1,3},{2,0},{3,1},{4,6},{5,7},{6,4},{7,5},{8,10},{9,11},{10,... | collective-permute-start | bytes 1572872 | tf_op jit(solution)/shard_map/ppermute | solution.py:16
  15.8 62.4 %collective-permute-start.5 = (bf16[512,1280]{1,0:T(8,128)(2,1)}, bf16[512,1280]{1,0:T(8,128)(2,1)S(1)}, u32[]{:S(2)}, u32[]{:S(2)}) collective-permute-start(bf16[512,1280]{1,0:T(8,128)(2,1)} %get-tuple-element.27), channel_id=1, source_target_pairs={{0,8},{4,12},{8,0},{12,4},{16,24},{20,28},{24,16},{28,20},{1,9},{5... | collective-permute-start | bytes 3932168 | tf_op jit(solution)/shard_map/ppermute | solution.py:16
  16.0 63.7 %collective-permute-start.6 = (bf16[512,1280]{1,0:T(8,128)(2,1)}, bf16[512,1280]{1,0:T(8,128)(2,1)S(1)}, u32[]{:S(2)}, u32[]{:S(2)}) collective-permute-start(bf16[512,1280]{1,0:T(8,128)(2,1)} %get-tuple-element.27), channel_id=1, source_target_pairs={{0,16},{4,20},{8,24},{12,28},{16,0},{20,4},{24,8},{28,12},{1,17},{... | collective-permute-start | bytes 3932168 | tf_op jit(solution)/shard_map/ppermute | solution.py:16
  36.9 7.4 %collective-permute-start.13 = (bf16[128,2048]{1,0:T(8,128)(2,1)}, bf16[128,2048]{1,0:T(8,128)(2,1)S(1)}, u32[]{:S(2)}, u32[]{:S(2)}) collective-permute-start(bf16[128,2048]{1,0:T(8,128)(2,1)} %pad_maximum_fusion.4), channel_id=1, source_target_pairs={{1,2},{2,1},{5,6},{6,5},{9,10},{10,9},{13,14},{14,13},{17,18},{18,... | collective-permute-start | bytes 1572872 | tf_op jit(solution)/shard_map/ppermute | solution.py:57
  37.6 37.6 %collective-permute-start.2 = (bf16[128,2048]{1,0:T(8,128)(2,1)}, bf16[128,2048]{1,0:T(8,128)(2,1)}, u32[]{:S(2)}, u32[]{:S(2)}) collective-permute-start(bf16[128,2048]{1,0:T(8,128)(2,1)} %pad_maximum_fusion.3), channel_id=1, source_target_pairs={{0,2},{1,3},{2,0},{3,1},{4,6},{5,7},{6,4},{7,5},{8,10},{9,11},{10,... | collective-permute-start | bytes 1572872 | tf_op jit(solution)/shard_map/ppermute | solution.py:16
  40.8 35.0 %collective-permute-start.14 = (bf16[128,2048]{1,0:T(8,128)(2,1)}, bf16[128,2048]{1,0:T(8,128)(2,1)}, u32[]{:S(2)}, u32[]{:S(2)}) collective-permute-start(bf16[128,2048]{1,0:T(8,128)(2,1)} %collective-permute-done.12), channel_id=1, source_target_pairs={{2,3},{1,0},{6,7},{5,4},{10,11},{9,8},{14,15},{13,12},{18,19},{17,... | collective-permute-start | bytes 1572872 | tf_op jit(solution)/shard_map/ppermute | solution.py:58
  44.3 54.2 %collective-permute-start.11 = (bf16[128,2048]{1,0:T(8,128)(2,1)}, bf16[128,2048]{1,0:T(8,128)(2,1)S(1)}, u32[]{:S(2)}, u32[]{:S(2)}) collective-permute-start(bf16[128,2048]{1,0:T(8,128)(2,1)} %pad_maximum_fusion.4), channel_id=1, source_target_pairs={{0,1},{1,0},{2,3},{3,2},{4,5},{5,4},{6,7},{7,6},{8,9},{9,8},{10,11... | collective-permute-start | bytes 1572872 | tf_op jit(solution)/shard_map/ppermute | solution.py:16
  75.1 6.0 %collective-permute-start.3 = (bf16[128,2048]{1,0:T(8,128)(2,1)}, bf16[128,2048]{1,0:T(8,128)(2,1)S(1)}, u32[]{:S(2)}, u32[]{:S(2)}) collective-permute-start(bf16[128,2048]{1,0:T(8,128)(2,1)} %pad_maximum_fusion.3), channel_id=1, source_target_pairs={{1,2},{2,1},{5,6},{6,5},{9,10},{10,9},{13,14},{14,13},{17,18},{18,... | collective-permute-start | bytes 1572872 | tf_op jit(solution)/shard_map/ppermute | solution.py:57
  75.8 22.4 %collective-permute-start.4 = (bf16[128,2048]{1,0:T(8,128)(2,1)}, bf16[128,2048]{1,0:T(8,128)(2,1)S(1)}, u32[]{:S(2)}, u32[]{:S(2)}) collective-permute-start(bf16[128,2048]{1,0:T(8,128)(2,1)} %collective-permute-done.2), channel_id=1, source_target_pairs={{2,3},{1,0},{6,7},{5,4},{10,11},{9,8},{14,15},{13,12},{18,19},{17,... | collective-permute-start | bytes 1572872 | tf_op jit(solution)/shard_map/ppermute | solution.py:58
  78.2 20.5 %collective-permute-start.18 = (bf16[512,512]{1,0:T(8,128)(2,1)S(1)}, bf16[512,512]{1,0:T(8,128)(2,1)S(1)}, u32[]{:S(2)}, u32[]{:S(2)}) collective-permute-start(bf16[512,512]{1,0:T(8,128)(2,1)S(1)} %slice.127), channel_id=1, source_target_pairs={{0,8},{4,12},{8,0},{12,4},{16,24},{20,28},{24,16},{28,20},{1,9},{5... | collective-permute-start | bytes 1572872 | tf_op jit(solution)/shard_map/ppermute | solution.py:16
  79.7 19.0 %collective-permute-start.17 = (bf16[512,512]{1,0:T(8,128)(2,1)S(1)}, bf16[512,512]{1,0:T(8,128)(2,1)S(1)}, u32[]{:S(2)}, u32[]{:S(2)}) collective-permute-start(bf16[512,512]{1,0:T(8,128)(2,1)S(1)} %slice.126), channel_id=1, source_target_pairs={{0,16},{4,20},{8,24},{12,28},{16,0},{20,4},{24,8},{28,12},{1,17},{... | collective-permute-start | bytes 1572872 | tf_op jit(solution)/shard_map/ppermute | solution.py:16
  81.1 32.9 %collective-permute-start.1 = (bf16[128,2048]{1,0:T(8,128)(2,1)}, bf16[128,2048]{1,0:T(8,128)(2,1)S(1)}, u32[]{:S(2)}, u32[]{:S(2)}) collective-permute-start(bf16[128,2048]{1,0:T(8,128)(2,1)} %pad_maximum_fusion.3), channel_id=1, source_target_pairs={{0,1},{1,0},{2,3},{3,2},{4,5},{5,4},{6,7},{7,6},{8,9},{9,8},{10,11... | collective-permute-start | bytes 1572872 | tf_op jit(solution)/shard_map/ppermute | solution.py:16
  98.2 15.7 %collective-permute-start.7 = (bf16[256,1280]{1,0:T(8,128)(2,1)S(1)}, bf16[256,1280]{1,0:T(8,128)(2,1)S(1)}, u32[]{:S(2)}, u32[]{:S(2)}) collective-permute-start(bf16[256,1280]{1,0:T(8,128)(2,1)S(1)} %slice.119), channel_id=1, source_target_pairs={{0,16},{4,20},{8,24},{12,28},{16,0},{20,4},{24,8},{28,12},{1,17},{... | collective-permute-start | bytes 1966088 | tf_op jit(solution)/shard_map/ppermute | solution.py:16
  98.5 15.4 %collective-permute-start.8 = (bf16[256,1280]{1,0:T(8,128)(2,1)S(1)}, bf16[256,1280]{1,0:T(8,128)(2,1)S(1)}, u32[]{:S(2)}, u32[]{:S(2)}) collective-permute-start(bf16[256,1280]{1,0:T(8,128)(2,1)S(1)} %slice.120), channel_id=1, source_target_pairs={{0,8},{4,12},{8,0},{12,4},{16,24},{20,28},{24,16},{28,20},{1,9},{5... | collective-permute-start | bytes 1966088 | tf_op jit(solution)/shard_map/ppermute | solution.py:16
  104.5 19.7 %collective-permute-start.19 = (bf16[4,64,1024]{2,1,0:T(8,128)(2,1)}, bf16[4,64,1024]{2,1,0:T(8,128)(2,1)}, u32[]{:S(2)}, u32[]{:S(2)}) collective-permute-start(bf16[4,64,1024]{2,1,0:T(8,128)(2,1)} %fusion.45), channel_id=1, source_target_pairs={{0,4},{4,0},{8,12},{12,8},{16,20},{20,16},{24,28},{28,24},{1,5},{5... | collective-permute-start | bytes 1572872 | tf_op jit(solution)/shard_map/ppermute | solution.py:16
  121.4 4.1 %collective-permute-start.9 = (bf16[4,64,1280]{2,1,0:T(8,128)(2,1)}, bf16[4,64,1280]{2,1,0:T(8,128)(2,1)S(1)}, u32[]{:S(2)}, u32[]{:S(2)}) collective-permute-start(bf16[4,64,1280]{2,1,0:T(8,128)(2,1)} %fusion.44), channel_id=1, source_target_pairs={{0,4},{4,0},{8,12},{12,8},{16,20},{20,16},{24,28},{28,24},{1,5},{5... | collective-permute-start | bytes 1966088 | tf_op jit(solution)/shard_map/ppermute | solution.py:16
  141.5 2.2 collective-permute-start.20
  150.4 12.8 %collective-permute-start.23 = (bf16[128,2048]{1,0:T(8,128)(2,1)}, bf16[128,2048]{1,0:T(8,128)(2,1)S(1)}, u32[]{:S(2)}, u32[]{:S(2)}) collective-permute-start(bf16[128,2048]{1,0:T(8,128)(2,1)} %slice.132), channel_id=1, source_target_pairs={{0,1},{3,2},{4,5},{7,6},{8,9},{11,10},{12,13},{15,14},{16,17},{19,... | collective-permute-start | bytes 1572872 | tf_op jit(solution)/shard_map/ppermute | solution.py:69
  153.2 20.2 %collective-permute-start.22 = (bf16[128,2048]{1,0:T(8,128)(2,1)}, bf16[128,2048]{1,0:T(8,128)(2,1)}, u32[]{:S(2)}, u32[]{:S(2)}) collective-permute-start(bf16[128,2048]{1,0:T(8,128)(2,1)} %slice.132), channel_id=1, source_target_pairs={{1,2},{2,1},{5,6},{6,5},{9,10},{10,9},{13,14},{14,13},{17,18},{18,... | collective-permute-start | bytes 1572872 | tf_op jit(solution)/shard_map/ppermute | solution.py:71
  164.3 25.3 %collective-permute-start.24 = (bf16[128,2048]{1,0:T(8,128)(2,1)}, bf16[128,2048]{1,0:T(8,128)(2,1)}, u32[]{:S(2)}, u32[]{:S(2)}) collective-permute-start(bf16[128,2048]{1,0:T(8,128)(2,1)} %get-tuple-element.8), channel_id=1, source_target_pairs={{0,2},{1,3},{2,0},{3,1},{4,6},{5,7},{6,4},{7,5},{8,10},{9,11},{10,... | collective-permute-start | bytes 1572872 | tf_op jit(solution)/shard_map/ppermute | solution.py:16
  166.2 23.4 %collective-permute-start.21 = (bf16[128,2048]{1,0:T(8,128)(2,1)}, bf16[128,2048]{1,0:T(8,128)(2,1)}, u32[]{:S(2)}, u32[]{:S(2)}) collective-permute-start(bf16[128,2048]{1,0:T(8,128)(2,1)} %get-tuple-element.7), channel_id=1, source_target_pairs={{0,1},{1,0},{2,3},{3,2},{4,5},{5,4},{6,7},{7,6},{8,9},{9,8},{10,11... | collective-permute-start | bytes 1572872 | tf_op jit(solution)/shard_map/ppermute | solution.py:16
  172.0 21.0 %collective-permute-start.26 = (bf16[256,1280]{1,0:T(8,128)(2,1)S(1)}, bf16[256,1280]{1,0:T(8,128)(2,1)S(1)}, u32[]{:S(2)}, u32[]{:S(2)}) collective-permute-start(bf16[256,1280]{1,0:T(8,128)(2,1)S(1)} %slice.138), channel_id=1, source_target_pairs={{0,16},{4,20},{8,24},{12,28},{16,0},{20,4},{24,8},{28,12},{1,17},{... | collective-permute-start | bytes 1966088 | tf_op jit(solution)/shard_map/ppermute | solution.py:16
  191.3 6.7 %collective-permute-start.25 = (bf16[64,2048]{1,0:T(8,128)(2,1)S(1)}, bf16[64,2048]{1,0:T(8,128)(2,1)S(1)}, u32[]{:S(2)}, u32[]{:S(2)}) collective-permute-start(bf16[64,2048]{1,0:T(8,128)(2,1)S(1)} %slice.176), channel_id=1, source_target_pairs={{0,4},{4,0},{8,12},{12,8},{16,20},{20,16},{24,28},{28,24},{1,5},{5... | collective-permute-start | bytes 786440 | tf_op jit(solution)/shard_map/ppermute | solution.py:16
  194.9 16.4 %collective-permute-start.30 = (bf16[256,1280]{1,0:T(8,128)(2,1)S(1)}, bf16[256,1280]{1,0:T(8,128)(2,1)S(1)}, u32[]{:S(2)}, u32[]{:S(2)}) collective-permute-start(bf16[256,1280]{1,0:T(8,128)(2,1)S(1)} %get-tuple-element.4), channel_id=1, source_target_pairs={{0,8},{4,12},{8,0},{12,4},{16,24},{20,28},{24,16},{28,20},{1,9},{5... | collective-permute-start | bytes 1966088 | tf_op jit(solution)/shard_map/ppermute | solution.py:16
  195.1 44.4 %collective-permute-start.29 = (bf16[256,1280]{1,0:T(8,128)(2,1)S(1)}, bf16[256,1280]{1,0:T(8,128)(2,1)S(1)}, u32[]{:S(2)}, u32[]{:S(2)}) collective-permute-start(bf16[256,1280]{1,0:T(8,128)(2,1)S(1)} %get-tuple-element.5), channel_id=1, source_target_pairs={{0,8},{4,12},{8,0},{12,4},{16,24},{20,28},{24,16},{28,20},{1,9},{5... | collective-permute-start | bytes 1966088 | tf_op jit(solution)/shard_map/ppermute | solution.py:16
  196.4 18.5 %collective-permute-start.28 = (bf16[256,1280]{1,0:T(8,128)(2,1)S(1)}, bf16[256,1280]{1,0:T(8,128)(2,1)S(1)}, u32[]{:S(2)}, u32[]{:S(2)}) collective-permute-start(bf16[256,1280]{1,0:T(8,128)(2,1)S(1)} %get-tuple-element.6), channel_id=1, source_target_pairs={{0,16},{4,20},{8,24},{12,28},{16,0},{20,4},{24,8},{28,12},{1,17},{... | collective-permute-start | bytes 1966088 | tf_op jit(solution)/shard_map/ppermute | solution.py:16
  197.7 41.7 %collective-permute-start.27 = (bf16[256,1280]{1,0:T(8,128)(2,1)S(1)}, bf16[256,1280]{1,0:T(8,128)(2,1)S(1)}, u32[]{:S(2)}, u32[]{:S(2)}) collective-permute-start(bf16[256,1280]{1,0:T(8,128)(2,1)S(1)} %get-tuple-element.3), channel_id=1, source_target_pairs={{0,8},{4,12},{8,0},{12,4},{16,24},{20,28},{24,16},{28,20},{1,9},{5... | collective-permute-start | bytes 1966088 | tf_op jit(solution)/shard_map/ppermute | solution.py:16
  212.5 27.1 %collective-permute-start.31 = (bf16[256,1280]{1,0:T(8,128)(2,1)S(1)}, bf16[256,1280]{1,0:T(8,128)(2,1)S(1)}, u32[]{:S(2)}, u32[]{:S(2)}) collective-permute-start(bf16[256,1280]{1,0:T(8,128)(2,1)S(1)} %slice_add_fusion), channel_id=1, source_target_pairs={{0,16},{4,20},{8,24},{12,28},{16,0},{20,4},{24,8},{28,12},{1,17},{... | collective-permute-start | bytes 1966088 | tf_op jit(solution)/shard_map/ppermute | solution.py:16
  (27 other events, 196.6 us)

commit v2 on v1

--- a/solution.py
+++ b/solution.py
@@ -16,61 +16,92 @@
     return lax.ppermute(value, axis, pairs)
 
 
-def gather_chips(value):
+def in_step(*streams):
+    results = [None] * len(streams)
+    waiting = {number: next(stream) for number, stream in enumerate(streams)}
+    while waiting:
+        ready = lax.optimization_barrier(tuple(waiting.values()))
+        following = {}
+        for number, values in zip(list(waiting), ready):
+            try:
+                following[number] = streams[number].send(values)
+            except StopIteration as end:
+                results[number] = end.value
+        waiting = following
+    return results
+
+
+def gather_chips(value, then=()):
     chips = lax.axis_size("dp") // 2
     if chips != 4:
-        return [value] + [swap(value, "dp", 2 * k) for k in range(1, chips)]
+        blocks = [value] + [swap(value, "dp", 2 * k) for k in range(1, chips)]
+        blocks, then = yield (blocks, then)
+        return blocks, then
     half = value.shape[0] // 2
     near_x = swap(value, "dp", 2)
     near_y = swap(value, "dp", 4)
+    value, near_x, near_y, then = yield (value, near_x, near_y, then)
     far_top = swap(near_x[:half], "dp", 4)
     far_bottom = swap(near_y[half:], "dp", 2)
-    return [value, near_x, near_y, jnp.concatenate([far_top, far_bottom], axis=0)]
+    far_top, far_bottom, then = yield (far_top, far_bottom, then)
+    return [value, near_x, near_y, jnp.concatenate([far_top, far_bottom], axis=0)], then
 
 
 def scatter_chips(blocks):
     chips = lax.axis_size("dp") // 2
-    total = blocks[0].astype(jnp.float32)
     if chips != 4:
-        for k in range(1, chips):
-            total = total + swap(blocks[k], "dp", 2 * k).astype(jnp.float32)
-        return total
+        parts = [blocks[0]] + [swap(blocks[k], "dp", 2 * k) for k in range(1, chips)]
+        parts = yield parts
+        return sum(part.astype(jnp.float32) for part in parts)
     half = blocks[0].shape[0] // 2
     far_top = swap(blocks[3][:half], "dp", 4)
     far_bottom = swap(blocks[3][half:], "dp", 2)
-    x_bottom = swap(blocks[1][half:], "dp", 2)
-    y_top = swap(blocks[2][:half], "dp", 4)
-    x_top = swap(blocks[1][:half] + far_top, "dp", 2)
-    y_bottom = swap(blocks[2][half:] + far_bottom, "dp", 4)
-    top = x_top.astype(jnp.float32) + y_top.astype(jnp.float32)
-    bottom = x_bottom.astype(jnp.float32) + y_bottom.astype(jnp.float32)
-    return total + jnp.concatenate([top, bottom], axis=0)
-
-
-def gather_tensor(value):
+    far_top, far_bottom = yield (far_top, far_bottom)
+    near_x = swap(
+        jnp.concatenate([blocks[1][:half] + far_top, blocks[1][half:]], axis=0), "dp", 2
+    )
+    near_y = swap(
+        jnp.concatenate([blocks[2][:half], blocks[2][half:] + far_bottom], axis=0), "dp", 4
+    )
+    near_x, near_y = yield (near_x, near_y)
+    return blocks[0].astype(jnp.float32) + near_x.astype(jnp.float32) + near_y.astype(jnp.float32)
+
+
+def gather_tensor(value, then=()):
     size = lax.axis_size("tensor")
     if size != 4:
-        return [value] + [swap(value, "tensor", k) for k in range(1, size)]
+        blocks = [value] + [swap(value, "tensor", k) for k in range(1, size)]
+        blocks, then = yield (blocks, then)
+        return blocks, then
     index = lax.axis_index("tensor")
     two = swap(value, "tensor", 2)
     one = swap(value, "tensor", 1)
+    value, one, two, then = yield (value, one, two, then)
     inner = lax.ppermute(value, "tensor", [(1, 2), (2, 1)])
     outer = lax.ppermute(two, "tensor", [(2, 3), (1, 0)])
-    return [value, one, two, jnp.where((index == 1) | (index == 2), inner, outer)]
+    inner, outer, then = yield (inner, outer, then)
+    return [value, one, two, jnp.where((index == 1) | (index == 2), inner, outer)], then
 
 
 def scatter_tensor(blocks):
     size = lax.axis_size("tensor")
-    total = blocks[0].astype(jnp.float32)
     if size != 4:
-        for k in range(1, size):
-            total = total + swap(blocks[k], "tensor", k).astype(jnp.float32)
-        return total
+        parts = [blocks[0]] + [swap(blocks[k], "tensor", k) for k in range(1, size)]
+        parts = yield parts
+        return sum(part.astype(jnp.float32) for part in parts)
     outer = lax.ppermute(blocks[3], "tensor", [(0, 1), (3, 2)])
+    inner = lax.ppermute(blocks[3], "tensor", [(1, 2), (2, 1)])
+    outer, inner = yield (outer, inner)
     one = swap(blocks[1], "tensor", 1)
-    inner = lax.ppermute(blocks[3], "tensor", [(1, 2), (2, 1)])
     two = swap(blocks[2] + outer, "tensor", 2)
-    return total + one.astype(jnp.float32) + inner.astype(jnp.float32) + two.astype(jnp.float32)
+    one, two = yield (one, two)
+    return sum(part.astype(jnp.float32) for part in (blocks[0], one, inner, two))
+
+
+def both(gather, first, second):
+    first, second = yield from gather(first, second)
+    second, _ = yield from gather(second)
+    return first, second
 
 
 def local(tokens, norm_gain, query_weight, kv_weight, out_weight, grad_out, doc_lengths):
@@ -99,23 +130,25 @@
         handed = swap(columns(value, 1 - core), "dp", 1)
         return jnp.concatenate([columns(value, core), handed], axis=0)
 
-    def all_rows(value):
-        return jnp.stack(gather_tensor(share(value)), axis=0).reshape(2 * length, width // 2)
+    def all_rows(blocks):
+        return jnp.stack(blocks, axis=0).reshape(2 * length, width // 2)
 
     def join(product):
         split = product.reshape(tensor_size, 2, rows, product.shape[1])
         handed = swap(split[:, 1].astype(jnp.bfloat16), "dp", 1)
         return (split[:, 0] + handed.astype(jnp.float32)).astype(jnp.bfloat16).reshape(length, -1)
 
-    out_blocks = gather_chips(out_weight)
-    joint_blocks = gather_chips(jnp.concatenate([query_weight, kv_weight], axis=1))
-
-    grad_rows = all_rows(grad_out)
     values32 = tokens.astype(jnp.float32)
     root_mean = jnp.sqrt(jnp.mean(values32 * values32, axis=-1) + epsilon)
     unit = values32 / root_mean[:, None]
     gain32 = norm_gain.astype(jnp.float32)
-    normed = all_rows((unit * gain32).astype(jnp.bfloat16))
+    normed_local = (unit * gain32).astype(jnp.bfloat16)
+    (out_blocks, joint_blocks), (grad_blocks, normed_blocks) = in_step(
+        both(gather_chips, out_weight, jnp.concatenate([query_weight, kv_weight], axis=1)),
+        both(gather_tensor, share(grad_out), share(normed_local)),
+    )
+    grad_rows = all_rows(grad_blocks)
+    normed = all_rows(normed_blocks)
 
     out_grad = join(
         lax.dot_general(
@@ -178,7 +211,7 @@
     combined = jnp.concatenate([query_grad, kv_partial.astype(jnp.bfloat16)], axis=1)
     joint_width = combined.shape[1]
     other = swap(combined, "dp", 1)
-    both = jnp.stack(
+    pair = jnp.stack(
         [
             combined.reshape(tensor_size, rows, joint_width),
             other.reshape(tensor_size, rows, joint_width),
@@ -187,18 +220,16 @@
     ).reshape(2 * length, joint_width)
 
     weight_terms = lax.dot_general(
-        normed, both, (((0,), (0,)), ((), ())), preferred_element_type=jnp.float32
+        normed, pair, (((0,), (0,)), ((), ())), preferred_element_type=jnp.float32
     ).astype(jnp.bfloat16)
-    weight_grads = (
-        scatter_chips([weight_terms[k * block : (k + 1) * block] for k in range(chips)]) / data_size
-    )
-
     row_terms = lax.dot_general(
-        both, joint_weight, contract_last, preferred_element_type=jnp.float32
+        pair, joint_weight, contract_last, preferred_element_type=jnp.float32
     ).astype(jnp.bfloat16)
-    normed_part = scatter_tensor(
-        [row_terms[k * 2 * rows : (k + 1) * 2 * rows] for k in range(tensor_size)]
-    )
+    weight_sums, normed_part = in_step(
+        scatter_chips([weight_terms[k * block : (k + 1) * block] for k in range(chips)]),
+        scatter_tensor([row_terms[k * 2 * rows : (k + 1) * 2 * rows] for k in range(tensor_size)]),
+    )
+    weight_grads = weight_sums / data_size
     handed = swap(normed_part[rows:].astype(jnp.bfloat16), "dp", 1).astype(jnp.float32)
     relative = jnp.concatenate([normed_part[:rows], handed], axis=1)
     normed_grad = jnp.concatenate(

time: 245 us -> 192 us (0.78)
  waiting for transfers between devices: 111 us -> 88.8 us
  starting transfers between devices: 57.9 us -> 42.7 us
  local copies, waits for them, and re-layouts: 20.3 us -> 12.9 us
  matrix products: 32.2 us -> 25.8 us
    ppermute x26 -> x24, waiting for transfers between devices: 92.8 us -> 64.2 us  [swap(): return lax.ppermute(value, axis, pairs)]
    ppermute x26 -> x24, starting transfers between devices: 51.2 us -> 36.3 us  [swap(): return lax.ppermute(value, axis, pairs)]
    unnamed x59 -> x45, local copies, waits for them, and re-layouts: 8.9 us -> 3.27 us
    ppermute x2, waiting for transfers between devices: 10.1 us -> 15.4 us  [gather_tensor(): outer = lax.ppermute(two, 'tensor', [(2, 3), (1, 0)])]
    dot_general x2, matrix products: 8.86 us -> 6.35 us  [the longest x1 3.22 us: local(): lax.dot_general(normed, pair, (((0,), (0,)), ((), ())), preferred_element...]
    add x5 -> x2, other arithmetic: 4.95 us -> 2.72 us  [the longest x1 1.67 us: scatter_tensor(): sum((part.astype(jnp.float32) for part in (blocks[0], one, inner, two)))]
  transfers between devices with their start and end apart: 32 -> 30, of which waited for: 9 -> 15; matrix products, arithmetic and copies ran while one was open for 15% -> 14% of each run, Pallas kernels for 0% -> 0%
where the time goes in v2:
time: 192 us; the launch traced here: 190 us
  waiting for transfers between devices  88.8 us (46%)
  starting transfers between devices  42.7 us (22%)
  matrix products  25.8 us (13%)
  other arithmetic  18.1 us (9%)
  local copies, waits for them, and re-layouts  12.9 us (7%)
    ppermute x24, waiting for transfers between devices, swap(): return lax.ppermute(value, axis, pairs)  64.2 us
    ppermute x24, starting transfers between devices, swap(): return lax.ppermute(value, axis, pairs)  36.3 us
    ppermute x2, waiting for transfers between devices, gather_tensor(): outer = lax.ppermute(two, 'tensor', [(2, 3), (1, 0)])  15.4 us
    ppermute x1, waiting for transfers between devices, scatter_tensor(): outer = lax.ppermute(blocks[3], 'tensor', [(0, 1), (3, 2)])  9.22 us
    dot_general x1, matrix products, local(): lax.dot_general(grad_rows, jnp.concatenate(out_blocks, axis=1), contract_...  4.87 us
  transfers between devices with their start and end apart: 30, of which 15 were waited for; matrix products, arithmetic and copies ran while one was open for 14% of the time, Pallas kernels for 0%

profile of v2, /device:TPU:1, one launch (start us, length us, event | category | flops | bytes accessed | tf_op | source)
XLA Modules:
  0.0 189.6 jit_solution(7372638858248653080)
XLA Ops:
  5.4 2.7 %collective-permute-start = (bf16[1024,512]{1,0:T(8,128)(2,1)}, bf16[1024,512]{1,0:T(8,128)(2,1)S(1)}, u32[]{:S(2)}, u32[]{:S(2)}) collective-permute-start(bf16[1024,512]{1,0:T(8,128)(2,1)} %param.11), channel_id=1, source_target_pairs={{0,8},{4,12},{8,0},{12,4},{16,24},{20,28},{24,16},{28,20},{1,9},{5... | collective-permute-start | bytes 3145736 | tf_op jit(solution)/shard_map/ppermute | solution.py:16
  10.7 2.3 %collective-permute-start.4 = (bf16[128,2048]{1,0:T(8,128)(2,1)S(1)}, bf16[128,2048]{1,0:T(8,128)(2,1)}, u32[]{:S(2)}, u32[]{:S(2)}) collective-permute-start(bf16[128,2048]{1,0:T(8,128)(2,1)S(1)} %pad_maximum_fusion.6), channel_id=1, source_target_pairs={{0,2},{1,3},{2,0},{3,1},{4,6},{5,7},{6,4},{7,5},{8,10},{9,11},{10,... | collective-permute-start | bytes 1572872 | tf_op jit(solution)/shard_map/ppermute | solution.py:16
  15.5 18.0 %collective-permute-done.3 = bf16[128,2048]{1,0:T(8,128)(2,1)S(1)} collective-permute-done((bf16[128,2048]{1,0:T(8,128)(2,1)S(1)}, bf16[128,2048]{1,0:T(8,128)(2,1)S(1)}, u32[]{:S(2)}, u32[]{:S(2)}) %collective-permute-start.3) | collective-permute-done | bytes 524320 | tf_op jit(solution)/shard_map/ppermute | solution.py:16
  38.7 5.7 %collective-permute-done.6 = bf16[512,512]{1,0:T(8,128)(2,1)} collective-permute-done((bf16[512,512]{1,0:T(8,128)(2,1)}, bf16[512,512]{1,0:T(8,128)(2,1)}, u32[]{:S(2)}, u32[]{:S(2)}) %collective-permute-start.6) | collective-permute-done | bytes 524320 | tf_op jit(solution)/shard_map/ppermute | solution.py:16
  44.4 1.7 collective-permute-done.7
  46.1 6.2 %collective-permute-done.9 = bf16[128,2048]{1,0:T(8,128)(2,1)S(1)} collective-permute-done((bf16[128,2048]{1,0:T(8,128)(2,1)}, bf16[128,2048]{1,0:T(8,128)(2,1)S(1)}, u32[]{:S(2)}, u32[]{:S(2)}) %collective-permute-start.9) | collective-permute-done | bytes 524320 | tf_op jit(solution)/shard_map/ppermute | solution.py:81
  53.8 2.2 %collective-permute-start.13 = (bf16[128,2048]{1,0:T(8,128)(2,1)S(1)}, bf16[128,2048]{1,0:T(8,128)(2,1)S(1)}, u32[]{:S(2)}, u32[]{:S(2)}) collective-permute-start(bf16[128,2048]{1,0:T(8,128)(2,1)S(1)} %pad_maximum_fusion.7), channel_id=1, source_target_pairs={{0,2},{1,3},{2,0},{3,1},{4,6},{5,7},{6,4},{7,5},{8,10},{9,11},{10,... | collective-permute-start | bytes 1572872 | tf_op jit(solution)/shard_map/ppermute | solution.py:16
  56.1 4.9 %fusion.4 = f32[4,2,64,1024]{3,2,1,0:T(8,128)S(1)} fusion(bf16[512,512]{1,0:T(8,128)(2,1)} %collective-permute-done.7, bf16[512,512]{1,0:T(8,128)(2,1)} %collective-permute-done.6, bf16[1024,512]{1,0:T(8,128)(2,1)} %copy-done.15, bf16[1024,512]{1,0:T(8,128)(2,1)} %copy-done.14, bf16[1024,512]{1,0:T(8,128)(2,1)} %param.11, ...), kind=kOutput, calls=%fused_computation.6 | convolution fusion | flops 2171600896 | bytes 8388608 | tf_op jit(solution)/shard_map/dot_general | solution.py:154
  61.0 4.7 %collective-permute-start.19 = (bf16[4,64,1024]{2,1,0:T(8,128)(2,1)S(1)}, bf16[4,64,1024]{2,1,0:T(8,128)(2,1)S(1)}, u32[]{:S(2)}, u32[]{:S(2)}) collective-permute-start(bf16[4,64,1024]{2,1,0:T(8,128)(2,1)S(1)} %fusion.44), channel_id=1, source_target_pairs={{0,4},{4,0},{8,12},{12,8},{16,20},{20,16},{24,28},{28,24},{1,5},{5... | collective-permute-start | bytes 1572872 | tf_op jit(solution)/shard_map/ppermute | solution.py:16
  65.8 11.2 %collective-permute-done.12 = bf16[128,2048]{1,0:T(8,128)(2,1)S(1)} collective-permute-done((bf16[128,2048]{1,0:T(8,128)(2,1)S(1)}, bf16[128,2048]{1,0:T(8,128)(2,1)S(1)}, u32[]{:S(2)}, u32[]{:S(2)}) %collective-permute-start.12) | collective-permute-done | bytes 524320 | tf_op jit(solution)/shard_map/ppermute | solution.py:16
  76.9 2.4 %collective-permute-done.10 = bf16[512,1280]{1,0:T(8,128)(2,1)S(1)} collective-permute-done((bf16[512,1280]{1,0:T(8,128)(2,1)S(1)}, bf16[512,1280]{1,0:T(8,128)(2,1)S(1)}, u32[]{:S(2)}, u32[]{:S(2)}) %collective-permute-start.10) | collective-permute-done | bytes 1310752 | tf_op jit(solution)/shard_map/ppermute | solution.py:16
  81.4 1.5 collective-permute-start.17
  83.2 9.2 %collective-permute-done.17 = bf16[128,2048]{1,0:T(8,128)(2,1)S(1)} collective-permute-done((bf16[128,2048]{1,0:T(8,128)(2,1)S(1)}, bf16[128,2048]{1,0:T(8,128)(2,1)S(1)}, u32[]{:S(2)}, u32[]{:S(2)}) %collective-permute-start.17) | collective-permute-done | bytes 524320 | tf_op jit(solution)/shard_map/ppermute | solution.py:81
  93.3 2.9 %fusion.2 = f32[4,2,64,1280]{3,2,1,0:T(8,128)S(1)} fusion(bf16[2048,1280]{1,0:T(8,128)(2,1)S(1)} %constant_dynamic-update-slice_fusion, bf16[1,2,64,2048]{3,2,1,0:T(8,128)(2,1)S(1)} %bitcast.123, bf16[1,2,64,2048]{3,2,1,0:T(8,128)(2,1)S(1)} %bitcast.133, bf16[1,2,64,2048]{3,2,1,0:T(8,128)(2,1)S(1)} %bitcast.131, bf16[1,2,64,2048]{3,2,1,0:T(8,128)(2,1)S(1)} %bitcast.121), kind=kOutput, calls=%fused_computation.3 | convolution fusion | flops 2687500288 | bytes 9961472 | tf_op jit(solution)/shard_map/dot_general | solution.py:162
  97.7 5.8 %collective-permute-start.18 = (bf16[4,64,1280]{2,1,0:T(8,128)(2,1)S(1)}, bf16[4,64,1280]{2,1,0:T(8,128)(2,1)S(1)}, u32[]{:S(2)}, u32[]{:S(2)}) collective-permute-start(bf16[4,64,1280]{2,1,0:T(8,128)(2,1)S(1)} %fusion.43), channel_id=1, source_target_pairs={{0,4},{4,0},{8,12},{12,8},{16,20},{20,16},{24,28},{28,24},{1,5},{5... | collective-permute-start | bytes 1966088 | tf_op jit(solution)/shard_map/ppermute | solution.py:16
  103.9 1.5 fusion.37
  107.4 3.1 %fusion.82 = (f32[8,256]{1,0:T(8,128)S(1)}, f32[8,256,256]{1,2,0:T(8,128)}) fusion(pred[256,256]{0,1:T(8,128)(4,1)S(1)} %compare_and_fusion, bf16[256,8,128]{0,2,1:T(8,128)(2,1)} %bitcast.129, bf16[256,1280]{1,0:T(8,128)(2,1)S(1)} %bitcast.113), kind=kOutput, calls=%fused_computation.167 | convolution fusion | flops 136315136 | bytes 2760704 | tf_op jit(solution)/shard_map/sub | solution.py:188
  110.5 2.0 %fusion.34 = bf16[256,128]{1,0:T(8,128)(2,1)S(1)} fusion(bf16[256,8,128]{2,1,0:T(8,128)(2,1)S(1)} %bitcast.119, f32[8,256,256]{1,2,0:T(8,128)} %get-tuple-element.92, f32[8,256]{1,0:T(8,128)S(1)} %get-tuple-element.91), kind=kOutput, calls=%fused_computation.70 | convolution fusion | flops 135299072 | bytes 2695168 | tf_op jit(solution)/shard_map/hqt,qhd->td/dot_general | solution.py:199
  112.5 3.0 %fusion.33 = bf16[256,128]{1,0:T(8,128)(2,1)S(1)} fusion(bf16[256,8,128]{0,2,1:T(8,128)(2,1)} %bitcast.130, f32[256,256,8]{1,0,2:T(8,128)S(1)} %fusion.46, f32[8,256,256]{1,2,0:T(8,128)} %get-tuple-element.92, f32[8,256]{1,0:T(8,128)S(1)} %get-tuple-element.91), kind=kOutput, calls=%fused_computation.69 | convolution fusion | flops 137922816 | bytes 4792320 | tf_op jit(solution)/shard_map/hqt,qhd->td/dot_general | solution.py:196
  115.6 3.0 %convolution_convert_fusion.2 = bf16[128,8,256]{2,0,1:T(8,128)(2,1)S(1)} fusion(f32[256,256,8]{1,0,2:T(8,128)S(1)} %fusion.46, bf16[256,1280]{1,0:T(8,128)(2,1)S(1)} %bitcast.114, f32[8,256,256]{1,2,0:T(8,128)} %get-tuple-element.92, f32[8,256]{1,0:T(8,128)S(1)} %get-tuple-element.91), kind=kOutput, calls=%fused_computation.66 | convolution fusion | flops 138152192 | bytes 8994816 | tf_op jit(solution)/shard_map/hqt,td->qhd/dot_general | solution.py:194
  119.7 1.8 pad_maximum_fusion
  125.2 3.2 %convolution_convert_fusion = bf16[2048,1280]{1,0:T(8,128)(2,1)S(1)} fusion(bf16[512,2048]{1,0:T(8,128)(2,1)S(1)} %bitcast.115, bf16[512,1280]{1,0:T(8,128)(2,1)S(1)} %bitcast.125), kind=kOutput, calls=%fused_computation.2 | convolution fusion | flops 2686976000 | bytes 8650752 | tf_op jit(solution)/shard_map/dot_general | solution.py:222
  128.5 1.5 collective-permute-start.21
  130.6 3.1 %convolution_convert_fusion.1 = bf16[512,2048]{1,0:T(8,128)(2,1)S(1)} fusion(bf16[512,1280]{1,0:T(8,128)(2,1)S(1)} %bitcast.126, bf16[2048,1280]{1,0:T(8,128)(2,1)S(1)} %bitcast.136), kind=kOutput, calls=%fused_computation.15 | convolution fusion | flops 2685403136 | bytes 8650752 | tf_op jit(solution)/shard_map/dot_general | solution.py:225
  136.0 9.2 %collective-permute-done.23 = bf16[128,2048]{1,0:T(8,128)(2,1)S(1)} collective-permute-done((bf16[128,2048]{1,0:T(8,128)(2,1)S(1)}, bf16[128,2048]{1,0:T(8,128)(2,1)S(1)}, u32[]{:S(2)}, u32[]{:S(2)}) %collective-permute-start.23) | collective-permute-done | bytes 524320 | tf_op jit(solution)/shard_map/ppermute | solution.py:92
  149.6 3.3 %collective-permute-start.27 = (bf16[128,2048]{1,0:T(8,128)(2,1)}, bf16[128,2048]{1,0:T(8,128)(2,1)}, u32[]{:S(2)}, u32[]{:S(2)}) collective-permute-start(bf16[128,2048]{1,0:T(8,128)(2,1)} %get-tuple-element.74), channel_id=1, source_target_pairs={{0,1},{1,0},{2,3},{3,2},{4,5},{5,4},{6,7},{7,6},{8,9},{9,8},{10,11... | collective-permute-start | bytes 1572872 | tf_op jit(solution)/shard_map/ppermute | solution.py:16
  154.1 20.3 %collective-permute-done.27 = bf16[128,2048]{1,0:T(8,128)(2,1)} collective-permute-done((bf16[128,2048]{1,0:T(8,128)(2,1)}, bf16[128,2048]{1,0:T(8,128)(2,1)}, u32[]{:S(2)}, u32[]{:S(2)}) %collective-permute-start.27) | collective-permute-done | bytes 524320 | tf_op jit(solution)/shard_map/ppermute | solution.py:16
  174.7 2.2 %collective-permute-done.26 = bf16[512,1280]{1,0:T(8,128)(2,1)} collective-permute-done((bf16[512,1280]{1,0:T(8,128)(2,1)}, bf16[512,1280]{1,0:T(8,128)(2,1)}, u32[]{:S(2)}, u32[]{:S(2)}) %collective-permute-start.26) | collective-permute-done | bytes 1310752 | tf_op jit(solution)/shard_map/ppermute | solution.py:16
  176.9 1.7 convert_add_fusion
  178.6 3.1 %collective-permute-start.29 = (bf16[64,2048]{1,0:T(8,128)(2,1)S(1)}, bf16[64,2048]{1,0:T(8,128)(2,1)S(1)}, u32[]{:S(2)}, u32[]{:S(2)}) collective-permute-start(bf16[64,2048]{1,0:T(8,128)(2,1)S(1)} %slice.172), channel_id=1, source_target_pairs={{0,4},{4,0},{8,12},{12,8},{16,20},{20,16},{24,28},{28,24},{1,5},{5... | collective-permute-start | bytes 786440 | tf_op jit(solution)/shard_map/ppermute | solution.py:16
  181.7 2.6 %add_multiply_fusion = f32[512,1280]{1,0:T(8,128)S(1)} fusion(bf16[512,1280]{1,0:T(8,128)(2,1)} %collective-permute-done.26, bf16[512,1280]{1,0:T(8,128)(2,1)} %collective-permute-done.25, bf16[2048,1280]{1,0:T(8,128)(2,1)} %copy-done.1), kind=kLoop, calls=%fused_computation.16 | loop fusion | flops 3932160 | bytes 6553600 | tf_op jit(solution)/shard_map/div | solution.py:232
  184.4 1.6 slice.139
  (141 shorter events, 40.6 us)
Async XLA Ops:
  5.3 4.0 %collective-permute-start.2 = (bf16[64,2048]{1,0:T(8,128)(2,1)S(1)}, bf16[64,2048]{1,0:T(8,128)(2,1)S(1)}, u32[]{:S(2)}, u32[]{:S(2)}) collective-permute-start(bf16[64,2048]{1,0:T(8,128)(2,1)S(1)} %pad_maximum_fusion.8), channel_id=1, source_target_pairs={{0,4},{4,0},{8,12},{12,8},{16,20},{20,16},{24,28},{28,24},{1,5},{5... | collective-permute-start | bytes 786440 | tf_op jit(solution)/shard_map/ppermute | solution.py:16
  5.4 28.1 %collective-permute-start = (bf16[1024,512]{1,0:T(8,128)(2,1)}, bf16[1024,512]{1,0:T(8,128)(2,1)S(1)}, u32[]{:S(2)}, u32[]{:S(2)}) collective-permute-start(bf16[1024,512]{1,0:T(8,128)(2,1)} %param.11), channel_id=1, source_target_pairs={{0,8},{4,12},{8,0},{12,4},{16,24},{20,28},{24,16},{28,20},{1,9},{5... | collective-permute-start | bytes 3145736 | tf_op jit(solution)/shard_map/ppermute | solution.py:16
  8.1 25.5 %collective-permute-start.1 = (bf16[1024,512]{1,0:T(8,128)(2,1)}, bf16[1024,512]{1,0:T(8,128)(2,1)S(1)}, u32[]{:S(2)}, u32[]{:S(2)}) collective-permute-start(bf16[1024,512]{1,0:T(8,128)(2,1)} %param.11), channel_id=1, source_target_pairs={{0,16},{4,20},{8,24},{12,28},{16,0},{20,4},{24,8},{28,12},{1,17},{... | collective-permute-start | bytes 3145736 | tf_op jit(solution)/shard_map/ppermute | solution.py:16
  9.3 24.1 %collective-permute-start.3 = (bf16[128,2048]{1,0:T(8,128)(2,1)S(1)}, bf16[128,2048]{1,0:T(8,128)(2,1)S(1)}, u32[]{:S(2)}, u32[]{:S(2)}) collective-permute-start(bf16[128,2048]{1,0:T(8,128)(2,1)S(1)} %pad_maximum_fusion.6), channel_id=1, source_target_pairs={{0,1},{1,0},{2,3},{3,2},{4,5},{5,4},{6,7},{7,6},{8,9},{9,8},{10,11... | collective-permute-start | bytes 1572872 | tf_op jit(solution)/shard_map/ppermute | solution.py:16
  10.7 22.8 %collective-permute-start.4 = (bf16[128,2048]{1,0:T(8,128)(2,1)S(1)}, bf16[128,2048]{1,0:T(8,128)(2,1)}, u32[]{:S(2)}, u32[]{:S(2)}) collective-permute-start(bf16[128,2048]{1,0:T(8,128)(2,1)S(1)} %pad_maximum_fusion.6), channel_id=1, source_target_pairs={{0,2},{1,3},{2,0},{3,1},{4,6},{5,7},{6,4},{7,5},{8,10},{9,11},{10,... | collective-permute-start | bytes 1572872 | tf_op jit(solution)/shard_map/ppermute | solution.py:16
  13.0 2.4 %collective-permute-start.5 = (bf16[64,2048]{1,0:T(8,128)(2,1)S(1)}, bf16[64,2048]{1,0:T(8,128)(2,1)S(1)}, u32[]{:S(2)}, u32[]{:S(2)}) collective-permute-start(bf16[64,2048]{1,0:T(8,128)(2,1)S(1)} %pad_maximum_fusion.9), channel_id=1, source_target_pairs={{0,4},{4,0},{8,12},{12,8},{16,20},{20,16},{24,28},{28,24},{1,5},{5... | collective-permute-start | bytes 786440 | tf_op jit(solution)/shard_map/ppermute | solution.py:16
  15.5 77.7 %copy-start.3 = (bf16[128,2048]{1,0:T(8,128)(2,1)}, bf16[128,2048]{1,0:T(8,128)(2,1)S(1)}, u32[]{:S(2)}) copy-start(bf16[128,2048]{1,0:T(8,128)(2,1)S(1)} %pad_maximum_fusion.7) | copy-start | bytes 1572868
  34.4 9.9 %collective-permute-start.6 = (bf16[512,512]{1,0:T(8,128)(2,1)}, bf16[512,512]{1,0:T(8,128)(2,1)}, u32[]{:S(2)}, u32[]{:S(2)}) collective-permute-start(bf16[512,512]{1,0:T(8,128)(2,1)} %slice.93), channel_id=1, source_target_pairs={{0,16},{4,20},{8,24},{12,28},{16,0},{20,4},{24,8},{28,12},{1,17},{... | collective-permute-start | bytes 1572872 | tf_op jit(solution)/shard_map/ppermute | solution.py:16
  36.0 10.1 %collective-permute-start.7 = (bf16[512,512]{1,0:T(8,128)(2,1)}, bf16[512,512]{1,0:T(8,128)(2,1)}, u32[]{:S(2)}, u32[]{:S(2)}) collective-permute-start(bf16[512,512]{1,0:T(8,128)(2,1)} %slice.94), channel_id=1, source_target_pairs={{0,8},{4,12},{8,0},{12,4},{16,24},{20,28},{24,16},{28,20},{1,9},{5... | collective-permute-start | bytes 1572872 | tf_op jit(solution)/shard_map/ppermute | solution.py:16
  36.7 9.4 %collective-permute-start.8 = (bf16[128,2048]{1,0:T(8,128)(2,1)S(1)}, bf16[128,2048]{1,0:T(8,128)(2,1)S(1)}, u32[]{:S(2)}, u32[]{:S(2)}) collective-permute-start(bf16[128,2048]{1,0:T(8,128)(2,1)S(1)} %pad_maximum_fusion.6), channel_id=1, source_target_pairs={{1,2},{2,1},{5,6},{6,5},{9,10},{10,9},{13,14},{14,13},{17,18},{18,... | collective-permute-start | bytes 1572872 | tf_op jit(solution)/shard_map/ppermute | solution.py:80
  37.4 14.9 %collective-permute-start.9 = (bf16[128,2048]{1,0:T(8,128)(2,1)}, bf16[128,2048]{1,0:T(8,128)(2,1)S(1)}, u32[]{:S(2)}, u32[]{:S(2)}) collective-permute-start(bf16[128,2048]{1,0:T(8,128)(2,1)} %collective-permute-done.4), channel_id=1, source_target_pairs={{2,3},{1,0},{6,7},{5,4},{10,11},{9,8},{14,15},{13,12},{18,19},{17,... | collective-permute-start | bytes 1572872 | tf_op jit(solution)/shard_map/ppermute | solution.py:81
  52.3 27.0 %collective-permute-start.10 = (bf16[512,1280]{1,0:T(8,128)(2,1)S(1)}, bf16[512,1280]{1,0:T(8,128)(2,1)S(1)}, u32[]{:S(2)}, u32[]{:S(2)}) collective-permute-start(bf16[512,1280]{1,0:T(8,128)(2,1)S(1)} %pad_maximum_fusion.1), channel_id=1, source_target_pairs={{0,8},{4,12},{8,0},{12,4},{16,24},{20,28},{24,16},{28,20},{1,9},{5... | collective-permute-start | bytes 3932168 | tf_op jit(solution)/shard_map/ppermute | solution.py:16
  53.0 26.8 %collective-permute-start.11 = (bf16[512,1280]{1,0:T(8,128)(2,1)S(1)}, bf16[512,1280]{1,0:T(8,128)(2,1)S(1)}, u32[]{:S(2)}, u32[]{:S(2)}) collective-permute-start(bf16[512,1280]{1,0:T(8,128)(2,1)S(1)} %pad_maximum_fusion.1), channel_id=1, source_target_pairs={{0,16},{4,20},{8,24},{12,28},{16,0},{20,4},{24,8},{28,12},{1,17},{... | collective-permute-start | bytes 3932168 | tf_op jit(solution)/shard_map/ppermute | solution.py:16
  53.5 23.4 %collective-permute-start.12 = (bf16[128,2048]{1,0:T(8,128)(2,1)S(1)}, bf16[128,2048]{1,0:T(8,128)(2,1)S(1)}, u32[]{:S(2)}, u32[]{:S(2)}) collective-permute-start(bf16[128,2048]{1,0:T(8,128)(2,1)S(1)} %pad_maximum_fusion.7), channel_id=1, source_target_pairs={{0,1},{1,0},{2,3},{3,2},{4,5},{5,4},{6,7},{7,6},{8,9},{9,8},{10,11... | collective-permute-start | bytes 1572872 | tf_op jit(solution)/shard_map/ppermute | solution.py:16
  53.8 23.1 %collective-permute-start.13 = (bf16[128,2048]{1,0:T(8,128)(2,1)S(1)}, bf16[128,2048]{1,0:T(8,128)(2,1)S(1)}, u32[]{:S(2)}, u32[]{:S(2)}) collective-permute-start(bf16[128,2048]{1,0:T(8,128)(2,1)S(1)} %pad_maximum_fusion.7), channel_id=1, source_target_pairs={{0,2},{1,3},{2,0},{3,1},{4,6},{5,7},{6,4},{7,5},{8,10},{9,11},{10,... | collective-permute-start | bytes 1572872 | tf_op jit(solution)/shard_map/ppermute | solution.py:16
  60.9 22.1 %copy-start.7 = (f32[4,2,64,1024]{3,2,1,0:T(8,128)}, f32[4,2,64,1024]{3,2,1,0:T(8,128)S(1)}, u32[]{:S(2)}) copy-start(f32[4,2,64,1024]{3,2,1,0:T(8,128)S(1)} %fusion.4) | copy-start | bytes 6291460
  61.0 42.9 %collective-permute-start.19 = (bf16[4,64,1024]{2,1,0:T(8,128)(2,1)S(1)}, bf16[4,64,1024]{2,1,0:T(8,128)(2,1)S(1)}, u32[]{:S(2)}, u32[]{:S(2)}) collective-permute-start(bf16[4,64,1024]{2,1,0:T(8,128)(2,1)S(1)} %fusion.44), channel_id=1, source_target_pairs={{0,4},{4,0},{8,12},{12,8},{16,20},{20,16},{24,28},{28,24},{1,5},{5... | collective-permute-start | bytes 1572872 | tf_op jit(solution)/shard_map/ppermute | solution.py:16
  79.9 13.1 %collective-permute-start.14 = (bf16[256,1280]{1,0:T(8,128)(2,1)S(1)}, bf16[256,1280]{1,0:T(8,128)(2,1)S(1)}, u32[]{:S(2)}, u32[]{:S(2)}) collective-permute-start(bf16[256,1280]{1,0:T(8,128)(2,1)S(1)} %slice.95), channel_id=1, source_target_pairs={{0,16},{4,20},{8,24},{12,28},{16,0},{20,4},{24,8},{28,12},{1,17},{... | collective-permute-start | bytes 1966088 | tf_op jit(solution)/shard_map/ppermute | solution.py:16
  80.1 12.9 %collective-permute-start.15 = (bf16[256,1280]{1,0:T(8,128)(2,1)S(1)}, bf16[256,1280]{1,0:T(8,128)(2,1)S(1)}, u32[]{:S(2)}, u32[]{:S(2)}) collective-permute-start(bf16[256,1280]{1,0:T(8,128)(2,1)S(1)} %slice.96), channel_id=1, source_target_pairs={{0,8},{4,12},{8,0},{12,4},{16,24},{20,28},{24,16},{28,20},{1,9},{5... | collective-permute-start | bytes 1966088 | tf_op jit(solution)/shard_map/ppermute | solution.py:16
  80.7 2.5 %collective-permute-start.16 = (bf16[128,2048]{1,0:T(8,128)(2,1)S(1)}, bf16[128,2048]{1,0:T(8,128)(2,1)S(1)}, u32[]{:S(2)}, u32[]{:S(2)}) collective-permute-start(bf16[128,2048]{1,0:T(8,128)(2,1)S(1)} %pad_maximum_fusion.7), channel_id=1, source_target_pairs={{1,2},{2,1},{5,6},{6,5},{9,10},{10,9},{13,14},{14,13},{17,18},{18,... | collective-permute-start | bytes 1572872 | tf_op jit(solution)/shard_map/ppermute | solution.py:80
  81.4 11.0 %collective-permute-start.17 = (bf16[128,2048]{1,0:T(8,128)(2,1)S(1)}, bf16[128,2048]{1,0:T(8,128)(2,1)S(1)}, u32[]{:S(2)}, u32[]{:S(2)}) collective-permute-start(bf16[128,2048]{1,0:T(8,128)(2,1)S(1)} %collective-permute-done.13), channel_id=1, source_target_pairs={{2,3},{1,0},{6,7},{5,4},{10,11},{9,8},{14,15},{13,12},{18,19},{17,... | collective-permute-start | bytes 1572872 | tf_op jit(solution)/shard_map/ppermute | solution.py:81
  97.7 7.9 %collective-permute-start.18 = (bf16[4,64,1280]{2,1,0:T(8,128)(2,1)S(1)}, bf16[4,64,1280]{2,1,0:T(8,128)(2,1)S(1)}, u32[]{:S(2)}, u32[]{:S(2)}) collective-permute-start(bf16[4,64,1280]{2,1,0:T(8,128)(2,1)S(1)} %fusion.43), channel_id=1, source_target_pairs={{0,4},{4,0},{8,12},{12,8},{16,20},{20,16},{24,28},{28,24},{1,5},{5... | collective-permute-start | bytes 1966088 | tf_op jit(solution)/shard_map/ppermute | solution.py:16
  119.7 4.1 %collective-permute-start.20 = (bf16[256,1280]{1,0:T(8,128)(2,1)}, bf16[256,1280]{1,0:T(8,128)(2,1)}, u32[]{:S(2)}, u32[]{:S(2)}) collective-permute-start(bf16[256,1280]{1,0:T(8,128)(2,1)} %pad_maximum_fusion.5), channel_id=1, source_target_pairs={{0,4},{4,0},{8,12},{12,8},{16,20},{20,16},{24,28},{28,24},{1,5},{5... | collective-permute-start | bytes 1966088 | tf_op jit(solution)/shard_map/ppermute | solution.py:16
  128.5 16.7 %collective-permute-start.21 = (bf16[256,1280]{1,0:T(8,128)(2,1)S(1)}, bf16[256,1280]{1,0:T(8,128)(2,1)S(1)}, u32[]{:S(2)}, u32[]{:S(2)}) collective-permute-start(bf16[256,1280]{1,0:T(8,128)(2,1)S(1)} %get-tuple-element.72), channel_id=1, source_target_pairs={{0,16},{4,20},{8,24},{12,28},{16,0},{20,4},{24,8},{28,12},{1,17},{... | collective-permute-start | bytes 1966088 | tf_op jit(solution)/shard_map/ppermute | solution.py:16
  130.1 15.5 %collective-permute-start.22 = (bf16[256,1280]{1,0:T(8,128)(2,1)S(1)}, bf16[256,1280]{1,0:T(8,128)(2,1)S(1)}, u32[]{:S(2)}, u32[]{:S(2)}) collective-permute-start(bf16[256,1280]{1,0:T(8,128)(2,1)S(1)} %get-tuple-element.71), channel_id=1, source_target_pairs={{0,8},{4,12},{8,0},{12,4},{16,24},{20,28},{24,16},{28,20},{1,9},{5... | collective-permute-start | bytes 1966088 | tf_op jit(solution)/shard_map/ppermute | solution.py:16
  133.8 11.5 %collective-permute-start.23 = (bf16[128,2048]{1,0:T(8,128)(2,1)S(1)}, bf16[128,2048]{1,0:T(8,128)(2,1)S(1)}, u32[]{:S(2)}, u32[]{:S(2)}) collective-permute-start(bf16[128,2048]{1,0:T(8,128)(2,1)S(1)} %slice.130), channel_id=1, source_target_pairs={{0,1},{3,2},{4,5},{7,6},{8,9},{11,10},{12,13},{15,14},{16,17},{19,... | collective-permute-start | bytes 1572872 | tf_op jit(solution)/shard_map/ppermute | solution.py:92
  135.1 10.1 %collective-permute-start.24 = (bf16[128,2048]{1,0:T(8,128)(2,1)S(1)}, bf16[128,2048]{1,0:T(8,128)(2,1)S(1)}, u32[]{:S(2)}, u32[]{:S(2)}) collective-permute-start(bf16[128,2048]{1,0:T(8,128)(2,1)S(1)} %slice.130), channel_id=1, source_target_pairs={{1,2},{2,1},{5,6},{6,5},{9,10},{10,9},{13,14},{14,13},{17,18},{18,... | collective-permute-start | bytes 1572872 | tf_op jit(solution)/shard_map/ppermute | solution.py:93
  146.2 28.5 %collective-permute-start.25 = (bf16[512,1280]{1,0:T(8,128)(2,1)S(1)}, bf16[512,1280]{1,0:T(8,128)(2,1)}, u32[]{:S(2)}, u32[]{:S(2)}) collective-permute-start(bf16[512,1280]{1,0:T(8,128)(2,1)S(1)} %pad_maximum_fusion.3), channel_id=1, source_target_pairs={{0,8},{4,12},{8,0},{12,4},{16,24},{20,28},{24,16},{28,20},{1,9},{5... | collective-permute-start | bytes 3932168 | tf_op jit(solution)/shard_map/ppermute | solution.py:16
  148.4 28.5 %collective-permute-start.26 = (bf16[512,1280]{1,0:T(8,128)(2,1)}, bf16[512,1280]{1,0:T(8,128)(2,1)}, u32[]{:S(2)}, u32[]{:S(2)}) collective-permute-start(bf16[512,1280]{1,0:T(8,128)(2,1)} %pad_maximum_fusion.4), channel_id=1, source_target_pairs={{0,16},{4,20},{8,24},{12,28},{16,0},{20,4},{24,8},{28,12},{1,17},{... | collective-permute-start | bytes 3932168 | tf_op jit(solution)/shard_map/ppermute | solution.py:16
  149.6 24.8 %collective-permute-start.27 = (bf16[128,2048]{1,0:T(8,128)(2,1)}, bf16[128,2048]{1,0:T(8,128)(2,1)}, u32[]{:S(2)}, u32[]{:S(2)}) collective-permute-start(bf16[128,2048]{1,0:T(8,128)(2,1)} %get-tuple-element.74), channel_id=1, source_target_pairs={{0,1},{1,0},{2,3},{3,2},{4,5},{5,4},{6,7},{7,6},{8,9},{9,8},{10,11... | collective-permute-start | bytes 1572872 | tf_op jit(solution)/shard_map/ppermute | solution.py:16
  152.9 21.5 %collective-permute-start.28 = (bf16[128,2048]{1,0:T(8,128)(2,1)}, bf16[128,2048]{1,0:T(8,128)(2,1)}, u32[]{:S(2)}, u32[]{:S(2)}) collective-permute-start(bf16[128,2048]{1,0:T(8,128)(2,1)} %get-tuple-element.73), channel_id=1, source_target_pairs={{0,2},{1,3},{2,0},{3,1},{4,6},{5,7},{6,4},{7,5},{8,10},{9,11},{10,... | collective-permute-start | bytes 1572872 | tf_op jit(solution)/shard_map/ppermute | solution.py:16
  178.6 8.2 %collective-permute-start.29 = (bf16[64,2048]{1,0:T(8,128)(2,1)S(1)}, bf16[64,2048]{1,0:T(8,128)(2,1)S(1)}, u32[]{:S(2)}, u32[]{:S(2)}) collective-permute-start(bf16[64,2048]{1,0:T(8,128)(2,1)S(1)} %slice.172), channel_id=1, source_target_pairs={{0,4},{4,0},{8,12},{12,8},{16,20},{20,16},{24,28},{28,24},{1,5},{5... | collective-permute-start | bytes 786440 | tf_op jit(solution)/shard_map/ppermute | solution.py:16
  (18 other events, 115.5 us)

commit v3 on v2

v3 whole, which is shorter than its diff:
```python
import functools
import math

import jax
import jax.numpy as jnp
from jax import lax
from jax.experimental import pallas as pl
from jax.experimental.pallas import tpu as pltpu
from jax.sharding import PartitionSpec as P

KVH = 4
HD = 128

epsilon = 1e-05
CONTRACT_LAST = (((1,), (1,)), ((), ()))
CONTRACT_FIRST = (((0,), (0,)), ((), ()))
WHOLE = pl.BlockSpec(memory_space=pltpu.VMEM)
SCALARS = pl.BlockSpec(memory_space=pltpu.SMEM)


def call(kernel, outs, operands, scalars=(), scratch=(), flops=0, megabytes=32):
    moved = sum(math.prod(a.shape) * a.dtype.itemsize for a in (*operands, *outs))
    return pl.pallas_call(
        kernel,
        out_shape=outs,
        in_specs=[SCALARS] * len(scalars) + [WHOLE] * len(operands),
        out_specs=[WHOLE] * len(outs),
        scratch_shapes=scratch,
        compiler_params=pltpu.CompilerParams(vmem_limit_bytes=megabytes * 2**20),
        cost_estimate=pl.CostEstimate(flops=flops, bytes_accessed=moved, transcendentals=0),
    )(*scalars, *operands)


def shaped(shape, dtype=jnp.bfloat16):
    return jax.ShapeDtypeStruct(shape, dtype)


def dot(left, right, contract=(((1,), (0,)), ((), ()))):
    return lax.dot_general(left, right, contract, preferred_element_type=jnp.float32)


def swap(value, axis, mask):
    pairs = [(source, source ^ mask) for source in range(lax.axis_size(axis))]
    return lax.ppermute(value, axis, pairs)


def in_step(*streams):
    results = [None] * len(streams)
    waiting = {}
    for number, stream in enumerate(streams):
        try:
            waiting[number] = next(stream)
        except StopIteration as end:
            results[number] = end.value
    while waiting:
        ready = lax.optimization_barrier(tuple(waiting.values()))
        following = {}
        for number, values in zip(list(waiting), ready):
            try:
                following[number] = streams[number].send(values)
            except StopIteration as end:
                results[number] = end.value
        waiting = following
    return results


def gather_chips(value, axis, then=()):
    chips = lax.axis_size("dp") // 2
    if chips != 4:
        blocks = [value] + [swap(value, "dp", 2 * k) for k in range(1, chips)]
        blocks, then = yield (blocks, then)
        return blocks, then
    near_x = swap(value, "dp", 2)
    near_y = swap(value, "dp", 4)
    value, near_x, near_y, then = yield (value, near_x, near_y, then)
    far_top = swap(jnp.split(near_x, 2, axis)[0], "dp", 4)
    far_bottom = swap(jnp.split(near_y, 2, axis)[1], "dp", 2)
    far_top, far_bottom, then = yield (far_top, far_bottom, then)
    return [value, near_x, near_y, far_top, far_bottom], then


def scatter_chips(blocks):
    chips = lax.axis_size("dp") // 2
    if chips != 4:
        return [blocks[0]] + [swap(blocks[k], "dp", 2 * k) for k in range(1, chips)]
        yield
    half = blocks[0].shape[0] // 2
    far_top = swap(blocks[3][:half], "dp", 4)
    far_bottom = swap(blocks[3][half:], "dp", 2)
    far_top, far_bottom = yield (far_top, far_bottom)
    near_x = swap(
        jnp.concatenate([blocks[1][:half] + far_top, blocks[1][half:]], axis=0), "dp", 2
    )
    near_y = swap(
        jnp.concatenate([blocks[2][:half], blocks[2][half:] + far_bottom], axis=0), "dp", 4
    )
    return [blocks[0], near_x, near_y]


def gather_tensor(value, then=()):
    size = lax.axis_size("tensor")
    if size != 4:
        blocks = [value] + [swap(value, "tensor", k) for k in range(1, size)]
        blocks, then = yield (blocks, then)
        return blocks, then
    two = swap(value, "tensor", 2)
    one = swap(value, "tensor", 1)
    value, one, two, then = yield (value, one, two, then)
    inner = lax.ppermute(value, "tensor", [(1, 2), (2, 1)])
    outer = lax.ppermute(two, "tensor", [(2, 3), (1, 0)])
    inner, outer, then = yield (inner, outer, then)
    return [value, one, two, inner, outer], then


def scatter_tensor(blocks):
    size = lax.axis_size("tensor")
    if size != 4:
        return [blocks[0]] + [swap(blocks[k], "tensor", k) for k in range(1, size)]
        yield
    outer = lax.ppermute(blocks[3], "tensor", [(0, 1), (3, 2)])
    inner = lax.ppermute(blocks[3], "tensor", [(1, 2), (2, 1)])
    outer, inner = yield (outer, inner)
    two = swap(blocks[2] + outer, "tensor", 2)
    one = swap(blocks[1], "tensor", 1)
    return [blocks[0], one, inner, two]


def weights_stream(out_weight, joint):
    first, joint = yield from gather_chips(out_weight, 1, joint)
    second, _ = yield from gather_chips(joint, 0)
    return first, second


def rows_stream(first, second):
    first, second = yield from gather_tensor(first, second)
    second, _ = yield from gather_tensor(second)
    return first, second


def column_start(place, k, which, block):
    return pl.multiple_of(((place[0] ^ k) * 2 + which) * block, 128)


def divide(place, source, keep, send, block):
    core = place[1]
    for k in range(keep.shape[1] // block):
        columns = slice(k * block, (k + 1) * block)
        keep[:, columns] = source[:, pl.ds(column_start(place, k, core, block), block)]
        send[:, columns] = source[:, pl.ds(column_start(place, k, 1 - core, block), block)]


def divide_kernel(block, place, source, keep, send):
    divide(place, source, keep, send, block)


def norm_kernel(block, place, tokens, gain, keep, send, normed):
    values = tokens[...].astype(jnp.float32)
    root_mean = jnp.sqrt(jnp.mean(values * values, axis=-1, keepdims=True) + epsilon)
    normed[...] = (values / root_mean * gain[...].astype(jnp.float32)).astype(jnp.bfloat16)
    divide(place, normed, keep, send, block)


def project_kernel(pieces, weights, size, transposed, place, *refs):
    row_refs, weight_refs = refs[:pieces], refs[pieces : pieces + weights]
    keep, send, pair = refs[pieces + weights :]
    rows = row_refs[0].shape[0] // 2
    length = rows * size
    for k in range(size):
        value = row_refs[k][...]
        if pieces > size and k == size - 1:
            middle = jnp.logical_or(place[2] == 1, place[2] == 2)
            value = jnp.where(middle, value, row_refs[k + 1][...])
        pair[k * rows : (k + 1) * rows] = value[:rows]
        pair[length + k * rows : length + (k + 1) * rows] = value[rows:]
    width = keep.shape[1]
    tile = 256 if width % 256 == 0 else width

    def step(columns):
        start, total = 0, None
        for weight in weight_refs:
            depth = weight.shape[1 if transposed else 0]
            left = pair[:, start : start + depth]
            if transposed:
                term = dot(left, weight[columns, :], CONTRACT_LAST)
            else:
                term = dot(left, weight[:, columns])
            total = term if total is None else total + term
            start += depth
        keep[:, columns] = total[:length]
        send[:, columns] = total[length:].astype(jnp.bfloat16)

    if tile == width:
        step(slice(0, width))
    else:

        @pl.loop(0, width // tile)
        def _(number):
            step(pl.ds(pl.multiple_of(number * tile, tile), tile))


def project(place, pieces, weights, transposed, size):
    rows = pieces[0].shape[0] // 2 * size
    half = pieces[0].shape[1]
    width = weights[0].shape[0 if transposed else 1]
    return call(
        functools.partial(project_kernel, len(pieces), len(weights), size, transposed),
        [
            shaped((rows, width), jnp.float32),
            shaped((rows, width)),
            shaped((2 * rows, half)),
        ],
        [*pieces, *weights],
        [place],
        flops=4 * rows * half * width,
    )


def attention_kernel(rows, heads, place, lengths, out_own, out_sent, own, sent, grads, partial):
    length = out_own.shape[0]
    width = heads * HD
    scale = 1 / math.sqrt(HD)
    tensor_index = place[2]

    def positions_of(dimension):
        order = lax.broadcasted_iota(jnp.int32, (length, length), dimension)
        return ((order // rows) ^ tensor_index) * rows + order % rows

    def labels_of(positions):
        labels, end = jnp.zeros((length, length), jnp.int32), 0
        for document in range(lengths.shape[1]):
            end = end + lengths[0, document]
            labels = labels + (end <= positions).astype(jnp.int32)
        return labels

    key_positions, query_positions = positions_of(0), positions_of(1)
    allowed = jnp.logical_and(
        labels_of(key_positions) == labels_of(query_positions), key_positions <= query_positions
    )

    def joined(first, second, columns):
        return (first[:, columns] + second[:, columns].astype(jnp.float32)).astype(jnp.bfloat16)

    keys = joined(own, sent, slice(width, width + HD))
    values = joined(own, sent, slice(width + HD, width + 2 * HD))
    key_total = value_total = None
    for head in range(heads):
        columns = slice(head * HD, (head + 1) * HD)
        queries = joined(own, sent, columns)
        out_grad = joined(out_own, out_sent, columns)
        scores = jnp.where(allowed, dot(keys, queries, CONTRACT_LAST) * scale, -1e30)
        expo = jnp.exp(scores - jnp.max(scores, axis=0, keepdims=True))
        probs = expo * (1 / jnp.sum(expo, axis=0, keepdims=True))
        prob_grad = dot(values, out_grad, CONTRACT_LAST)
        inner = jnp.sum(probs * prob_grad, axis=0, keepdims=True)
        score_grad = (probs * (prob_grad - inner) * scale).astype(jnp.bfloat16)
        grads[:, columns] = dot(score_grad, keys, CONTRACT_FIRST).astype(jnp.bfloat16)
        key_term = dot(score_grad, queries)
        value_term = dot(probs.astype(jnp.bfloat16), out_grad)
        key_total = key_term if head == 0 else key_total + key_term
        value_total = value_term if head == 0 else value_total + value_term
    if partial is None:
        grads[:, width : width + HD] = key_total.astype(jnp.bfloat16)
        grads[:, width + HD :] = value_total.astype(jnp.bfloat16)
    else:
        partial[:, :HD] = key_total
        partial[:, HD:] = value_total


def attention(place, lengths, out_own, out_sent, own, sent, rows, split):
    length, width = out_own.shape
    outs = [shaped((length, width if split else width + 2 * HD))]
    if split:
        outs.append(shaped((length, 2 * HD), jnp.float32))

    def kernel(*refs):
        attention_kernel(rows, width // HD, *(refs if split else (*refs, None)))

    return call(
        kernel,
        outs,
        [out_own, out_sent, own, sent],
        [place, lengths],
        flops=10 * length * length * width,
    )


def weight_kernel(first, block, pair, own, other, *outs):
    length = own.shape[0]
    tile = min(block, 256)
    for number, out in enumerate(outs):
        for part in range(block // tile):
            start = (first + number) * block + part * tile
            out[part * tile : (part + 1) * tile] = (
                dot(pair[:length, start : start + tile], own[...], CONTRACT_FIRST)
                + dot(pair[length:, start : start + tile], other[...], CONTRACT_FIRST)
            ).astype(jnp.bfloat16)


def weight_terms(pair, own, other, first, count, block):
    return call(
        functools.partial(weight_kernel, first, block),
        [shaped((block, own.shape[1]))] * count,
        [pair, own, other],
        flops=2 * pair.shape[0] * block * count * own.shape[1],
    )


def row_kernel(weights, own, other, *refs):
    weight_refs, outs = refs[:weights], refs[weights:]
    length = own.shape[0]
    rows = length // len(outs)
    start = 0
    for weight in weight_refs:
        tile = min(weight.shape[0], 256)
        for part in range(weight.shape[0] // tile):
            right = weight[part * tile : (part + 1) * tile, :]
            for offset, left in ((0, own), (rows, other)):
                term = dot(left[...], right, CONTRACT_LAST).astype(jnp.bfloat16)
                for k, out in enumerate(outs):
                    out[offset : offset + rows, start : start + tile] = term[
                        k * rows : (k + 1) * rows
                    ]
            start += tile


def row_terms(own, other, weights, size):
    length, width = own.shape
    half = sum(weight.shape[0] for weight in weights)
    return call(
        functools.partial(row_kernel, len(weights)),
        [shaped((2 * length // size, half))] * size,
        [own, other, *weights],
        flops=4 * length * width * half,
    )


def finish_kernel(count, share, *refs):
    total = refs[0][...].astype(jnp.float32)
    for part in refs[1:count]:
        total = total + part[...].astype(jnp.float32)
    total = total * share
    query_out, kv_out = refs[count:]
    width = query_out.shape[1]
    query_out[...] = total[:, :width]
    kv_out[...] = total[:, width:]


def finish(parts, query_width, share):
    block, width = parts[0].shape
    step = min(block, 128)

    def spec(columns):
        return pl.BlockSpec((step, columns), lambda i: (i, 0))

    return pl.pallas_call(
        functools.partial(finish_kernel, len(parts), share),
        grid=(block // step,),
        out_shape=[
            shaped((block, query_width), jnp.float32),
            shaped((block, width - query_width), jnp.float32),
        ],
        in_specs=[spec(width)] * len(parts),
        out_specs=[spec(query_width), spec(width - query_width)],
        compiler_params=pltpu.CompilerParams(vmem_limit_bytes=32 * 2**20),
        cost_estimate=pl.CostEstimate(
            flops=0, bytes_accessed=(2 * len(parts) + 4) * block * width, transcendentals=0
        ),
    )(*parts)


def input_kernel(count, block, place, tokens, gain, grad_out, handed, *refs):
    parts, out, gathered = refs[:count], refs[count], refs[count + 1]
    rows = tokens.shape[0]
    core = place[1]
    total = parts[0][:rows].astype(jnp.float32)
    for part in parts[1:]:
        total = total + part[:rows].astype(jnp.float32)
    for k in range(total.shape[1] // block):
        columns = slice(k * block, (k + 1) * block)
        gathered[:, pl.ds(column_start(place, k, core, block), block)] = total[:, columns]
        gathered[:, pl.ds(column_start(place, k, 1 - core, block), block)] = handed[
            :, columns
        ].astype(jnp.float32)
    values = tokens[...].astype(jnp.float32)
    root_mean = jnp.sqrt(jnp.mean(values * values, axis=-1, keepdims=True) + epsilon)
    unit = values / root_mean
    scaled = gathered[...] * gain[...].astype(jnp.float32)
    correction = unit * jnp.mean(scaled * unit, axis=-1, keepdims=True)
    out[...] = (grad_out[...].astype(jnp.float32) + (scaled - correction) / root_mean).astype(
        jnp.bfloat16
    )


def local(tokens, norm_gain, query_weight, kv_weight, out_weight, grad_out, doc_lengths):
    tensor_size = lax.axis_size("tensor")
    data_size = lax.axis_size("dp")
    tensor_index = lax.axis_index("tensor")
    data_index = lax.axis_index("dp")
    chips = data_size // 2
    place = jnp.stack([data_index >> 1, data_index & 1, tensor_index]).astype(jnp.int32)
    sharers = tensor_size // KVH
    levels = sharers.bit_length() - 1
    rows, width = tokens.shape
    block = width // data_size
    query_width = query_weight.shape[1]
    gain = norm_gain.reshape(1, width)
    halves = [shaped((rows, width // 2))] * 2

    keep, send = call(functools.partial(divide_kernel, block), halves, [grad_out], [place])
    grad_pair = jnp.concatenate([keep, swap(send, "dp", 1)], axis=0)
    tokens, gain, grad_pair = lax.optimization_barrier((tokens, gain, grad_pair))
    keep, send = call(
        functools.partial(norm_kernel, block),
        halves,
        [tokens, gain],
        [place],
        [pltpu.VMEM((rows, width), jnp.bfloat16)],
    )
    normed_pair = jnp.concatenate([keep, swap(send, "dp", 1)], axis=0)
    joint = jnp.concatenate([query_weight, kv_weight], axis=1)
    (out_blocks, joint_blocks), (grad_blocks, normed_blocks) = in_step(
        weights_stream(out_weight, joint), rows_stream(grad_pair, normed_pair)
    )

    out_own, out_sent, _ = project(place, grad_blocks, out_blocks, True, tensor_size)
    out_sent = swap(out_sent, "dp", 1)
    own, sent, normed = project(place, normed_blocks, joint_blocks, False, tensor_size)
    sent = swap(sent, "dp", 1)
    if levels:
        joined = (own + sent.astype(jnp.float32)).astype(jnp.bfloat16)
        keyvals = joined[:, query_width:]
        for bit_index in range(levels):
            partner = swap(keyvals, "tensor", 2**bit_index)
            upper = tensor_index >> bit_index & 1 == 1
            keyvals = jnp.concatenate(
                [jnp.where(upper, partner, keyvals), jnp.where(upper, keyvals, partner)], axis=1
            )
        own = jnp.concatenate([joined[:, :query_width], keyvals], axis=1).astype(jnp.float32)
        sent = jnp.zeros(own.shape, jnp.bfloat16)
    combined, *partial = attention(
        place, doc_lengths, out_own, out_sent, own, sent, rows, levels > 0
    )
    if levels:
        kv_partial = partial[0]
        for bit_index in reversed(range(levels)):
            half_cols = kv_partial.shape[1] // 2
            upper = tensor_index >> bit_index & 1 == 1
            lower_cols = kv_partial[:, :half_cols]
            higher_cols = kv_partial[:, half_cols:]
            kept = jnp.where(upper, higher_cols, lower_cols)
            handed = jnp.where(upper, lower_cols, higher_cols)
            kv_partial = kept + swap(handed.astype(jnp.bfloat16), "tensor", 2**bit_index).astype(
                jnp.float32
            )
        combined = jnp.concatenate([combined, kv_partial.astype(jnp.bfloat16)], axis=1)
    other = swap(combined, "dp", 1)

    far = weight_terms(normed, combined, other, chips - 1, 1, block)
    near = weight_terms(normed, combined, other, 0, chips - 1, block)
    weight_parts, row_parts = in_step(
        scatter_chips([*near, *far]),
        scatter_tensor(row_terms(combined, other, joint_blocks, tensor_size)),
    )
    handed = sum(part[rows:].astype(jnp.float32) for part in row_parts).astype(jnp.bfloat16)
    (input_grad,) = call(
        functools.partial(input_kernel, len(row_parts), block),
        [shaped((rows, width))],
        [tokens, gain, grad_out, swap(handed, "dp", 1), *row_parts],
        [place],
        [pltpu.VMEM((rows, width), jnp.float32)],
    )
    query_grad, kv_grad = finish(weight_parts, query_width, 1 / data_size)
    return (input_grad, query_grad, kv_grad)


def solution(mesh):
    placed = (
        P(("dp", "tensor"), None),
        P(),
        P("dp", "tensor"),
        P("dp", "tensor"),
        P("tensor", "dp"),
        P(("dp", "tensor"), None),
        P("dp", None),
    )
    return jax.shard_map(
        local,
        mesh=mesh,
        in_specs=placed,
        out_specs=(P(("dp", "tensor"), None), P("dp", "tensor"), P("dp", "tensor")),
        check_vma=False,
    )
```

time: 192 us -> 173 us (0.901)
  matrix products: 25.8 us -> 0 us
  Pallas kernels: 0 us -> 24.5 us
  other arithmetic: 18.1 us -> 0.99 us
  waiting for transfers between devices: 88.8 us -> 99.8 us
  local copies, waits for them, and re-layouts: 12.9 us -> 2.02 us
    pallas_call x0 -> x10, Pallas kernels: none -> 24.5 us  [the longest x9 22.4 us: call(): pl.pallas_call(kernel, out_shape=outs, in_specs=[SCALARS] * len(scalars)...]
    dot_general x8 -> x0, matrix products: 22.7 us -> none  [the longest x1 4.87 us: local(): lax.dot_general(grad_rows, jnp.concatenate(out_blocks, axis=1), contract_...]
    ppermute x24, waiting for transfers between devices: 64.2 us -> 76.1 us  [swap(): return lax.ppermute(value, axis, pairs)]
    slice x11 -> x0, local copies, waits for them, and re-layouts: 5.4 us -> none  [the longest x1 1.58 us: local(): weight_grads[:, :query_width]]
    convert_element_type x6 -> x1, other arithmetic: 4.79 us -> 0.13 us  [local(): sum((part[rows:].astype(jnp.float32) for part in row_parts))]
    sub x1 -> x0, matrix products: 3.12 us -> none  [local(): expo = jnp.exp(scores - peak)]
    another operation x3 -> x1, other arithmetic: 3.14 us -> 0.08 us  [local(): jnp.stack([data_index >> 1, data_index & 1, tensor_index]).astype(jnp.int32)]
    ppermute x1, starting transfers between devices: 1.32 us -> 4.19 us  [scatter_tensor(): outer = lax.ppermute(blocks[3], 'tensor', [(0, 1), (3, 2)])]
  transfers between devices with their start and end apart: 30 -> 30, of which waited for: 15 -> 15; matrix products, arithmetic and copies ran while one was open for 14% -> 1% of each run, Pallas kernels for 0% -> 8%
where the time goes in v3:
time: 173 us; the launch traced here: 172 us
  waiting for transfers between devices  99.8 us (58%)
  starting transfers between devices  44.2 us (26%)
  Pallas kernels  24.5 us (14%)
  local copies, waits for them, and re-layouts  2.02 us (1%)
    ppermute x24, waiting for transfers between devices, swap(): return lax.ppermute(value, axis, pairs)  76.1 us
    ppermute x24, starting transfers between devices, swap(): return lax.ppermute(value, axis, pairs)  35.4 us
    pallas_call x9, Pallas kernels, call(): pl.pallas_call(kernel, out_shape=outs, in_specs=[SCALARS] * len(scalars)...  22.4 us
    ppermute x2, waiting for transfers between devices, gather_tensor(): outer = lax.ppermute(two, 'tensor', [(2, 3), (1, 0)])  15.9 us
    ppermute x1, waiting for transfers between devices, scatter_tensor(): outer = lax.ppermute(blocks[3], 'tensor', [(0, 1), (3, 2)])  7.72 us
    ppermute x1, starting transfers between devices, scatter_tensor(): outer = lax.ppermute(blocks[3], 'tensor', [(0, 1), (3, 2)])  4.19 us
  transfers between devices with their start and end apart: 30, of which 15 were waited for; matrix products, arithmetic and copies ran while one was open for 1% of the time, Pallas kernels for 8%

profile of v3, /device:TPU:1, one launch (start us, length us, event | category | flops | bytes accessed | tf_op | source)
XLA Modules:
  0.0 172.4 jit_solution(4532332453000076465)
XLA Ops:
  0.6 2.1 %collective-permute-start.1 = (bf16[1024,512]{1,0:T(8,128)(2,1)}, bf16[1024,512]{1,0:T(8,128)(2,1)S(1)}, u32[]{:S(2)}, u32[]{:S(2)}) collective-permute-start(bf16[1024,512]{1,0:T(8,128)(2,1)} %refs_5_), channel_id=1, source_target_pairs={{0,8},{4,12},{8,0},{12,4},{16,24},{20,28},{24,16},{28,20},{1,9},{5... | collective-permute-start | bytes 3145736 | tf_op jit(solution)/shard_map/ppermute | solution.py:44
  2.7 1.2 collective-permute-start.2
  5.7 1.3 collective-permute-start
  8.2 2.4 %collective-permute-start.4 = (bf16[128,2048]{1,0:T(8,128)(2,1)S(1)}, bf16[128,2048]{1,0:T(8,128)(2,1)S(1)}, u32[]{:S(2)}, u32[]{:S(2)}) collective-permute-start(bf16[128,2048]{1,0:T(8,128)(2,1)S(1)} %pad_maximum_fusion.3.refs_0_), channel_id=1, source_target_pairs={{0,2},{1,3},{2,0},{3,1},{4,6},{5,7},{6,4},{7,5},{8,10},{9,11},{10,... | collective-permute-start | bytes 1572872 | tf_op jit(solution)/shard_map/ppermute | solution.py:44
  10.6 1.3 collective-permute-start.3
  15.0 18.6 %collective-permute-done.4.refs_2_ = bf16[128,2048]{1,0:T(8,128)(2,1)S(1)} collective-permute-done((bf16[128,2048]{1,0:T(8,128)(2,1)S(1)}, bf16[128,2048]{1,0:T(8,128)(2,1)S(1)}, u32[]{:S(2)}, u32[]{:S(2)}) %collective-permute-start.4) | collective-permute-done | bytes 524320 | tf_op jit(solution)/shard_map/ppermute | solution.py:44
  35.2 1.3 collective-permute-start.9
  36.5 9.2 %collective-permute-done.7.refs_9_ = bf16[1024,256]{1,0:T(8,128)(2,1)S(1)} collective-permute-done((bf16[1024,256]{1,0:T(8,128)(2,1)S(1)}, bf16[1024,256]{1,0:T(8,128)(2,1)S(1)}, u32[]{:S(2)}, u32[]{:S(2)}) %collective-permute-start.7) | collective-permute-done | bytes 524320 | tf_op jit(solution)/shard_map/ppermute | solution.py:44
  45.7 3.5 %collective-permute-done.9.refs_4_ = bf16[128,2048]{1,0:T(8,128)(2,1)S(1)} collective-permute-done((bf16[128,2048]{1,0:T(8,128)(2,1)S(1)}, bf16[128,2048]{1,0:T(8,128)(2,1)S(1)}, u32[]{:S(2)}, u32[]{:S(2)}) %collective-permute-start.9) | collective-permute-done | bytes 524320 | tf_op jit(solution)/shard_map/ppermute | solution.py:110
  49.2 1.2 collective-permute-start.12
  51.6 2.0 %collective-permute-start.14 = (bf16[128,2048]{1,0:T(8,128)(2,1)S(1)}, bf16[128,2048]{1,0:T(8,128)(2,1)S(1)}, u32[]{:S(2)}, u32[]{:S(2)}) collective-permute-start(bf16[128,2048]{1,0:T(8,128)(2,1)S(1)} %pad_maximum_fusion.4.refs_0_), channel_id=1, source_target_pairs={{0,2},{1,3},{2,0},{3,1},{4,6},{5,7},{6,4},{7,5},{8,10},{9,11},{10,... | collective-permute-start | bytes 1572872 | tf_op jit(solution)/shard_map/ppermute | solution.py:44
  53.6 2.2 %collective-permute-start.13 = (bf16[128,2048]{1,0:T(8,128)(2,1)S(1)}, bf16[128,2048]{1,0:T(8,128)(2,1)S(1)}, u32[]{:S(2)}, u32[]{:S(2)}) collective-permute-start(bf16[128,2048]{1,0:T(8,128)(2,1)S(1)} %pad_maximum_fusion.4.refs_0_), channel_id=1, source_target_pairs={{0,1},{1,0},{2,3},{3,2},{4,5},{5,4},{6,7},{7,6},{8,9},{9,8},{10,11... | collective-permute-start | bytes 1572872 | tf_op jit(solution)/shard_map/ppermute | solution.py:44
  55.8 20.2 %collective-permute-done.14.refs_2_ = bf16[128,2048]{1,0:T(8,128)(2,1)S(1)} collective-permute-done((bf16[128,2048]{1,0:T(8,128)(2,1)S(1)}, bf16[128,2048]{1,0:T(8,128)(2,1)S(1)}, u32[]{:S(2)}, u32[]{:S(2)}) %collective-permute-start.14) | collective-permute-done | bytes 524320 | tf_op jit(solution)/shard_map/ppermute | solution.py:44
  77.8 1.3 collective-permute-start.16
  80.1 1.3 collective-permute-start.18
  81.4 12.5 %collective-permute-done.18.refs_4_ = bf16[128,2048]{1,0:T(8,128)(2,1)S(1)} collective-permute-done((bf16[128,2048]{1,0:T(8,128)(2,1)S(1)}, bf16[128,2048]{1,0:T(8,128)(2,1)S(1)}, u32[]{:S(2)}, u32[]{:S(2)}) %collective-permute-start.18) | collective-permute-done | bytes 524320 | tf_op jit(solution)/shard_map/ppermute | solution.py:110
  93.9 4.3 %shard_map.97 = (f32[256,1280]{1,0:T(8,128)S(1)}, bf16[256,1280]{1,0:T(8,128)(2,1)S(1)}, bf16[512,2048]{1,0:T(8,128)(2,1)S(1)}) custom-call(s32[3]{0:T(128)S(1)} %pad_add_fusion.place.refs_0_, bf16[128,2048]{1,0:T(8,128)(2,1)S(1)} %pad_maximum_fusion.4.refs_0_, bf16[128,2048]{1,0:T(8,128)(2,1)S(1)} %collective-permute-done.13.refs_1_, ...), custom_call_target="tpu_custom_call" | custom-call | flops 2684354560 | bytes 11927552 | tf_op jit(solution)/shard_map/pallas_call | solution.py:23
  98.2 4.7 %collective-permute-start.19 = (bf16[256,1280]{1,0:T(8,128)(2,1)S(1)}, bf16[256,1280]{1,0:T(8,128)(2,1)S(1)}, u32[]{:S(2)}, u32[]{:S(2)}) collective-permute-start(bf16[256,1280]{1,0:T(8,128)(2,1)S(1)} %get-tuple-element.86), channel_id=1, source_target_pairs={{0,4},{4,0},{8,12},{12,8},{16,20},{20,16},{24,28},{28,24},{1,5},{5... | collective-permute-start | bytes 1966088 | tf_op jit(solution)/shard_map/ppermute | solution.py:44
  102.8 4.4 %shard_map.96 = (f32[256,1024]{1,0:T(8,128)S(1)}, bf16[256,1024]{1,0:T(8,128)(2,1)S(1)}, bf16[512,2048]{1,0:T(8,128)(2,1)}) custom-call(s32[3]{0:T(128)S(1)} %pad_add_fusion.place.refs_0_, bf16[128,2048]{1,0:T(8,128)(2,1)S(1)} %pad_maximum_fusion.3.refs_0_, bf16[128,2048]{1,0:T(8,128)(2,1)S(1)} %collective-permute-done.3.refs_1_, ...), custom_call_target="tpu_custom_call" | custom-call | flops 2147483648 | bytes 10485760 | tf_op jit(solution)/shard_map/pallas_call | solution.py:23
  107.2 1.9 %collective-permute-done.10.refs_3_ = bf16[256,1024]{1,0:T(8,128)(2,1)S(1)} collective-permute-done((bf16[256,1024]{1,0:T(8,128)(2,1)S(1)}, bf16[256,1024]{1,0:T(8,128)(2,1)S(1)}, u32[]{:S(2)}, u32[]{:S(2)}) %collective-permute-start.10) | collective-permute-done | bytes 524320 | tf_op jit(solution)/shard_map/ppermute | solution.py:44
  109.1 4.0 %shard_map.98.own = bf16[256,1280]{1,0:T(8,128)(2,1)S(1)} custom-call(s32[3]{0:T(128)S(1)} %pad_add_fusion.place.refs_0_, s32[1,4]{1,0:T(1,128)S(1)} %copy-done.3, f32[256,1024]{1,0:T(8,128)S(1)} %get-tuple-element.71.refs_2_, bf16[256,1024]{1,0:T(8,128)(2,1)S(1)} %collective-permute-done.10.refs_3_, f32[256,1280]{1,0:T(8,128)S(1)} %get-tuple-element.85.refs_4_, ...), custom_call_target="tpu_custom_call" | custom-call | flops 671088640 | bytes 4194304 | tf_op jit(solution)/shard_map/pallas_call | solution.py:23
  113.4 2.0 %collective-permute-done.20.other = bf16[256,1280]{1,0:T(8,128)(2,1)S(1)} collective-permute-done((bf16[256,1280]{1,0:T(8,128)(2,1)S(1)}, bf16[256,1280]{1,0:T(8,128)(2,1)S(1)}, u32[]{:S(2)}, u32[]{:S(2)}) %collective-permute-start.20) | collective-permute-done | bytes 655392 | tf_op jit(solution)/shard_map/ppermute | solution.py:44
  117.8 2.9 %shard_map.99 = (bf16[128,2048]{1,0:T(8,128)(2,1)S(1)}, bf16[128,2048]{1,0:T(8,128)(2,1)S(1)}, bf16[128,2048]{1,0:T(8,128)(2,1)S(1)}, bf16[128,2048]{1,0:T(8,128)(2,1)S(1)}) custom-call(bf16[256,1280]{1,0:T(8,128)(2,1)S(1)} %shard_map.98.own, bf16[256,1280]{1,0:T(8,128)(2,1)S(1)} %collective-permute-done.20.other, ...), custom_call_target="tpu_custom_call" | custom-call | flops 2684354560 | bytes 8650752 | tf_op jit(solution)/shard_map/pallas_call | solution.py:23
  121.4 4.2 %collective-permute-start.24 = (bf16[128,2048]{1,0:T(8,128)(2,1)S(1)}, bf16[128,2048]{1,0:T(8,128)(2,1)S(1)}, u32[]{:S(2)}, u32[]{:S(2)}) collective-permute-start(bf16[128,2048]{1,0:T(8,128)(2,1)S(1)} %get-tuple-element.90), channel_id=1, source_target_pairs={{0,1},{3,2},{4,5},{7,6},{8,9},{11,10},{12,13},{15,14},{16,17},{19,... | collective-permute-start | bytes 1572872 | tf_op jit(solution)/shard_map/ppermute | solution.py:120
  125.6 2.3 %shard_map.102 = (bf16[512,1280]{1,0:T(8,128)(2,1)S(1)}, bf16[512,1280]{1,0:T(8,128)(2,1)S(1)}, bf16[512,1280]{1,0:T(8,128)(2,1)S(1)}) custom-call(bf16[512,2048]{1,0:T(8,128)(2,1)S(1)} %get-tuple-element.89.pair, bf16[256,1280]{1,0:T(8,128)(2,1)S(1)} %shard_map.98.own, bf16[256,1280]{1,0:T(8,128)(2,1)S(1)} %collective-permute-done.20.other), custom_call_target="tpu_custom_call" | custom-call | flops 2013265920 | bytes 7340032 | tf_op jit(solution)/shard_map/pallas_call | solution.py:23
  127.9 7.7 %collective-permute-done.24 = bf16[128,2048]{1,0:T(8,128)(2,1)S(1)} collective-permute-done((bf16[128,2048]{1,0:T(8,128)(2,1)S(1)}, bf16[128,2048]{1,0:T(8,128)(2,1)S(1)}, u32[]{:S(2)}, u32[]{:S(2)}) %collective-permute-start.24) | collective-permute-done | bytes 524320 | tf_op jit(solution)/shard_map/ppermute | solution.py:120
  136.5 1.3 collective-permute-start.28
  137.7 2.2 %collective-permute-start.21 = (bf16[128,2048]{1,0:T(8,128)(2,1)S(1)}, bf16[128,2048]{1,0:T(8,128)(2,1)S(1)}, u32[]{:S(2)}, u32[]{:S(2)}) collective-permute-start(bf16[128,2048]{1,0:T(8,128)(2,1)S(1)} %get-tuple-element.88), channel_id=1, source_target_pairs={{0,1},{1,0},{2,3},{3,2},{4,5},{5,4},{6,7},{7,6},{8,9},{9,8},{10,11... | collective-permute-start | bytes 1572872 | tf_op jit(solution)/shard_map/ppermute | solution.py:44
  140.2 19.4 %collective-permute-done.21.refs_1_ = bf16[128,2048]{1,0:T(8,128)(2,1)S(1)} collective-permute-done((bf16[128,2048]{1,0:T(8,128)(2,1)S(1)}, bf16[128,2048]{1,0:T(8,128)(2,1)S(1)}, u32[]{:S(2)}, u32[]{:S(2)}) %collective-permute-start.21) | collective-permute-done | bytes 524320 | tf_op jit(solution)/shard_map/ppermute | solution.py:44
  160.1 6.8 %collective-permute-start.27 = (bf16[64,2048]{1,0:T(8,128)(2,1)S(1)}, bf16[64,2048]{1,0:T(8,128)(2,1)S(1)}, u32[]{:S(2)}, u32[]{:S(2)}) collective-permute-start(bf16[64,2048]{1,0:T(8,128)(2,1)S(1)} %add_convert_fusion), channel_id=1, source_target_pairs={{0,4},{4,0},{8,12},{12,8},{16,20},{20,16},{24,28},{28,24},{1,5},{5... | collective-permute-start | bytes 786440 | tf_op jit(solution)/shard_map/ppermute | solution.py:44
  168.0 2.2 %shard_map.101 = bf16[64,4096]{1,0:T(8,128)(2,1)} custom-call(s32[3]{0:T(128)S(1)} %pad_add_fusion.place.refs_0_, bf16[64,4096]{1,0:T(8,128)(2,1)S(1)} %copy-done, bf16[1,4096]{1,0:T(2,128)(2,1)S(1)} %reshape.9.gain, bf16[64,4096]{1,0:T(8,128)(2,1)S(1)} %copy-done.2, bf16[64,2048]{1,0:T(8,128)(2,1)S(1)} %collective-permute-done.27.handed, ...), custom_call_target="tpu_custom_call" | custom-call | bytes 3940352 | tf_op jit(solution)/shard_map/pallas_call | solution.py:23
  170.3 2.1 %shard_map.103 = (f32[512,1024]{1,0:T(8,128)}, f32[512,256]{1,0:T(8,128)}) custom-call(bf16[512,1280]{1,0:T(8,128)(2,1)S(1)} %get-tuple-element.94.refs_0_, bf16[512,1280]{1,0:T(8,128)(2,1)S(1)} %collective-permute-done.28.refs_1_, bf16[512,1280]{1,0:T(8,128)(2,1)S(1)} %collective-permute-done.29.refs_2_), custom_call_target="tpu_custom_call" | custom-call | bytes 6553600 | tf_op jit(solution)/shard_map/pallas_call | solution.py:355
  (67 shorter events, 17.7 us)
Async XLA Ops:
  0.6 33.0 %collective-permute-start.1 = (bf16[1024,512]{1,0:T(8,128)(2,1)}, bf16[1024,512]{1,0:T(8,128)(2,1)S(1)}, u32[]{:S(2)}, u32[]{:S(2)}) collective-permute-start(bf16[1024,512]{1,0:T(8,128)(2,1)} %refs_5_), channel_id=1, source_target_pairs={{0,8},{4,12},{8,0},{12,4},{16,24},{20,28},{24,16},{28,20},{1,9},{5... | collective-permute-start | bytes 3145736 | tf_op jit(solution)/shard_map/ppermute | solution.py:44
  2.7 30.9 %collective-permute-start.2 = (bf16[1024,512]{1,0:T(8,128)(2,1)}, bf16[1024,512]{1,0:T(8,128)(2,1)S(1)}, u32[]{:S(2)}, u32[]{:S(2)}) collective-permute-start(bf16[1024,512]{1,0:T(8,128)(2,1)} %refs_5_), channel_id=1, source_target_pairs={{0,16},{4,20},{8,24},{12,28},{16,0},{20,4},{24,8},{28,12},{1,17},{... | collective-permute-start | bytes 3145736 | tf_op jit(solution)/shard_map/ppermute | solution.py:44
  5.7 2.5 %collective-permute-start = (bf16[64,2048]{1,0:T(8,128)(2,1)S(1)}, bf16[64,2048]{1,0:T(8,128)(2,1)S(1)}, u32[]{:S(2)}, u32[]{:S(2)}) collective-permute-start(bf16[64,2048]{1,0:T(8,128)(2,1)S(1)} %get-tuple-element.53), channel_id=1, source_target_pairs={{0,4},{4,0},{8,12},{12,8},{16,20},{20,16},{24,28},{28,24},{1,5},{5... | collective-permute-start | bytes 786440 | tf_op jit(solution)/shard_map/ppermute | solution.py:44
  8.2 25.4 %collective-permute-start.4 = (bf16[128,2048]{1,0:T(8,128)(2,1)S(1)}, bf16[128,2048]{1,0:T(8,128)(2,1)S(1)}, u32[]{:S(2)}, u32[]{:S(2)}) collective-permute-start(bf16[128,2048]{1,0:T(8,128)(2,1)S(1)} %pad_maximum_fusion.3.refs_0_), channel_id=1, source_target_pairs={{0,2},{1,3},{2,0},{3,1},{4,6},{5,7},{6,4},{7,5},{8,10},{9,11},{10,... | collective-permute-start | bytes 1572872 | tf_op jit(solution)/shard_map/ppermute | solution.py:44
  10.6 23.0 %collective-permute-start.3 = (bf16[128,2048]{1,0:T(8,128)(2,1)S(1)}, bf16[128,2048]{1,0:T(8,128)(2,1)S(1)}, u32[]{:S(2)}, u32[]{:S(2)}) collective-permute-start(bf16[128,2048]{1,0:T(8,128)(2,1)S(1)} %pad_maximum_fusion.3.refs_0_), channel_id=1, source_target_pairs={{0,1},{1,0},{2,3},{3,2},{4,5},{5,4},{6,7},{7,6},{8,9},{9,8},{10,11... | collective-permute-start | bytes 1572872 | tf_op jit(solution)/shard_map/ppermute | solution.py:44
  12.8 2.2 %collective-permute-start.5 = (bf16[64,2048]{1,0:T(8,128)(2,1)S(1)}, bf16[64,2048]{1,0:T(8,128)(2,1)S(1)}, u32[]{:S(2)}, u32[]{:S(2)}) collective-permute-start(bf16[64,2048]{1,0:T(8,128)(2,1)S(1)} %get-tuple-element.58), channel_id=1, source_target_pairs={{0,4},{4,0},{8,12},{12,8},{16,20},{20,16},{24,28},{28,24},{1,5},{5... | collective-permute-start | bytes 786440 | tf_op jit(solution)/shard_map/ppermute | solution.py:44
  33.7 12.0 %collective-permute-start.7 = (bf16[1024,256]{1,0:T(8,128)(2,1)S(1)}, bf16[1024,256]{1,0:T(8,128)(2,1)S(1)}, u32[]{:S(2)}, u32[]{:S(2)}) collective-permute-start(bf16[1024,256]{1,0:T(8,128)(2,1)S(1)} %split.13), channel_id=1, source_target_pairs={{0,8},{4,12},{8,0},{12,4},{16,24},{20,28},{24,16},{28,20},{1,9},{5... | collective-permute-start | bytes 1572872 | tf_op jit(solution)/shard_map/ppermute | solution.py:44
  34.0 11.7 %collective-permute-start.6 = (bf16[1024,256]{1,0:T(8,128)(2,1)S(1)}, bf16[1024,256]{1,0:T(8,128)(2,1)S(1)}, u32[]{:S(2)}, u32[]{:S(2)}) collective-permute-start(bf16[1024,256]{1,0:T(8,128)(2,1)S(1)} %split.12), channel_id=1, source_target_pairs={{0,16},{4,20},{8,24},{12,28},{16,0},{20,4},{24,8},{28,12},{1,17},{... | collective-permute-start | bytes 1572872 | tf_op jit(solution)/shard_map/ppermute | solution.py:44
  34.5 11.2 %collective-permute-start.8 = (bf16[128,2048]{1,0:T(8,128)(2,1)S(1)}, bf16[128,2048]{1,0:T(8,128)(2,1)S(1)}, u32[]{:S(2)}, u32[]{:S(2)}) collective-permute-start(bf16[128,2048]{1,0:T(8,128)(2,1)S(1)} %pad_maximum_fusion.3.refs_0_), channel_id=1, source_target_pairs={{1,2},{2,1},{5,6},{6,5},{9,10},{10,9},{13,14},{14,13},{17,18},{18,... | collective-permute-start | bytes 1572872 | tf_op jit(solution)/shard_map/ppermute | solution.py:109
  35.2 14.0 %collective-permute-start.9 = (bf16[128,2048]{1,0:T(8,128)(2,1)S(1)}, bf16[128,2048]{1,0:T(8,128)(2,1)S(1)}, u32[]{:S(2)}, u32[]{:S(2)}) collective-permute-start(bf16[128,2048]{1,0:T(8,128)(2,1)S(1)} %collective-permute-done.4.refs_2_), channel_id=1, source_target_pairs={{2,3},{1,0},{6,7},{5,4},{10,11},{9,8},{14,15},{13,12},{18,19},{17,... | collective-permute-start | bytes 1572872 | tf_op jit(solution)/shard_map/ppermute | solution.py:110
  49.2 27.6 %collective-permute-start.12 = (bf16[512,1280]{1,0:T(8,128)(2,1)S(1)}, bf16[512,1280]{1,0:T(8,128)(2,1)S(1)}, u32[]{:S(2)}, u32[]{:S(2)}) collective-permute-start(bf16[512,1280]{1,0:T(8,128)(2,1)S(1)} %pad_maximum_fusion.refs_5_.refs_0_), channel_id=1, source_target_pairs={{0,16},{4,20},{8,24},{12,28},{16,0},{20,4},{24,8},{28,12},{1,17},{... | collective-permute-start | bytes 3932168 | tf_op jit(solution)/shard_map/ppermute | solution.py:44
  50.4 27.3 %collective-permute-start.11 = (bf16[512,1280]{1,0:T(8,128)(2,1)S(1)}, bf16[512,1280]{1,0:T(8,128)(2,1)S(1)}, u32[]{:S(2)}, u32[]{:S(2)}) collective-permute-start(bf16[512,1280]{1,0:T(8,128)(2,1)S(1)} %pad_maximum_fusion.refs_5_.refs_0_), channel_id=1, source_target_pairs={{0,8},{4,12},{8,0},{12,4},{16,24},{20,28},{24,16},{28,20},{1,9},{5... | collective-permute-start | bytes 3932168 | tf_op jit(solution)/shard_map/ppermute | solution.py:44
  51.6 24.4 %collective-permute-start.14 = (bf16[128,2048]{1,0:T(8,128)(2,1)S(1)}, bf16[128,2048]{1,0:T(8,128)(2,1)S(1)}, u32[]{:S(2)}, u32[]{:S(2)}) collective-permute-start(bf16[128,2048]{1,0:T(8,128)(2,1)S(1)} %pad_maximum_fusion.4.refs_0_), channel_id=1, source_target_pairs={{0,2},{1,3},{2,0},{3,1},{4,6},{5,7},{6,4},{7,5},{8,10},{9,11},{10,... | collective-permute-start | bytes 1572872 | tf_op jit(solution)/shard_map/ppermute | solution.py:44
  53.6 22.4 %collective-permute-start.13 = (bf16[128,2048]{1,0:T(8,128)(2,1)S(1)}, bf16[128,2048]{1,0:T(8,128)(2,1)S(1)}, u32[]{:S(2)}, u32[]{:S(2)}) collective-permute-start(bf16[128,2048]{1,0:T(8,128)(2,1)S(1)} %pad_maximum_fusion.4.refs_0_), channel_id=1, source_target_pairs={{0,1},{1,0},{2,3},{3,2},{4,5},{5,4},{6,7},{7,6},{8,9},{9,8},{10,11... | collective-permute-start | bytes 1572872 | tf_op jit(solution)/shard_map/ppermute | solution.py:44
  77.8 25.0 %copy-start.4 = (bf16[1024,512]{1,0:T(8,128)(2,1)S(1)}, bf16[1024,512]{1,0:T(8,128)(2,1)}, u32[]{:S(2)}) copy-start(bf16[1024,512]{1,0:T(8,128)(2,1)} %refs_5_) | copy-start | bytes 3145732
  77.8 16.0 %collective-permute-start.16 = (bf16[256,1280]{1,0:T(8,128)(2,1)S(1)}, bf16[256,1280]{1,0:T(8,128)(2,1)S(1)}, u32[]{:S(2)}, u32[]{:S(2)}) collective-permute-start(bf16[256,1280]{1,0:T(8,128)(2,1)S(1)} %split.15), channel_id=1, source_target_pairs={{0,8},{4,12},{8,0},{12,4},{16,24},{20,28},{24,16},{28,20},{1,9},{5... | collective-permute-start | bytes 1966088 | tf_op jit(solution)/shard_map/ppermute | solution.py:44
  79.1 14.8 %collective-permute-start.15 = (bf16[256,1280]{1,0:T(8,128)(2,1)S(1)}, bf16[256,1280]{1,0:T(8,128)(2,1)S(1)}, u32[]{:S(2)}, u32[]{:S(2)}) collective-permute-start(bf16[256,1280]{1,0:T(8,128)(2,1)S(1)} %split.14), channel_id=1, source_target_pairs={{0,16},{4,20},{8,24},{12,28},{16,0},{20,4},{24,8},{28,12},{1,17},{... | collective-permute-start | bytes 1966088 | tf_op jit(solution)/shard_map/ppermute | solution.py:44
  79.4 2.0 %collective-permute-start.17 = (bf16[128,2048]{1,0:T(8,128)(2,1)S(1)}, bf16[128,2048]{1,0:T(8,128)(2,1)S(1)}, u32[]{:S(2)}, u32[]{:S(2)}) collective-permute-start(bf16[128,2048]{1,0:T(8,128)(2,1)S(1)} %pad_maximum_fusion.4.refs_0_), channel_id=1, source_target_pairs={{1,2},{2,1},{5,6},{6,5},{9,10},{10,9},{13,14},{14,13},{17,18},{18,... | collective-permute-start | bytes 1572872 | tf_op jit(solution)/shard_map/ppermute | solution.py:109
  80.1 13.8 %collective-permute-start.18 = (bf16[128,2048]{1,0:T(8,128)(2,1)S(1)}, bf16[128,2048]{1,0:T(8,128)(2,1)S(1)}, u32[]{:S(2)}, u32[]{:S(2)}) collective-permute-start(bf16[128,2048]{1,0:T(8,128)(2,1)S(1)} %collective-permute-done.14.refs_2_), channel_id=1, source_target_pairs={{2,3},{1,0},{6,7},{5,4},{10,11},{9,8},{14,15},{13,12},{18,19},{17,... | collective-permute-start | bytes 1572872 | tf_op jit(solution)/shard_map/ppermute | solution.py:110
  98.2 11.0 %collective-permute-start.19 = (bf16[256,1280]{1,0:T(8,128)(2,1)S(1)}, bf16[256,1280]{1,0:T(8,128)(2,1)S(1)}, u32[]{:S(2)}, u32[]{:S(2)}) collective-permute-start(bf16[256,1280]{1,0:T(8,128)(2,1)S(1)} %get-tuple-element.86), channel_id=1, source_target_pairs={{0,4},{4,0},{8,12},{12,8},{16,20},{20,16},{24,28},{28,24},{1,5},{5... | collective-permute-start | bytes 1966088 | tf_op jit(solution)/shard_map/ppermute | solution.py:44
  107.2 1.9 %collective-permute-start.10 = (bf16[256,1024]{1,0:T(8,128)(2,1)S(1)}, bf16[256,1024]{1,0:T(8,128)(2,1)S(1)}, u32[]{:S(2)}, u32[]{:S(2)}) collective-permute-start(bf16[256,1024]{1,0:T(8,128)(2,1)S(1)} %get-tuple-element.72), channel_id=1, source_target_pairs={{0,4},{4,0},{8,12},{12,8},{16,20},{20,16},{24,28},{28,24},{1,5},{5... | collective-permute-start | bytes 1572872 | tf_op jit(solution)/shard_map/ppermute | solution.py:44
  113.2 2.2 %collective-permute-start.20 = (bf16[256,1280]{1,0:T(8,128)(2,1)S(1)}, bf16[256,1280]{1,0:T(8,128)(2,1)S(1)}, u32[]{:S(2)}, u32[]{:S(2)}) collective-permute-start(bf16[256,1280]{1,0:T(8,128)(2,1)S(1)} %shard_map.98.own), channel_id=1, source_target_pairs={{0,4},{4,0},{8,12},{12,8},{16,20},{20,16},{24,28},{28,24},{1,5},{5... | collective-permute-start | bytes 1966088 | tf_op jit(solution)/shard_map/ppermute | solution.py:44
  116.3 19.3 %collective-permute-start.23 = (bf16[256,1280]{1,0:T(8,128)(2,1)S(1)}, bf16[256,1280]{1,0:T(8,128)(2,1)S(1)}, u32[]{:S(2)}, u32[]{:S(2)}) collective-permute-start(bf16[256,1280]{1,0:T(8,128)(2,1)S(1)} %get-tuple-element.105), channel_id=1, source_target_pairs={{0,8},{4,12},{8,0},{12,4},{16,24},{20,28},{24,16},{28,20},{1,9},{5... | collective-permute-start | bytes 1966088 | tf_op jit(solution)/shard_map/ppermute | solution.py:44
  116.6 19.0 %collective-permute-start.22 = (bf16[256,1280]{1,0:T(8,128)(2,1)S(1)}, bf16[256,1280]{1,0:T(8,128)(2,1)S(1)}, u32[]{:S(2)}, u32[]{:S(2)}) collective-permute-start(bf16[256,1280]{1,0:T(8,128)(2,1)S(1)} %get-tuple-element.106), channel_id=1, source_target_pairs={{0,16},{4,20},{8,24},{12,28},{16,0},{20,4},{24,8},{28,12},{1,17},{... | collective-permute-start | bytes 1966088 | tf_op jit(solution)/shard_map/ppermute | solution.py:44
  120.7 7.2 %collective-permute-start.25 = (bf16[128,2048]{1,0:T(8,128)(2,1)S(1)}, bf16[128,2048]{1,0:T(8,128)(2,1)S(1)}, u32[]{:S(2)}, u32[]{:S(2)}) collective-permute-start(bf16[128,2048]{1,0:T(8,128)(2,1)S(1)} %get-tuple-element.90), channel_id=1, source_target_pairs={{1,2},{2,1},{5,6},{6,5},{9,10},{10,9},{13,14},{14,13},{17,18},{18,... | collective-permute-start | bytes 1572872 | tf_op jit(solution)/shard_map/ppermute | solution.py:121
  121.4 14.2 %collective-permute-start.24 = (bf16[128,2048]{1,0:T(8,128)(2,1)S(1)}, bf16[128,2048]{1,0:T(8,128)(2,1)S(1)}, u32[]{:S(2)}, u32[]{:S(2)}) collective-permute-start(bf16[128,2048]{1,0:T(8,128)(2,1)S(1)} %get-tuple-element.90), channel_id=1, source_target_pairs={{0,1},{3,2},{4,5},{7,6},{8,9},{11,10},{12,13},{15,14},{16,17},{19,... | collective-permute-start | bytes 1572872 | tf_op jit(solution)/shard_map/ppermute | solution.py:120
  136.0 34.3 %collective-permute-start.29 = (bf16[512,1280]{1,0:T(8,128)(2,1)S(1)}, bf16[512,1280]{1,0:T(8,128)(2,1)S(1)}, u32[]{:S(2)}, u32[]{:S(2)}) collective-permute-start(bf16[512,1280]{1,0:T(8,128)(2,1)S(1)} %pad_maximum_fusion.2), channel_id=1, source_target_pairs={{0,16},{4,20},{8,24},{12,28},{16,0},{20,4},{24,8},{28,12},{1,17},{... | collective-permute-start | bytes 3932168 | tf_op jit(solution)/shard_map/ppermute | solution.py:44
  136.5 33.8 %collective-permute-start.28 = (bf16[512,1280]{1,0:T(8,128)(2,1)S(1)}, bf16[512,1280]{1,0:T(8,128)(2,1)S(1)}, u32[]{:S(2)}, u32[]{:S(2)}) collective-permute-start(bf16[512,1280]{1,0:T(8,128)(2,1)S(1)} %pad_maximum_fusion.1), channel_id=1, source_target_pairs={{0,8},{4,12},{8,0},{12,4},{16,24},{20,28},{24,16},{28,20},{1,9},{5... | collective-permute-start | bytes 3932168 | tf_op jit(solution)/shard_map/ppermute | solution.py:44
  137.7 21.8 %collective-permute-start.21 = (bf16[128,2048]{1,0:T(8,128)(2,1)S(1)}, bf16[128,2048]{1,0:T(8,128)(2,1)S(1)}, u32[]{:S(2)}, u32[]{:S(2)}) collective-permute-start(bf16[128,2048]{1,0:T(8,128)(2,1)S(1)} %get-tuple-element.88), channel_id=1, source_target_pairs={{0,1},{1,0},{2,3},{3,2},{4,5},{5,4},{6,7},{7,6},{8,9},{9,8},{10,11... | collective-permute-start | bytes 1572872 | tf_op jit(solution)/shard_map/ppermute | solution.py:44
  139.9 28.1 %copy-start.2 = (bf16[64,4096]{1,0:T(8,128)(2,1)S(1)}, bf16[64,4096]{1,0:T(8,128)(2,1)}, u32[]{:S(2)}) copy-start(bf16[64,4096]{1,0:T(8,128)(2,1)} %grad_out.1) | copy-start | bytes 1572868
  140.1 19.9 %collective-permute-start.26 = (bf16[128,2048]{1,0:T(8,128)(2,1)S(1)}, bf16[128,2048]{1,0:T(8,128)(2,1)S(1)}, u32[]{:S(2)}, u32[]{:S(2)}) collective-permute-start(bf16[128,2048]{1,0:T(8,128)(2,1)S(1)} %add.20), channel_id=1, source_target_pairs={{0,2},{1,3},{2,0},{3,1},{4,6},{5,7},{6,4},{7,5},{8,10},{9,11},{10,... | collective-permute-start | bytes 1572872 | tf_op jit(solution)/shard_map/ppermute | solution.py:44
  160.1 7.9 %collective-permute-start.27 = (bf16[64,2048]{1,0:T(8,128)(2,1)S(1)}, bf16[64,2048]{1,0:T(8,128)(2,1)S(1)}, u32[]{:S(2)}, u32[]{:S(2)}) collective-permute-start(bf16[64,2048]{1,0:T(8,128)(2,1)S(1)} %add_convert_fusion), channel_id=1, source_target_pairs={{0,4},{4,0},{8,12},{12,8},{16,20},{20,16},{24,28},{28,24},{1,5},{5... | collective-permute-start | bytes 786440 | tf_op jit(solution)/shard_map/ppermute | solution.py:44
  (5 other events, 40.6 us)

commit v4 on v3

--- a/solution.py
+++ b/solution.py
@@ -44,50 +44,62 @@
     return lax.ppermute(value, axis, pairs)
 
 
-def in_step(*streams):
-    results = [None] * len(streams)
-    waiting = {}
-    for number, stream in enumerate(streams):
-        try:
-            waiting[number] = next(stream)
-        except StopIteration as end:
-            results[number] = end.value
-    while waiting:
-        ready = lax.optimization_barrier(tuple(waiting.values()))
-        following = {}
-        for number, values in zip(list(waiting), ready):
-            try:
-                following[number] = streams[number].send(values)
-            except StopIteration as end:
-                results[number] = end.value
-        waiting = following
-    return results
-
-
-def gather_chips(value, axis, then=()):
-    chips = lax.axis_size("dp") // 2
-    if chips != 4:
-        blocks = [value] + [swap(value, "dp", 2 * k) for k in range(1, chips)]
-        blocks, then = yield (blocks, then)
-        return blocks, then
-    near_x = swap(value, "dp", 2)
-    near_y = swap(value, "dp", 4)
-    value, near_x, near_y, then = yield (value, near_x, near_y, then)
-    far_top = swap(jnp.split(near_x, 2, axis)[0], "dp", 4)
-    far_bottom = swap(jnp.split(near_y, 2, axis)[1], "dp", 2)
-    far_top, far_bottom, then = yield (far_top, far_bottom, then)
-    return [value, near_x, near_y, far_top, far_bottom], then
+def tied(*values):
+    return lax.optimization_barrier(values)
+
+
+def gather_outward(value):
+    size = lax.axis_size("dp")
+    groups = [list(range(core, size, 2)) for core in range(2)]
+    return lax.all_gather(value, "dp", axis=1, tiled=True, axis_index_groups=groups)
+
+
+def everyone(value, axis, unit):
+    size = lax.axis_size(axis) // unit
+    return [value] + [swap(value, axis, unit * k) for k in range(1, size)]
+
+
+def inner_pair(value):
+    return lax.ppermute(value, "tensor", [(1, 2), (2, 1)])
+
+
+def outer_pair(value, outward=True):
+    pairs = [(2, 3), (1, 0)] if outward else [(3, 2), (0, 1)]
+    return lax.ppermute(value, "tensor", pairs)
+
+
+def staged_gathers(grad, normed_later, joint, project_out):
+    half = joint.shape[0] // 2
+    two_g, one_g = swap(grad, "tensor", 2), swap(grad, "tensor", 1)
+    near_x, near_y = swap(joint, "dp", 2), swap(joint, "dp", 4)
+    normed = normed_later()
+    grad, two_g, one_g, near_x, near_y, normed = tied(grad, two_g, one_g, near_x, near_y, normed)
+    outer_g, inner_g = outer_pair(two_g), inner_pair(grad)
+    two_n, one_n = swap(normed, "tensor", 2), swap(normed, "tensor", 1)
+    far_top = swap(near_x[:half], "dp", 4)
+    outer_g, inner_g, two_n, one_n, far_top, normed, near_y = tied(
+        outer_g, inner_g, two_n, one_n, far_top, normed, near_y
+    )
+    outer_n, inner_n = outer_pair(two_n), inner_pair(normed)
+    far_bottom = swap(near_y[half:], "dp", 2)
+    out_own, out_sent = project_out([grad, one_g, two_g, inner_g, outer_g])
+    outer_n, inner_n, far_bottom, out_own, out_sent = tied(
+        outer_n, inner_n, far_bottom, out_own, out_sent
+    )
+    return (
+        [normed, one_n, two_n, inner_n, outer_n],
+        [joint, near_x, near_y, far_top, far_bottom],
+        out_own,
+        out_sent,
+    )
 
 
 def scatter_chips(blocks):
-    chips = lax.axis_size("dp") // 2
-    if chips != 4:
-        return [blocks[0]] + [swap(blocks[k], "dp", 2 * k) for k in range(1, chips)]
-        yield
+    if len(blocks) != 4:
+        return [blocks[0]] + [swap(blocks[k], "dp", 2 * k) for k in range(1, len(blocks))]
     half = blocks[0].shape[0] // 2
     far_top = swap(blocks[3][:half], "dp", 4)
     far_bottom = swap(blocks[3][half:], "dp", 2)
-    far_top, far_bottom = yield (far_top, far_bottom)
     near_x = swap(
         jnp.concatenate([blocks[1][:half] + far_top, blocks[1][half:]], axis=0), "dp", 2
     )
@@ -97,67 +109,35 @@
     return [blocks[0], near_x, near_y]
 
 
-def gather_tensor(value, then=()):
-    size = lax.axis_size("tensor")
-    if size != 4:
-        blocks = [value] + [swap(value, "tensor", k) for k in range(1, size)]
-        blocks, then = yield (blocks, then)
-        return blocks, then
-    two = swap(value, "tensor", 2)
-    one = swap(value, "tensor", 1)
-    value, one, two, then = yield (value, one, two, then)
-    inner = lax.ppermute(value, "tensor", [(1, 2), (2, 1)])
-    outer = lax.ppermute(two, "tensor", [(2, 3), (1, 0)])
-    inner, outer, then = yield (inner, outer, then)
-    return [value, one, two, inner, outer], then
-
-
 def scatter_tensor(blocks):
-    size = lax.axis_size("tensor")
-    if size != 4:
-        return [blocks[0]] + [swap(blocks[k], "tensor", k) for k in range(1, size)]
-        yield
-    outer = lax.ppermute(blocks[3], "tensor", [(0, 1), (3, 2)])
-    inner = lax.ppermute(blocks[3], "tensor", [(1, 2), (2, 1)])
-    outer, inner = yield (outer, inner)
-    two = swap(blocks[2] + outer, "tensor", 2)
-    one = swap(blocks[1], "tensor", 1)
+    if len(blocks) != 4:
+        return [blocks[0]] + [swap(blocks[k], "tensor", k) for k in range(1, len(blocks))]
+    outer, inner = outer_pair(blocks[3], False), inner_pair(blocks[3])
+    outer, inner = tied(outer, inner)
+    two, one = swap(blocks[2] + outer, "tensor", 2), swap(blocks[1], "tensor", 1)
     return [blocks[0], one, inner, two]
 
 
-def weights_stream(out_weight, joint):
-    first, joint = yield from gather_chips(out_weight, 1, joint)
-    second, _ = yield from gather_chips(joint, 0)
-    return first, second
-
-
-def rows_stream(first, second):
-    first, second = yield from gather_tensor(first, second)
-    second, _ = yield from gather_tensor(second)
-    return first, second
-
-
-def column_start(place, k, which, block):
-    return pl.multiple_of(((place[0] ^ k) * 2 + which) * block, 128)
-
-
-def divide(place, source, keep, send, block):
-    core = place[1]
+def column_start(chip, which, block):
+    return pl.multiple_of((chip * 2 + which) * block, 128)
+
+
+def divide(chip, core, source, keep, send, block):
     for k in range(keep.shape[1] // block):
         columns = slice(k * block, (k + 1) * block)
-        keep[:, columns] = source[:, pl.ds(column_start(place, k, core, block), block)]
-        send[:, columns] = source[:, pl.ds(column_start(place, k, 1 - core, block), block)]
+        keep[:, columns] = source[:, pl.ds(column_start(chip ^ k, core, block), block)]
+        send[:, columns] = source[:, pl.ds(column_start(chip ^ k, 1 - core, block), block)]
 
 
 def divide_kernel(block, place, source, keep, send):
-    divide(place, source, keep, send, block)
+    divide(0, place[1], source, keep, send, block)
 
 
 def norm_kernel(block, place, tokens, gain, keep, send, normed):
     values = tokens[...].astype(jnp.float32)
     root_mean = jnp.sqrt(jnp.mean(values * values, axis=-1, keepdims=True) + epsilon)
     normed[...] = (values / root_mean * gain[...].astype(jnp.float32)).astype(jnp.bfloat16)
-    divide(place, normed, keep, send, block)
+    divide(place[0], place[1], normed, keep, send, block)
 
 
 def project_kernel(pieces, weights, size, transposed, place, *refs):
@@ -198,19 +178,18 @@
             step(pl.ds(pl.multiple_of(number * tile, tile), tile))
 
 
-def project(place, pieces, weights, transposed, size):
+def project(place, pieces, weights, transposed, size, keep_pair):
     rows = pieces[0].shape[0] // 2 * size
     half = pieces[0].shape[1]
     width = weights[0].shape[0 if transposed else 1]
+    outs = [shaped((rows, width), jnp.float32), shaped((rows, width))]
+    pair = shaped((2 * rows, half))
     return call(
         functools.partial(project_kernel, len(pieces), len(weights), size, transposed),
-        [
-            shaped((rows, width), jnp.float32),
-            shaped((rows, width)),
-            shaped((2 * rows, half)),
-        ],
+        [*outs, pair] if keep_pair else outs,
         [*pieces, *weights],
         [place],
+        () if keep_pair else [pltpu.VMEM(pair.shape, pair.dtype)],
         flops=4 * rows * half * width,
     )
 
@@ -377,8 +356,8 @@
         total = total + part[:rows].astype(jnp.float32)
     for k in range(total.shape[1] // block):
         columns = slice(k * block, (k + 1) * block)
-        gathered[:, pl.ds(column_start(place, k, core, block), block)] = total[:, columns]
-        gathered[:, pl.ds(column_start(place, k, 1 - core, block), block)] = handed[
+        gathered[:, pl.ds(column_start(place[0] ^ k, core, block), block)] = total[:, columns]
+        gathered[:, pl.ds(column_start(place[0] ^ k, 1 - core, block), block)] = handed[
             :, columns
         ].astype(jnp.float32)
     values = tokens[...].astype(jnp.float32)
@@ -406,25 +385,37 @@
     gain = norm_gain.reshape(1, width)
     halves = [shaped((rows, width // 2))] * 2
 
+    out_half = gather_outward(out_weight)
     keep, send = call(functools.partial(divide_kernel, block), halves, [grad_out], [place])
     grad_pair = jnp.concatenate([keep, swap(send, "dp", 1)], axis=0)
-    tokens, gain, grad_pair = lax.optimization_barrier((tokens, gain, grad_pair))
-    keep, send = call(
-        functools.partial(norm_kernel, block),
-        halves,
-        [tokens, gain],
-        [place],
-        [pltpu.VMEM((rows, width), jnp.bfloat16)],
-    )
-    normed_pair = jnp.concatenate([keep, swap(send, "dp", 1)], axis=0)
-    joint = jnp.concatenate([query_weight, kv_weight], axis=1)
-    (out_blocks, joint_blocks), (grad_blocks, normed_blocks) = in_step(
-        weights_stream(out_weight, joint), rows_stream(grad_pair, normed_pair)
-    )
-
-    out_own, out_sent, _ = project(place, grad_blocks, out_blocks, True, tensor_size)
-    out_sent = swap(out_sent, "dp", 1)
-    own, sent, normed = project(place, normed_blocks, joint_blocks, False, tensor_size)
+    grad_pair, joint_parts, inputs = lax.optimization_barrier(
+        (grad_pair, (query_weight, kv_weight), (tokens, gain))
+    )
+    joint = jnp.concatenate(joint_parts, axis=1)
+
+    def normed_pair():
+        keep, send = call(
+            functools.partial(norm_kernel, block),
+            halves,
+            inputs,
+            [place],
+            [pltpu.VMEM((rows, width), jnp.bfloat16)],
+        )
+        return jnp.concatenate([keep, swap(send, "dp", 1)], axis=0)
+
+    def project_out(blocks):
+        own, sent = project(place, blocks, [out_half], True, tensor_size, False)
+        return own, swap(sent, "dp", 1)
+
+    if chips == 4 and tensor_size == 4:
+        normed_blocks, joint_blocks, out_own, out_sent = staged_gathers(
+            grad_pair, normed_pair, joint, project_out
+        )
+    else:
+        out_own, out_sent = project_out(everyone(grad_pair, "tensor", 1))
+        normed_blocks = everyone(normed_pair(), "tensor", 1)
+        joint_blocks = everyone(joint, "dp", 2)
+    own, sent, normed = project(place, normed_blocks, joint_blocks, False, tensor_size, True)
     sent = swap(sent, "dp", 1)
     if levels:
         joined = (own + sent.astype(jnp.float32)).astype(jnp.bfloat16)
@@ -455,12 +446,12 @@
         combined = jnp.concatenate([combined, kv_partial.astype(jnp.bfloat16)], axis=1)
     other = swap(combined, "dp", 1)
 
+    row_blocks = row_terms(combined, other, joint_blocks, tensor_size)
+    normed, *row_blocks = tied(normed, *row_blocks)
     far = weight_terms(normed, combined, other, chips - 1, 1, block)
     near = weight_terms(normed, combined, other, 0, chips - 1, block)
-    weight_parts, row_parts = in_step(
-        scatter_chips([*near, *far]),
-        scatter_tensor(row_terms(combined, other, joint_blocks, tensor_size)),
-    )
+    row_parts = scatter_tensor(row_blocks)
+    weight_parts = scatter_chips([*near, *far])
     handed = sum(part[rows:].astype(jnp.float32) for part in row_parts).astype(jnp.bfloat16)
     (input_grad,) = call(
         functools.partial(input_kernel, len(row_parts), block),

time: 173 us -> 199 us (1.15)
  between operations: 0.89 us -> 14.3 us
  local copies, waits for them, and re-layouts: 2.02 us -> 13.4 us
  waiting for transfers between devices: 99.8 us -> 92.3 us
  starting transfers between devices: 44.2 us -> 49.5 us
    ppermute x6, waiting for transfers between devices: 23.7 us -> 3.54 us  [the longest x3 3.53 us: outer_pair(): return lax.ppermute(value, 'tensor', pairs)]
    ppermute x24 -> x20, waiting for transfers between devices: 76.1 us -> 88.1 us  [swap(): return lax.ppermute(value, axis, pairs)]
    unnamed x14 -> x47, local copies, waits for them, and re-layouts: 1.07 us -> 12.3 us
    ppermute x6, starting transfers between devices: 8.83 us -> 14.3 us  [the longest x3 11.5 us: outer_pair(): return lax.ppermute(value, 'tensor', pairs)]
    ppermute x24 -> x20, starting transfers between devices: 35.4 us -> 35.2 us  [swap(): return lax.ppermute(value, axis, pairs)]
  transfers between devices with their start and end apart: 30 -> 27, of which waited for: 15 -> 15; matrix products, arithmetic and copies ran while one was open for 1% -> 1% of each run, Pallas kernels for 8% -> 5%
where the time goes in v4:
time: 199 us; the launch traced here: 196 us
  waiting for transfers between devices  92.3 us (46%)
  starting transfers between devices  49.5 us (25%)
  Pallas kernels  25.9 us (13%)
  between operations  14.3 us (7%)
  local copies, waits for them, and re-layouts  13.4 us (7%)
    ppermute x20, waiting for transfers between devices, swap(): return lax.ppermute(value, axis, pairs)  88.1 us
    ppermute x20, starting transfers between devices, swap(): return lax.ppermute(value, axis, pairs)  35.2 us
    pallas_call x9, Pallas kernels, call(): pl.pallas_call(kernel, out_shape=outs, in_specs=[SCALARS] * len(scalars)...  23.8 us
    unnamed x47, local copies, waits for them, and re-layouts  12.3 us
    ppermute x3, starting transfers between devices, outer_pair(): return lax.ppermute(value, 'tensor', pairs)  11.5 us
  transfers between devices with their start and end apart: 27, of which 15 were waited for; matrix products, arithmetic and copies ran while one was open for 1% of the time, Pallas kernels for 5%

profile of v4, /device:TPU:1, one launch (start us, length us, event | category | flops | bytes accessed | tf_op | source)
XLA Modules:
  0.0 196.4 jit_solution(15562622538898602220)
XLA Ops:
  8.9 1.5 collective-permute-done
  11.4 2.4 %collective-permute-start.4 = (bf16[512,1280]{1,0:T(8,128)(2,1)S(1)}, bf16[512,1280]{1,0:T(8,128)(2,1)S(1)}, u32[]{:S(2)}, u32[]{:S(2)}) collective-permute-start(bf16[512,1280]{1,0:T(8,128)(2,1)S(1)} %constant_dynamic-update-slice_fusion.refs_5_.refs_0_), channel_id=1, source_target_pairs={{0,16},{4,20},{8,24},{12,28},{16,0},{20,4},{24,8},{28,12},{1,17},{... | collective-permute-start | bytes 3932168 | tf_op jit(solution)/shard_map/ppermute | solution.py:44
  15.0 1.3 collective-permute-start.2
  16.3 2.3 %collective-permute-start.1 = (bf16[128,2048]{1,0:T(8,128)(2,1)S(1)}, bf16[128,2048]{1,0:T(8,128)(2,1)S(1)}, u32[]{:S(2)}, u32[]{:S(2)}) collective-permute-start(bf16[128,2048]{1,0:T(8,128)(2,1)S(1)} %pad_maximum_fusion.2.refs_0_), channel_id=1, source_target_pairs={{0,2},{1,3},{2,0},{3,1},{4,6},{5,7},{6,4},{7,5},{8,10},{9,11},{10,... | collective-permute-start | bytes 1572872 | tf_op jit(solution)/shard_map/ppermute | solution.py:44
  19.5 1.6 collective-permute-start.5
  22.3 16.4 %collective-permute-done.2.refs_1_ = bf16[128,2048]{1,0:T(8,128)(2,1)S(1)} collective-permute-done((bf16[128,2048]{1,0:T(8,128)(2,1)S(1)}, bf16[128,2048]{1,0:T(8,128)(2,1)S(1)}, u32[]{:S(2)}, u32[]{:S(2)}) %collective-permute-start.2) | collective-permute-done | bytes 524320 | tf_op jit(solution)/shard_map/ppermute | solution.py:44
  39.5 14.8 %collective-permute-done.4.refs_7_.refs_2_ = bf16[512,1280]{1,0:T(8,128)(2,1)S(1)} collective-permute-done((bf16[512,1280]{1,0:T(8,128)(2,1)S(1)}, bf16[512,1280]{1,0:T(8,128)(2,1)S(1)}, u32[]{:S(2)}, u32[]{:S(2)}) %collective-permute-start.4) | collective-permute-done | bytes 1310752 | tf_op jit(solution)/shard_map/ppermute | solution.py:44
  54.3 1.7 collective-permute-done.3.refs_6_.refs_1_
  59.5 5.8 %collective-permute-start.9 = (bf16[128,2048]{1,0:T(8,128)(2,1)S(1)}, bf16[128,2048]{1,0:T(8,128)(2,1)S(1)}, u32[]{:S(2)}, u32[]{:S(2)}) collective-permute-start(bf16[128,2048]{1,0:T(8,128)(2,1)S(1)} %pad_maximum_fusion.3.refs_0_), channel_id=1, source_target_pairs={{0,1},{1,0},{2,3},{3,2},{4,5},{5,4},{6,7},{7,6},{8,9},{9,8},{10,11... | collective-permute-start | bytes 1572872 | tf_op jit(solution)/shard_map/ppermute | solution.py:44
  65.3 3.5 %collective-permute-done.6.refs_4_ = bf16[128,2048]{1,0:T(8,128)(2,1)S(1)} collective-permute-done((bf16[128,2048]{1,0:T(8,128)(2,1)S(1)}, bf16[128,2048]{1,0:T(8,128)(2,1)S(1)}, u32[]{:S(2)}, u32[]{:S(2)}) %collective-permute-start.6) | collective-permute-done | bytes 524320 | tf_op jit(solution)/shard_map/ppermute | solution.py:68
  70.5 12.1 %collective-permute-done.9.refs_1_ = bf16[128,2048]{1,0:T(8,128)(2,1)S(1)} collective-permute-done((bf16[128,2048]{1,0:T(8,128)(2,1)S(1)}, bf16[128,2048]{1,0:T(8,128)(2,1)S(1)}, u32[]{:S(2)}, u32[]{:S(2)}) %collective-permute-start.9) | collective-permute-done | bytes 524320 | tf_op jit(solution)/shard_map/ppermute | solution.py:44
  83.4 12.8 %collective-permute-done.8.refs_2_ = bf16[128,2048]{1,0:T(8,128)(2,1)} collective-permute-done((bf16[128,2048]{1,0:T(8,128)(2,1)S(1)}, bf16[128,2048]{1,0:T(8,128)(2,1)}, u32[]{:S(2)}, u32[]{:S(2)}) %collective-permute-start.8) | collective-permute-done | bytes 524320 | tf_op jit(solution)/shard_map/ppermute | solution.py:44
  97.0 1.4 collective-permute-start.12
  100.7 1.4 collective-permute-start.13
  102.1 2.2 %copy-done.7 = bf16[1024,2048]{1,0:T(8,128)(2,1)S(1)} copy-done((bf16[1024,2048]{1,0:T(8,128)(2,1)S(1)}, bf16[1024,2048]{1,0:T(8,128)(2,1)}, u32[]{:S(2)}) %copy-start.7) | copy-done | bytes 4194328
  108.5 3.7 %shard_map.96 = (f32[256,1024]{1,0:T(8,128)S(1)}, bf16[256,1024]{1,0:T(8,128)(2,1)S(1)}) custom-call(s32[3]{0:T(128)S(1)} %pad_add_fusion.place.refs_0_, bf16[128,2048]{1,0:T(8,128)(2,1)S(1)} %pad_maximum_fusion.2.refs_0_, bf16[128,2048]{1,0:T(8,128)(2,1)S(1)} %copy-done.11, bf16[128,2048]{1,0:T(8,128)(2,1)S(1)} %copy-done.13, ...), custom_call_target="tpu_custom_call" | custom-call | flops 2147483648 | bytes 8388608 | tf_op jit(solution)/shard_map/pallas_call | solution.py:23
  112.2 4.9 %collective-permute-start.14 = (bf16[256,1024]{1,0:T(8,128)(2,1)S(1)}, bf16[256,1024]{1,0:T(8,128)(2,1)S(1)}, u32[]{:S(2)}, u32[]{:S(2)}) collective-permute-start(bf16[256,1024]{1,0:T(8,128)(2,1)S(1)} %get-tuple-element.73), channel_id=1, source_target_pairs={{0,4},{4,0},{8,12},{12,8},{16,20},{20,16},{24,28},{28,24},{1,5},{5... | collective-permute-start | bytes 1572872 | tf_op jit(solution)/shard_map/ppermute | solution.py:44
  117.1 1.5 collective-permute-done.14.refs_3_
  118.7 5.3 %shard_map.97 = (f32[256,1280]{1,0:T(8,128)S(1)}, bf16[256,1280]{1,0:T(8,128)(2,1)S(1)}, bf16[512,2048]{1,0:T(8,128)(2,1)S(1)}) custom-call(s32[3]{0:T(128)S(1)} %pad_add_fusion.place.refs_0_, bf16[128,2048]{1,0:T(8,128)(2,1)S(1)} %pad_maximum_fusion.3.refs_0_, bf16[128,2048]{1,0:T(8,128)(2,1)S(1)} %copy-done.15, ...), custom_call_target="tpu_custom_call" | custom-call | flops 2684354560 | bytes 11927552 | tf_op jit(solution)/shard_map/pallas_call | solution.py:23
  124.4 1.7 collective-permute-done.15.refs_5_
  126.2 4.0 %shard_map.98.own = bf16[256,1280]{1,0:T(8,128)(2,1)S(1)} custom-call(s32[3]{0:T(128)S(1)} %pad_add_fusion.place.refs_0_, s32[1,4]{1,0:T(1,128)S(1)} %copy-done.6, f32[256,1024]{1,0:T(8,128)S(1)} %get-tuple-element.79.refs_2_, bf16[256,1024]{1,0:T(8,128)(2,1)S(1)} %collective-permute-done.14.refs_3_, f32[256,1280]{1,0:T(8,128)S(1)} %get-tuple-element.81.refs_4_, ...), custom_call_target="tpu_custom_call" | custom-call | flops 671088640 | bytes 4194304 | tf_op jit(solution)/shard_map/pallas_call | solution.py:23
  130.6 1.7 collective-permute-done.16.other
  132.4 4.0 %shard_map.99 = (bf16[128,2048]{1,0:T(8,128)(2,1)S(1)}, bf16[128,2048]{1,0:T(8,128)(2,1)S(1)}, bf16[128,2048]{1,0:T(8,128)(2,1)S(1)}, bf16[128,2048]{1,0:T(8,128)(2,1)S(1)}) custom-call(bf16[256,1280]{1,0:T(8,128)(2,1)S(1)} %shard_map.98.own, bf16[256,1280]{1,0:T(8,128)(2,1)S(1)} %collective-permute-done.16.other, ...), custom_call_target="tpu_custom_call" | custom-call | flops 2684354560 | bytes 8650752 | tf_op jit(solution)/shard_map/pallas_call | solution.py:23
  139.8 8.9 %collective-permute-start.18 = (bf16[128,2048]{1,0:T(8,128)(2,1)S(1)}, bf16[128,2048]{1,0:T(8,128)(2,1)S(1)}, u32[]{:S(2)}, u32[]{:S(2)}) collective-permute-start(bf16[128,2048]{1,0:T(8,128)(2,1)S(1)} %get-tuple-element.89), channel_id=1, source_target_pairs={{3,2},{0,1},{7,6},{4,5},{11,10},{8,9},{15,14},{12,13},{19,18},{16,... | collective-permute-start | bytes 1572872 | tf_op jit(solution)/shard_map/ppermute | solution.py:68
  148.7 2.3 %shard_map.101 = (bf16[512,1280]{1,0:T(8,128)(2,1)S(1)}, bf16[512,1280]{1,0:T(8,128)(2,1)S(1)}, bf16[512,1280]{1,0:T(8,128)(2,1)S(1)}) custom-call(bf16[512,2048]{1,0:T(8,128)(2,1)S(1)} %get-tuple-element.93.pair, bf16[256,1280]{1,0:T(8,128)(2,1)S(1)} %shard_map.98.own, bf16[256,1280]{1,0:T(8,128)(2,1)S(1)} %collective-permute-done.16.other), custom_call_target="tpu_custom_call" | custom-call | flops 2013265920 | bytes 7340032 | tf_op jit(solution)/shard_map/pallas_call | solution.py:23
  151.0 2.4 %collective-permute-done.24 = bf16[256,1280]{1,0:T(8,128)(2,1)S(1)} collective-permute-done((bf16[256,1280]{1,0:T(8,128)(2,1)S(1)}, bf16[256,1280]{1,0:T(8,128)(2,1)S(1)}, u32[]{:S(2)}, u32[]{:S(2)}) %collective-permute-start.24) | collective-permute-done | bytes 655392 | tf_op jit(solution)/shard_map/ppermute | solution.py:44
  156.6 3.2 %collective-permute-start.17 = (bf16[128,2048]{1,0:T(8,128)(2,1)S(1)}, bf16[128,2048]{1,0:T(8,128)(2,1)S(1)}, u32[]{:S(2)}, u32[]{:S(2)}) collective-permute-start(bf16[128,2048]{1,0:T(8,128)(2,1)S(1)} %get-tuple-element.88), channel_id=1, source_target_pairs={{0,1},{1,0},{2,3},{3,2},{4,5},{5,4},{6,7},{7,6},{8,9},{9,8},{10,11... | collective-permute-start | bytes 1572872 | tf_op jit(solution)/shard_map/ppermute | solution.py:44
  159.9 2.4 %collective-permute-start.20 = (bf16[128,2048]{1,0:T(8,128)(2,1)S(1)}, bf16[128,2048]{1,0:T(8,128)(2,1)S(1)}, u32[]{:S(2)}, u32[]{:S(2)}) collective-permute-start(bf16[128,2048]{1,0:T(8,128)(2,1)S(1)} %add.20), channel_id=1, source_target_pairs={{0,2},{1,3},{2,0},{3,1},{4,6},{5,7},{6,4},{7,5},{8,10},{9,11},{10,... | collective-permute-start | bytes 1572872 | tf_op jit(solution)/shard_map/ppermute | solution.py:44
  162.2 18.9 %collective-permute-done.17.refs_1_ = bf16[128,2048]{1,0:T(8,128)(2,1)S(1)} collective-permute-done((bf16[128,2048]{1,0:T(8,128)(2,1)S(1)}, bf16[128,2048]{1,0:T(8,128)(2,1)S(1)}, u32[]{:S(2)}, u32[]{:S(2)}) %collective-permute-start.17) | collective-permute-done | bytes 524320 | tf_op jit(solution)/shard_map/ppermute | solution.py:44
  181.2 2.8 %collective-permute-start.21 = (bf16[64,2048]{1,0:T(8,128)(2,1)S(1)}, bf16[64,2048]{1,0:T(8,128)(2,1)S(1)}, u32[]{:S(2)}, u32[]{:S(2)}) collective-permute-start(bf16[64,2048]{1,0:T(8,128)(2,1)S(1)} %add_convert_fusion), channel_id=1, source_target_pairs={{0,4},{4,0},{8,12},{12,8},{16,20},{20,16},{24,28},{28,24},{1,5},{5... | collective-permute-start | bytes 786440 | tf_op jit(solution)/shard_map/ppermute | solution.py:44
  185.2 2.2 %shard_map.100 = bf16[64,4096]{1,0:T(8,128)(2,1)} custom-call(s32[3]{0:T(128)S(1)} %pad_add_fusion.place.refs_0_, bf16[64,4096]{1,0:T(8,128)(2,1)S(1)} %copy-done, bf16[1,4096]{1,0:T(2,128)(2,1)S(1)} %reshape.9.gain, bf16[64,4096]{1,0:T(8,128)(2,1)S(1)} %copy-done.1, bf16[64,2048]{1,0:T(8,128)(2,1)S(1)} %collective-permute-done.21.handed, ...), custom_call_target="tpu_custom_call" | custom-call | bytes 3940352 | tf_op jit(solution)/shard_map/pallas_call | solution.py:23
  187.5 2.1 %shard_map.103 = (f32[512,1024]{1,0:T(8,128)}, f32[512,256]{1,0:T(8,128)}) custom-call(bf16[512,1280]{1,0:T(8,128)(2,1)S(1)} %get-tuple-element.94.refs_0_, bf16[512,1280]{1,0:T(8,128)(2,1)S(1)} %collective-permute-done.23.refs_1_, bf16[512,1280]{1,0:T(8,128)(2,1)S(1)} %collective-permute-done.25.refs_2_), custom_call_target="tpu_custom_call" | custom-call | bytes 6553600 | tf_op jit(solution)/shard_map/pallas_call | solution.py:334
  (93 shorter events, 28.8 us)
Async XLA Ops:
  7.2 94.9 %all-gather.2.cloned.1.call-start = ((), (), s32[]{:S(2)}) async-start(), calls=%async_computation | async-start | bytes 5242880 | tf_op jit(solution)/shard_map/all_gather | solution.py:54
  8.8 1.6 collective-permute-start
  11.4 43.0 %collective-permute-start.4 = (bf16[512,1280]{1,0:T(8,128)(2,1)S(1)}, bf16[512,1280]{1,0:T(8,128)(2,1)S(1)}, u32[]{:S(2)}, u32[]{:S(2)}) collective-permute-start(bf16[512,1280]{1,0:T(8,128)(2,1)S(1)} %constant_dynamic-update-slice_fusion.refs_5_.refs_0_), channel_id=1, source_target_pairs={{0,16},{4,20},{8,24},{12,28},{16,0},{20,4},{24,8},{28,12},{1,17},{... | collective-permute-start | bytes 3932168 | tf_op jit(solution)/shard_map/ppermute | solution.py:44
  13.8 42.2 %collective-permute-start.3 = (bf16[512,1280]{1,0:T(8,128)(2,1)S(1)}, bf16[512,1280]{1,0:T(8,128)(2,1)S(1)}, u32[]{:S(2)}, u32[]{:S(2)}) collective-permute-start(bf16[512,1280]{1,0:T(8,128)(2,1)S(1)} %constant_dynamic-update-slice_fusion.refs_5_.refs_0_), channel_id=1, source_target_pairs={{0,8},{4,12},{8,0},{12,4},{16,24},{20,28},{24,16},{28,20},{1,9},{5... | collective-permute-start | bytes 3932168 | tf_op jit(solution)/shard_map/ppermute | solution.py:44
  15.0 23.7 %collective-permute-start.2 = (bf16[128,2048]{1,0:T(8,128)(2,1)S(1)}, bf16[128,2048]{1,0:T(8,128)(2,1)S(1)}, u32[]{:S(2)}, u32[]{:S(2)}) collective-permute-start(bf16[128,2048]{1,0:T(8,128)(2,1)S(1)} %pad_maximum_fusion.2.refs_0_), channel_id=1, source_target_pairs={{0,1},{1,0},{2,3},{3,2},{4,5},{5,4},{6,7},{7,6},{8,9},{9,8},{10,11... | collective-permute-start | bytes 1572872 | tf_op jit(solution)/shard_map/ppermute | solution.py:44
  16.3 23.2 %collective-permute-start.1 = (bf16[128,2048]{1,0:T(8,128)(2,1)S(1)}, bf16[128,2048]{1,0:T(8,128)(2,1)S(1)}, u32[]{:S(2)}, u32[]{:S(2)}) collective-permute-start(bf16[128,2048]{1,0:T(8,128)(2,1)S(1)} %pad_maximum_fusion.2.refs_0_), channel_id=1, source_target_pairs={{0,2},{1,3},{2,0},{3,1},{4,6},{5,7},{6,4},{7,5},{8,10},{9,11},{10,... | collective-permute-start | bytes 1572872 | tf_op jit(solution)/shard_map/ppermute | solution.py:44
  19.5 2.7 %collective-permute-start.5 = (bf16[64,2048]{1,0:T(8,128)(2,1)S(1)}, bf16[64,2048]{1,0:T(8,128)(2,1)S(1)}, u32[]{:S(2)}, u32[]{:S(2)}) collective-permute-start(bf16[64,2048]{1,0:T(8,128)(2,1)S(1)} %get-tuple-element.59), channel_id=1, source_target_pairs={{0,4},{4,0},{8,12},{12,8},{16,20},{20,16},{24,28},{28,24},{1,5},{5... | collective-permute-start | bytes 786440 | tf_op jit(solution)/shard_map/ppermute | solution.py:44
  54.3 46.3 %copy-start.2 = (bf16[512,1280]{1,0:T(8,128)(2,1)}, bf16[512,1280]{1,0:T(8,128)(2,1)S(1)}, u32[]{:S(2)}) copy-start(bf16[512,1280]{1,0:T(8,128)(2,1)S(1)} %collective-permute-done.4.refs_7_.refs_2_) | copy-start | bytes 3932164
  56.0 44.7 %copy-start.4 = (bf16[512,1280]{1,0:T(8,128)(2,1)}, bf16[512,1280]{1,0:T(8,128)(2,1)S(1)}, u32[]{:S(2)}) copy-start(bf16[512,1280]{1,0:T(8,128)(2,1)S(1)} %collective-permute-done.3.refs_6_.refs_1_) | copy-start | bytes 3932164
  56.1 40.1 %collective-permute-start.10 = (bf16[256,1280]{1,0:T(8,128)(2,1)S(1)}, bf16[256,1280]{1,0:T(8,128)(2,1)S(1)}, u32[]{:S(2)}, u32[]{:S(2)}) collective-permute-start(bf16[256,1280]{1,0:T(8,128)(2,1)S(1)} %slice.36), channel_id=1, source_target_pairs={{0,16},{4,20},{8,24},{12,28},{16,0},{20,4},{24,8},{28,12},{1,17},{... | collective-permute-start | bytes 1966088 | tf_op jit(solution)/shard_map/ppermute | solution.py:44
  56.7 12.2 %collective-permute-start.6 = (bf16[128,2048]{1,0:T(8,128)(2,1)S(1)}, bf16[128,2048]{1,0:T(8,128)(2,1)S(1)}, u32[]{:S(2)}, u32[]{:S(2)}) collective-permute-start(bf16[128,2048]{1,0:T(8,128)(2,1)S(1)} %collective-permute-done.1.refs_2_), channel_id=1, source_target_pairs={{2,3},{1,0},{6,7},{5,4},{10,11},{9,8},{14,15},{13,12},{18,19},{17,... | collective-permute-start | bytes 1572872 | tf_op jit(solution)/shard_map/ppermute | solution.py:68
  58.8 10.9 %collective-permute-start.7 = (bf16[128,2048]{1,0:T(8,128)(2,1)S(1)}, bf16[128,2048]{1,0:T(8,128)(2,1)S(1)}, u32[]{:S(2)}, u32[]{:S(2)}) collective-permute-start(bf16[128,2048]{1,0:T(8,128)(2,1)S(1)} %pad_maximum_fusion.2.refs_0_), channel_id=1, source_target_pairs={{1,2},{2,1},{5,6},{6,5},{9,10},{10,9},{13,14},{14,13},{17,18},{18,... | collective-permute-start | bytes 1572872 | tf_op jit(solution)/shard_map/ppermute | solution.py:63
  59.5 23.1 %collective-permute-start.9 = (bf16[128,2048]{1,0:T(8,128)(2,1)S(1)}, bf16[128,2048]{1,0:T(8,128)(2,1)S(1)}, u32[]{:S(2)}, u32[]{:S(2)}) collective-permute-start(bf16[128,2048]{1,0:T(8,128)(2,1)S(1)} %pad_maximum_fusion.3.refs_0_), channel_id=1, source_target_pairs={{0,1},{1,0},{2,3},{3,2},{4,5},{5,4},{6,7},{7,6},{8,9},{9,8},{10,11... | collective-permute-start | bytes 1572872 | tf_op jit(solution)/shard_map/ppermute | solution.py:44
  65.3 30.9 %collective-permute-start.8 = (bf16[128,2048]{1,0:T(8,128)(2,1)S(1)}, bf16[128,2048]{1,0:T(8,128)(2,1)}, u32[]{:S(2)}, u32[]{:S(2)}) collective-permute-start(bf16[128,2048]{1,0:T(8,128)(2,1)S(1)} %pad_maximum_fusion.3.refs_0_), channel_id=1, source_target_pairs={{0,2},{1,3},{2,0},{3,1},{4,6},{5,7},{6,4},{7,5},{8,10},{9,11},{10,... | collective-permute-start | bytes 1572872 | tf_op jit(solution)/shard_map/ppermute | solution.py:44
  97.0 20.1 %collective-permute-start.12 = (bf16[128,2048]{1,0:T(8,128)(2,1)S(1)}, bf16[128,2048]{1,0:T(8,128)(2,1)}, u32[]{:S(2)}, u32[]{:S(2)}) collective-permute-start(bf16[128,2048]{1,0:T(8,128)(2,1)S(1)} %pad_maximum_fusion.3.refs_0_), channel_id=1, source_target_pairs={{1,2},{2,1},{5,6},{6,5},{9,10},{10,9},{13,14},{14,13},{17,18},{18,... | collective-permute-start | bytes 1572872 | tf_op jit(solution)/shard_map/ppermute | solution.py:63
  98.5 18.7 %collective-permute-start.11 = (bf16[128,2048]{1,0:T(8,128)(2,1)}, bf16[128,2048]{1,0:T(8,128)(2,1)}, u32[]{:S(2)}, u32[]{:S(2)}) collective-permute-start(bf16[128,2048]{1,0:T(8,128)(2,1)} %collective-permute-done.8.refs_2_), channel_id=1, source_target_pairs={{2,3},{1,0},{6,7},{5,4},{10,11},{9,8},{14,15},{13,12},{18,19},{17,... | collective-permute-start | bytes 1572872 | tf_op jit(solution)/shard_map/ppermute | solution.py:68
  100.7 16.4 %collective-permute-start.13 = (bf16[256,1280]{1,0:T(8,128)(2,1)}, bf16[256,1280]{1,0:T(8,128)(2,1)}, u32[]{:S(2)}, u32[]{:S(2)}) collective-permute-start(bf16[256,1280]{1,0:T(8,128)(2,1)} %slice.37), channel_id=1, source_target_pairs={{0,8},{4,12},{8,0},{12,4},{16,24},{20,28},{24,16},{28,20},{1,9},{5... | collective-permute-start | bytes 1966088 | tf_op jit(solution)/shard_map/ppermute | solution.py:44
  108.5 10.2 %copy-start.5 = (bf16[512,1280]{1,0:T(8,128)(2,1)S(1)}, bf16[512,1280]{1,0:T(8,128)(2,1)}, u32[]{:S(2)}) copy-start(bf16[512,1280]{1,0:T(8,128)(2,1)} %copy-done.4) | copy-start | bytes 3932164
  108.5 10.2 %copy-start.9 = (bf16[256,1280]{1,0:T(8,128)(2,1)S(1)}, bf16[256,1280]{1,0:T(8,128)(2,1)}, u32[]{:S(2)}) copy-start(bf16[256,1280]{1,0:T(8,128)(2,1)} %copy-done.8) | copy-start | bytes 1966084
  108.5 10.2 %copy-start.15 = (bf16[128,2048]{1,0:T(8,128)(2,1)S(1)}, bf16[128,2048]{1,0:T(8,128)(2,1)}, u32[]{:S(2)}) copy-start(bf16[128,2048]{1,0:T(8,128)(2,1)} %copy-done.14) | copy-start | bytes 1572868
  112.2 6.5 %collective-permute-start.14 = (bf16[256,1024]{1,0:T(8,128)(2,1)S(1)}, bf16[256,1024]{1,0:T(8,128)(2,1)S(1)}, u32[]{:S(2)}, u32[]{:S(2)}) collective-permute-start(bf16[256,1024]{1,0:T(8,128)(2,1)S(1)} %get-tuple-element.73), channel_id=1, source_target_pairs={{0,4},{4,0},{8,12},{12,8},{16,20},{20,16},{24,28},{28,24},{1,5},{5... | collective-permute-start | bytes 1572872 | tf_op jit(solution)/shard_map/ppermute | solution.py:44
  124.0 2.2 %collective-permute-start.15 = (bf16[256,1280]{1,0:T(8,128)(2,1)S(1)}, bf16[256,1280]{1,0:T(8,128)(2,1)S(1)}, u32[]{:S(2)}, u32[]{:S(2)}) collective-permute-start(bf16[256,1280]{1,0:T(8,128)(2,1)S(1)} %get-tuple-element.82), channel_id=1, source_target_pairs={{0,4},{4,0},{8,12},{12,8},{16,20},{20,16},{24,28},{28,24},{1,5},{5... | collective-permute-start | bytes 1966088 | tf_op jit(solution)/shard_map/ppermute | solution.py:44
  130.2 2.2 %collective-permute-start.16 = (bf16[256,1280]{1,0:T(8,128)(2,1)S(1)}, bf16[256,1280]{1,0:T(8,128)(2,1)S(1)}, u32[]{:S(2)}, u32[]{:S(2)}) collective-permute-start(bf16[256,1280]{1,0:T(8,128)(2,1)S(1)} %shard_map.98.own), channel_id=1, source_target_pairs={{0,4},{4,0},{8,12},{12,8},{16,20},{20,16},{24,28},{28,24},{1,5},{5... | collective-permute-start | bytes 1966088 | tf_op jit(solution)/shard_map/ppermute | solution.py:44
  137.3 16.0 %collective-permute-start.24 = (bf16[256,1280]{1,0:T(8,128)(2,1)S(1)}, bf16[256,1280]{1,0:T(8,128)(2,1)S(1)}, u32[]{:S(2)}, u32[]{:S(2)}) collective-permute-start(bf16[256,1280]{1,0:T(8,128)(2,1)S(1)} %get-tuple-element.101), channel_id=1, source_target_pairs={{0,8},{4,12},{8,0},{12,4},{16,24},{20,28},{24,16},{28,20},{1,9},{5... | collective-permute-start | bytes 1966088 | tf_op jit(solution)/shard_map/ppermute | solution.py:44
  137.9 15.6 %collective-permute-start.22 = (bf16[256,1280]{1,0:T(8,128)(2,1)S(1)}, bf16[256,1280]{1,0:T(8,128)(2,1)S(1)}, u32[]{:S(2)}, u32[]{:S(2)}) collective-permute-start(bf16[256,1280]{1,0:T(8,128)(2,1)S(1)} %get-tuple-element.102), channel_id=1, source_target_pairs={{0,16},{4,20},{8,24},{12,28},{16,0},{20,4},{24,8},{28,12},{1,17},{... | collective-permute-start | bytes 1966088 | tf_op jit(solution)/shard_map/ppermute | solution.py:44
  139.1 20.6 %collective-permute-start.19 = (bf16[128,2048]{1,0:T(8,128)(2,1)S(1)}, bf16[128,2048]{1,0:T(8,128)(2,1)S(1)}, u32[]{:S(2)}, u32[]{:S(2)}) collective-permute-start(bf16[128,2048]{1,0:T(8,128)(2,1)S(1)} %get-tuple-element.89), channel_id=1, source_target_pairs={{1,2},{2,1},{5,6},{6,5},{9,10},{10,9},{13,14},{14,13},{17,18},{18,... | collective-permute-start | bytes 1572872 | tf_op jit(solution)/shard_map/ppermute | solution.py:63
  139.8 19.9 %collective-permute-start.18 = (bf16[128,2048]{1,0:T(8,128)(2,1)S(1)}, bf16[128,2048]{1,0:T(8,128)(2,1)S(1)}, u32[]{:S(2)}, u32[]{:S(2)}) collective-permute-start(bf16[128,2048]{1,0:T(8,128)(2,1)S(1)} %get-tuple-element.89), channel_id=1, source_target_pairs={{3,2},{0,1},{7,6},{4,5},{11,10},{8,9},{15,14},{12,13},{19,18},{16,... | collective-permute-start | bytes 1572872 | tf_op jit(solution)/shard_map/ppermute | solution.py:68
  154.0 33.5 %collective-permute-start.25 = (bf16[512,1280]{1,0:T(8,128)(2,1)S(1)}, bf16[512,1280]{1,0:T(8,128)(2,1)S(1)}, u32[]{:S(2)}, u32[]{:S(2)}) collective-permute-start(bf16[512,1280]{1,0:T(8,128)(2,1)S(1)} %pad_maximum_fusion.1), channel_id=1, source_target_pairs={{0,16},{4,20},{8,24},{12,28},{16,0},{20,4},{24,8},{28,12},{1,17},{... | collective-permute-start | bytes 3932168 | tf_op jit(solution)/shard_map/ppermute | solution.py:44
  155.4 32.1 %collective-permute-start.23 = (bf16[512,1280]{1,0:T(8,128)(2,1)S(1)}, bf16[512,1280]{1,0:T(8,128)(2,1)S(1)}, u32[]{:S(2)}, u32[]{:S(2)}) collective-permute-start(bf16[512,1280]{1,0:T(8,128)(2,1)S(1)} %pad_maximum_fusion), channel_id=1, source_target_pairs={{0,8},{4,12},{8,0},{12,4},{16,24},{20,28},{24,16},{28,20},{1,9},{5... | collective-permute-start | bytes 3932168 | tf_op jit(solution)/shard_map/ppermute | solution.py:44
  156.6 24.5 %collective-permute-start.17 = (bf16[128,2048]{1,0:T(8,128)(2,1)S(1)}, bf16[128,2048]{1,0:T(8,128)(2,1)S(1)}, u32[]{:S(2)}, u32[]{:S(2)}) collective-permute-start(bf16[128,2048]{1,0:T(8,128)(2,1)S(1)} %get-tuple-element.88), channel_id=1, source_target_pairs={{0,1},{1,0},{2,3},{3,2},{4,5},{5,4},{6,7},{7,6},{8,9},{9,8},{10,11... | collective-permute-start | bytes 1572872 | tf_op jit(solution)/shard_map/ppermute | solution.py:44
  159.9 21.3 %collective-permute-start.20 = (bf16[128,2048]{1,0:T(8,128)(2,1)S(1)}, bf16[128,2048]{1,0:T(8,128)(2,1)S(1)}, u32[]{:S(2)}, u32[]{:S(2)}) collective-permute-start(bf16[128,2048]{1,0:T(8,128)(2,1)S(1)} %add.20), channel_id=1, source_target_pairs={{0,2},{1,3},{2,0},{3,1},{4,6},{5,7},{6,4},{7,5},{8,10},{9,11},{10,... | collective-permute-start | bytes 1572872 | tf_op jit(solution)/shard_map/ppermute | solution.py:44
  181.2 3.9 %collective-permute-start.21 = (bf16[64,2048]{1,0:T(8,128)(2,1)S(1)}, bf16[64,2048]{1,0:T(8,128)(2,1)S(1)}, u32[]{:S(2)}, u32[]{:S(2)}) collective-permute-start(bf16[64,2048]{1,0:T(8,128)(2,1)S(1)} %add_convert_fusion), channel_id=1, source_target_pairs={{0,4},{4,0},{8,12},{12,8},{16,20},{20,16},{24,28},{28,24},{1,5},{5... | collective-permute-start | bytes 786440 | tf_op jit(solution)/shard_map/ppermute | solution.py:44
  (18 other events, 43.4 us)
Sparse Core Ops, SparseCore 0:
  9.8 81.1 all-gather.1

commit v5 on v4

--- a/solution.py
+++ b/solution.py
@@ -48,50 +48,61 @@
     return lax.optimization_barrier(values)
 
 
-def gather_outward(value):
-    size = lax.axis_size("dp")
-    groups = [list(range(core, size, 2)) for core in range(2)]
-    return lax.all_gather(value, "dp", axis=1, tiled=True, axis_index_groups=groups)
-
-
 def everyone(value, axis, unit):
     size = lax.axis_size(axis) // unit
     return [value] + [swap(value, axis, unit * k) for k in range(1, size)]
 
 
+def gather_chips(value, axis):
+    if lax.axis_size("dp") != 8:
+        return everyone(value, "dp", 2)
+    near_x = swap(value, "dp", 2)
+    near_y = swap(value, "dp", 4)
+    near_x, near_y = tied(near_x, near_y)
+    far_top = swap(jnp.split(near_x, 2, axis)[0], "dp", 4)
+    far_bottom = swap(jnp.split(near_y, 2, axis)[1], "dp", 2)
+    return [value, near_x, near_y, far_top, far_bottom]
+
+
+def along(value, pairs):
+    return lax.ppermute(value, "tensor", pairs)
+
+
+def gather_tensor(value):
+    if lax.axis_size("tensor") != 4:
+        return everyone(value, "tensor", 1)
+    right_one = along(value, [(0, 1), (1, 2), (2, 3)])
+    left_one = along(value, [(1, 0), (2, 1), (3, 2)])
+    right_one, left_one = tied(right_one, left_one)
+    right_two = along(right_one, [(1, 2), (2, 3)])
+    left_two = along(left_one, [(1, 0), (2, 1)])
+    right_two, left_two = tied(right_two, left_two)
+    last = along(
+        jnp.where(lax.axis_index("tensor") == 1, left_two, right_two), [(1, 0), (2, 3)]
+    )
+    return [value, right_one, left_one, right_two, left_two, last]
+
+
+def pick(index, pieces, size, k, rows):
+    if len(pieces) == size:
+        return pieces[k][rows]
+    own, right_one, left_one, right_two, left_two, last = [piece.at[rows] for piece in pieces]
+    if k == 0:
+        return own[...]
+    if k == 1:
+        return jnp.where(index % 2 == 1, right_one[...], left_one[...])
+    if k == 2:
+        return jnp.where(index >= 2, right_two[...], left_two[...])
+    near = jnp.where(index == 1, left_one[...], right_one[...])
+    return jnp.where(jnp.logical_or(index == 0, index == 3), last[...], near)
+
+
 def inner_pair(value):
-    return lax.ppermute(value, "tensor", [(1, 2), (2, 1)])
-
-
-def outer_pair(value, outward=True):
-    pairs = [(2, 3), (1, 0)] if outward else [(3, 2), (0, 1)]
-    return lax.ppermute(value, "tensor", pairs)
-
-
-def staged_gathers(grad, normed_later, joint, project_out):
-    half = joint.shape[0] // 2
-    two_g, one_g = swap(grad, "tensor", 2), swap(grad, "tensor", 1)
-    near_x, near_y = swap(joint, "dp", 2), swap(joint, "dp", 4)
-    normed = normed_later()
-    grad, two_g, one_g, near_x, near_y, normed = tied(grad, two_g, one_g, near_x, near_y, normed)
-    outer_g, inner_g = outer_pair(two_g), inner_pair(grad)
-    two_n, one_n = swap(normed, "tensor", 2), swap(normed, "tensor", 1)
-    far_top = swap(near_x[:half], "dp", 4)
-    outer_g, inner_g, two_n, one_n, far_top, normed, near_y = tied(
-        outer_g, inner_g, two_n, one_n, far_top, normed, near_y
-    )
-    outer_n, inner_n = outer_pair(two_n), inner_pair(normed)
-    far_bottom = swap(near_y[half:], "dp", 2)
-    out_own, out_sent = project_out([grad, one_g, two_g, inner_g, outer_g])
-    outer_n, inner_n, far_bottom, out_own, out_sent = tied(
-        outer_n, inner_n, far_bottom, out_own, out_sent
-    )
-    return (
-        [normed, one_n, two_n, inner_n, outer_n],
-        [joint, near_x, near_y, far_top, far_bottom],
-        out_own,
-        out_sent,
-    )
+    return along(value, [(1, 2), (2, 1)])
+
+
+def outer_pair(value):
+    return along(value, [(3, 2), (0, 1)])
 
 
 def scatter_chips(blocks):
@@ -112,46 +123,40 @@
 def scatter_tensor(blocks):
     if len(blocks) != 4:
         return [blocks[0]] + [swap(blocks[k], "tensor", k) for k in range(1, len(blocks))]
-    outer, inner = outer_pair(blocks[3], False), inner_pair(blocks[3])
+    outer, inner = outer_pair(blocks[3]), inner_pair(blocks[3])
     outer, inner = tied(outer, inner)
     two, one = swap(blocks[2] + outer, "tensor", 2), swap(blocks[1], "tensor", 1)
     return [blocks[0], one, inner, two]
 
 
-def column_start(chip, which, block):
-    return pl.multiple_of((chip * 2 + which) * block, 128)
-
-
-def divide(chip, core, source, keep, send, block):
-    for k in range(keep.shape[1] // block):
-        columns = slice(k * block, (k + 1) * block)
-        keep[:, columns] = source[:, pl.ds(column_start(chip ^ k, core, block), block)]
-        send[:, columns] = source[:, pl.ds(column_start(chip ^ k, 1 - core, block), block)]
-
-
-def divide_kernel(block, place, source, keep, send):
-    divide(0, place[1], source, keep, send, block)
-
-
-def norm_kernel(block, place, tokens, gain, keep, send, normed):
+def column_start(place, k, which, block):
+    return pl.multiple_of(((place[0] ^ k) * 2 + which) * block, 128)
+
+
+def prepare_kernel(block, place, grad_out, tokens, gain, keep, send, normed):
+    rows, core = tokens.shape[0], place[1]
     values = tokens[...].astype(jnp.float32)
     root_mean = jnp.sqrt(jnp.mean(values * values, axis=-1, keepdims=True) + epsilon)
     normed[...] = (values / root_mean * gain[...].astype(jnp.float32)).astype(jnp.bfloat16)
-    divide(place[0], place[1], normed, keep, send, block)
-
-
-def project_kernel(pieces, weights, size, transposed, place, *refs):
+    for start, source in ((0, grad_out), (rows, normed)):
+        for k in range(keep.shape[1] // block):
+            place_out = (slice(start, start + rows), slice(k * block, (k + 1) * block))
+            keep[place_out] = source[:, pl.ds(column_start(place, k, core, block), block)]
+            send[place_out] = source[:, pl.ds(column_start(place, k, 1 - core, block), block)]
+
+
+def project_kernel(pieces, weights, size, first, transposed, place, *refs):
     row_refs, weight_refs = refs[:pieces], refs[pieces : pieces + weights]
     keep, send, pair = refs[pieces + weights :]
-    rows = row_refs[0].shape[0] // 2
+    rows = row_refs[0].shape[0] // 4
     length = rows * size
-    for k in range(size):
-        value = row_refs[k][...]
-        if pieces > size and k == size - 1:
-            middle = jnp.logical_or(place[2] == 1, place[2] == 2)
-            value = jnp.where(middle, value, row_refs[k + 1][...])
-        pair[k * rows : (k + 1) * rows] = value[:rows]
-        pair[length + k * rows : length + (k + 1) * rows] = value[rows:]
+    for core in range(2):
+        start = first + 2 * core * rows
+        for k in range(size):
+            target = core * length + k * rows
+            pair[target : target + rows] = pick(
+                place[2], row_refs, size, k, slice(start, start + rows)
+            )
     width = keep.shape[1]
     tile = 256 if width % 256 == 0 else width
 
@@ -178,14 +183,14 @@
             step(pl.ds(pl.multiple_of(number * tile, tile), tile))
 
 
-def project(place, pieces, weights, transposed, size, keep_pair):
-    rows = pieces[0].shape[0] // 2 * size
+def project(place, pieces, weights, first, transposed, size, keep_pair):
+    rows = pieces[0].shape[0] // 4 * size
     half = pieces[0].shape[1]
     width = weights[0].shape[0 if transposed else 1]
     outs = [shaped((rows, width), jnp.float32), shaped((rows, width))]
     pair = shaped((2 * rows, half))
     return call(
-        functools.partial(project_kernel, len(pieces), len(weights), size, transposed),
+        functools.partial(project_kernel, len(pieces), len(weights), size, first, transposed),
         [*outs, pair] if keep_pair else outs,
         [*pieces, *weights],
         [place],
@@ -356,8 +361,8 @@
         total = total + part[:rows].astype(jnp.float32)
     for k in range(total.shape[1] // block):
         columns = slice(k * block, (k + 1) * block)
-        gathered[:, pl.ds(column_start(place[0] ^ k, core, block), block)] = total[:, columns]
-        gathered[:, pl.ds(column_start(place[0] ^ k, 1 - core, block), block)] = handed[
+        gathered[:, pl.ds(column_start(place, k, core, block), block)] = total[:, columns]
+        gathered[:, pl.ds(column_start(place, k, 1 - core, block), block)] = handed[
             :, columns
         ].astype(jnp.float32)
     values = tokens[...].astype(jnp.float32)
@@ -383,40 +388,25 @@
     block = width // data_size
     query_width = query_weight.shape[1]
     gain = norm_gain.reshape(1, width)
-    halves = [shaped((rows, width // 2))] * 2
-
-    out_half = gather_outward(out_weight)
-    keep, send = call(functools.partial(divide_kernel, block), halves, [grad_out], [place])
-    grad_pair = jnp.concatenate([keep, swap(send, "dp", 1)], axis=0)
-    grad_pair, joint_parts, inputs = lax.optimization_barrier(
-        (grad_pair, (query_weight, kv_weight), (tokens, gain))
-    )
-    joint = jnp.concatenate(joint_parts, axis=1)
-
-    def normed_pair():
-        keep, send = call(
-            functools.partial(norm_kernel, block),
-            halves,
-            inputs,
-            [place],
-            [pltpu.VMEM((rows, width), jnp.bfloat16)],
-        )
-        return jnp.concatenate([keep, swap(send, "dp", 1)], axis=0)
-
-    def project_out(blocks):
-        own, sent = project(place, blocks, [out_half], True, tensor_size, False)
-        return own, swap(sent, "dp", 1)
-
-    if chips == 4 and tensor_size == 4:
-        normed_blocks, joint_blocks, out_own, out_sent = staged_gathers(
-            grad_pair, normed_pair, joint, project_out
-        )
-    else:
-        out_own, out_sent = project_out(everyone(grad_pair, "tensor", 1))
-        normed_blocks = everyone(normed_pair(), "tensor", 1)
-        joint_blocks = everyone(joint, "dp", 2)
-    own, sent, normed = project(place, normed_blocks, joint_blocks, False, tensor_size, True)
+
+    keep, send = call(
+        functools.partial(prepare_kernel, block),
+        [shaped((2 * rows, width // 2))] * 2,
+        [grad_out, tokens, gain],
+        [place],
+        [pltpu.VMEM((rows, width), jnp.bfloat16)],
+    )
+    row_pieces = gather_tensor(jnp.concatenate([keep, swap(send, "dp", 1)], axis=0))
+    joint_blocks = gather_chips(jnp.concatenate([query_weight, kv_weight], axis=1), 0)
+    *joint_blocks, out_weight = tied(*joint_blocks, out_weight)
+    out_blocks = gather_chips(out_weight, 1)
+
+    own, sent, normed = project(
+        place, row_pieces, joint_blocks, rows, False, tensor_size, True
+    )
     sent = swap(sent, "dp", 1)
+    out_own, out_sent = project(place, row_pieces, out_blocks, 0, True, tensor_size, False)
+    out_sent = swap(out_sent, "dp", 1)
     if levels:
         joined = (own + sent.astype(jnp.float32)).astype(jnp.bfloat16)
         keyvals = joined[:, query_width:]
@@ -446,11 +436,9 @@
         combined = jnp.concatenate([combined, kv_partial.astype(jnp.bfloat16)], axis=1)
     other = swap(combined, "dp", 1)
 
-    row_blocks = row_terms(combined, other, joint_blocks, tensor_size)
-    normed, *row_blocks = tied(normed, *row_blocks)
     far = weight_terms(normed, combined, other, chips - 1, 1, block)
     near = weight_terms(normed, combined, other, 0, chips - 1, block)
-    row_parts = scatter_tensor(row_blocks)
+    row_parts = scatter_tensor(row_terms(combined, other, joint_blocks, tensor_size))
     weight_parts = scatter_chips([*near, *far])
     handed = sum(part[rows:].astype(jnp.float32) for part in row_parts).astype(jnp.bfloat16)
     (input_grad,) = call(

time: 199 us -> 168 us (0.84)
  between operations: 14.3 us -> 0.92 us
  starting transfers between devices: 49.5 us -> 40.5 us
  local copies, waits for them, and re-layouts: 13.4 us -> 5.99 us
    ppermute x6 -> x7, waiting for transfers between devices: 3.54 us -> 28.3 us  [along(): return lax.ppermute(value, 'tensor', pairs)]
    ppermute x20 -> x19, waiting for transfers between devices: 88.1 us -> 63.5 us  [swap(): return lax.ppermute(value, axis, pairs)]
    ppermute x20 -> x19, starting transfers between devices: 35.2 us -> 25.7 us  [swap(): return lax.ppermute(value, axis, pairs)]
    unnamed x47 -> x30, local copies, waits for them, and re-layouts: 12.3 us -> 3.3 us
    pallas_call x9 -> x8, Pallas kernels: 23.8 us -> 24.9 us  [call(): pl.pallas_call(kernel, out_shape=outs, in_specs=[SCALARS] * len(scalars)...]
    ppermute x6 -> x7, starting transfers between devices: 14.3 us -> 14.8 us  [along(): return lax.ppermute(value, 'tensor', pairs)]
  transfers between devices with their start and end apart: 27 -> 26, of which waited for: 15 -> 17; matrix products, arithmetic and copies ran while one was open for 1% -> 2% of each run, Pallas kernels for 5% -> 11%
where the time goes in v5:
time: 168 us; the launch traced here: 167 us
  waiting for transfers between devices  91.8 us (55%)
  starting transfers between devices  40.5 us (24%)
  Pallas kernels  27 us (16%)
  local copies, waits for them, and re-layouts  5.99 us (4%)
    ppermute x19, waiting for transfers between devices, swap(): return lax.ppermute(value, axis, pairs)  63.5 us
    ppermute x7, waiting for transfers between devices, along(): return lax.ppermute(value, 'tensor', pairs)  28.3 us
    ppermute x19, starting transfers between devices, swap(): return lax.ppermute(value, axis, pairs)  25.7 us
    pallas_call x8, Pallas kernels, call(): pl.pallas_call(kernel, out_shape=outs, in_specs=[SCALARS] * len(scalars)...  24.9 us
    ppermute x7, starting transfers between devices, along(): return lax.ppermute(value, 'tensor', pairs)  14.8 us
  transfers between devices with their start and end apart: 26, of which 17 were waited for; matrix products, arithmetic and copies ran while one was open for 2% of the time, Pallas kernels for 11%

profile of v5, /device:TPU:1, one launch (start us, length us, event | category | flops | bytes accessed | tf_op | source)
XLA Modules:
  0.0 167.1 jit_solution(7788051521769279595)
XLA Ops:
  4.6 1.8 %collective-permute-done = bf16[128,2048]{1,0:T(8,128)(2,1)S(1)} collective-permute-done((bf16[128,2048]{1,0:T(8,128)(2,1)S(1)}, bf16[128,2048]{1,0:T(8,128)(2,1)S(1)}, u32[]{:S(2)}, u32[]{:S(2)}) %collective-permute-start) | collective-permute-done | bytes 524320 | tf_op jit(solution)/shard_map/ppermute | solution.py:44
  6.5 5.3 %collective-permute-start.1 = (bf16[256,2048]{1,0:T(8,128)(2,1)S(1)}, bf16[256,2048]{1,0:T(8,128)(2,1)}, u32[]{:S(2)}, u32[]{:S(2)}) collective-permute-start(bf16[256,2048]{1,0:T(8,128)(2,1)S(1)} %constant_dynamic-update-slice_fusion.refs_0_), channel_id=1, source_target_pairs={{0,1},{1,2},{2,3},{4,5},{5,6},{6,7},{8,9},{9,10},{10,11},{12,13},{... | collective-permute-start | bytes 3145736 | tf_op jit(solution)/shard_map/ppermute | solution.py:68
  11.8 1.3 collective-permute-start.2
  13.2 1.3 collective-permute-start.6
  14.5 1.2 collective-permute-start.7
  15.8 17.2 %collective-permute-done.1.refs_1_ = bf16[256,2048]{1,0:T(8,128)(2,1)} collective-permute-done((bf16[256,2048]{1,0:T(8,128)(2,1)S(1)}, bf16[256,2048]{1,0:T(8,128)(2,1)}, u32[]{:S(2)}, u32[]{:S(2)}) %collective-permute-start.1) | collective-permute-done | bytes 1048608 | tf_op jit(solution)/shard_map/ppermute | solution.py:68
  33.0 4.9 %collective-permute-done.2.refs_2_ = bf16[256,2048]{1,0:T(8,128)(2,1)} collective-permute-done((bf16[256,2048]{1,0:T(8,128)(2,1)S(1)}, bf16[256,2048]{1,0:T(8,128)(2,1)}, u32[]{:S(2)}, u32[]{:S(2)}) %collective-permute-start.2) | collective-permute-done | bytes 1048608 | tf_op jit(solution)/shard_map/ppermute | solution.py:68
  38.6 1.3 collective-permute-start.4
  39.9 3.1 %collective-permute-done.6.refs_7_.refs_1_ = bf16[512,1280]{1,0:T(8,128)(2,1)S(1)} collective-permute-done((bf16[512,1280]{1,0:T(8,128)(2,1)S(1)}, bf16[512,1280]{1,0:T(8,128)(2,1)S(1)}, u32[]{:S(2)}, u32[]{:S(2)}) %collective-permute-start.6) | collective-permute-done | bytes 1310752 | tf_op jit(solution)/shard_map/ppermute | solution.py:44
  48.3 11.1 %collective-permute-done.8.refs_9_.refs_3_ = bf16[256,1280]{1,0:T(8,128)(2,1)} collective-permute-done((bf16[256,1280]{1,0:T(8,128)(2,1)}, bf16[256,1280]{1,0:T(8,128)(2,1)}, u32[]{:S(2)}, u32[]{:S(2)}) %collective-permute-start.8) | collective-permute-done | bytes 655392 | tf_op jit(solution)/shard_map/ppermute | solution.py:44
  59.5 2.9 %collective-permute-done.9.refs_10_.refs_4_ = bf16[256,1280]{1,0:T(8,128)(2,1)} collective-permute-done((bf16[256,1280]{1,0:T(8,128)(2,1)}, bf16[256,1280]{1,0:T(8,128)(2,1)}, u32[]{:S(2)}, u32[]{:S(2)}) %collective-permute-start.9) | collective-permute-done | bytes 655392 | tf_op jit(solution)/shard_map/ppermute | solution.py:44
  62.9 2.3 %collective-permute-done.4.refs_4_ = bf16[256,2048]{1,0:T(8,128)(2,1)S(1)} collective-permute-done((bf16[256,2048]{1,0:T(8,128)(2,1)}, bf16[256,2048]{1,0:T(8,128)(2,1)S(1)}, u32[]{:S(2)}, u32[]{:S(2)}) %collective-permute-start.4) | collective-permute-done | bytes 1048608 | tf_op jit(solution)/shard_map/ppermute | solution.py:68
  65.3 1.6 collective-permute-start.5
  66.9 17.3 %collective-permute-done.10.refs_7_ = bf16[1024,512]{1,0:T(8,128)(2,1)S(1)} collective-permute-done((bf16[1024,512]{1,0:T(8,128)(2,1)}, bf16[1024,512]{1,0:T(8,128)(2,1)S(1)}, u32[]{:S(2)}, u32[]{:S(2)}) %collective-permute-start.10) | collective-permute-done | bytes 1048608 | tf_op jit(solution)/shard_map/ppermute | solution.py:44
  85.8 3.9 %collective-permute-done.5.refs_5_ = bf16[256,2048]{1,0:T(8,128)(2,1)S(1)} collective-permute-done((bf16[256,2048]{1,0:T(8,128)(2,1)S(1)}, bf16[256,2048]{1,0:T(8,128)(2,1)S(1)}, u32[]{:S(2)}, u32[]{:S(2)}) %collective-permute-start.5) | collective-permute-done | bytes 1048608 | tf_op jit(solution)/shard_map/ppermute | solution.py:68
  89.7 5.7 %shard_map.96 = (f32[256,1280]{1,0:T(8,128)S(1)}, bf16[256,1280]{1,0:T(8,128)(2,1)S(1)}, bf16[512,2048]{1,0:T(8,128)(2,1)S(1)}) custom-call(s32[3]{0:T(128)S(1)} %pad_add_fusion.place.refs_0_, bf16[256,2048]{1,0:T(8,128)(2,1)S(1)} %constant_dynamic-update-slice_fusion.refs_0_, bf16[256,2048]{1,0:T(8,128)(2,1)} %collective-permute-done.1.refs_1_, ...), custom_call_target="tpu_custom_call" | custom-call | flops 2684354560 | bytes 15597568 | tf_op jit(solution)/shard_map/pallas_call | solution.py:23
  95.4 3.4 %collective-permute-start.15 = (bf16[256,1280]{1,0:T(8,128)(2,1)S(1)}, bf16[256,1280]{1,0:T(8,128)(2,1)S(1)}, u32[]{:S(2)}, u32[]{:S(2)}) collective-permute-start(bf16[256,1280]{1,0:T(8,128)(2,1)S(1)} %get-tuple-element.54), channel_id=1, source_target_pairs={{0,4},{4,0},{8,12},{12,8},{16,20},{20,16},{24,28},{28,24},{1,5},{5... | collective-permute-start | bytes 1966088 | tf_op jit(solution)/shard_map/ppermute | solution.py:44
  98.9 4.7 %shard_map.95 = (f32[256,1024]{1,0:T(8,128)S(1)}, bf16[256,1024]{1,0:T(8,128)(2,1)S(1)}) custom-call(s32[3]{0:T(128)S(1)} %pad_add_fusion.place.refs_0_, bf16[256,2048]{1,0:T(8,128)(2,1)S(1)} %constant_dynamic-update-slice_fusion.refs_0_, bf16[256,2048]{1,0:T(8,128)(2,1)} %collective-permute-done.1.refs_1_, ...), custom_call_target="tpu_custom_call" | custom-call | flops 2147483648 | bytes 12058624 | tf_op jit(solution)/shard_map/pallas_call | solution.py:23
  104.5 1.5 collective-permute-done.14.refs_3_
  106.1 4.0 %shard_map.97.own = bf16[256,1280]{1,0:T(8,128)(2,1)S(1)} custom-call(s32[3]{0:T(128)S(1)} %pad_add_fusion.place.refs_0_, s32[1,4]{1,0:T(1,128)S(1)} %copy-done.11, f32[256,1024]{1,0:T(8,128)S(1)} %get-tuple-element.46.refs_2_, bf16[256,1024]{1,0:T(8,128)(2,1)S(1)} %collective-permute-done.14.refs_3_, f32[256,1280]{1,0:T(8,128)S(1)} %get-tuple-element.53.refs_4_, ...), custom_call_target="tpu_custom_call" | custom-call | flops 671088640 | bytes 4194304 | tf_op jit(solution)/shard_map/pallas_call | solution.py:23
  110.5 1.7 %collective-permute-done.16.other = bf16[256,1280]{1,0:T(8,128)(2,1)S(1)} collective-permute-done((bf16[256,1280]{1,0:T(8,128)(2,1)S(1)}, bf16[256,1280]{1,0:T(8,128)(2,1)S(1)}, u32[]{:S(2)}, u32[]{:S(2)}) %collective-permute-start.16) | collective-permute-done | bytes 655392 | tf_op jit(solution)/shard_map/ppermute | solution.py:44
  115.3 4.2 %shard_map.98 = (bf16[128,2048]{1,0:T(8,128)(2,1)S(1)}, bf16[128,2048]{1,0:T(8,128)(2,1)S(1)}, bf16[128,2048]{1,0:T(8,128)(2,1)S(1)}, bf16[128,2048]{1,0:T(8,128)(2,1)S(1)}) custom-call(bf16[256,1280]{1,0:T(8,128)(2,1)S(1)} %shard_map.97.own, bf16[256,1280]{1,0:T(8,128)(2,1)S(1)} %collective-permute-done.16.other, bf16[512,1280]{1,0:T(8,128)(2,1)S(1)} %copy-done.1, ...), custom_call_target="tpu_custom_call" | custom-call | flops 2684354560 | bytes 8650752 | tf_op jit(solution)/shard_map/pallas_call | solution.py:23
  119.5 3.7 %collective-permute-start.18 = (bf16[128,2048]{1,0:T(8,128)(2,1)S(1)}, bf16[128,2048]{1,0:T(8,128)(2,1)S(1)}, u32[]{:S(2)}, u32[]{:S(2)}) collective-permute-start(bf16[128,2048]{1,0:T(8,128)(2,1)S(1)} %get-tuple-element.57), channel_id=1, source_target_pairs={{3,2},{0,1},{7,6},{4,5},{11,10},{8,9},{15,14},{12,13},{19,18},{16,... | collective-permute-start | bytes 1572872 | tf_op jit(solution)/shard_map/ppermute | solution.py:68
  124.1 2.2 %shard_map.100 = (bf16[512,1280]{1,0:T(8,128)(2,1)S(1)}, bf16[512,1280]{1,0:T(8,128)(2,1)S(1)}, bf16[512,1280]{1,0:T(8,128)(2,1)S(1)}) custom-call(bf16[512,2048]{1,0:T(8,128)(2,1)S(1)} %get-tuple-element.61.pair, bf16[256,1280]{1,0:T(8,128)(2,1)S(1)} %shard_map.97.own, bf16[256,1280]{1,0:T(8,128)(2,1)S(1)} %collective-permute-done.16.other), custom_call_target="tpu_custom_call" | custom-call | flops 2013265920 | bytes 7340032 | tf_op jit(solution)/shard_map/pallas_call | solution.py:23
  126.3 2.9 %collective-permute-done.22 = bf16[256,1280]{1,0:T(8,128)(2,1)S(1)} collective-permute-done((bf16[256,1280]{1,0:T(8,128)(2,1)S(1)}, bf16[256,1280]{1,0:T(8,128)(2,1)S(1)}, u32[]{:S(2)}, u32[]{:S(2)}) %collective-permute-start.22) | collective-permute-done | bytes 655392 | tf_op jit(solution)/shard_map/ppermute | solution.py:44
  132.0 1.5 collective-permute-start.17
  133.7 3.5 %collective-permute-start.20 = (bf16[128,2048]{1,0:T(8,128)(2,1)S(1)}, bf16[128,2048]{1,0:T(8,128)(2,1)S(1)}, u32[]{:S(2)}, u32[]{:S(2)}) collective-permute-start(bf16[128,2048]{1,0:T(8,128)(2,1)S(1)} %add.20), channel_id=1, source_target_pairs={{0,2},{1,3},{2,0},{3,1},{4,6},{5,7},{6,4},{7,5},{8,10},{9,11},{10,... | collective-permute-start | bytes 1572872 | tf_op jit(solution)/shard_map/ppermute | solution.py:44
  137.2 16.2 %collective-permute-done.17.refs_1_ = bf16[128,2048]{1,0:T(8,128)(2,1)S(1)} collective-permute-done((bf16[128,2048]{1,0:T(8,128)(2,1)S(1)}, bf16[128,2048]{1,0:T(8,128)(2,1)S(1)}, u32[]{:S(2)}, u32[]{:S(2)}) %collective-permute-start.17) | collective-permute-done | bytes 524320 | tf_op jit(solution)/shard_map/ppermute | solution.py:44
  153.4 2.3 %collective-permute-done.20.refs_3_ = bf16[128,2048]{1,0:T(8,128)(2,1)S(1)} collective-permute-done((bf16[128,2048]{1,0:T(8,128)(2,1)S(1)}, bf16[128,2048]{1,0:T(8,128)(2,1)S(1)}, u32[]{:S(2)}, u32[]{:S(2)}) %collective-permute-start.20) | collective-permute-done | bytes 524320 | tf_op jit(solution)/shard_map/ppermute | solution.py:44
  155.8 5.7 %collective-permute-start.21 = (bf16[64,2048]{1,0:T(8,128)(2,1)S(1)}, bf16[64,2048]{1,0:T(8,128)(2,1)S(1)}, u32[]{:S(2)}, u32[]{:S(2)}) collective-permute-start(bf16[64,2048]{1,0:T(8,128)(2,1)S(1)} %add_convert_fusion), channel_id=1, source_target_pairs={{0,4},{4,0},{8,12},{12,8},{16,20},{20,16},{24,28},{28,24},{1,5},{5... | collective-permute-start | bytes 786440 | tf_op jit(solution)/shard_map/ppermute | solution.py:44
  162.7 2.2 %shard_map.99 = bf16[64,4096]{1,0:T(8,128)(2,1)} custom-call(s32[3]{0:T(128)S(1)} %pad_add_fusion.place.refs_0_, bf16[64,4096]{1,0:T(8,128)(2,1)S(1)} %copy-done.7, bf16[1,4096]{1,0:T(2,128)(2,1)S(1)} %reshape.9.gain, bf16[64,4096]{1,0:T(8,128)(2,1)S(1)} %copy-done.9, bf16[64,2048]{1,0:T(8,128)(2,1)S(1)} %collective-permute-done.21.handed, ...), custom_call_target="tpu_custom_call" | custom-call | bytes 3940352 | tf_op jit(solution)/shard_map/pallas_call | solution.py:23
  164.9 2.1 %shard_map.102 = (f32[512,1024]{1,0:T(8,128)}, f32[512,256]{1,0:T(8,128)}) custom-call(bf16[512,1280]{1,0:T(8,128)(2,1)S(1)} %get-tuple-element.62.refs_0_, bf16[512,1280]{1,0:T(8,128)(2,1)S(1)} %collective-permute-done.23.refs_1_, bf16[512,1280]{1,0:T(8,128)(2,1)S(1)} %collective-permute-done.25.refs_2_), custom_call_target="tpu_custom_call" | custom-call | bytes 6553600 | tf_op jit(solution)/shard_map/pallas_call | solution.py:339
  (74 shorter events, 22.0 us)
Async XLA Ops:
  4.5 2.0 %collective-permute-start = (bf16[128,2048]{1,0:T(8,128)(2,1)S(1)}, bf16[128,2048]{1,0:T(8,128)(2,1)S(1)}, u32[]{:S(2)}, u32[]{:S(2)}) collective-permute-start(bf16[128,2048]{1,0:T(8,128)(2,1)S(1)} %get-tuple-element.36), channel_id=1, source_target_pairs={{0,4},{4,0},{8,12},{12,8},{16,20},{20,16},{24,28},{28,24},{1,5},{5... | collective-permute-start | bytes 1572872 | tf_op jit(solution)/shard_map/ppermute | solution.py:44
  6.5 26.5 %collective-permute-start.1 = (bf16[256,2048]{1,0:T(8,128)(2,1)S(1)}, bf16[256,2048]{1,0:T(8,128)(2,1)}, u32[]{:S(2)}, u32[]{:S(2)}) collective-permute-start(bf16[256,2048]{1,0:T(8,128)(2,1)S(1)} %constant_dynamic-update-slice_fusion.refs_0_), channel_id=1, source_target_pairs={{0,1},{1,2},{2,3},{4,5},{5,6},{6,7},{8,9},{9,10},{10,11},{12,13},{... | collective-permute-start | bytes 3145736 | tf_op jit(solution)/shard_map/ppermute | solution.py:68
  11.8 26.0 %collective-permute-start.2 = (bf16[256,2048]{1,0:T(8,128)(2,1)S(1)}, bf16[256,2048]{1,0:T(8,128)(2,1)}, u32[]{:S(2)}, u32[]{:S(2)}) collective-permute-start(bf16[256,2048]{1,0:T(8,128)(2,1)S(1)} %constant_dynamic-update-slice_fusion.refs_0_), channel_id=1, source_target_pairs={{1,0},{2,1},{3,2},{5,4},{6,5},{7,6},{9,8},{10,9},{11,10},{13,12},{... | collective-permute-start | bytes 3145736 | tf_op jit(solution)/shard_map/ppermute | solution.py:68
  13.2 33.6 %copy-start = (bf16[512,1280]{1,0:T(8,128)(2,1)}, bf16[512,1280]{1,0:T(8,128)(2,1)S(1)}, u32[]{:S(2)}) copy-start(bf16[512,1280]{1,0:T(8,128)(2,1)S(1)} %constant_dynamic-update-slice_fusion.2.refs_6_.refs_0_) | copy-start | bytes 3932164
  13.2 29.7 %collective-permute-start.6 = (bf16[512,1280]{1,0:T(8,128)(2,1)S(1)}, bf16[512,1280]{1,0:T(8,128)(2,1)S(1)}, u32[]{:S(2)}, u32[]{:S(2)}) collective-permute-start(bf16[512,1280]{1,0:T(8,128)(2,1)S(1)} %constant_dynamic-update-slice_fusion.2.refs_6_.refs_0_), channel_id=1, source_target_pairs={{0,8},{4,12},{8,0},{12,4},{16,24},{20,28},{24,16},{28,20},{1,9},{5... | collective-permute-start | bytes 3932168 | tf_op jit(solution)/shard_map/ppermute | solution.py:44
  14.5 29.3 %collective-permute-start.7 = (bf16[512,1280]{1,0:T(8,128)(2,1)S(1)}, bf16[512,1280]{1,0:T(8,128)(2,1)S(1)}, u32[]{:S(2)}, u32[]{:S(2)}) collective-permute-start(bf16[512,1280]{1,0:T(8,128)(2,1)S(1)} %constant_dynamic-update-slice_fusion.2.refs_6_.refs_0_), channel_id=1, source_target_pairs={{0,16},{4,20},{8,24},{12,28},{16,0},{20,4},{24,8},{28,12},{1,17},{... | collective-permute-start | bytes 3932168 | tf_op jit(solution)/shard_map/ppermute | solution.py:44
  37.9 25.1 %collective-permute-start.3 = (bf16[256,2048]{1,0:T(8,128)(2,1)}, bf16[256,2048]{1,0:T(8,128)(2,1)S(1)}, u32[]{:S(2)}, u32[]{:S(2)}) collective-permute-start(bf16[256,2048]{1,0:T(8,128)(2,1)} %collective-permute-done.1.refs_1_), channel_id=1, source_target_pairs={{1,2},{2,3},{5,6},{6,7},{9,10},{10,11},{13,14},{14,15},{17,18},{18... | collective-permute-start | bytes 3145736 | tf_op jit(solution)/shard_map/ppermute | solution.py:68
  38.6 26.6 %collective-permute-start.4 = (bf16[256,2048]{1,0:T(8,128)(2,1)}, bf16[256,2048]{1,0:T(8,128)(2,1)S(1)}, u32[]{:S(2)}, u32[]{:S(2)}) collective-permute-start(bf16[256,2048]{1,0:T(8,128)(2,1)} %collective-permute-done.2.refs_2_), channel_id=1, source_target_pairs={{1,0},{2,1},{5,4},{6,5},{9,8},{10,9},{13,12},{14,13},{17,16},{18,1... | collective-permute-start | bytes 3145736 | tf_op jit(solution)/shard_map/ppermute | solution.py:68
  44.8 14.7 %collective-permute-start.8 = (bf16[256,1280]{1,0:T(8,128)(2,1)}, bf16[256,1280]{1,0:T(8,128)(2,1)}, u32[]{:S(2)}, u32[]{:S(2)}) collective-permute-start(bf16[256,1280]{1,0:T(8,128)(2,1)} %split.12), channel_id=1, source_target_pairs={{0,16},{4,20},{8,24},{12,28},{16,0},{20,4},{24,8},{28,12},{1,17},{... | collective-permute-start | bytes 1966088 | tf_op jit(solution)/shard_map/ppermute | solution.py:44
  47.9 14.4 %collective-permute-start.9 = (bf16[256,1280]{1,0:T(8,128)(2,1)}, bf16[256,1280]{1,0:T(8,128)(2,1)}, u32[]{:S(2)}, u32[]{:S(2)}) collective-permute-start(bf16[256,1280]{1,0:T(8,128)(2,1)} %split.13), channel_id=1, source_target_pairs={{0,8},{4,12},{8,0},{12,4},{16,24},{20,28},{24,16},{28,20},{1,9},{5... | collective-permute-start | bytes 1966088 | tf_op jit(solution)/shard_map/ppermute | solution.py:44
  62.4 21.8 %collective-permute-start.10 = (bf16[1024,512]{1,0:T(8,128)(2,1)}, bf16[1024,512]{1,0:T(8,128)(2,1)S(1)}, u32[]{:S(2)}, u32[]{:S(2)}) collective-permute-start(bf16[1024,512]{1,0:T(8,128)(2,1)} %refs_6_), channel_id=1, source_target_pairs={{0,8},{4,12},{8,0},{12,4},{16,24},{20,28},{24,16},{28,20},{1,9},{5... | collective-permute-start | bytes 3145736 | tf_op jit(solution)/shard_map/ppermute | solution.py:44
  62.7 21.5 %collective-permute-start.11 = (bf16[1024,512]{1,0:T(8,128)(2,1)}, bf16[1024,512]{1,0:T(8,128)(2,1)S(1)}, u32[]{:S(2)}, u32[]{:S(2)}) collective-permute-start(bf16[1024,512]{1,0:T(8,128)(2,1)} %refs_6_), channel_id=1, source_target_pairs={{0,16},{4,20},{8,24},{12,28},{16,0},{20,4},{24,8},{28,12},{1,17},{... | collective-permute-start | bytes 3145736 | tf_op jit(solution)/shard_map/ppermute | solution.py:44
  65.2 24.5 %copy-start.3 = (bf16[512,1280]{1,0:T(8,128)(2,1)S(1)}, bf16[512,1280]{1,0:T(8,128)(2,1)}, u32[]{:S(2)}) copy-start(bf16[512,1280]{1,0:T(8,128)(2,1)} %copy-done.2) | copy-start | bytes 3932164
  65.2 24.5 %copy-start.5 = (bf16[512,1280]{1,0:T(8,128)(2,1)S(1)}, bf16[512,1280]{1,0:T(8,128)(2,1)}, u32[]{:S(2)}) copy-start(bf16[512,1280]{1,0:T(8,128)(2,1)} %copy-done.4) | copy-start | bytes 3932164
  65.3 24.4 %copy-start.1 = (bf16[512,1280]{1,0:T(8,128)(2,1)S(1)}, bf16[512,1280]{1,0:T(8,128)(2,1)}, u32[]{:S(2)}) copy-start(bf16[512,1280]{1,0:T(8,128)(2,1)} %copy-done) | copy-start | bytes 3932164
  65.3 24.4 %collective-permute-start.5 = (bf16[256,2048]{1,0:T(8,128)(2,1)S(1)}, bf16[256,2048]{1,0:T(8,128)(2,1)S(1)}, u32[]{:S(2)}, u32[]{:S(2)}) collective-permute-start(bf16[256,2048]{1,0:T(8,128)(2,1)S(1)} %broadcast_select_fusion), channel_id=1, source_target_pairs={{1,0},{2,3},{5,4},{6,7},{9,8},{10,11},{13,12},{14,15},{17,16},{18,... | collective-permute-start | bytes 3145736 | tf_op jit(solution)/shard_map/ppermute | solution.py:68
  84.2 14.7 %collective-permute-start.12 = (bf16[1024,256]{1,0:T(8,128)(2,1)S(1)}, bf16[1024,256]{1,0:T(8,128)(2,1)S(1)}, u32[]{:S(2)}, u32[]{:S(2)}) collective-permute-start(bf16[1024,256]{1,0:T(8,128)(2,1)S(1)} %split.14), channel_id=1, source_target_pairs={{0,16},{4,20},{8,24},{12,28},{16,0},{20,4},{24,8},{28,12},{1,17},{... | collective-permute-start | bytes 1572872 | tf_op jit(solution)/shard_map/ppermute | solution.py:44
  84.6 14.3 %collective-permute-start.13 = (bf16[1024,256]{1,0:T(8,128)(2,1)S(1)}, bf16[1024,256]{1,0:T(8,128)(2,1)S(1)}, u32[]{:S(2)}, u32[]{:S(2)}) collective-permute-start(bf16[1024,256]{1,0:T(8,128)(2,1)S(1)} %split.15), channel_id=1, source_target_pairs={{0,8},{4,12},{8,0},{12,4},{16,24},{20,28},{24,16},{28,20},{1,9},{5... | collective-permute-start | bytes 1572872 | tf_op jit(solution)/shard_map/ppermute | solution.py:44
  95.4 10.6 %collective-permute-start.15 = (bf16[256,1280]{1,0:T(8,128)(2,1)S(1)}, bf16[256,1280]{1,0:T(8,128)(2,1)S(1)}, u32[]{:S(2)}, u32[]{:S(2)}) collective-permute-start(bf16[256,1280]{1,0:T(8,128)(2,1)S(1)} %get-tuple-element.54), channel_id=1, source_target_pairs={{0,4},{4,0},{8,12},{12,8},{16,20},{20,16},{24,28},{28,24},{1,5},{5... | collective-permute-start | bytes 1966088 | tf_op jit(solution)/shard_map/ppermute | solution.py:44
  103.6 2.4 %collective-permute-start.14 = (bf16[256,1024]{1,0:T(8,128)(2,1)S(1)}, bf16[256,1024]{1,0:T(8,128)(2,1)S(1)}, u32[]{:S(2)}, u32[]{:S(2)}) collective-permute-start(bf16[256,1024]{1,0:T(8,128)(2,1)S(1)} %get-tuple-element.47), channel_id=1, source_target_pairs={{0,4},{4,0},{8,12},{12,8},{16,20},{20,16},{24,28},{28,24},{1,5},{5... | collective-permute-start | bytes 1572872 | tf_op jit(solution)/shard_map/ppermute | solution.py:44
  110.1 2.2 %collective-permute-start.16 = (bf16[256,1280]{1,0:T(8,128)(2,1)S(1)}, bf16[256,1280]{1,0:T(8,128)(2,1)S(1)}, u32[]{:S(2)}, u32[]{:S(2)}) collective-permute-start(bf16[256,1280]{1,0:T(8,128)(2,1)S(1)} %shard_map.97.own), channel_id=1, source_target_pairs={{0,4},{4,0},{8,12},{12,8},{16,20},{20,16},{24,28},{28,24},{1,5},{5... | collective-permute-start | bytes 1966088 | tf_op jit(solution)/shard_map/ppermute | solution.py:44
  113.2 16.0 %collective-permute-start.22 = (bf16[256,1280]{1,0:T(8,128)(2,1)S(1)}, bf16[256,1280]{1,0:T(8,128)(2,1)S(1)}, u32[]{:S(2)}, u32[]{:S(2)}) collective-permute-start(bf16[256,1280]{1,0:T(8,128)(2,1)S(1)} %get-tuple-element.70), channel_id=1, source_target_pairs={{0,16},{4,20},{8,24},{12,28},{16,0},{20,4},{24,8},{28,12},{1,17},{... | collective-permute-start | bytes 1966088 | tf_op jit(solution)/shard_map/ppermute | solution.py:44
  114.2 15.6 %collective-permute-start.24 = (bf16[256,1280]{1,0:T(8,128)(2,1)S(1)}, bf16[256,1280]{1,0:T(8,128)(2,1)S(1)}, u32[]{:S(2)}, u32[]{:S(2)}) collective-permute-start(bf16[256,1280]{1,0:T(8,128)(2,1)S(1)} %get-tuple-element.69), channel_id=1, source_target_pairs={{0,8},{4,12},{8,0},{12,4},{16,24},{20,28},{24,16},{28,20},{1,9},{5... | collective-permute-start | bytes 1966088 | tf_op jit(solution)/shard_map/ppermute | solution.py:44
  119.5 14.1 %collective-permute-start.18 = (bf16[128,2048]{1,0:T(8,128)(2,1)S(1)}, bf16[128,2048]{1,0:T(8,128)(2,1)S(1)}, u32[]{:S(2)}, u32[]{:S(2)}) collective-permute-start(bf16[128,2048]{1,0:T(8,128)(2,1)S(1)} %get-tuple-element.57), channel_id=1, source_target_pairs={{3,2},{0,1},{7,6},{4,5},{11,10},{8,9},{15,14},{12,13},{19,18},{16,... | collective-permute-start | bytes 1572872 | tf_op jit(solution)/shard_map/ppermute | solution.py:68
  123.2 10.4 %collective-permute-start.19 = (bf16[128,2048]{1,0:T(8,128)(2,1)S(1)}, bf16[128,2048]{1,0:T(8,128)(2,1)S(1)}, u32[]{:S(2)}, u32[]{:S(2)}) collective-permute-start(bf16[128,2048]{1,0:T(8,128)(2,1)S(1)} %get-tuple-element.57), channel_id=1, source_target_pairs={{1,2},{2,1},{5,6},{6,5},{9,10},{10,9},{13,14},{14,13},{17,18},{18,... | collective-permute-start | bytes 1572872 | tf_op jit(solution)/shard_map/ppermute | solution.py:68
  130.1 34.8 %collective-permute-start.23 = (bf16[512,1280]{1,0:T(8,128)(2,1)S(1)}, bf16[512,1280]{1,0:T(8,128)(2,1)S(1)}, u32[]{:S(2)}, u32[]{:S(2)}) collective-permute-start(bf16[512,1280]{1,0:T(8,128)(2,1)S(1)} %pad_maximum_fusion), channel_id=1, source_target_pairs={{0,8},{4,12},{8,0},{12,4},{16,24},{20,28},{24,16},{28,20},{1,9},{5... | collective-permute-start | bytes 3932168 | tf_op jit(solution)/shard_map/ppermute | solution.py:44
  131.4 33.6 %collective-permute-start.25 = (bf16[512,1280]{1,0:T(8,128)(2,1)S(1)}, bf16[512,1280]{1,0:T(8,128)(2,1)S(1)}, u32[]{:S(2)}, u32[]{:S(2)}) collective-permute-start(bf16[512,1280]{1,0:T(8,128)(2,1)S(1)} %pad_maximum_fusion.1), channel_id=1, source_target_pairs={{0,16},{4,20},{8,24},{12,28},{16,0},{20,4},{24,8},{28,12},{1,17},{... | collective-permute-start | bytes 3932168 | tf_op jit(solution)/shard_map/ppermute | solution.py:44
  132.0 21.3 %collective-permute-start.17 = (bf16[128,2048]{1,0:T(8,128)(2,1)S(1)}, bf16[128,2048]{1,0:T(8,128)(2,1)S(1)}, u32[]{:S(2)}, u32[]{:S(2)}) collective-permute-start(bf16[128,2048]{1,0:T(8,128)(2,1)S(1)} %get-tuple-element.56), channel_id=1, source_target_pairs={{0,1},{1,0},{2,3},{3,2},{4,5},{5,4},{6,7},{7,6},{8,9},{9,8},{10,11... | collective-permute-start | bytes 1572872 | tf_op jit(solution)/shard_map/ppermute | solution.py:44
  133.6 29.1 %copy-start.7 = (bf16[64,4096]{1,0:T(8,128)(2,1)S(1)}, bf16[64,4096]{1,0:T(8,128)(2,1)}, u32[]{:S(2)}) copy-start(bf16[64,4096]{1,0:T(8,128)(2,1)} %tokens.3) | copy-start | bytes 1572868
  133.6 29.1 %copy-start.9 = (bf16[64,4096]{1,0:T(8,128)(2,1)S(1)}, bf16[64,4096]{1,0:T(8,128)(2,1)}, u32[]{:S(2)}) copy-start(bf16[64,4096]{1,0:T(8,128)(2,1)} %grad_out.3) | copy-start | bytes 1572868
  133.7 22.0 %collective-permute-start.20 = (bf16[128,2048]{1,0:T(8,128)(2,1)S(1)}, bf16[128,2048]{1,0:T(8,128)(2,1)S(1)}, u32[]{:S(2)}, u32[]{:S(2)}) collective-permute-start(bf16[128,2048]{1,0:T(8,128)(2,1)S(1)} %add.20), channel_id=1, source_target_pairs={{0,2},{1,3},{2,0},{3,1},{4,6},{5,7},{6,4},{7,5},{8,10},{9,11},{10,... | collective-permute-start | bytes 1572872 | tf_op jit(solution)/shard_map/ppermute | solution.py:44
  155.8 6.9 %collective-permute-start.21 = (bf16[64,2048]{1,0:T(8,128)(2,1)S(1)}, bf16[64,2048]{1,0:T(8,128)(2,1)S(1)}, u32[]{:S(2)}, u32[]{:S(2)}) collective-permute-start(bf16[64,2048]{1,0:T(8,128)(2,1)S(1)} %add_convert_fusion), channel_id=1, source_target_pairs={{0,4},{4,0},{8,12},{12,8},{16,20},{20,16},{24,28},{28,24},{1,5},{5... | collective-permute-start | bytes 786440 | tf_op jit(solution)/shard_map/ppermute | solution.py:44
  (8 other events, 49.3 us)

commit v6 on v5

--- a/solution.py
+++ b/solution.py
@@ -18,7 +18,7 @@
 SCALARS = pl.BlockSpec(memory_space=pltpu.SMEM)
 
 
-def call(kernel, outs, operands, scalars=(), scratch=(), flops=0, megabytes=32):
+def call(kernel, outs, operands, scalars=(), scratch=(), flops=0, megabytes=24):
     moved = sum(math.prod(a.shape) * a.dtype.itemsize for a in (*operands, *outs))
     return pl.pallas_call(
         kernel,
@@ -53,15 +53,16 @@
     return [value] + [swap(value, axis, unit * k) for k in range(1, size)]
 
 
-def gather_chips(value, axis):
+def gather_chips(value):
     if lax.axis_size("dp") != 8:
-        return everyone(value, "dp", 2)
+        return everyone(value, "dp", 2), []
+    half = value.shape[0] // 2
     near_x = swap(value, "dp", 2)
     near_y = swap(value, "dp", 4)
     near_x, near_y = tied(near_x, near_y)
-    far_top = swap(jnp.split(near_x, 2, axis)[0], "dp", 4)
-    far_bottom = swap(jnp.split(near_y, 2, axis)[1], "dp", 2)
-    return [value, near_x, near_y, far_top, far_bottom]
+    far_top = swap(near_x[:half], "dp", 4)
+    far_bottom = swap(near_y[half:], "dp", 2)
+    return [value, near_x, near_y], [far_top, far_bottom]
 
 
 def along(value, pairs):
@@ -125,7 +126,8 @@
         return [blocks[0]] + [swap(blocks[k], "tensor", k) for k in range(1, len(blocks))]
     outer, inner = outer_pair(blocks[3]), inner_pair(blocks[3])
     outer, inner = tied(outer, inner)
-    two, one = swap(blocks[2] + outer, "tensor", 2), swap(blocks[1], "tensor", 1)
+    carried, adjacent = tied(blocks[2] + outer, blocks[1])
+    two, one = swap(carried, "tensor", 2), swap(adjacent, "tensor", 1)
     return [blocks[0], one, inner, two]
 
 
@@ -145,62 +147,104 @@
             send[place_out] = source[:, pl.ds(column_start(place, k, 1 - core, block), block)]
 
 
-def project_kernel(pieces, weights, size, first, transposed, place, *refs):
+def merge_kernel(out_weight, query_weight, kv_weight, merged):
+    block, start = merged.shape[0], 0
+    for chunk in range(out_weight.shape[0] // block):
+        merged[:, start : start + block] = out_weight[chunk * block : (chunk + 1) * block]
+        start += block
+    for weight in (query_weight, kv_weight):
+        merged[:, start : start + weight.shape[1]] = weight[...]
+        start += weight.shape[1]
+
+
+def products(grads, normed, weights, first, out_width, block, columns):
+    chunks = out_width // block
+    size = weights[0].shape[0]
+    if columns < out_width:
+        chunk = columns // block
+        for row in range(0, block, min(size, 256)):
+            total = None
+            if size == block:
+                for k, weight in enumerate(weights):
+                    right = weight[row : row + min(size, 256), chunk * block : (chunk + 1) * block]
+                    left = grads[:, first + k * block : first + (k + 1) * block]
+                    term = dot(left, right, CONTRACT_LAST)
+                    total = term if total is None else total + term
+            else:
+                right = weights[row // size][:, chunk * block : (chunk + 1) * block]
+                total = dot(grads[:, first : first + block], right, CONTRACT_LAST)
+            yield slice(columns + row, columns + row + min(size, 256)), total
+    else:
+        width = min(256, weights[0].shape[1] - columns)
+        total = None
+        for k, weight in enumerate(weights):
+            left = normed[:, first + k * size : first + (k + 1) * size]
+            term = dot(left, weight[:, columns : columns + width])
+            total = term if total is None else total + term
+        yield slice(columns, columns + width), total
+
+
+def column_steps(out_width, width, block):
+    return [*range(0, out_width, block), *range(out_width, width, 256)]
+
+
+def early_kernel(pieces, weights, size, out_width, place, *refs):
     row_refs, weight_refs = refs[:pieces], refs[pieces : pieces + weights]
-    keep, send, pair = refs[pieces + weights :]
+    total, grads, normed = refs[pieces + weights :]
     rows = row_refs[0].shape[0] // 4
-    length = rows * size
+    block = weight_refs[0].shape[0]
     for core in range(2):
-        start = first + 2 * core * rows
-        for k in range(size):
-            target = core * length + k * rows
-            pair[target : target + rows] = pick(
-                place[2], row_refs, size, k, slice(start, start + rows)
-            )
-    width = keep.shape[1]
-    tile = 256 if width % 256 == 0 else width
-
-    def step(columns):
-        start, total = 0, None
-        for weight in weight_refs:
-            depth = weight.shape[1 if transposed else 0]
-            left = pair[:, start : start + depth]
-            if transposed:
-                term = dot(left, weight[columns, :], CONTRACT_LAST)
-            else:
-                term = dot(left, weight[:, columns])
-            total = term if total is None else total + term
-            start += depth
-        keep[:, columns] = total[:length]
-        send[:, columns] = total[length:].astype(jnp.bfloat16)
-
-    if tile == width:
-        step(slice(0, width))
-    else:
-
-        @pl.loop(0, width // tile)
-        def _(number):
-            step(pl.ds(pl.multiple_of(number * tile, tile), tile))
-
-
-def project(place, pieces, weights, first, transposed, size, keep_pair):
+        for number, pair in enumerate((grads, normed)):
+            start = (2 * core + number) * rows
+            for k in range(size):
+                target = (core * size + k) * rows
+                pair[target : target + rows] = pick(
+                    place[2], row_refs, size, k, slice(start, start + rows)
+                )
+    for columns in column_steps(out_width, total.shape[1], block):
+        for place_out, value in products(grads, normed, weight_refs, 0, out_width, block, columns):
+            total[:, place_out] = value
+
+
+def late_kernel(first, out_width, block, total, grads, normed, *refs):
+    weight_refs, (keep, send) = refs[:-2], refs[-2:]
+    length = keep.shape[0]
+    if not weight_refs:
+        keep[...] = total[:length]
+        send[...] = total[length:].astype(jnp.bfloat16)
+    for columns in column_steps(out_width, keep.shape[1], block) if weight_refs else []:
+        for place_out, value in products(
+            grads, normed, weight_refs, first, out_width, block, columns
+        ):
+            keep[:, place_out] = total[:length, place_out] + value[:length]
+            send[:, place_out] = (total[length:, place_out] + value[length:]).astype(jnp.bfloat16)
+
+
+def project(place, pieces, early, late, size, out_width):
     rows = pieces[0].shape[0] // 4 * size
     half = pieces[0].shape[1]
-    width = weights[0].shape[0 if transposed else 1]
-    outs = [shaped((rows, width), jnp.float32), shaped((rows, width))]
-    pair = shaped((2 * rows, half))
-    return call(
-        functools.partial(project_kernel, len(pieces), len(weights), size, first, transposed),
-        [*outs, pair] if keep_pair else outs,
-        [*pieces, *weights],
+    block, width = early[0].shape
+    first = len(early) * block
+    total, grads, normed = call(
+        functools.partial(early_kernel, len(pieces), len(early), size, out_width),
+        [shaped((2 * rows, width), jnp.float32)] + [shaped((2 * rows, half))] * 2,
+        [*pieces, *early],
         [place],
-        () if keep_pair else [pltpu.VMEM(pair.shape, pair.dtype)],
-        flops=4 * rows * half * width,
-    )
-
-
-def attention_kernel(rows, heads, place, lengths, out_own, out_sent, own, sent, grads, partial):
-    length = out_own.shape[0]
+        flops=4 * rows * first * width,
+        megabytes=24,
+    )
+    own, sent = call(
+        functools.partial(late_kernel, first, out_width, block),
+        [shaped((rows, width), jnp.float32), shaped((rows, width))],
+        [total, grads, normed, *late],
+        flops=4 * rows * (half - first) * width,
+        megabytes=24,
+    )
+    return own, sent, normed
+
+
+def attention_kernel(rows, heads, place, lengths, own, sent, grads, partial):
+    length = own.shape[0]
     width = heads * HD
     scale = 1 / math.sqrt(HD)
     tensor_index = place[2]
@@ -224,13 +268,13 @@
     def joined(first, second, columns):
         return (first[:, columns] + second[:, columns].astype(jnp.float32)).astype(jnp.bfloat16)
 
-    keys = joined(own, sent, slice(width, width + HD))
-    values = joined(own, sent, slice(width + HD, width + 2 * HD))
+    keys = joined(own, sent, slice(2 * width, 2 * width + HD))
+    values = joined(own, sent, slice(2 * width + HD, 2 * width + 2 * HD))
     key_total = value_total = None
     for head in range(heads):
         columns = slice(head * HD, (head + 1) * HD)
-        queries = joined(own, sent, columns)
-        out_grad = joined(out_own, out_sent, columns)
+        out_grad = joined(own, sent, columns)
+        queries = joined(own, sent, slice(width + head * HD, width + (head + 1) * HD))
         scores = jnp.where(allowed, dot(keys, queries, CONTRACT_LAST) * scale, -1e30)
         expo = jnp.exp(scores - jnp.max(scores, axis=0, keepdims=True))
         probs = expo * (1 / jnp.sum(expo, axis=0, keepdims=True))
@@ -250,8 +294,8 @@
         partial[:, HD:] = value_total
 
 
-def attention(place, lengths, out_own, out_sent, own, sent, rows, split):
-    length, width = out_own.shape
+def attention(place, lengths, own, sent, rows, width, split):
+    length = own.shape[0]
     outs = [shaped((length, width if split else width + 2 * HD))]
     if split:
         outs.append(shaped((length, 2 * HD), jnp.float32))
@@ -262,7 +306,7 @@
     return call(
         kernel,
         outs,
-        [out_own, out_sent, own, sent],
+        [own, sent],
         [place, lengths],
         flops=10 * length * length * width,
     )
@@ -289,7 +333,7 @@
     )
 
 
-def row_kernel(weights, own, other, *refs):
+def row_kernel(weights, offset_columns, own, other, *refs):
     weight_refs, outs = refs[:weights], refs[weights:]
     length = own.shape[0]
     rows = length // len(outs)
@@ -297,7 +341,7 @@
     for weight in weight_refs:
         tile = min(weight.shape[0], 256)
         for part in range(weight.shape[0] // tile):
-            right = weight[part * tile : (part + 1) * tile, :]
+            right = weight[part * tile : (part + 1) * tile, offset_columns:]
             for offset, left in ((0, own), (rows, other)):
                 term = dot(left[...], right, CONTRACT_LAST).astype(jnp.bfloat16)
                 for k, out in enumerate(outs):
@@ -307,11 +351,11 @@
             start += tile
 
 
-def row_terms(own, other, weights, size):
+def row_terms(own, other, weights, size, out_width):
     length, width = own.shape
     half = sum(weight.shape[0] for weight in weights)
     return call(
-        functools.partial(row_kernel, len(weights)),
+        functools.partial(row_kernel, len(weights), out_width),
         [shaped((2 * length // size, half))] * size,
         [own, other, *weights],
         flops=4 * length * width * half,
@@ -396,31 +440,31 @@
         [place],
         [pltpu.VMEM((rows, width), jnp.bfloat16)],
     )
+    out_width = out_weight.shape[0]
+    send, out_weight, query_weight, kv_weight = tied(send, out_weight, query_weight, kv_weight)
     row_pieces = gather_tensor(jnp.concatenate([keep, swap(send, "dp", 1)], axis=0))
-    joint_blocks = gather_chips(jnp.concatenate([query_weight, kv_weight], axis=1), 0)
-    *joint_blocks, out_weight = tied(*joint_blocks, out_weight)
-    out_blocks = gather_chips(out_weight, 1)
-
-    own, sent, normed = project(
-        place, row_pieces, joint_blocks, rows, False, tensor_size, True
-    )
+    (merged,) = call(
+        merge_kernel,
+        [shaped((block, out_width + query_width + kv_weight.shape[1]))],
+        [out_weight, query_weight, kv_weight],
+    )
+    early, late = gather_chips(merged)
+    own, sent, normed = project(place, row_pieces, early, late, tensor_size, out_width)
     sent = swap(sent, "dp", 1)
-    out_own, out_sent = project(place, row_pieces, out_blocks, 0, True, tensor_size, False)
-    out_sent = swap(out_sent, "dp", 1)
     if levels:
         joined = (own + sent.astype(jnp.float32)).astype(jnp.bfloat16)
-        keyvals = joined[:, query_width:]
+        keyvals = joined[:, out_width + query_width :]
         for bit_index in range(levels):
             partner = swap(keyvals, "tensor", 2**bit_index)
             upper = tensor_index >> bit_index & 1 == 1
             keyvals = jnp.concatenate(
                 [jnp.where(upper, partner, keyvals), jnp.where(upper, keyvals, partner)], axis=1
             )
-        own = jnp.concatenate([joined[:, :query_width], keyvals], axis=1).astype(jnp.float32)
+        own = jnp.concatenate(
+            [joined[:, : out_width + query_width], keyvals], axis=1
+        ).astype(jnp.float32)
         sent = jnp.zeros(own.shape, jnp.bfloat16)
-    combined, *partial = attention(
-        place, doc_lengths, out_own, out_sent, own, sent, rows, levels > 0
-    )
+    combined, *partial = attention(place, doc_lengths, own, sent, rows, query_width, levels > 0)
     if levels:
         kv_partial = partial[0]
         for bit_index in reversed(range(levels)):
@@ -438,17 +482,19 @@
 
     far = weight_terms(normed, combined, other, chips - 1, 1, block)
     near = weight_terms(normed, combined, other, 0, chips - 1, block)
-    row_parts = scatter_tensor(row_terms(combined, other, joint_blocks, tensor_size))
+    row_parts = scatter_tensor(row_terms(combined, other, early + late, tensor_size, out_width))
     weight_parts = scatter_chips([*near, *far])
     handed = sum(part[rows:].astype(jnp.float32) for part in row_parts).astype(jnp.bfloat16)
+    handed = swap(handed, "dp", 1)
+    query_grad, kv_grad = finish(weight_parts, query_width, 1 / data_size)
+    handed, query_grad, kv_grad = tied(handed, query_grad, kv_grad)
     (input_grad,) = call(
         functools.partial(input_kernel, len(row_parts), block),
         [shaped((rows, width))],
-        [tokens, gain, grad_out, swap(handed, "dp", 1), *row_parts],
+        [tokens, gain, grad_out, handed, *row_parts],
         [place],
         [pltpu.VMEM((rows, width), jnp.float32)],
     )
-    query_grad, kv_grad = finish(weight_parts, query_width, 1 / data_size)
     return (input_grad, query_grad, kv_grad)
 
 

time: 168 us -> 167 us (level)
  waiting for transfers between devices: 91.8 us -> 96.8 us
  starting transfers between devices: 40.5 us -> 35.7 us
    ppermute x7, waiting for transfers between devices: 28.3 us -> 66.3 us  [along(): return lax.ppermute(value, 'tensor', pairs)]
    ppermute x19 -> x14, waiting for transfers between devices: 63.5 us -> 30.5 us  [swap(): return lax.ppermute(value, axis, pairs)]
    ppermute x19 -> x14, starting transfers between devices: 25.7 us -> 22.9 us  [swap(): return lax.ppermute(value, axis, pairs)]
    slice x0 -> x2, local copies, waits for them, and re-layouts: none -> 2.69 us  [the longest x1 1.35 us: gather_chips(): far_top = swap(near_x[:half], 'dp', 4)]
    ppermute x7, starting transfers between devices: 14.8 us -> 12.8 us  [along(): return lax.ppermute(value, 'tensor', pairs)]
    split x4 -> x0, local copies, waits for them, and re-layouts: 1.83 us -> none  [the longest x2 0.92 us: gather_chips(): far_top = swap(jnp.split(near_x, 2, axis)[0], 'dp', 4)]
    pallas_call x8 -> x9, Pallas kernels: 24.9 us -> 24.6 us  [call(): pl.pallas_call(kernel, out_shape=outs, in_specs=[SCALARS] * len(scalars)...]
  transfers between devices with their start and end apart: 26 -> 21, of which waited for: 17 -> 12; matrix products, arithmetic and copies ran while one was open for 2% -> 2% of each run, Pallas kernels for 11% -> 10%
where the time goes in v6:
time: 167 us
  waiting for transfers between devices  96.8 us (58%)
  starting transfers between devices  35.7 us (21%)
  Pallas kernels  26.7 us (16%)
  local copies, waits for them, and re-layouts  5.7 us (3%)
    ppermute x7, waiting for transfers between devices, along(): return lax.ppermute(value, 'tensor', pairs)  66.3 us
    ppermute x14, waiting for transfers between devices, swap(): return lax.ppermute(value, axis, pairs)  30.5 us
    pallas_call x9, Pallas kernels, call(): pl.pallas_call(kernel, out_shape=outs, in_specs=[SCALARS] * len(scalars)...  24.6 us
    ppermute x14, starting transfers between devices, swap(): return lax.ppermute(value, axis, pairs)  22.9 us
    ppermute x7, starting transfers between devices, along(): return lax.ppermute(value, 'tensor', pairs)  12.8 us
  transfers between devices with their start and end apart: 21, of which 12 were waited for; matrix products, arithmetic and copies ran while one was open for 2% of the time, Pallas kernels for 10%

profile of v6, /device:TPU:1, one launch (start us, length us, event | category | flops | bytes accessed | tf_op | source)
XLA Modules:
  0.0 166.7 jit_solution(15956387599573052869)
XLA Ops:
  4.7 1.8 %collective-permute-done = bf16[128,2048]{1,0:T(8,128)(2,1)S(1)} collective-permute-done((bf16[128,2048]{1,0:T(8,128)(2,1)S(1)}, bf16[128,2048]{1,0:T(8,128)(2,1)S(1)}, u32[]{:S(2)}, u32[]{:S(2)}) %collective-permute-start) | collective-permute-done | bytes 524320 | tf_op jit(solution)/shard_map/ppermute | solution.py:44
  6.5 5.3 %collective-permute-start.1 = (bf16[256,2048]{1,0:T(8,128)(2,1)S(1)}, bf16[256,2048]{1,0:T(8,128)(2,1)}, u32[]{:S(2)}, u32[]{:S(2)}) collective-permute-start(bf16[256,2048]{1,0:T(8,128)(2,1)S(1)} %constant_dynamic-update-slice_fusion.refs_0_), channel_id=1, source_target_pairs={{0,1},{1,2},{2,3},{4,5},{5,6},{6,7},{8,9},{9,10},{10,11},{12,13},{... | collective-permute-start | bytes 3145736 | tf_op jit(solution)/shard_map/ppermute | solution.py:69
  11.9 1.3 collective-permute-start.2
  13.4 1.3 collective-permute-start.6
  14.6 1.2 collective-permute-start.7
  15.9 17.1 %collective-permute-done.1.refs_1_ = bf16[256,2048]{1,0:T(8,128)(2,1)} collective-permute-done((bf16[256,2048]{1,0:T(8,128)(2,1)S(1)}, bf16[256,2048]{1,0:T(8,128)(2,1)}, u32[]{:S(2)}, u32[]{:S(2)}) %collective-permute-start.1) | collective-permute-done | bytes 1048608 | tf_op jit(solution)/shard_map/ppermute | solution.py:69
  33.0 4.9 %collective-permute-done.2.refs_2_ = bf16[256,2048]{1,0:T(8,128)(2,1)} collective-permute-done((bf16[256,2048]{1,0:T(8,128)(2,1)S(1)}, bf16[256,2048]{1,0:T(8,128)(2,1)}, u32[]{:S(2)}, u32[]{:S(2)}) %collective-permute-start.2) | collective-permute-done | bytes 1048608 | tf_op jit(solution)/shard_map/ppermute | solution.py:69
  38.6 1.3 collective-permute-start.4
  39.9 25.4 %collective-permute-done.4.refs_4_ = bf16[256,2048]{1,0:T(8,128)(2,1)} collective-permute-done((bf16[256,2048]{1,0:T(8,128)(2,1)}, bf16[256,2048]{1,0:T(8,128)(2,1)}, u32[]{:S(2)}, u32[]{:S(2)}) %collective-permute-start.4) | collective-permute-done | bytes 1048608 | tf_op jit(solution)/shard_map/ppermute | solution.py:69
  65.5 1.3 collective-permute-start.5
  66.8 1.3 slice.36
  68.2 1.3 collective-permute-start.8
  69.5 1.3 slice.37
  70.8 1.3 collective-permute-start.9
  72.1 17.8 %collective-permute-done.5.refs_5_ = bf16[256,2048]{1,0:T(8,128)(2,1)S(1)} collective-permute-done((bf16[256,2048]{1,0:T(8,128)(2,1)S(1)}, bf16[256,2048]{1,0:T(8,128)(2,1)S(1)}, u32[]{:S(2)}, u32[]{:S(2)}) %collective-permute-start.5) | collective-permute-done | bytes 1048608 | tf_op jit(solution)/shard_map/ppermute | solution.py:69
  89.9 7.3 %shard_map.96 = (f32[512,2304]{1,0:T(8,128)S(1)}, bf16[512,2048]{1,0:T(8,128)(2,1)S(1)}, bf16[512,2048]{1,0:T(8,128)(2,1)S(1)}) custom-call(s32[3]{0:T(128)S(1)} %pad_add_fusion.place.refs_0_, bf16[256,2048]{1,0:T(8,128)(2,1)S(1)} %copy-done.8, bf16[256,2048]{1,0:T(8,128)(2,1)} %collective-permute-done.1.refs_1_, ...), custom_call_target="tpu_custom_call" | custom-call | flops 3623878656 | bytes 22282240 | tf_op jit(solution)/shard_map/pallas_call | solution.py:23
  97.3 1.5 shard_map.97
  98.8 3.4 %collective-permute-start.10 = (bf16[256,2304]{1,0:T(8,128)(2,1)S(1)}, bf16[256,2304]{1,0:T(8,128)(2,1)S(1)}, u32[]{:S(2)}, u32[]{:S(2)}) collective-permute-start(bf16[256,2304]{1,0:T(8,128)(2,1)S(1)} %get-tuple-element.52), channel_id=1, source_target_pairs={{0,4},{4,0},{8,12},{12,8},{16,20},{20,16},{24,28},{28,24},{1,5},{5... | collective-permute-start | bytes 3538952 | tf_op jit(solution)/shard_map/ppermute | solution.py:44
  102.2 2.5 %collective-permute-done.10.refs_3_ = bf16[256,2304]{1,0:T(8,128)(2,1)S(1)} collective-permute-done((bf16[256,2304]{1,0:T(8,128)(2,1)S(1)}, bf16[256,2304]{1,0:T(8,128)(2,1)S(1)}, u32[]{:S(2)}, u32[]{:S(2)}) %collective-permute-start.10) | collective-permute-done | bytes 1179680 | tf_op jit(solution)/shard_map/ppermute | solution.py:44
  104.7 4.0 %shard_map.98.own = bf16[256,1280]{1,0:T(8,128)(2,1)S(1)} custom-call(s32[3]{0:T(128)S(1)} %pad_add_fusion.place.refs_0_, s32[1,4]{1,0:T(1,128)S(1)} %copy-done.9, f32[256,2304]{1,0:T(8,128)S(1)} %get-tuple-element.51.refs_2_, bf16[256,2304]{1,0:T(8,128)(2,1)S(1)} %collective-permute-done.10.refs_3_), custom_call_target="tpu_custom_call" | custom-call | flops 671088640 | bytes 4194304 | tf_op jit(solution)/shard_map/pallas_call | solution.py:23
  109.1 1.7 %collective-permute-done.11.other = bf16[256,1280]{1,0:T(8,128)(2,1)S(1)} collective-permute-done((bf16[256,1280]{1,0:T(8,128)(2,1)S(1)}, bf16[256,1280]{1,0:T(8,128)(2,1)S(1)}, u32[]{:S(2)}, u32[]{:S(2)}) %collective-permute-start.11) | collective-permute-done | bytes 655392 | tf_op jit(solution)/shard_map/ppermute | solution.py:44
  111.8 1.3 collective-permute-start.17
  114.4 5.3 %shard_map.99 = (bf16[128,2048]{1,0:T(8,128)(2,1)S(1)}, bf16[128,2048]{1,0:T(8,128)(2,1)S(1)}, bf16[128,2048]{1,0:T(8,128)(2,1)S(1)}, bf16[128,2048]{1,0:T(8,128)(2,1)S(1)}) custom-call(bf16[256,1280]{1,0:T(8,128)(2,1)S(1)} %shard_map.98.own, bf16[256,1280]{1,0:T(8,128)(2,1)S(1)} %collective-permute-done.11.other, ...), custom_call_target="tpu_custom_call" | custom-call | flops 2684354560 | bytes 12845056 | tf_op jit(solution)/shard_map/pallas_call | solution.py:23
  119.6 2.0 %collective-permute-start.12 = (bf16[128,2048]{1,0:T(8,128)(2,1)S(1)}, bf16[128,2048]{1,0:T(8,128)(2,1)S(1)}, u32[]{:S(2)}, u32[]{:S(2)}) collective-permute-start(bf16[128,2048]{1,0:T(8,128)(2,1)S(1)} %get-tuple-element.55), channel_id=1, source_target_pairs={{3,2},{0,1},{7,6},{4,5},{11,10},{8,9},{15,14},{12,13},{19,18},{16,... | collective-permute-start | bytes 1572872 | tf_op jit(solution)/shard_map/ppermute | solution.py:69
  122.6 2.3 %shard_map.100 = (bf16[512,1280]{1,0:T(8,128)(2,1)S(1)}, bf16[512,1280]{1,0:T(8,128)(2,1)S(1)}, bf16[512,1280]{1,0:T(8,128)(2,1)S(1)}) custom-call(bf16[512,2048]{1,0:T(8,128)(2,1)S(1)} %get-tuple-element.50.normed.pair, bf16[256,1280]{1,0:T(8,128)(2,1)S(1)} %shard_map.98.own, bf16[256,1280]{1,0:T(8,128)(2,1)S(1)} %collective-permute-done.11.other), custom_call_target="tpu_custom_call" | custom-call | flops 2013265920 | bytes 7340032 | tf_op jit(solution)/shard_map/pallas_call | solution.py:23
  124.8 3.0 %collective-permute-done.17 = bf16[256,1280]{1,0:T(8,128)(2,1)S(1)} collective-permute-done((bf16[256,1280]{1,0:T(8,128)(2,1)S(1)}, bf16[256,1280]{1,0:T(8,128)(2,1)S(1)}, u32[]{:S(2)}, u32[]{:S(2)}) %collective-permute-start.17) | collective-permute-done | bytes 655392 | tf_op jit(solution)/shard_map/ppermute | solution.py:44
  129.6 1.3 collective-permute-start.18
  132.1 3.6 %collective-permute-start.14 = (bf16[128,2048]{1,0:T(8,128)(2,1)S(1)}, bf16[128,2048]{1,0:T(8,128)(2,1)S(1)}, u32[]{:S(2)}, u32[]{:S(2)}) collective-permute-start(bf16[128,2048]{1,0:T(8,128)(2,1)S(1)} %get-tuple-element.58), channel_id=1, source_target_pairs={{0,1},{1,0},{2,3},{3,2},{4,5},{5,4},{6,7},{7,6},{8,9},{9,8},{10,11... | collective-permute-start | bytes 1572872 | tf_op jit(solution)/shard_map/ppermute | solution.py:44
  135.7 20.4 %collective-permute-done.14.refs_1_ = bf16[128,2048]{1,0:T(8,128)(2,1)S(1)} collective-permute-done((bf16[128,2048]{1,0:T(8,128)(2,1)S(1)}, bf16[128,2048]{1,0:T(8,128)(2,1)S(1)}, u32[]{:S(2)}, u32[]{:S(2)}) %collective-permute-start.14) | collective-permute-done | bytes 524320 | tf_op jit(solution)/shard_map/ppermute | solution.py:44
  156.4 5.9 %collective-permute-start.16 = (bf16[64,2048]{1,0:T(8,128)(2,1)S(1)}, bf16[64,2048]{1,0:T(8,128)(2,1)S(1)}, u32[]{:S(2)}, u32[]{:S(2)}) collective-permute-start(bf16[64,2048]{1,0:T(8,128)(2,1)S(1)} %add_convert_fusion), channel_id=1, source_target_pairs={{0,4},{4,0},{8,12},{12,8},{16,20},{20,16},{24,28},{28,24},{1,5},{5... | collective-permute-start | bytes 786440 | tf_op jit(solution)/shard_map/ppermute | solution.py:44
  162.4 2.1 %shard_map.102 = (f32[512,1024]{1,0:T(8,128)}, f32[512,256]{1,0:T(8,128)}) custom-call(bf16[512,1280]{1,0:T(8,128)(2,1)S(1)} %get-tuple-element.61.refs_0_, bf16[512,1280]{1,0:T(8,128)(2,1)S(1)} %collective-permute-done.18.refs_1_, bf16[512,1280]{1,0:T(8,128)(2,1)S(1)} %collective-permute-done.20.refs_2_), custom_call_target="tpu_custom_call" | custom-call | bytes 6553600 | tf_op jit(solution)/shard_map/pallas_call | solution.py:383
  164.5 2.2 %shard_map.103 = bf16[64,4096]{1,0:T(8,128)(2,1)} custom-call(s32[3]{0:T(128)S(1)} %pad_add_fusion.place.refs_0_, bf16[64,4096]{1,0:T(8,128)(2,1)S(1)} %copy-done.1, bf16[1,4096]{1,0:T(2,128)(2,1)S(1)} %reshape.9.gain, bf16[64,4096]{1,0:T(8,128)(2,1)S(1)} %copy-done.3, bf16[64,2048]{1,0:T(8,128)(2,1)S(1)} %collective-permute-done.16.handed, ...), custom_call_target="tpu_custom_call" | custom-call | bytes 3940352 | tf_op jit(solution)/shard_map/pallas_call | solution.py:23
  (53 shorter events, 11.8 us)
Async XLA Ops:
  1.4 1.0 copy-start
  2.5 1.0 copy-start.2
  3.5 9.6 %copy-start.6 = (bf16[512,256]{1,0:T(8,128)(2,1)S(1)}, bf16[512,256]{1,0:T(8,128)(2,1)}, u32[]{:S(2)}) copy-start(bf16[512,256]{1,0:T(8,128)(2,1)} %kv_weight) | copy-start | bytes 786436
  4.5 8.7 %copy-start.4 = (bf16[1024,512]{1,0:T(8,128)(2,1)S(1)}, bf16[1024,512]{1,0:T(8,128)(2,1)}, u32[]{:S(2)}) copy-start(bf16[1024,512]{1,0:T(8,128)(2,1)} %out_weight) | copy-start | bytes 3145732
  4.5 8.7 %copy-start.5 = (bf16[512,1024]{1,0:T(8,128)(2,1)S(1)}, bf16[512,1024]{1,0:T(8,128)(2,1)}, u32[]{:S(2)}) copy-start(bf16[512,1024]{1,0:T(8,128)(2,1)} %query_weight) | copy-start | bytes 3145732
  4.5 2.0 %collective-permute-start = (bf16[128,2048]{1,0:T(8,128)(2,1)S(1)}, bf16[128,2048]{1,0:T(8,128)(2,1)S(1)}, u32[]{:S(2)}, u32[]{:S(2)}) collective-permute-start(bf16[128,2048]{1,0:T(8,128)(2,1)S(1)} %get-tuple-element.38), channel_id=1, source_target_pairs={{0,4},{4,0},{8,12},{12,8},{16,20},{20,16},{24,28},{28,24},{1,5},{5... | collective-permute-start | bytes 1572872 | tf_op jit(solution)/shard_map/ppermute | solution.py:44
  6.5 6.8 %copy-start.7 = (bf16[256,2048]{1,0:T(8,128)(2,1)}, bf16[256,2048]{1,0:T(8,128)(2,1)S(1)}, u32[]{:S(2)}) copy-start(bf16[256,2048]{1,0:T(8,128)(2,1)S(1)} %constant_dynamic-update-slice_fusion.refs_0_) | copy-start | bytes 3145732
  6.5 26.5 %collective-permute-start.1 = (bf16[256,2048]{1,0:T(8,128)(2,1)S(1)}, bf16[256,2048]{1,0:T(8,128)(2,1)}, u32[]{:S(2)}, u32[]{:S(2)}) collective-permute-start(bf16[256,2048]{1,0:T(8,128)(2,1)S(1)} %constant_dynamic-update-slice_fusion.refs_0_), channel_id=1, source_target_pairs={{0,1},{1,2},{2,3},{4,5},{5,6},{6,7},{8,9},{9,10},{10,11},{12,13},{... | collective-permute-start | bytes 3145736 | tf_op jit(solution)/shard_map/ppermute | solution.py:69
  11.9 26.0 %collective-permute-start.2 = (bf16[256,2048]{1,0:T(8,128)(2,1)S(1)}, bf16[256,2048]{1,0:T(8,128)(2,1)}, u32[]{:S(2)}, u32[]{:S(2)}) collective-permute-start(bf16[256,2048]{1,0:T(8,128)(2,1)S(1)} %constant_dynamic-update-slice_fusion.refs_0_), channel_id=1, source_target_pairs={{1,0},{2,1},{3,2},{5,4},{6,5},{7,6},{9,8},{10,9},{11,10},{13,12},{... | collective-permute-start | bytes 3145736 | tf_op jit(solution)/shard_map/ppermute | solution.py:69
  13.4 53.4 %collective-permute-start.6 = (bf16[512,2304]{1,0:T(8,128)(2,1)S(1)}, bf16[512,2304]{1,0:T(8,128)(2,1)}, u32[]{:S(2)}, u32[]{:S(2)}) collective-permute-start(bf16[512,2304]{1,0:T(8,128)(2,1)S(1)} %shard_map.95.refs_6_.refs_0_), channel_id=1, source_target_pairs={{0,8},{4,12},{8,0},{12,4},{16,24},{20,28},{24,16},{28,20},{1,9},{5... | collective-permute-start | bytes 7077896 | tf_op jit(solution)/shard_map/ppermute | solution.py:44
  14.6 52.2 %collective-permute-start.7 = (bf16[512,2304]{1,0:T(8,128)(2,1)S(1)}, bf16[512,2304]{1,0:T(8,128)(2,1)}, u32[]{:S(2)}, u32[]{:S(2)}) collective-permute-start(bf16[512,2304]{1,0:T(8,128)(2,1)S(1)} %shard_map.95.refs_6_.refs_0_), channel_id=1, source_target_pairs={{0,16},{4,20},{8,24},{12,28},{16,0},{20,4},{24,8},{28,12},{1,17},{... | collective-permute-start | bytes 7077896 | tf_op jit(solution)/shard_map/ppermute | solution.py:44
  37.9 2.0 %collective-permute-start.3 = (bf16[256,2048]{1,0:T(8,128)(2,1)}, bf16[256,2048]{1,0:T(8,128)(2,1)S(1)}, u32[]{:S(2)}, u32[]{:S(2)}) collective-permute-start(bf16[256,2048]{1,0:T(8,128)(2,1)} %collective-permute-done.1.refs_1_), channel_id=1, source_target_pairs={{1,2},{2,3},{5,6},{6,7},{9,10},{10,11},{13,14},{14,15},{17,18},{18... | collective-permute-start | bytes 3145736 | tf_op jit(solution)/shard_map/ppermute | solution.py:69
  38.6 26.7 %collective-permute-start.4 = (bf16[256,2048]{1,0:T(8,128)(2,1)}, bf16[256,2048]{1,0:T(8,128)(2,1)}, u32[]{:S(2)}, u32[]{:S(2)}) collective-permute-start(bf16[256,2048]{1,0:T(8,128)(2,1)} %collective-permute-done.2.refs_2_), channel_id=1, source_target_pairs={{1,0},{2,1},{5,4},{6,5},{9,8},{10,9},{13,12},{14,13},{17,16},{18,1... | collective-permute-start | bytes 3145736 | tf_op jit(solution)/shard_map/ppermute | solution.py:69
  65.5 24.4 %collective-permute-start.5 = (bf16[256,2048]{1,0:T(8,128)(2,1)S(1)}, bf16[256,2048]{1,0:T(8,128)(2,1)S(1)}, u32[]{:S(2)}, u32[]{:S(2)}) collective-permute-start(bf16[256,2048]{1,0:T(8,128)(2,1)S(1)} %broadcast_select_fusion), channel_id=1, source_target_pairs={{1,0},{2,3},{5,4},{6,7},{9,8},{10,11},{13,12},{14,15},{17,16},{18,... | collective-permute-start | bytes 3145736 | tf_op jit(solution)/shard_map/ppermute | solution.py:69
  68.1 21.7 %copy-start.8 = (bf16[256,2048]{1,0:T(8,128)(2,1)S(1)}, bf16[256,2048]{1,0:T(8,128)(2,1)}, u32[]{:S(2)}) copy-start(bf16[256,2048]{1,0:T(8,128)(2,1)} %copy-done.7) | copy-start | bytes 3145732
  68.2 29.1 %collective-permute-start.8 = (bf16[256,2304]{1,0:T(8,128)(2,1)S(1)}, bf16[256,2304]{1,0:T(8,128)(2,1)S(1)}, u32[]{:S(2)}, u32[]{:S(2)}) collective-permute-start(bf16[256,2304]{1,0:T(8,128)(2,1)S(1)} %slice.36), channel_id=1, source_target_pairs={{0,16},{4,20},{8,24},{12,28},{16,0},{20,4},{24,8},{28,12},{1,17},{... | collective-permute-start | bytes 3538952 | tf_op jit(solution)/shard_map/ppermute | solution.py:44
  70.8 26.4 %collective-permute-start.9 = (bf16[256,2304]{1,0:T(8,128)(2,1)S(1)}, bf16[256,2304]{1,0:T(8,128)(2,1)S(1)}, u32[]{:S(2)}, u32[]{:S(2)}) collective-permute-start(bf16[256,2304]{1,0:T(8,128)(2,1)S(1)} %slice.37), channel_id=1, source_target_pairs={{0,8},{4,12},{8,0},{12,4},{16,24},{20,28},{24,16},{28,20},{1,9},{5... | collective-permute-start | bytes 3538952 | tf_op jit(solution)/shard_map/ppermute | solution.py:44
  97.3 7.4 %copy-start.9 = (s32[1,4]{1,0:T(1,128)S(1)}, s32[1,4]{1,0:T(1,128)}, u32[]{:S(2)}) copy-start(s32[1,4]{1,0:T(1,128)} %refs_1_.1) | copy-start | bytes 52
  98.8 5.9 %collective-permute-start.10 = (bf16[256,2304]{1,0:T(8,128)(2,1)S(1)}, bf16[256,2304]{1,0:T(8,128)(2,1)S(1)}, u32[]{:S(2)}, u32[]{:S(2)}) collective-permute-start(bf16[256,2304]{1,0:T(8,128)(2,1)S(1)} %get-tuple-element.52), channel_id=1, source_target_pairs={{0,4},{4,0},{8,12},{12,8},{16,20},{20,16},{24,28},{28,24},{1,5},{5... | collective-permute-start | bytes 3538952 | tf_op jit(solution)/shard_map/ppermute | solution.py:44
  108.7 2.2 %collective-permute-start.11 = (bf16[256,1280]{1,0:T(8,128)(2,1)S(1)}, bf16[256,1280]{1,0:T(8,128)(2,1)S(1)}, u32[]{:S(2)}, u32[]{:S(2)}) collective-permute-start(bf16[256,1280]{1,0:T(8,128)(2,1)S(1)} %shard_map.98.own), channel_id=1, source_target_pairs={{0,4},{4,0},{8,12},{12,8},{16,20},{20,16},{24,28},{28,24},{1,5},{5... | collective-permute-start | bytes 1966088 | tf_op jit(solution)/shard_map/ppermute | solution.py:44
  111.8 16.0 %collective-permute-start.17 = (bf16[256,1280]{1,0:T(8,128)(2,1)S(1)}, bf16[256,1280]{1,0:T(8,128)(2,1)S(1)}, u32[]{:S(2)}, u32[]{:S(2)}) collective-permute-start(bf16[256,1280]{1,0:T(8,128)(2,1)S(1)} %get-tuple-element.72), channel_id=1, source_target_pairs={{0,16},{4,20},{8,24},{12,28},{16,0},{20,4},{24,8},{28,12},{1,17},{... | collective-permute-start | bytes 1966088 | tf_op jit(solution)/shard_map/ppermute | solution.py:44
  113.1 15.6 %collective-permute-start.19 = (bf16[256,1280]{1,0:T(8,128)(2,1)S(1)}, bf16[256,1280]{1,0:T(8,128)(2,1)S(1)}, u32[]{:S(2)}, u32[]{:S(2)}) collective-permute-start(bf16[256,1280]{1,0:T(8,128)(2,1)S(1)} %get-tuple-element.71), channel_id=1, source_target_pairs={{0,8},{4,12},{8,0},{12,4},{16,24},{20,28},{24,16},{28,20},{1,9},{5... | collective-permute-start | bytes 1966088 | tf_op jit(solution)/shard_map/ppermute | solution.py:44
  119.6 12.3 %collective-permute-start.12 = (bf16[128,2048]{1,0:T(8,128)(2,1)S(1)}, bf16[128,2048]{1,0:T(8,128)(2,1)S(1)}, u32[]{:S(2)}, u32[]{:S(2)}) collective-permute-start(bf16[128,2048]{1,0:T(8,128)(2,1)S(1)} %get-tuple-element.55), channel_id=1, source_target_pairs={{3,2},{0,1},{7,6},{4,5},{11,10},{8,9},{15,14},{12,13},{19,18},{16,... | collective-permute-start | bytes 1572872 | tf_op jit(solution)/shard_map/ppermute | solution.py:69
  121.7 10.2 %collective-permute-start.13 = (bf16[128,2048]{1,0:T(8,128)(2,1)S(1)}, bf16[128,2048]{1,0:T(8,128)(2,1)S(1)}, u32[]{:S(2)}, u32[]{:S(2)}) collective-permute-start(bf16[128,2048]{1,0:T(8,128)(2,1)S(1)} %get-tuple-element.55), channel_id=1, source_target_pairs={{1,2},{2,1},{5,6},{6,5},{9,10},{10,9},{13,14},{14,13},{17,18},{18,... | collective-permute-start | bytes 1572872 | tf_op jit(solution)/shard_map/ppermute | solution.py:69
  129.1 33.3 %collective-permute-start.20 = (bf16[512,1280]{1,0:T(8,128)(2,1)S(1)}, bf16[512,1280]{1,0:T(8,128)(2,1)S(1)}, u32[]{:S(2)}, u32[]{:S(2)}) collective-permute-start(bf16[512,1280]{1,0:T(8,128)(2,1)S(1)} %pad_maximum_fusion.1), channel_id=1, source_target_pairs={{0,16},{4,20},{8,24},{12,28},{16,0},{20,4},{24,8},{28,12},{1,17},{... | collective-permute-start | bytes 3932168 | tf_op jit(solution)/shard_map/ppermute | solution.py:44
  129.6 32.8 %collective-permute-start.18 = (bf16[512,1280]{1,0:T(8,128)(2,1)S(1)}, bf16[512,1280]{1,0:T(8,128)(2,1)S(1)}, u32[]{:S(2)}, u32[]{:S(2)}) collective-permute-start(bf16[512,1280]{1,0:T(8,128)(2,1)S(1)} %pad_maximum_fusion), channel_id=1, source_target_pairs={{0,8},{4,12},{8,0},{12,4},{16,24},{20,28},{24,16},{28,20},{1,9},{5... | collective-permute-start | bytes 3932168 | tf_op jit(solution)/shard_map/ppermute | solution.py:44
  132.1 24.1 %collective-permute-start.14 = (bf16[128,2048]{1,0:T(8,128)(2,1)S(1)}, bf16[128,2048]{1,0:T(8,128)(2,1)S(1)}, u32[]{:S(2)}, u32[]{:S(2)}) collective-permute-start(bf16[128,2048]{1,0:T(8,128)(2,1)S(1)} %get-tuple-element.58), channel_id=1, source_target_pairs={{0,1},{1,0},{2,3},{3,2},{4,5},{5,4},{6,7},{7,6},{8,9},{9,8},{10,11... | collective-permute-start | bytes 1572872 | tf_op jit(solution)/shard_map/ppermute | solution.py:44
  135.6 20.7 %collective-permute-start.15 = (bf16[128,2048]{1,0:T(8,128)(2,1)S(1)}, bf16[128,2048]{1,0:T(8,128)(2,1)S(1)}, u32[]{:S(2)}, u32[]{:S(2)}) collective-permute-start(bf16[128,2048]{1,0:T(8,128)(2,1)S(1)} %add.18), channel_id=1, source_target_pairs={{0,2},{1,3},{2,0},{3,1},{4,6},{5,7},{6,4},{7,5},{8,10},{9,11},{10,... | collective-permute-start | bytes 1572872 | tf_op jit(solution)/shard_map/ppermute | solution.py:44
  156.4 8.1 %collective-permute-start.16 = (bf16[64,2048]{1,0:T(8,128)(2,1)S(1)}, bf16[64,2048]{1,0:T(8,128)(2,1)S(1)}, u32[]{:S(2)}, u32[]{:S(2)}) collective-permute-start(bf16[64,2048]{1,0:T(8,128)(2,1)S(1)} %add_convert_fusion), channel_id=1, source_target_pairs={{0,4},{4,0},{8,12},{12,8},{16,20},{20,16},{24,28},{28,24},{1,5},{5... | collective-permute-start | bytes 786440 | tf_op jit(solution)/shard_map/ppermute | solution.py:44
  162.3 2.1 %copy-start.1 = (bf16[64,4096]{1,0:T(8,128)(2,1)S(1)}, bf16[64,4096]{1,0:T(8,128)(2,1)}, u32[]{:S(2)}) copy-start(bf16[64,4096]{1,0:T(8,128)(2,1)} %tokens.3) | copy-start | bytes 1572868
  162.4 2.1 %copy-start.3 = (bf16[64,4096]{1,0:T(8,128)(2,1)S(1)}, bf16[64,4096]{1,0:T(8,128)(2,1)}, u32[]{:S(2)}) copy-start(bf16[64,4096]{1,0:T(8,128)(2,1)} %grad_out.3) | copy-start | bytes 1572868

commit v7 on v6

--- a/solution.py
+++ b/solution.py
@@ -135,16 +135,18 @@
     return pl.multiple_of(((place[0] ^ k) * 2 + which) * block, 128)
 
 
-def prepare_kernel(block, place, grad_out, tokens, gain, keep, send, normed):
+def prepare_kernel(block, place, grad_out, tokens, gain, grad_keep, normed_keep, send, normed):
     rows, core = tokens.shape[0], place[1]
     values = tokens[...].astype(jnp.float32)
     root_mean = jnp.sqrt(jnp.mean(values * values, axis=-1, keepdims=True) + epsilon)
     normed[...] = (values / root_mean * gain[...].astype(jnp.float32)).astype(jnp.bfloat16)
-    for start, source in ((0, grad_out), (rows, normed)):
+    for start, source, keep in ((0, grad_out, grad_keep), (rows, normed, normed_keep)):
         for k in range(keep.shape[1] // block):
-            place_out = (slice(start, start + rows), slice(k * block, (k + 1) * block))
-            keep[place_out] = source[:, pl.ds(column_start(place, k, core, block), block)]
-            send[place_out] = source[:, pl.ds(column_start(place, k, 1 - core, block), block)]
+            columns = slice(k * block, (k + 1) * block)
+            keep[:, columns] = source[:, pl.ds(column_start(place, k, core, block), block)]
+            send[start : start + rows, columns] = source[
+                :, pl.ds(column_start(place, k, 1 - core, block), block)
+            ]
 
 
 def merge_kernel(out_weight, query_weight, kv_weight, merged):
@@ -191,15 +193,15 @@
 def early_kernel(pieces, weights, size, out_width, place, *refs):
     row_refs, weight_refs = refs[:pieces], refs[pieces : pieces + weights]
     total, grads, normed = refs[pieces + weights :]
-    rows = row_refs[0].shape[0] // 4
+    rows = row_refs[0].shape[0] // 2
     block = weight_refs[0].shape[0]
-    for core in range(2):
-        for number, pair in enumerate((grads, normed)):
-            start = (2 * core + number) * rows
+    halves = row_refs[: pieces // 2], row_refs[pieces // 2 :]
+    for pair, gathered in zip((grads, normed), halves):
+        for core in range(2):
             for k in range(size):
                 target = (core * size + k) * rows
                 pair[target : target + rows] = pick(
-                    place[2], row_refs, size, k, slice(start, start + rows)
+                    place[2], gathered, size, k, slice(core * rows, (core + 1) * rows)
                 )
     for columns in column_steps(out_width, total.shape[1], block):
         for place_out, value in products(grads, normed, weight_refs, 0, out_width, block, columns):
@@ -221,7 +223,7 @@
 
 
 def project(place, pieces, early, late, size, out_width):
-    rows = pieces[0].shape[0] // 4 * size
+    rows = pieces[0].shape[0] // 2 * size
     half = pieces[0].shape[1]
     block, width = early[0].shape
     first = len(early) * block
@@ -433,16 +435,18 @@
     query_width = query_weight.shape[1]
     gain = norm_gain.reshape(1, width)
 
-    keep, send = call(
+    grad_keep, normed_keep, send = call(
         functools.partial(prepare_kernel, block),
-        [shaped((2 * rows, width // 2))] * 2,
+        [shaped((rows, width // 2))] * 2 + [shaped((2 * rows, width // 2))],
         [grad_out, tokens, gain],
         [place],
         [pltpu.VMEM((rows, width), jnp.bfloat16)],
     )
     out_width = out_weight.shape[0]
     send, out_weight, query_weight, kv_weight = tied(send, out_weight, query_weight, kv_weight)
-    row_pieces = gather_tensor(jnp.concatenate([keep, swap(send, "dp", 1)], axis=0))
+    sent = swap(send, "dp", 1)
+    row_pieces = gather_tensor(jnp.concatenate([grad_keep, sent[:rows]], axis=0))
+    row_pieces += gather_tensor(jnp.concatenate([normed_keep, sent[rows:]], axis=0))
     (merged,) = call(
         merge_kernel,
         [shaped((block, out_width + query_width + kv_weight.shape[1]))],

time: 167 us -> 161 us (0.964)
  waiting for transfers between devices: 96.8 us -> 76.6 us
  starting transfers between devices: 35.7 us -> 43.8 us
  local copies, waits for them, and re-layouts: 5.7 us -> 8.76 us
  other arithmetic: 0.84 us -> 3 us
    ppermute x7 -> x12, waiting for transfers between devices: 66.3 us -> 48.1 us  [along(): return lax.ppermute(value, 'tensor', pairs)]
    ppermute x7 -> x12, starting transfers between devices: 12.8 us -> 23 us  [along(): return lax.ppermute(value, 'tensor', pairs)]
    unnamed x21 -> x20, local copies, waits for them, and re-layouts: 2.17 us -> 5.24 us
    select_n x1 -> x2, other arithmetic: 0.11 us -> 2.2 us  [gather_tensor(): jnp.where(lax.axis_index('tensor') == 1, left_two, right_two)]
    ppermute x14, waiting for transfers between devices: 30.5 us -> 28.4 us  [swap(): return lax.ppermute(value, axis, pairs)]
    ppermute x14, starting transfers between devices: 22.9 us -> 20.8 us  [swap(): return lax.ppermute(value, axis, pairs)]
  transfers between devices with their start and end apart: 21 -> 26, of which waited for: 12 -> 14; matrix products, arithmetic and copies ran while one was open for 2% -> 4% of each run, Pallas kernels for 10% -> 11%
where the time goes in v7:
time: 161 us; the launch traced here: 160 us
  waiting for transfers between devices  76.6 us (48%)
  starting transfers between devices  43.8 us (27%)
  Pallas kernels  26.8 us (17%)
  local copies, waits for them, and re-layouts  8.76 us (5%)
  other arithmetic  3 us (2%)
    ppermute x12, waiting for transfers between devices, along(): return lax.ppermute(value, 'tensor', pairs)  48.1 us
    ppermute x14, waiting for transfers between devices, swap(): return lax.ppermute(value, axis, pairs)  28.4 us
    pallas_call x9, Pallas kernels, call(): pl.pallas_call(kernel, out_shape=outs, in_specs=[SCALARS] * len(scalars)...  24.7 us
    ppermute x12, starting transfers between devices, along(): return lax.ppermute(value, 'tensor', pairs)  23 us
    ppermute x14, starting transfers between devices, swap(): return lax.ppermute(value, axis, pairs)  20.8 us
    unnamed x20, local copies, waits for them, and re-layouts  5.24 us
  transfers between devices with their start and end apart: 26, of which 14 were waited for; matrix products, arithmetic and copies ran while one was open for 4% of the time, Pallas kernels for 11%

profile of v7, /device:TPU:1, one launch (start us, length us, event | category | flops | bytes accessed | tf_op | source)
XLA Modules:
  0.0 159.9 jit_solution(11681511606709163410)
XLA Ops:
  7.1 2.6 %collective-permute-start.11 = (bf16[512,2304]{1,0:T(8,128)(2,1)S(1)}, bf16[512,2304]{1,0:T(8,128)(2,1)}, u32[]{:S(2)}, u32[]{:S(2)}) collective-permute-start(bf16[512,2304]{1,0:T(8,128)(2,1)S(1)} %shard_map.95.refs_12_.refs_0_), channel_id=1, source_target_pairs={{0,8},{4,12},{8,0},{12,4},{16,24},{20,28},{24,16},{28,20},{1,9},{5... | collective-permute-start | bytes 7077896 | tf_op jit(solution)/shard_map/ppermute | solution.py:44
  11.0 3.2 %collective-permute-start.6 = (bf16[128,2048]{1,0:T(8,128)(2,1)S(1)}, bf16[128,2048]{1,0:T(8,128)(2,1)S(1)}, u32[]{:S(2)}, u32[]{:S(2)}) collective-permute-start(bf16[128,2048]{1,0:T(8,128)(2,1)S(1)} %pad_maximum_fusion.3.refs_6_), channel_id=1, source_target_pairs={{0,1},{1,2},{2,3},{4,5},{5,6},{6,7},{8,9},{9,10},{10,11},{12,13},{... | collective-permute-start | bytes 1572872 | tf_op jit(solution)/shard_map/ppermute | solution.py:69
  15.6 4.8 %collective-permute-start.1 = (bf16[128,2048]{1,0:T(8,128)(2,1)S(1)}, bf16[128,2048]{1,0:T(8,128)(2,1)}, u32[]{:S(2)}, u32[]{:S(2)}) collective-permute-start(bf16[128,2048]{1,0:T(8,128)(2,1)S(1)} %pad_maximum_fusion.2.refs_0_), channel_id=1, source_target_pairs={{0,1},{1,2},{2,3},{4,5},{5,6},{6,7},{8,9},{9,10},{10,11},{12,13},{... | collective-permute-start | bytes 1572872 | tf_op jit(solution)/shard_map/ppermute | solution.py:69
  20.4 4.2 %collective-permute-done.6.refs_7_ = bf16[128,2048]{1,0:T(8,128)(2,1)S(1)} collective-permute-done((bf16[128,2048]{1,0:T(8,128)(2,1)S(1)}, bf16[128,2048]{1,0:T(8,128)(2,1)S(1)}, u32[]{:S(2)}, u32[]{:S(2)}) %collective-permute-start.6) | collective-permute-done | bytes 524320 | tf_op jit(solution)/shard_map/ppermute | solution.py:69
  25.9 2.6 %collective-permute-done.7.refs_8_ = bf16[128,2048]{1,0:T(8,128)(2,1)} collective-permute-done((bf16[128,2048]{1,0:T(8,128)(2,1)S(1)}, bf16[128,2048]{1,0:T(8,128)(2,1)}, u32[]{:S(2)}, u32[]{:S(2)}) %collective-permute-start.7) | collective-permute-done | bytes 524320 | tf_op jit(solution)/shard_map/ppermute | solution.py:69
  28.6 1.5 collective-permute-start.8
  30.9 5.0 %collective-permute-done.1.refs_1_ = bf16[128,2048]{1,0:T(8,128)(2,1)} collective-permute-done((bf16[128,2048]{1,0:T(8,128)(2,1)S(1)}, bf16[128,2048]{1,0:T(8,128)(2,1)}, u32[]{:S(2)}, u32[]{:S(2)}) %collective-permute-start.1) | collective-permute-done | bytes 524320 | tf_op jit(solution)/shard_map/ppermute | solution.py:69
  38.4 1.5 collective-permute-start.3
  41.1 9.6 %collective-permute-done.9.refs_10_ = bf16[128,2048]{1,0:T(8,128)(2,1)} collective-permute-done((bf16[128,2048]{1,0:T(8,128)(2,1)}, bf16[128,2048]{1,0:T(8,128)(2,1)}, u32[]{:S(2)}, u32[]{:S(2)}) %collective-permute-start.9) | collective-permute-done | bytes 524320 | tf_op jit(solution)/shard_map/ppermute | solution.py:69
  53.1 8.8 %collective-permute-done.4.refs_4_ = bf16[128,2048]{1,0:T(8,128)(2,1)} collective-permute-done((bf16[128,2048]{1,0:T(8,128)(2,1)}, bf16[128,2048]{1,0:T(8,128)(2,1)}, u32[]{:S(2)}, u32[]{:S(2)}) %collective-permute-start.4) | collective-permute-done | bytes 524320 | tf_op jit(solution)/shard_map/ppermute | solution.py:69
  62.1 1.3 slice.44
  63.4 1.3 collective-permute-start.13
  64.7 1.3 slice.45
  67.6 1.5 collective-permute-start.5
  69.1 4.0 %collective-permute-done.10.refs_11_ = bf16[128,2048]{1,0:T(8,128)(2,1)S(1)} collective-permute-done((bf16[128,2048]{1,0:T(8,128)(2,1)S(1)}, bf16[128,2048]{1,0:T(8,128)(2,1)S(1)}, u32[]{:S(2)}, u32[]{:S(2)}) %collective-permute-start.10) | collective-permute-done | bytes 524320 | tf_op jit(solution)/shard_map/ppermute | solution.py:69
  73.1 11.2 %collective-permute-done.5.refs_5_ = bf16[128,2048]{1,0:T(8,128)(2,1)S(1)} collective-permute-done((bf16[128,2048]{1,0:T(8,128)(2,1)S(1)}, bf16[128,2048]{1,0:T(8,128)(2,1)S(1)}, u32[]{:S(2)}, u32[]{:S(2)}) %collective-permute-start.5) | collective-permute-done | bytes 524320 | tf_op jit(solution)/shard_map/ppermute | solution.py:69
  84.3 7.5 %shard_map.96 = (f32[512,2304]{1,0:T(8,128)S(1)}, bf16[512,2048]{1,0:T(8,128)(2,1)S(1)}, bf16[512,2048]{1,0:T(8,128)(2,1)S(1)}) custom-call(s32[3]{0:T(128)S(1)} %pad_add_fusion.place.refs_0_, bf16[128,2048]{1,0:T(8,128)(2,1)S(1)} %pad_maximum_fusion.2.refs_0_, bf16[128,2048]{1,0:T(8,128)(2,1)} %collective-permute-done.1.refs_1_, ...), custom_call_target="tpu_custom_call" | custom-call | flops 3623878656 | bytes 22282240 | tf_op jit(solution)/shard_map/pallas_call | solution.py:23
  91.8 1.5 shard_map.97
  93.3 2.8 %collective-permute-start.15 = (bf16[256,2304]{1,0:T(8,128)(2,1)S(1)}, bf16[256,2304]{1,0:T(8,128)(2,1)S(1)}, u32[]{:S(2)}, u32[]{:S(2)}) collective-permute-start(bf16[256,2304]{1,0:T(8,128)(2,1)S(1)} %get-tuple-element.62), channel_id=1, source_target_pairs={{0,4},{4,0},{8,12},{12,8},{16,20},{20,16},{24,28},{28,24},{1,5},{5... | collective-permute-start | bytes 3538952 | tf_op jit(solution)/shard_map/ppermute | solution.py:44
  96.1 2.5 %collective-permute-done.15.refs_3_ = bf16[256,2304]{1,0:T(8,128)(2,1)S(1)} collective-permute-done((bf16[256,2304]{1,0:T(8,128)(2,1)S(1)}, bf16[256,2304]{1,0:T(8,128)(2,1)S(1)}, u32[]{:S(2)}, u32[]{:S(2)}) %collective-permute-start.15) | collective-permute-done | bytes 1179680 | tf_op jit(solution)/shard_map/ppermute | solution.py:44
  98.6 4.0 %shard_map.98.own = bf16[256,1280]{1,0:T(8,128)(2,1)S(1)} custom-call(s32[3]{0:T(128)S(1)} %pad_add_fusion.place.refs_0_, s32[1,4]{1,0:T(1,128)S(1)} %copy-done.7, f32[256,2304]{1,0:T(8,128)S(1)} %get-tuple-element.61.refs_2_, bf16[256,2304]{1,0:T(8,128)(2,1)S(1)} %collective-permute-done.15.refs_3_), custom_call_target="tpu_custom_call" | custom-call | flops 671088640 | bytes 4194304 | tf_op jit(solution)/shard_map/pallas_call | solution.py:23
  103.0 1.7 %collective-permute-done.16.other = bf16[256,1280]{1,0:T(8,128)(2,1)S(1)} collective-permute-done((bf16[256,1280]{1,0:T(8,128)(2,1)S(1)}, bf16[256,1280]{1,0:T(8,128)(2,1)S(1)}, u32[]{:S(2)}, u32[]{:S(2)}) %collective-permute-start.16) | collective-permute-done | bytes 655392 | tf_op jit(solution)/shard_map/ppermute | solution.py:44
  106.4 5.3 %shard_map.99 = (bf16[128,2048]{1,0:T(8,128)(2,1)S(1)}, bf16[128,2048]{1,0:T(8,128)(2,1)S(1)}, bf16[128,2048]{1,0:T(8,128)(2,1)S(1)}, bf16[128,2048]{1,0:T(8,128)(2,1)S(1)}) custom-call(bf16[256,1280]{1,0:T(8,128)(2,1)S(1)} %shard_map.98.own, bf16[256,1280]{1,0:T(8,128)(2,1)S(1)} %collective-permute-done.16.other, ...), custom_call_target="tpu_custom_call" | custom-call | flops 2684354560 | bytes 12845056 | tf_op jit(solution)/shard_map/pallas_call | solution.py:23
  111.7 3.2 %collective-permute-start.17 = (bf16[128,2048]{1,0:T(8,128)(2,1)S(1)}, bf16[128,2048]{1,0:T(8,128)(2,1)S(1)}, u32[]{:S(2)}, u32[]{:S(2)}) collective-permute-start(bf16[128,2048]{1,0:T(8,128)(2,1)S(1)} %get-tuple-element.65), channel_id=1, source_target_pairs={{3,2},{0,1},{7,6},{4,5},{11,10},{8,9},{15,14},{12,13},{19,18},{16,... | collective-permute-start | bytes 1572872 | tf_op jit(solution)/shard_map/ppermute | solution.py:69
  115.8 2.3 %shard_map.100 = (bf16[512,1280]{1,0:T(8,128)(2,1)S(1)}, bf16[512,1280]{1,0:T(8,128)(2,1)S(1)}, bf16[512,1280]{1,0:T(8,128)(2,1)S(1)}) custom-call(bf16[512,2048]{1,0:T(8,128)(2,1)S(1)} %get-tuple-element.60.normed.pair, bf16[256,1280]{1,0:T(8,128)(2,1)S(1)} %shard_map.98.own, bf16[256,1280]{1,0:T(8,128)(2,1)S(1)} %collective-permute-done.16.other), custom_call_target="tpu_custom_call" | custom-call | flops 2013265920 | bytes 7340032 | tf_op jit(solution)/shard_map/pallas_call | solution.py:23
  118.0 3.7 %collective-permute-done.22 = bf16[256,1280]{1,0:T(8,128)(2,1)S(1)} collective-permute-done((bf16[256,1280]{1,0:T(8,128)(2,1)S(1)}, bf16[256,1280]{1,0:T(8,128)(2,1)S(1)}, u32[]{:S(2)}, u32[]{:S(2)}) %collective-permute-start.22) | collective-permute-done | bytes 655392 | tf_op jit(solution)/shard_map/ppermute | solution.py:44
  123.7 1.4 collective-permute-done.17
  125.2 3.6 %collective-permute-start.19 = (bf16[128,2048]{1,0:T(8,128)(2,1)S(1)}, bf16[128,2048]{1,0:T(8,128)(2,1)S(1)}, u32[]{:S(2)}, u32[]{:S(2)}) collective-permute-start(bf16[128,2048]{1,0:T(8,128)(2,1)S(1)} %get-tuple-element.68), channel_id=1, source_target_pairs={{0,1},{1,0},{2,3},{3,2},{4,5},{5,4},{6,7},{7,6},{8,9},{9,8},{10,11... | collective-permute-start | bytes 1572872 | tf_op jit(solution)/shard_map/ppermute | solution.py:44
  129.9 20.4 %collective-permute-done.19.refs_1_ = bf16[128,2048]{1,0:T(8,128)(2,1)S(1)} collective-permute-done((bf16[128,2048]{1,0:T(8,128)(2,1)S(1)}, bf16[128,2048]{1,0:T(8,128)(2,1)S(1)}, u32[]{:S(2)}, u32[]{:S(2)}) %collective-permute-start.19) | collective-permute-done | bytes 524320 | tf_op jit(solution)/shard_map/ppermute | solution.py:44
  150.5 5.1 %collective-permute-start.21 = (bf16[64,2048]{1,0:T(8,128)(2,1)S(1)}, bf16[64,2048]{1,0:T(8,128)(2,1)S(1)}, u32[]{:S(2)}, u32[]{:S(2)}) collective-permute-start(bf16[64,2048]{1,0:T(8,128)(2,1)S(1)} %add_convert_fusion), channel_id=1, source_target_pairs={{0,4},{4,0},{8,12},{12,8},{16,20},{20,16},{24,28},{28,24},{1,5},{5... | collective-permute-start | bytes 786440 | tf_op jit(solution)/shard_map/ppermute | solution.py:44
  155.6 2.1 %shard_map.102 = (f32[512,1024]{1,0:T(8,128)}, f32[512,256]{1,0:T(8,128)}) custom-call(bf16[512,1280]{1,0:T(8,128)(2,1)S(1)} %get-tuple-element.71.refs_0_, bf16[512,1280]{1,0:T(8,128)(2,1)S(1)} %collective-permute-done.23.refs_1_, bf16[512,1280]{1,0:T(8,128)(2,1)S(1)} %collective-permute-done.25.refs_2_), custom_call_target="tpu_custom_call" | custom-call | bytes 6553600 | tf_op jit(solution)/shard_map/pallas_call | solution.py:385
  157.7 2.2 %shard_map.103 = bf16[64,4096]{1,0:T(8,128)(2,1)} custom-call(s32[3]{0:T(128)S(1)} %pad_add_fusion.place.refs_0_, bf16[64,4096]{1,0:T(8,128)(2,1)S(1)} %copy-done.1, bf16[1,4096]{1,0:T(2,128)(2,1)S(1)} %reshape.9.gain, bf16[64,4096]{1,0:T(8,128)(2,1)S(1)} %copy-done.3, bf16[64,2048]{1,0:T(8,128)(2,1)S(1)} %collective-permute-done.21.handed, ...), custom_call_target="tpu_custom_call" | custom-call | bytes 3940352 | tf_op jit(solution)/shard_map/pallas_call | solution.py:23
  (65 shorter events, 25.3 us)
Async XLA Ops:
  3.5 1.2 copy-start.4
  4.5 6.4 %collective-permute-start = (bf16[128,2048]{1,0:T(8,128)(2,1)S(1)}, bf16[128,2048]{1,0:T(8,128)(2,1)S(1)}, u32[]{:S(2)}, u32[]{:S(2)}) collective-permute-start(bf16[128,2048]{1,0:T(8,128)(2,1)S(1)} %get-tuple-element.43), channel_id=1, source_target_pairs={{0,4},{4,0},{8,12},{12,8},{16,20},{20,16},{24,28},{28,24},{1,5},{5... | collective-permute-start | bytes 1572872 | tf_op jit(solution)/shard_map/ppermute | solution.py:44
  4.7 1.2 copy-start.5
  7.1 54.9 %collective-permute-start.11 = (bf16[512,2304]{1,0:T(8,128)(2,1)S(1)}, bf16[512,2304]{1,0:T(8,128)(2,1)}, u32[]{:S(2)}, u32[]{:S(2)}) collective-permute-start(bf16[512,2304]{1,0:T(8,128)(2,1)S(1)} %shard_map.95.refs_12_.refs_0_), channel_id=1, source_target_pairs={{0,8},{4,12},{8,0},{12,4},{16,24},{20,28},{24,16},{28,20},{1,9},{5... | collective-permute-start | bytes 7077896 | tf_op jit(solution)/shard_map/ppermute | solution.py:44
  9.6 52.4 %collective-permute-start.12 = (bf16[512,2304]{1,0:T(8,128)(2,1)S(1)}, bf16[512,2304]{1,0:T(8,128)(2,1)}, u32[]{:S(2)}, u32[]{:S(2)}) collective-permute-start(bf16[512,2304]{1,0:T(8,128)(2,1)S(1)} %shard_map.95.refs_12_.refs_0_), channel_id=1, source_target_pairs={{0,16},{4,20},{8,24},{12,28},{16,0},{20,4},{24,8},{28,12},{1,17},{... | collective-permute-start | bytes 7077896 | tf_op jit(solution)/shard_map/ppermute | solution.py:44
  11.0 13.7 %collective-permute-start.6 = (bf16[128,2048]{1,0:T(8,128)(2,1)S(1)}, bf16[128,2048]{1,0:T(8,128)(2,1)S(1)}, u32[]{:S(2)}, u32[]{:S(2)}) collective-permute-start(bf16[128,2048]{1,0:T(8,128)(2,1)S(1)} %pad_maximum_fusion.3.refs_6_), channel_id=1, source_target_pairs={{0,1},{1,2},{2,3},{4,5},{5,6},{6,7},{8,9},{9,10},{10,11},{12,13},{... | collective-permute-start | bytes 1572872 | tf_op jit(solution)/shard_map/ppermute | solution.py:69
  14.2 14.4 %collective-permute-start.7 = (bf16[128,2048]{1,0:T(8,128)(2,1)S(1)}, bf16[128,2048]{1,0:T(8,128)(2,1)}, u32[]{:S(2)}, u32[]{:S(2)}) collective-permute-start(bf16[128,2048]{1,0:T(8,128)(2,1)S(1)} %pad_maximum_fusion.3.refs_6_), channel_id=1, source_target_pairs={{1,0},{2,1},{3,2},{5,4},{6,5},{7,6},{9,8},{10,9},{11,10},{13,12},{... | collective-permute-start | bytes 1572872 | tf_op jit(solution)/shard_map/ppermute | solution.py:69
  15.6 20.3 %collective-permute-start.1 = (bf16[128,2048]{1,0:T(8,128)(2,1)S(1)}, bf16[128,2048]{1,0:T(8,128)(2,1)}, u32[]{:S(2)}, u32[]{:S(2)}) collective-permute-start(bf16[128,2048]{1,0:T(8,128)(2,1)S(1)} %pad_maximum_fusion.2.refs_0_), channel_id=1, source_target_pairs={{0,1},{1,2},{2,3},{4,5},{5,6},{6,7},{8,9},{9,10},{10,11},{12,13},{... | collective-permute-start | bytes 1572872 | tf_op jit(solution)/shard_map/ppermute | solution.py:69
  24.6 13.7 %collective-permute-start.2 = (bf16[128,2048]{1,0:T(8,128)(2,1)S(1)}, bf16[128,2048]{1,0:T(8,128)(2,1)}, u32[]{:S(2)}, u32[]{:S(2)}) collective-permute-start(bf16[128,2048]{1,0:T(8,128)(2,1)S(1)} %pad_maximum_fusion.2.refs_0_), channel_id=1, source_target_pairs={{1,0},{2,1},{3,2},{5,4},{6,5},{7,6},{9,8},{10,9},{11,10},{13,12},{... | collective-permute-start | bytes 1572872 | tf_op jit(solution)/shard_map/ppermute | solution.py:69
  28.6 11.2 %collective-permute-start.8 = (bf16[128,2048]{1,0:T(8,128)(2,1)S(1)}, bf16[128,2048]{1,0:T(8,128)(2,1)}, u32[]{:S(2)}, u32[]{:S(2)}) collective-permute-start(bf16[128,2048]{1,0:T(8,128)(2,1)S(1)} %collective-permute-done.6.refs_7_), channel_id=1, source_target_pairs={{1,2},{2,3},{5,6},{6,7},{9,10},{10,11},{13,14},{14,15},{17,18},{18... | collective-permute-start | bytes 1572872 | tf_op jit(solution)/shard_map/ppermute | solution.py:69
  35.9 14.8 %collective-permute-start.9 = (bf16[128,2048]{1,0:T(8,128)(2,1)}, bf16[128,2048]{1,0:T(8,128)(2,1)}, u32[]{:S(2)}, u32[]{:S(2)}) collective-permute-start(bf16[128,2048]{1,0:T(8,128)(2,1)} %collective-permute-done.7.refs_8_), channel_id=1, source_target_pairs={{1,0},{2,1},{5,4},{6,5},{9,8},{10,9},{13,12},{14,13},{17,16},{18,1... | collective-permute-start | bytes 1572872 | tf_op jit(solution)/shard_map/ppermute | solution.py:69
  38.4 14.8 %collective-permute-start.3 = (bf16[128,2048]{1,0:T(8,128)(2,1)}, bf16[128,2048]{1,0:T(8,128)(2,1)}, u32[]{:S(2)}, u32[]{:S(2)}) collective-permute-start(bf16[128,2048]{1,0:T(8,128)(2,1)} %collective-permute-done.1.refs_1_), channel_id=1, source_target_pairs={{1,2},{2,3},{5,6},{6,7},{9,10},{10,11},{13,14},{14,15},{17,18},{18... | collective-permute-start | bytes 1572872 | tf_op jit(solution)/shard_map/ppermute | solution.py:69
  39.8 22.1 %collective-permute-start.4 = (bf16[128,2048]{1,0:T(8,128)(2,1)}, bf16[128,2048]{1,0:T(8,128)(2,1)}, u32[]{:S(2)}, u32[]{:S(2)}) collective-permute-start(bf16[128,2048]{1,0:T(8,128)(2,1)} %collective-permute-done.2.refs_2_), channel_id=1, source_target_pairs={{1,0},{2,1},{5,4},{6,5},{9,8},{10,9},{13,12},{14,13},{17,16},{18,1... | collective-permute-start | bytes 1572872 | tf_op jit(solution)/shard_map/ppermute | solution.py:69
  51.8 21.3 %collective-permute-start.10 = (bf16[128,2048]{1,0:T(8,128)(2,1)S(1)}, bf16[128,2048]{1,0:T(8,128)(2,1)S(1)}, u32[]{:S(2)}, u32[]{:S(2)}) collective-permute-start(bf16[128,2048]{1,0:T(8,128)(2,1)S(1)} %broadcast_select_fusion), channel_id=1, source_target_pairs={{1,0},{2,3},{5,4},{6,7},{9,8},{10,11},{13,12},{14,15},{17,16},{18,... | collective-permute-start | bytes 1572872 | tf_op jit(solution)/shard_map/ppermute | solution.py:69
  63.4 28.4 %collective-permute-start.13 = (bf16[256,2304]{1,0:T(8,128)(2,1)S(1)}, bf16[256,2304]{1,0:T(8,128)(2,1)S(1)}, u32[]{:S(2)}, u32[]{:S(2)}) collective-permute-start(bf16[256,2304]{1,0:T(8,128)(2,1)S(1)} %slice.44), channel_id=1, source_target_pairs={{0,16},{4,20},{8,24},{12,28},{16,0},{20,4},{24,8},{28,12},{1,17},{... | collective-permute-start | bytes 3538952 | tf_op jit(solution)/shard_map/ppermute | solution.py:44
  66.1 18.2 %copy-start.9 = (bf16[128,2048]{1,0:T(8,128)(2,1)S(1)}, bf16[128,2048]{1,0:T(8,128)(2,1)}, u32[]{:S(2)}) copy-start(bf16[128,2048]{1,0:T(8,128)(2,1)} %copy-done.8) | copy-start | bytes 1572868
  66.1 25.7 %collective-permute-start.14 = (bf16[256,2304]{1,0:T(8,128)(2,1)S(1)}, bf16[256,2304]{1,0:T(8,128)(2,1)S(1)}, u32[]{:S(2)}, u32[]{:S(2)}) collective-permute-start(bf16[256,2304]{1,0:T(8,128)(2,1)S(1)} %slice.45), channel_id=1, source_target_pairs={{0,8},{4,12},{8,0},{12,4},{16,24},{20,28},{24,16},{28,20},{1,9},{5... | collective-permute-start | bytes 3538952 | tf_op jit(solution)/shard_map/ppermute | solution.py:44
  67.6 16.7 %collective-permute-start.5 = (bf16[128,2048]{1,0:T(8,128)(2,1)S(1)}, bf16[128,2048]{1,0:T(8,128)(2,1)S(1)}, u32[]{:S(2)}, u32[]{:S(2)}) collective-permute-start(bf16[128,2048]{1,0:T(8,128)(2,1)S(1)} %broadcast_select_fusion.1), channel_id=1, source_target_pairs={{1,0},{2,3},{5,4},{6,7},{9,8},{10,11},{13,12},{14,15},{17,16},{18,... | collective-permute-start | bytes 1572872 | tf_op jit(solution)/shard_map/ppermute | solution.py:69
  91.8 6.7 %copy-start.7 = (s32[1,4]{1,0:T(1,128)S(1)}, s32[1,4]{1,0:T(1,128)}, u32[]{:S(2)}) copy-start(s32[1,4]{1,0:T(1,128)} %refs_1_.1) | copy-start | bytes 52
  93.3 5.2 %collective-permute-start.15 = (bf16[256,2304]{1,0:T(8,128)(2,1)S(1)}, bf16[256,2304]{1,0:T(8,128)(2,1)S(1)}, u32[]{:S(2)}, u32[]{:S(2)}) collective-permute-start(bf16[256,2304]{1,0:T(8,128)(2,1)S(1)} %get-tuple-element.62), channel_id=1, source_target_pairs={{0,4},{4,0},{8,12},{12,8},{16,20},{20,16},{24,28},{28,24},{1,5},{5... | collective-permute-start | bytes 3538952 | tf_op jit(solution)/shard_map/ppermute | solution.py:44
  102.6 2.2 %collective-permute-start.16 = (bf16[256,1280]{1,0:T(8,128)(2,1)S(1)}, bf16[256,1280]{1,0:T(8,128)(2,1)S(1)}, u32[]{:S(2)}, u32[]{:S(2)}) collective-permute-start(bf16[256,1280]{1,0:T(8,128)(2,1)S(1)} %shard_map.98.own), channel_id=1, source_target_pairs={{0,4},{4,0},{8,12},{12,8},{16,20},{20,16},{24,28},{28,24},{1,5},{5... | collective-permute-start | bytes 1966088 | tf_op jit(solution)/shard_map/ppermute | solution.py:44
  105.7 16.0 %collective-permute-start.22 = (bf16[256,1280]{1,0:T(8,128)(2,1)S(1)}, bf16[256,1280]{1,0:T(8,128)(2,1)S(1)}, u32[]{:S(2)}, u32[]{:S(2)}) collective-permute-start(bf16[256,1280]{1,0:T(8,128)(2,1)S(1)} %get-tuple-element.82), channel_id=1, source_target_pairs={{0,16},{4,20},{8,24},{12,28},{16,0},{20,4},{24,8},{28,12},{1,17},{... | collective-permute-start | bytes 1966088 | tf_op jit(solution)/shard_map/ppermute | solution.py:44
  106.0 15.7 %collective-permute-start.24 = (bf16[256,1280]{1,0:T(8,128)(2,1)S(1)}, bf16[256,1280]{1,0:T(8,128)(2,1)S(1)}, u32[]{:S(2)}, u32[]{:S(2)}) collective-permute-start(bf16[256,1280]{1,0:T(8,128)(2,1)S(1)} %get-tuple-element.81), channel_id=1, source_target_pairs={{0,8},{4,12},{8,0},{12,4},{16,24},{20,28},{24,16},{28,20},{1,9},{5... | collective-permute-start | bytes 1966088 | tf_op jit(solution)/shard_map/ppermute | solution.py:44
  111.7 13.4 %collective-permute-start.17 = (bf16[128,2048]{1,0:T(8,128)(2,1)S(1)}, bf16[128,2048]{1,0:T(8,128)(2,1)S(1)}, u32[]{:S(2)}, u32[]{:S(2)}) collective-permute-start(bf16[128,2048]{1,0:T(8,128)(2,1)S(1)} %get-tuple-element.65), channel_id=1, source_target_pairs={{3,2},{0,1},{7,6},{4,5},{11,10},{8,9},{15,14},{12,13},{19,18},{16,... | collective-permute-start | bytes 1572872 | tf_op jit(solution)/shard_map/ppermute | solution.py:69
  114.9 10.2 %collective-permute-start.18 = (bf16[128,2048]{1,0:T(8,128)(2,1)S(1)}, bf16[128,2048]{1,0:T(8,128)(2,1)S(1)}, u32[]{:S(2)}, u32[]{:S(2)}) collective-permute-start(bf16[128,2048]{1,0:T(8,128)(2,1)S(1)} %get-tuple-element.65), channel_id=1, source_target_pairs={{1,2},{2,1},{5,6},{6,5},{9,10},{10,9},{13,14},{14,13},{17,18},{18,... | collective-permute-start | bytes 1572872 | tf_op jit(solution)/shard_map/ppermute | solution.py:69
  122.1 33.5 %collective-permute-start.25 = (bf16[512,1280]{1,0:T(8,128)(2,1)S(1)}, bf16[512,1280]{1,0:T(8,128)(2,1)S(1)}, u32[]{:S(2)}, u32[]{:S(2)}) collective-permute-start(bf16[512,1280]{1,0:T(8,128)(2,1)S(1)} %pad_maximum_fusion.1), channel_id=1, source_target_pairs={{0,16},{4,20},{8,24},{12,28},{16,0},{20,4},{24,8},{28,12},{1,17},{... | collective-permute-start | bytes 3932168 | tf_op jit(solution)/shard_map/ppermute | solution.py:44
  123.3 32.2 %collective-permute-start.23 = (bf16[512,1280]{1,0:T(8,128)(2,1)S(1)}, bf16[512,1280]{1,0:T(8,128)(2,1)S(1)}, u32[]{:S(2)}, u32[]{:S(2)}) collective-permute-start(bf16[512,1280]{1,0:T(8,128)(2,1)S(1)} %pad_maximum_fusion), channel_id=1, source_target_pairs={{0,8},{4,12},{8,0},{12,4},{16,24},{20,28},{24,16},{28,20},{1,9},{5... | collective-permute-start | bytes 3932168 | tf_op jit(solution)/shard_map/ppermute | solution.py:44
  125.2 25.1 %collective-permute-start.19 = (bf16[128,2048]{1,0:T(8,128)(2,1)S(1)}, bf16[128,2048]{1,0:T(8,128)(2,1)S(1)}, u32[]{:S(2)}, u32[]{:S(2)}) collective-permute-start(bf16[128,2048]{1,0:T(8,128)(2,1)S(1)} %get-tuple-element.68), channel_id=1, source_target_pairs={{0,1},{1,0},{2,3},{3,2},{4,5},{5,4},{6,7},{7,6},{8,9},{9,8},{10,11... | collective-permute-start | bytes 1572872 | tf_op jit(solution)/shard_map/ppermute | solution.py:44
  128.8 21.5 %collective-permute-start.20 = (bf16[128,2048]{1,0:T(8,128)(2,1)S(1)}, bf16[128,2048]{1,0:T(8,128)(2,1)S(1)}, u32[]{:S(2)}, u32[]{:S(2)}) collective-permute-start(bf16[128,2048]{1,0:T(8,128)(2,1)S(1)} %add.18), channel_id=1, source_target_pairs={{0,2},{1,3},{2,0},{3,1},{4,6},{5,7},{6,4},{7,5},{8,10},{9,11},{10,... | collective-permute-start | bytes 1572872 | tf_op jit(solution)/shard_map/ppermute | solution.py:44
  150.5 7.2 %collective-permute-start.21 = (bf16[64,2048]{1,0:T(8,128)(2,1)S(1)}, bf16[64,2048]{1,0:T(8,128)(2,1)S(1)}, u32[]{:S(2)}, u32[]{:S(2)}) collective-permute-start(bf16[64,2048]{1,0:T(8,128)(2,1)S(1)} %add_convert_fusion), channel_id=1, source_target_pairs={{0,4},{4,0},{8,12},{12,8},{16,20},{20,16},{24,28},{28,24},{1,5},{5... | collective-permute-start | bytes 786440 | tf_op jit(solution)/shard_map/ppermute | solution.py:44
  155.5 2.1 %copy-start.1 = (bf16[64,4096]{1,0:T(8,128)(2,1)S(1)}, bf16[64,4096]{1,0:T(8,128)(2,1)}, u32[]{:S(2)}) copy-start(bf16[64,4096]{1,0:T(8,128)(2,1)} %tokens.3) | copy-start | bytes 1572868
  155.5 2.1 %copy-start.3 = (bf16[64,4096]{1,0:T(8,128)(2,1)S(1)}, bf16[64,4096]{1,0:T(8,128)(2,1)}, u32[]{:S(2)}) copy-start(bf16[64,4096]{1,0:T(8,128)(2,1)} %grad_out.3) | copy-start | bytes 1572868
  (4 other events, 3.8 us)

commit v8 on v7

--- a/solution.py
+++ b/solution.py
@@ -53,31 +53,32 @@
     return [value] + [swap(value, axis, unit * k) for k in range(1, size)]
 
 
-def gather_chips(value):
+def gather_near(value):
     if lax.axis_size("dp") != 8:
         return everyone(value, "dp", 2), []
     half = value.shape[0] // 2
     near_x = swap(value, "dp", 2)
     near_y = swap(value, "dp", 4)
     near_x, near_y = tied(near_x, near_y)
-    far_top = swap(near_x[:half], "dp", 4)
-    far_bottom = swap(near_y[half:], "dp", 2)
-    return [value, near_x, near_y], [far_top, far_bottom]
+    return [value, near_x, near_y], [near_x[:half], near_y[half:]]
+
+
+def gather_far(parts):
+    return [swap(part, "dp", mask) for part, mask in zip(parts, (4, 2))]
 
 
 def along(value, pairs):
     return lax.ppermute(value, "tensor", pairs)
 
 
-def gather_tensor(value):
+def gather_tensor(value, after=()):
     if lax.axis_size("tensor") != 4:
         return everyone(value, "tensor", 1)
     right_one = along(value, [(0, 1), (1, 2), (2, 3)])
     left_one = along(value, [(1, 0), (2, 1), (3, 2)])
-    right_one, left_one = tied(right_one, left_one)
     right_two = along(right_one, [(1, 2), (2, 3)])
     left_two = along(left_one, [(1, 0), (2, 1)])
-    right_two, left_two = tied(right_two, left_two)
+    right_two, left_two, *_ = tied(right_two, left_two, *after)
     last = along(
         jnp.where(lax.axis_index("tensor") == 1, left_two, right_two), [(1, 0), (2, 3)]
     )
@@ -85,17 +86,22 @@
 
 
 def pick(index, pieces, size, k, rows):
-    if len(pieces) == size:
+    if size != 4:
         return pieces[k][rows]
-    own, right_one, left_one, right_two, left_two, last = [piece.at[rows] for piece in pieces]
+    own, right_one, left_one, right_two, left_two = [piece.at[rows] for piece in pieces[:5]]
     if k == 0:
         return own[...]
     if k == 1:
         return jnp.where(index % 2 == 1, right_one[...], left_one[...])
-    if k == 2:
-        return jnp.where(index >= 2, right_two[...], left_two[...])
-    near = jnp.where(index == 1, left_one[...], right_one[...])
-    return jnp.where(jnp.logical_or(index == 0, index == 3), last[...], near)
+    return jnp.where(index >= 2, right_two[...], left_two[...])
+
+
+def last_slot(index, pieces, rows):
+    if len(pieces) == 1:
+        return pieces[0][rows]
+    right_one, left_one, last = [piece[rows] for piece in pieces]
+    near = jnp.where(index == 1, left_one, right_one)
+    return jnp.where(jnp.logical_or(index == 0, index == 3), last, near)
 
 
 def inner_pair(value):
@@ -198,8 +204,8 @@
     halves = row_refs[: pieces // 2], row_refs[pieces // 2 :]
     for pair, gathered in zip((grads, normed), halves):
         for core in range(2):
-            for k in range(size):
-                target = (core * size + k) * rows
+            for k in range(size - 1):
+                target = (core * (size - 1) + k) * rows
                 pair[target : target + rows] = pick(
                     place[2], gathered, size, k, slice(core * rows, (core + 1) * rows)
                 )
@@ -208,39 +214,67 @@
             total[:, place_out] = value
 
 
-def late_kernel(first, out_width, block, total, grads, normed, *refs):
-    weight_refs, (keep, send) = refs[:-2], refs[-2:]
-    length = keep.shape[0]
-    if not weight_refs:
-        keep[...] = total[:length]
-        send[...] = total[length:].astype(jnp.bfloat16)
-    for columns in column_steps(out_width, keep.shape[1], block) if weight_refs else []:
-        for place_out, value in products(
-            grads, normed, weight_refs, first, out_width, block, columns
-        ):
-            keep[:, place_out] = total[:length, place_out] + value[:length]
-            send[:, place_out] = (total[length:, place_out] + value[length:]).astype(jnp.bfloat16)
-
-
-def project(place, pieces, early, late, size, out_width):
-    rows = pieces[0].shape[0] // 2 * size
-    half = pieces[0].shape[1]
+def late_kernel(pieces, early, late, size, out_width, place, *refs):
+    total, grads, normed = refs[:3]
+    row_refs, refs = refs[3 : 3 + pieces], refs[3 + pieces :]
+    early_refs, late_refs, refs = refs[:early], refs[early : early + late], refs[early + late :]
+    keep, send, pair, last_grads, last_normed = refs
+    rows = row_refs[0].shape[0] // 2
+    block = early_refs[0].shape[0]
+    first, most, length = early * block, (size - 1) * rows, size * rows
+    halves = row_refs[: pieces // 2], row_refs[pieces // 2 :]
+    for target, gathered in zip((last_grads, last_normed), halves):
+        for core in range(2):
+            some = slice(core * rows, (core + 1) * rows)
+            target[some] = last_slot(place[2], gathered, some)
+    for core in range(2):
+        pair[core * length : core * length + most] = normed[core * most : (core + 1) * most]
+        pair[core * length + most : (core + 1) * length] = last_normed[
+            core * rows : (core + 1) * rows
+        ]
+    for columns in column_steps(out_width, keep.shape[1], block):
+        arguments = out_width, block, columns
+        ends = products(last_grads, last_normed, early_refs, 0, *arguments)
+        if late:
+            far = products(grads, normed, late_refs, first, *arguments)
+            far_ends = products(last_grads, last_normed, late_refs, first, *arguments)
+        for place_out, end in ends:
+            value = total[:, place_out]
+            if late:
+                value = value + next(far)[1]
+                end = end + next(far_ends)[1]
+            keep[:most, place_out] = value[:most]
+            keep[most:, place_out] = end[:rows]
+            send[:most, place_out] = value[most:].astype(jnp.bfloat16)
+            send[most:, place_out] = end[rows:].astype(jnp.bfloat16)
+
+
+def project(place, grad_pieces, normed_pieces, early, late, size, out_width):
+    pair_rows, half = grad_pieces[0].shape
+    rows = pair_rows // 2 * size
     block, width = early[0].shape
-    first = len(early) * block
+    most = pair_rows * (size - 1)
+    pieces = [*grad_pieces[:-1], *normed_pieces[:-1]]
     total, grads, normed = call(
         functools.partial(early_kernel, len(pieces), len(early), size, out_width),
-        [shaped((2 * rows, width), jnp.float32)] + [shaped((2 * rows, half))] * 2,
+        [shaped((most, width), jnp.float32)] + [shaped((most, half))] * 2,
         [*pieces, *early],
         [place],
-        flops=4 * rows * first * width,
-        megabytes=24,
-    )
-    own, sent = call(
-        functools.partial(late_kernel, first, out_width, block),
-        [shaped((rows, width), jnp.float32), shaped((rows, width))],
-        [total, grads, normed, *late],
-        flops=4 * rows * (half - first) * width,
-        megabytes=24,
+        flops=2 * most * len(early) * block * width,
+    )
+    needed = (1, 2, 5) if size == 4 else (-1,)
+    pieces = [gathered[k] for gathered in (grad_pieces, normed_pieces) for k in needed]
+    own, sent, normed = call(
+        functools.partial(late_kernel, len(pieces), len(early), len(late), size, out_width),
+        [
+            shaped((rows, width), jnp.float32),
+            shaped((rows, width)),
+            shaped((2 * rows, half)),
+        ],
+        [total, grads, normed, *pieces, *early, *late],
+        [place],
+        [pltpu.VMEM((pair_rows, half), jnp.bfloat16)] * 2,
+        flops=2 * (pair_rows * half + most * block) * width,
     )
     return own, sent, normed
 
@@ -335,32 +369,34 @@
     )
 
 
-def row_kernel(weights, offset_columns, own, other, *refs):
-    weight_refs, outs = refs[:weights], refs[weights:]
-    length = own.shape[0]
-    rows = length // len(outs)
+def row_kernel(weights, offset_columns, blocks, own, other, *refs):
+    weight_refs, outs, left = refs[:weights], refs[weights:-1], refs[-1]
+    rows = outs[0].shape[0] // 2
+    for number, k in enumerate(blocks):
+        for start, source in ((2 * number, own), (2 * number + 1, other)):
+            left[start * rows : (start + 1) * rows] = source[k * rows : (k + 1) * rows]
     start = 0
     for weight in weight_refs:
         tile = min(weight.shape[0], 256)
         for part in range(weight.shape[0] // tile):
             right = weight[part * tile : (part + 1) * tile, offset_columns:]
-            for offset, left in ((0, own), (rows, other)):
-                term = dot(left[...], right, CONTRACT_LAST).astype(jnp.bfloat16)
-                for k, out in enumerate(outs):
-                    out[offset : offset + rows, start : start + tile] = term[
-                        k * rows : (k + 1) * rows
-                    ]
+            term = dot(left[...], right, CONTRACT_LAST).astype(jnp.bfloat16)
+            for number, out in enumerate(outs):
+                out[:, start : start + tile] = term[2 * number * rows : 2 * (number + 1) * rows]
             start += tile
 
 
-def row_terms(own, other, weights, size, out_width):
+def row_terms(own, other, weights, size, out_width, blocks):
     length, width = own.shape
     half = sum(weight.shape[0] for weight in weights)
+    pair_rows = 2 * length // size
     return call(
-        functools.partial(row_kernel, len(weights), out_width),
-        [shaped((2 * length // size, half))] * size,
+        functools.partial(row_kernel, len(weights), out_width, blocks),
+        [shaped((pair_rows, half))] * len(blocks),
         [own, other, *weights],
-        flops=4 * length * width * half,
+        (),
+        [pltpu.VMEM((pair_rows * len(blocks), width), jnp.bfloat16)],
+        flops=2 * pair_rows * len(blocks) * width * half,
     )
 
 
@@ -445,15 +481,18 @@
     out_width = out_weight.shape[0]
     send, out_weight, query_weight, kv_weight = tied(send, out_weight, query_weight, kv_weight)
     sent = swap(send, "dp", 1)
-    row_pieces = gather_tensor(jnp.concatenate([grad_keep, sent[:rows]], axis=0))
-    row_pieces += gather_tensor(jnp.concatenate([normed_keep, sent[rows:]], axis=0))
+    normed_pieces = gather_tensor(jnp.concatenate([normed_keep, sent[rows:]], axis=0))
     (merged,) = call(
         merge_kernel,
         [shaped((block, out_width + query_width + kv_weight.shape[1]))],
         [out_weight, query_weight, kv_weight],
     )
-    early, late = gather_chips(merged)
-    own, sent, normed = project(place, row_pieces, early, late, tensor_size, out_width)
+    early, parts = gather_near(merged)
+    late = gather_far(parts)
+    grad_pieces = gather_tensor(jnp.concatenate([grad_keep, sent[:rows]], axis=0), parts)
+    own, sent, normed = project(
+        place, grad_pieces, normed_pieces, early, late, tensor_size, out_width
+    )
     sent = swap(sent, "dp", 1)
     if levels:
         joined = (own + sent.astype(jnp.float32)).astype(jnp.bfloat16)
@@ -486,7 +525,11 @@
 
     far = weight_terms(normed, combined, other, chips - 1, 1, block)
     near = weight_terms(normed, combined, other, 0, chips - 1, block)
-    row_parts = scatter_tensor(row_terms(combined, other, early + late, tensor_size, out_width))
+    row_blocks = []
+    for blocks in ([tensor_size - 1], list(range(tensor_size - 1))):
+        some = row_terms(combined, other, early + late, tensor_size, out_width, blocks)
+        row_blocks = [*some, *row_blocks]
+    row_parts = scatter_tensor(row_blocks)
     weight_parts = scatter_chips([*near, *far])
     handed = sum(part[rows:].astype(jnp.float32) for part in row_parts).astype(jnp.bfloat16)
     handed = swap(handed, "dp", 1)

time: 161 us -> 168 us (1.043)
  Pallas kernels: 26.8 us -> 33.7 us
  waiting for transfers between devices: 76.6 us -> 72 us
  starting transfers between devices: 43.8 us -> 47.5 us
    ppermute x12, waiting for transfers between devices: 48.1 us -> 37.3 us  [along(): return lax.ppermute(value, 'tensor', pairs)]
    pallas_call x9 -> x10, Pallas kernels: 24.7 us -> 31.6 us  [call(): pl.pallas_call(kernel, out_shape=outs, in_specs=[SCALARS] * len(scalars)...]
    ppermute x14, waiting for transfers between devices: 28.4 us -> 34.7 us  [swap(): return lax.ppermute(value, axis, pairs)]
    ppermute x12, starting transfers between devices: 23 us -> 26.1 us  [along(): return lax.ppermute(value, 'tensor', pairs)]
    unnamed x20 -> x28, local copies, waits for them, and re-layouts: 5.24 us -> 6.04 us
  transfers between devices with their start and end apart: 26 -> 26, of which waited for: 14 -> 11; matrix products, arithmetic and copies ran while one was open for 4% -> 3% of each run, Pallas kernels for 11% -> 12%
where the time goes in v8:
time: 168 us; the launch traced here: 167 us
  waiting for transfers between devices  72 us (43%)
  starting transfers between devices  47.5 us (28%)
  Pallas kernels  33.7 us (20%)
  local copies, waits for them, and re-layouts  9.63 us (6%)
  other arithmetic  3.05 us (2%)
    ppermute x12, waiting for transfers between devices, along(): return lax.ppermute(value, 'tensor', pairs)  37.3 us
    ppermute x14, waiting for transfers between devices, swap(): return lax.ppermute(value, axis, pairs)  34.7 us
    pallas_call x10, Pallas kernels, call(): pl.pallas_call(kernel, out_shape=outs, in_specs=[SCALARS] * len(scalars)...  31.6 us
    ppermute x12, starting transfers between devices, along(): return lax.ppermute(value, 'tensor', pairs)  26.1 us
    ppermute x14, starting transfers between devices, swap(): return lax.ppermute(value, axis, pairs)  21.5 us
    unnamed x28, local copies, waits for them, and re-layouts  6.04 us
  transfers between devices with their start and end apart: 26, of which 11 were waited for; matrix products, arithmetic and copies ran while one was open for 3% of the time, Pallas kernels for 12%

profile of v8, /device:TPU:1, one launch (start us, length us, event | category | flops | bytes accessed | tf_op | source)
XLA Modules:
  0.0 166.9 jit_solution(7201359022739691753)
XLA Ops:
  7.1 2.6 %collective-permute-start.6 = (bf16[512,2304]{1,0:T(8,128)(2,1)S(1)}, bf16[512,2304]{1,0:T(8,128)(2,1)}, u32[]{:S(2)}, u32[]{:S(2)}) collective-permute-start(bf16[512,2304]{1,0:T(8,128)(2,1)S(1)} %shard_map.95.refs_10_.refs_9_.refs_0_), channel_id=1, source_target_pairs={{0,16},{4,20},{8,24},{12,28},{16,0},{20,4},{24,8},{28,12},{1,17},{... | collective-permute-start | bytes 7077896 | tf_op jit(solution)/shard_map/ppermute | solution.py:44
  11.0 1.3 collective-permute-start.2
  13.6 5.4 %collective-permute-start.7 = (bf16[128,2048]{1,0:T(8,128)(2,1)S(1)}, bf16[128,2048]{1,0:T(8,128)(2,1)}, u32[]{:S(2)}, u32[]{:S(2)}) collective-permute-start(bf16[128,2048]{1,0:T(8,128)(2,1)S(1)} %pad_maximum_fusion.3.refs_5_), channel_id=1, source_target_pairs={{0,1},{1,2},{2,3},{4,5},{5,6},{6,7},{8,9},{9,10},{10,11},{12,13},{... | collective-permute-start | bytes 1572872 | tf_op jit(solution)/shard_map/ppermute | solution.py:71
  19.9 5.8 %collective-permute-done.2.refs_2_.refs_4_ = bf16[128,2048]{1,0:T(8,128)(2,1)S(1)} collective-permute-done((bf16[128,2048]{1,0:T(8,128)(2,1)S(1)}, bf16[128,2048]{1,0:T(8,128)(2,1)S(1)}, u32[]{:S(2)}, u32[]{:S(2)}) %collective-permute-start.2) | collective-permute-done | bytes 524320 | tf_op jit(solution)/shard_map/ppermute | solution.py:71
  25.7 4.0 %collective-permute-start.1 = (bf16[128,2048]{1,0:T(8,128)(2,1)S(1)}, bf16[128,2048]{1,0:T(8,128)(2,1)}, u32[]{:S(2)}, u32[]{:S(2)}) collective-permute-start(bf16[128,2048]{1,0:T(8,128)(2,1)S(1)} %pad_maximum_fusion.2.refs_0_), channel_id=1, source_target_pairs={{0,1},{1,2},{2,3},{4,5},{5,6},{6,7},{8,9},{9,10},{10,11},{12,13},{... | collective-permute-start | bytes 1572872 | tf_op jit(solution)/shard_map/ppermute | solution.py:71
  29.7 7.2 %collective-permute-done.8.refs_7_ = bf16[128,2048]{1,0:T(8,128)(2,1)S(1)} collective-permute-done((bf16[128,2048]{1,0:T(8,128)(2,1)S(1)}, bf16[128,2048]{1,0:T(8,128)(2,1)S(1)}, u32[]{:S(2)}, u32[]{:S(2)}) %collective-permute-start.8) | collective-permute-done | bytes 524320 | tf_op jit(solution)/shard_map/ppermute | solution.py:71
  38.2 1.5 collective-permute-start.9
  41.0 9.8 %collective-permute-done.10.refs_9_ = bf16[128,2048]{1,0:T(8,128)(2,1)S(1)} collective-permute-done((bf16[128,2048]{1,0:T(8,128)(2,1)S(1)}, bf16[128,2048]{1,0:T(8,128)(2,1)S(1)}, u32[]{:S(2)}, u32[]{:S(2)}) %collective-permute-start.10) | collective-permute-done | bytes 524320 | tf_op jit(solution)/shard_map/ppermute | solution.py:71
  51.5 1.5 collective-permute-start.3
  53.0 8.3 %collective-permute-done.6.refs_12_.refs_11_.refs_2_ = bf16[512,2304]{1,0:T(8,128)(2,1)} collective-permute-done((bf16[512,2304]{1,0:T(8,128)(2,1)S(1)}, bf16[512,2304]{1,0:T(8,128)(2,1)}, u32[]{:S(2)}, u32[]{:S(2)}) %collective-permute-start.6) | collective-permute-done | bytes 2359328 | tf_op jit(solution)/shard_map/ppermute | solution.py:44
  62.1 1.3 slice.43
  63.5 1.4 slice.44
  67.6 1.3 collective-permute-start.12
  70.0 1.5 collective-permute-start.11
  71.5 6.3 %shard_map.96 = (f32[384,2304]{1,0:T(8,128)S(1)}, bf16[384,2048]{1,0:T(8,128)(2,1)S(1)}, bf16[384,2048]{1,0:T(8,128)(2,1)S(1)}) custom-call(s32[3]{0:T(128)S(1)} %pad_add_fusion.place.refs_0_, bf16[128,2048]{1,0:T(8,128)(2,1)S(1)} %copy-done.1, bf16[128,2048]{1,0:T(8,128)(2,1)} %collective-permute-done.1.refs_1_.refs_3_, ...), custom_call_target="tpu_custom_call" | custom-call | flops 2717908992 | bytes 19005440 | tf_op jit(solution)/shard_map/pallas_call | solution.py:23
  77.8 3.3 %collective-permute-done.12.refs_8_ = bf16[128,2048]{1,0:T(8,128)(2,1)S(1)} collective-permute-done((bf16[128,2048]{1,0:T(8,128)(2,1)S(1)}, bf16[128,2048]{1,0:T(8,128)(2,1)S(1)}, u32[]{:S(2)}, u32[]{:S(2)}) %collective-permute-start.12) | collective-permute-done | bytes 524320 | tf_op jit(solution)/shard_map/ppermute | solution.py:71
  81.1 11.2 %collective-permute-done.11.refs_5_ = bf16[128,2048]{1,0:T(8,128)(2,1)S(1)} collective-permute-done((bf16[128,2048]{1,0:T(8,128)(2,1)S(1)}, bf16[128,2048]{1,0:T(8,128)(2,1)S(1)}, u32[]{:S(2)}, u32[]{:S(2)}) %collective-permute-start.11) | collective-permute-done | bytes 524320 | tf_op jit(solution)/shard_map/ppermute | solution.py:71
  92.3 6.0 %shard_map.97 = (f32[256,2304]{1,0:T(8,128)S(1)}, bf16[256,2304]{1,0:T(8,128)(2,1)S(1)}, bf16[512,2048]{1,0:T(8,128)(2,1)S(1)}) custom-call(s32[3]{0:T(128)S(1)} %pad_add_fusion.place.refs_0_, f32[384,2304]{1,0:T(8,128)S(1)} %get-tuple-element.50.refs_0_, bf16[384,2048]{1,0:T(8,128)(2,1)S(1)} %get-tuple-element.51.refs_1_, ...), custom_call_target="tpu_custom_call" | custom-call | flops 2113929216 | bytes 24903680 | tf_op jit(solution)/shard_map/pallas_call | solution.py:23
  98.4 2.8 %collective-permute-start.15 = (bf16[256,2304]{1,0:T(8,128)(2,1)S(1)}, bf16[256,2304]{1,0:T(8,128)(2,1)S(1)}, u32[]{:S(2)}, u32[]{:S(2)}) collective-permute-start(bf16[256,2304]{1,0:T(8,128)(2,1)S(1)} %get-tuple-element.54), channel_id=1, source_target_pairs={{0,4},{4,0},{8,12},{12,8},{16,20},{20,16},{24,28},{28,24},{1,5},{5... | collective-permute-start | bytes 3538952 | tf_op jit(solution)/shard_map/ppermute | solution.py:44
  101.2 2.5 %collective-permute-done.15.refs_3_ = bf16[256,2304]{1,0:T(8,128)(2,1)S(1)} collective-permute-done((bf16[256,2304]{1,0:T(8,128)(2,1)S(1)}, bf16[256,2304]{1,0:T(8,128)(2,1)S(1)}, u32[]{:S(2)}, u32[]{:S(2)}) %collective-permute-start.15) | collective-permute-done | bytes 1179680 | tf_op jit(solution)/shard_map/ppermute | solution.py:44
  103.7 4.0 %shard_map.98.own = bf16[256,1280]{1,0:T(8,128)(2,1)S(1)} custom-call(s32[3]{0:T(128)S(1)} %pad_add_fusion.place.refs_0_, s32[1,4]{1,0:T(1,128)S(1)} %copy-done.13, f32[256,2304]{1,0:T(8,128)S(1)} %get-tuple-element.53.refs_2_, bf16[256,2304]{1,0:T(8,128)(2,1)S(1)} %collective-permute-done.15.refs_3_), custom_call_target="tpu_custom_call" | custom-call | flops 671088640 | bytes 4194304 | tf_op jit(solution)/shard_map/pallas_call | solution.py:23
  108.1 1.7 %collective-permute-done.16.other = bf16[256,1280]{1,0:T(8,128)(2,1)S(1)} collective-permute-done((bf16[256,1280]{1,0:T(8,128)(2,1)S(1)}, bf16[256,1280]{1,0:T(8,128)(2,1)S(1)}, u32[]{:S(2)}, u32[]{:S(2)}) %collective-permute-start.16) | collective-permute-done | bytes 655392 | tf_op jit(solution)/shard_map/ppermute | solution.py:44
  112.3 4.2 %shard_map.100 = bf16[128,2048]{1,0:T(8,128)(2,1)S(1)} custom-call(bf16[256,1280]{1,0:T(8,128)(2,1)S(1)} %shard_map.98.own, bf16[256,1280]{1,0:T(8,128)(2,1)S(1)} %collective-permute-done.16.other, bf16[512,2304]{1,0:T(8,128)(2,1)S(1)} %shard_map.95.refs_10_.refs_9_.refs_0_, bf16[512,2304]{1,0:T(8,128)(2,1)} %collective-permute-done.5.refs_11_.refs_10_.refs_1_, ...), custom_call_target="tpu_custom_call" | custom-call | flops 671088640 | bytes 11272192 | tf_op jit(solution)/shard_map/pallas_call | solution.py:23
  117.2 5.1 %collective-permute-start.17 = (bf16[128,2048]{1,0:T(8,128)(2,1)S(1)}, bf16[128,2048]{1,0:T(8,128)(2,1)S(1)}, u32[]{:S(2)}, u32[]{:S(2)}) collective-permute-start(bf16[128,2048]{1,0:T(8,128)(2,1)S(1)} %shard_map.100), channel_id=1, source_target_pairs={{3,2},{0,1},{7,6},{4,5},{11,10},{8,9},{15,14},{12,13},{19,18},{16,... | collective-permute-start | bytes 1572872 | tf_op jit(solution)/shard_map/ppermute | solution.py:71
  122.3 2.3 %shard_map.101 = (bf16[512,1280]{1,0:T(8,128)(2,1)S(1)}, bf16[512,1280]{1,0:T(8,128)(2,1)S(1)}, bf16[512,1280]{1,0:T(8,128)(2,1)S(1)}) custom-call(bf16[512,2048]{1,0:T(8,128)(2,1)S(1)} %get-tuple-element.62.pair, bf16[256,1280]{1,0:T(8,128)(2,1)S(1)} %shard_map.98.own, bf16[256,1280]{1,0:T(8,128)(2,1)S(1)} %collective-permute-done.16.other), custom_call_target="tpu_custom_call" | custom-call | flops 2013265920 | bytes 7340032 | tf_op jit(solution)/shard_map/pallas_call | solution.py:23
  124.6 2.3 %collective-permute-done.24 = bf16[256,1280]{1,0:T(8,128)(2,1)S(1)} collective-permute-done((bf16[256,1280]{1,0:T(8,128)(2,1)S(1)}, bf16[256,1280]{1,0:T(8,128)(2,1)S(1)}, u32[]{:S(2)}, u32[]{:S(2)}) %collective-permute-start.24) | collective-permute-done | bytes 655392 | tf_op jit(solution)/shard_map/ppermute | solution.py:44
  129.7 4.6 %shard_map.99 = (bf16[128,2048]{1,0:T(8,128)(2,1)S(1)}, bf16[128,2048]{1,0:T(8,128)(2,1)S(1)}, bf16[128,2048]{1,0:T(8,128)(2,1)S(1)}) custom-call(bf16[256,1280]{1,0:T(8,128)(2,1)S(1)} %shard_map.98.own, bf16[256,1280]{1,0:T(8,128)(2,1)S(1)} %collective-permute-done.16.other, bf16[512,2304]{1,0:T(8,128)(2,1)S(1)} %shard_map.95.refs_10_.refs_9_.refs_0_, ...), custom_call_target="tpu_custom_call" | custom-call | flops 2013265920 | bytes 12320768 | tf_op jit(solution)/shard_map/pallas_call | solution.py:23
  134.6 3.6 %collective-permute-start.20 = (bf16[128,2048]{1,0:T(8,128)(2,1)S(1)}, bf16[128,2048]{1,0:T(8,128)(2,1)S(1)}, u32[]{:S(2)}, u32[]{:S(2)}) collective-permute-start(bf16[128,2048]{1,0:T(8,128)(2,1)S(1)} %add.18), channel_id=1, source_target_pairs={{0,2},{1,3},{2,0},{3,1},{4,6},{5,7},{6,4},{7,5},{8,10},{9,11},{10,... | collective-permute-start | bytes 1572872 | tf_op jit(solution)/shard_map/ppermute | solution.py:44
  138.2 19.0 %collective-permute-done.19.refs_1_ = bf16[128,2048]{1,0:T(8,128)(2,1)S(1)} collective-permute-done((bf16[128,2048]{1,0:T(8,128)(2,1)S(1)}, bf16[128,2048]{1,0:T(8,128)(2,1)S(1)}, u32[]{:S(2)}, u32[]{:S(2)}) %collective-permute-start.19) | collective-permute-done | bytes 524320 | tf_op jit(solution)/shard_map/ppermute | solution.py:44
  157.3 5.2 %collective-permute-start.21 = (bf16[64,2048]{1,0:T(8,128)(2,1)S(1)}, bf16[64,2048]{1,0:T(8,128)(2,1)S(1)}, u32[]{:S(2)}, u32[]{:S(2)}) collective-permute-start(bf16[64,2048]{1,0:T(8,128)(2,1)S(1)} %add_convert_fusion), channel_id=1, source_target_pairs={{0,4},{4,0},{8,12},{12,8},{16,20},{20,16},{24,28},{28,24},{1,5},{5... | collective-permute-start | bytes 786440 | tf_op jit(solution)/shard_map/ppermute | solution.py:44
  162.5 2.1 %shard_map.103 = (f32[512,1024]{1,0:T(8,128)}, f32[512,256]{1,0:T(8,128)}) custom-call(bf16[512,1280]{1,0:T(8,128)(2,1)S(1)} %get-tuple-element.63.refs_0_, bf16[512,1280]{1,0:T(8,128)(2,1)S(1)} %collective-permute-done.23.refs_1_, bf16[512,1280]{1,0:T(8,128)(2,1)S(1)} %collective-permute-done.25.refs_2_), custom_call_target="tpu_custom_call" | custom-call | bytes 6553600 | tf_op jit(solution)/shard_map/pallas_call | solution.py:421
  164.7 2.2 %shard_map.104 = bf16[64,4096]{1,0:T(8,128)(2,1)} custom-call(s32[3]{0:T(128)S(1)} %pad_add_fusion.place.refs_0_, bf16[64,4096]{1,0:T(8,128)(2,1)S(1)} %copy-done.7, bf16[1,4096]{1,0:T(2,128)(2,1)S(1)} %reshape.9.gain, bf16[64,4096]{1,0:T(8,128)(2,1)S(1)} %copy-done.9, bf16[64,2048]{1,0:T(8,128)(2,1)S(1)} %collective-permute-done.21.handed, ...), custom_call_target="tpu_custom_call" | custom-call | bytes 3940352 | tf_op jit(solution)/shard_map/pallas_call | solution.py:23
  (74 shorter events, 24.6 us)
Async XLA Ops:
  4.5 6.4 %collective-permute-start = (bf16[128,2048]{1,0:T(8,128)(2,1)S(1)}, bf16[128,2048]{1,0:T(8,128)(2,1)S(1)}, u32[]{:S(2)}, u32[]{:S(2)}) collective-permute-start(bf16[128,2048]{1,0:T(8,128)(2,1)S(1)} %get-tuple-element.39), channel_id=1, source_target_pairs={{0,4},{4,0},{8,12},{12,8},{16,20},{20,16},{24,28},{28,24},{1,5},{5... | collective-permute-start | bytes 1572872 | tf_op jit(solution)/shard_map/ppermute | solution.py:44
  7.1 54.2 %collective-permute-start.6 = (bf16[512,2304]{1,0:T(8,128)(2,1)S(1)}, bf16[512,2304]{1,0:T(8,128)(2,1)}, u32[]{:S(2)}, u32[]{:S(2)}) collective-permute-start(bf16[512,2304]{1,0:T(8,128)(2,1)S(1)} %shard_map.95.refs_10_.refs_9_.refs_0_), channel_id=1, source_target_pairs={{0,16},{4,20},{8,24},{12,28},{16,0},{20,4},{24,8},{28,12},{1,17},{... | collective-permute-start | bytes 7077896 | tf_op jit(solution)/shard_map/ppermute | solution.py:44
  9.7 52.4 %collective-permute-start.5 = (bf16[512,2304]{1,0:T(8,128)(2,1)S(1)}, bf16[512,2304]{1,0:T(8,128)(2,1)}, u32[]{:S(2)}, u32[]{:S(2)}) collective-permute-start(bf16[512,2304]{1,0:T(8,128)(2,1)S(1)} %shard_map.95.refs_10_.refs_9_.refs_0_), channel_id=1, source_target_pairs={{0,8},{4,12},{8,0},{12,4},{16,24},{20,28},{24,16},{28,20},{1,9},{5... | collective-permute-start | bytes 7077896 | tf_op jit(solution)/shard_map/ppermute | solution.py:44
  11.0 39.8 %copy-start = (bf16[128,2048]{1,0:T(8,128)(2,1)}, bf16[128,2048]{1,0:T(8,128)(2,1)S(1)}, u32[]{:S(2)}) copy-start(bf16[128,2048]{1,0:T(8,128)(2,1)S(1)} %pad_maximum_fusion.2.refs_0_) | copy-start | bytes 1572868
  11.0 14.7 %collective-permute-start.2 = (bf16[128,2048]{1,0:T(8,128)(2,1)S(1)}, bf16[128,2048]{1,0:T(8,128)(2,1)S(1)}, u32[]{:S(2)}, u32[]{:S(2)}) collective-permute-start(bf16[128,2048]{1,0:T(8,128)(2,1)S(1)} %pad_maximum_fusion.2.refs_0_), channel_id=1, source_target_pairs={{1,0},{2,1},{3,2},{5,4},{6,5},{7,6},{9,8},{10,9},{11,10},{13,12},{... | collective-permute-start | bytes 1572872 | tf_op jit(solution)/shard_map/ppermute | solution.py:71
  12.3 24.6 %collective-permute-start.8 = (bf16[128,2048]{1,0:T(8,128)(2,1)S(1)}, bf16[128,2048]{1,0:T(8,128)(2,1)S(1)}, u32[]{:S(2)}, u32[]{:S(2)}) collective-permute-start(bf16[128,2048]{1,0:T(8,128)(2,1)S(1)} %pad_maximum_fusion.3.refs_5_), channel_id=1, source_target_pairs={{1,0},{2,1},{3,2},{5,4},{6,5},{7,6},{9,8},{10,9},{11,10},{13,12},{... | collective-permute-start | bytes 1572872 | tf_op jit(solution)/shard_map/ppermute | solution.py:71
  13.6 24.6 %collective-permute-start.7 = (bf16[128,2048]{1,0:T(8,128)(2,1)S(1)}, bf16[128,2048]{1,0:T(8,128)(2,1)}, u32[]{:S(2)}, u32[]{:S(2)}) collective-permute-start(bf16[128,2048]{1,0:T(8,128)(2,1)S(1)} %pad_maximum_fusion.3.refs_5_), channel_id=1, source_target_pairs={{0,1},{1,2},{2,3},{4,5},{5,6},{6,7},{8,9},{9,10},{10,11},{12,13},{... | collective-permute-start | bytes 1572872 | tf_op jit(solution)/shard_map/ppermute | solution.py:71
  25.7 14.0 %collective-permute-start.1 = (bf16[128,2048]{1,0:T(8,128)(2,1)S(1)}, bf16[128,2048]{1,0:T(8,128)(2,1)}, u32[]{:S(2)}, u32[]{:S(2)}) collective-permute-start(bf16[128,2048]{1,0:T(8,128)(2,1)S(1)} %pad_maximum_fusion.2.refs_0_), channel_id=1, source_target_pairs={{0,1},{1,2},{2,3},{4,5},{5,6},{6,7},{8,9},{9,10},{10,11},{12,13},{... | collective-permute-start | bytes 1572872 | tf_op jit(solution)/shard_map/ppermute | solution.py:71
  36.9 13.8 %collective-permute-start.10 = (bf16[128,2048]{1,0:T(8,128)(2,1)S(1)}, bf16[128,2048]{1,0:T(8,128)(2,1)S(1)}, u32[]{:S(2)}, u32[]{:S(2)}) collective-permute-start(bf16[128,2048]{1,0:T(8,128)(2,1)S(1)} %collective-permute-done.8.refs_7_), channel_id=1, source_target_pairs={{1,0},{2,1},{5,4},{6,5},{9,8},{10,9},{13,12},{14,13},{17,16},{18,1... | collective-permute-start | bytes 1572872 | tf_op jit(solution)/shard_map/ppermute | solution.py:71
  38.2 14.8 %collective-permute-start.9 = (bf16[128,2048]{1,0:T(8,128)(2,1)}, bf16[128,2048]{1,0:T(8,128)(2,1)}, u32[]{:S(2)}, u32[]{:S(2)}) collective-permute-start(bf16[128,2048]{1,0:T(8,128)(2,1)} %collective-permute-done.7.refs_6_), channel_id=1, source_target_pairs={{1,2},{2,3},{5,6},{6,7},{9,10},{10,11},{13,14},{14,15},{17,18},{18... | collective-permute-start | bytes 1572872 | tf_op jit(solution)/shard_map/ppermute | solution.py:71
  39.7 29.2 %collective-permute-start.4 = (bf16[128,2048]{1,0:T(8,128)(2,1)S(1)}, bf16[128,2048]{1,0:T(8,128)(2,1)}, u32[]{:S(2)}, u32[]{:S(2)}) collective-permute-start(bf16[128,2048]{1,0:T(8,128)(2,1)S(1)} %collective-permute-done.2.refs_2_.refs_4_), channel_id=1, source_target_pairs={{1,0},{2,1},{5,4},{6,5},{9,8},{10,9},{13,12},{14,13},{17,16},{18,1... | collective-permute-start | bytes 1572872 | tf_op jit(solution)/shard_map/ppermute | solution.py:71
  51.5 17.4 %collective-permute-start.3 = (bf16[128,2048]{1,0:T(8,128)(2,1)}, bf16[128,2048]{1,0:T(8,128)(2,1)}, u32[]{:S(2)}, u32[]{:S(2)}) collective-permute-start(bf16[128,2048]{1,0:T(8,128)(2,1)} %collective-permute-done.1.refs_1_.refs_3_), channel_id=1, source_target_pairs={{1,2},{2,3},{5,6},{6,7},{9,10},{10,11},{13,14},{14,15},{17,18},{18... | collective-permute-start | bytes 1572872 | tf_op jit(solution)/shard_map/ppermute | solution.py:71
  63.5 3.0 %copy-start.5 = (bf16[128,2048]{1,0:T(8,128)(2,1)S(1)}, bf16[128,2048]{1,0:T(8,128)(2,1)}, u32[]{:S(2)}) copy-start(bf16[128,2048]{1,0:T(8,128)(2,1)} %copy-done.4) | copy-start | bytes 1572868
  64.9 6.6 %copy-start.1 = (bf16[128,2048]{1,0:T(8,128)(2,1)S(1)}, bf16[128,2048]{1,0:T(8,128)(2,1)}, u32[]{:S(2)}) copy-start(bf16[128,2048]{1,0:T(8,128)(2,1)} %copy-done) | copy-start | bytes 1572868
  64.9 6.6 %copy-start.3 = (bf16[128,2048]{1,0:T(8,128)(2,1)S(1)}, bf16[128,2048]{1,0:T(8,128)(2,1)}, u32[]{:S(2)}) copy-start(bf16[128,2048]{1,0:T(8,128)(2,1)} %copy-done.2) | copy-start | bytes 1572868
  64.9 27.4 %collective-permute-start.14 = (bf16[256,2304]{1,0:T(8,128)(2,1)S(1)}, bf16[256,2304]{1,0:T(8,128)(2,1)S(1)}, u32[]{:S(2)}, u32[]{:S(2)}) collective-permute-start(bf16[256,2304]{1,0:T(8,128)(2,1)S(1)} %slice.44), channel_id=1, source_target_pairs={{0,8},{4,12},{8,0},{12,4},{16,24},{20,28},{24,16},{28,20},{1,9},{5... | collective-permute-start | bytes 3538952 | tf_op jit(solution)/shard_map/ppermute | solution.py:44
  66.2 26.2 %collective-permute-start.13 = (bf16[256,2304]{1,0:T(8,128)(2,1)S(1)}, bf16[256,2304]{1,0:T(8,128)(2,1)S(1)}, u32[]{:S(2)}, u32[]{:S(2)}) collective-permute-start(bf16[256,2304]{1,0:T(8,128)(2,1)S(1)} %slice.43), channel_id=1, source_target_pairs={{0,16},{4,20},{8,24},{12,28},{16,0},{20,4},{24,8},{28,12},{1,17},{... | collective-permute-start | bytes 3538952 | tf_op jit(solution)/shard_map/ppermute | solution.py:44
  67.6 13.5 %collective-permute-start.12 = (bf16[128,2048]{1,0:T(8,128)(2,1)S(1)}, bf16[128,2048]{1,0:T(8,128)(2,1)S(1)}, u32[]{:S(2)}, u32[]{:S(2)}) collective-permute-start(bf16[128,2048]{1,0:T(8,128)(2,1)S(1)} %broadcast_select_fusion), channel_id=1, source_target_pairs={{1,0},{2,3},{5,4},{6,7},{9,8},{10,11},{13,12},{14,15},{17,16},{18,... | collective-permute-start | bytes 1572872 | tf_op jit(solution)/shard_map/ppermute | solution.py:71
  70.0 22.3 %collective-permute-start.11 = (bf16[128,2048]{1,0:T(8,128)(2,1)S(1)}, bf16[128,2048]{1,0:T(8,128)(2,1)S(1)}, u32[]{:S(2)}, u32[]{:S(2)}) collective-permute-start(bf16[128,2048]{1,0:T(8,128)(2,1)S(1)} %broadcast_select_fusion.1), channel_id=1, source_target_pairs={{1,0},{2,3},{5,4},{6,7},{9,8},{10,11},{13,12},{14,15},{17,16},{18,... | collective-permute-start | bytes 1572872 | tf_op jit(solution)/shard_map/ppermute | solution.py:71
  92.3 11.3 %copy-start.13 = (s32[1,4]{1,0:T(1,128)S(1)}, s32[1,4]{1,0:T(1,128)}, u32[]{:S(2)}) copy-start(s32[1,4]{1,0:T(1,128)} %refs_1_.1) | copy-start | bytes 52
  98.4 5.3 %collective-permute-start.15 = (bf16[256,2304]{1,0:T(8,128)(2,1)S(1)}, bf16[256,2304]{1,0:T(8,128)(2,1)S(1)}, u32[]{:S(2)}, u32[]{:S(2)}) collective-permute-start(bf16[256,2304]{1,0:T(8,128)(2,1)S(1)} %get-tuple-element.54), channel_id=1, source_target_pairs={{0,4},{4,0},{8,12},{12,8},{16,20},{20,16},{24,28},{28,24},{1,5},{5... | collective-permute-start | bytes 3538952 | tf_op jit(solution)/shard_map/ppermute | solution.py:44
  107.7 2.2 %collective-permute-start.16 = (bf16[256,1280]{1,0:T(8,128)(2,1)S(1)}, bf16[256,1280]{1,0:T(8,128)(2,1)S(1)}, u32[]{:S(2)}, u32[]{:S(2)}) collective-permute-start(bf16[256,1280]{1,0:T(8,128)(2,1)S(1)} %shard_map.98.own), channel_id=1, source_target_pairs={{0,4},{4,0},{8,12},{12,8},{16,20},{20,16},{24,28},{28,24},{1,5},{5... | collective-permute-start | bytes 1966088 | tf_op jit(solution)/shard_map/ppermute | solution.py:44
  110.8 16.0 %collective-permute-start.24 = (bf16[256,1280]{1,0:T(8,128)(2,1)S(1)}, bf16[256,1280]{1,0:T(8,128)(2,1)S(1)}, u32[]{:S(2)}, u32[]{:S(2)}) collective-permute-start(bf16[256,1280]{1,0:T(8,128)(2,1)S(1)} %get-tuple-element.73), channel_id=1, source_target_pairs={{0,8},{4,12},{8,0},{12,4},{16,24},{20,28},{24,16},{28,20},{1,9},{5... | collective-permute-start | bytes 1966088 | tf_op jit(solution)/shard_map/ppermute | solution.py:44
  111.3 15.6 %collective-permute-start.22 = (bf16[256,1280]{1,0:T(8,128)(2,1)S(1)}, bf16[256,1280]{1,0:T(8,128)(2,1)S(1)}, u32[]{:S(2)}, u32[]{:S(2)}) collective-permute-start(bf16[256,1280]{1,0:T(8,128)(2,1)S(1)} %get-tuple-element.74), channel_id=1, source_target_pairs={{0,16},{4,20},{8,24},{12,28},{16,0},{20,4},{24,8},{28,12},{1,17},{... | collective-permute-start | bytes 1966088 | tf_op jit(solution)/shard_map/ppermute | solution.py:44
  116.5 17.8 %collective-permute-start.18 = (bf16[128,2048]{1,0:T(8,128)(2,1)S(1)}, bf16[128,2048]{1,0:T(8,128)(2,1)S(1)}, u32[]{:S(2)}, u32[]{:S(2)}) collective-permute-start(bf16[128,2048]{1,0:T(8,128)(2,1)S(1)} %shard_map.100), channel_id=1, source_target_pairs={{1,2},{2,1},{5,6},{6,5},{9,10},{10,9},{13,14},{14,13},{17,18},{18,... | collective-permute-start | bytes 1572872 | tf_op jit(solution)/shard_map/ppermute | solution.py:71
  117.2 17.1 %collective-permute-start.17 = (bf16[128,2048]{1,0:T(8,128)(2,1)S(1)}, bf16[128,2048]{1,0:T(8,128)(2,1)S(1)}, u32[]{:S(2)}, u32[]{:S(2)}) collective-permute-start(bf16[128,2048]{1,0:T(8,128)(2,1)S(1)} %shard_map.100), channel_id=1, source_target_pairs={{3,2},{0,1},{7,6},{4,5},{11,10},{8,9},{15,14},{12,13},{19,18},{16,... | collective-permute-start | bytes 1572872 | tf_op jit(solution)/shard_map/ppermute | solution.py:71
  127.2 35.3 %collective-permute-start.25 = (bf16[512,1280]{1,0:T(8,128)(2,1)S(1)}, bf16[512,1280]{1,0:T(8,128)(2,1)S(1)}, u32[]{:S(2)}, u32[]{:S(2)}) collective-permute-start(bf16[512,1280]{1,0:T(8,128)(2,1)S(1)} %pad_maximum_fusion.1), channel_id=1, source_target_pairs={{0,16},{4,20},{8,24},{12,28},{16,0},{20,4},{24,8},{28,12},{1,17},{... | collective-permute-start | bytes 3932168 | tf_op jit(solution)/shard_map/ppermute | solution.py:44
  128.5 34.0 %collective-permute-start.23 = (bf16[512,1280]{1,0:T(8,128)(2,1)S(1)}, bf16[512,1280]{1,0:T(8,128)(2,1)S(1)}, u32[]{:S(2)}, u32[]{:S(2)}) collective-permute-start(bf16[512,1280]{1,0:T(8,128)(2,1)S(1)} %pad_maximum_fusion), channel_id=1, source_target_pairs={{0,8},{4,12},{8,0},{12,4},{16,24},{20,28},{24,16},{28,20},{1,9},{5... | collective-permute-start | bytes 3932168 | tf_op jit(solution)/shard_map/ppermute | solution.py:44
  134.5 22.7 %collective-permute-start.19 = (bf16[128,2048]{1,0:T(8,128)(2,1)S(1)}, bf16[128,2048]{1,0:T(8,128)(2,1)S(1)}, u32[]{:S(2)}, u32[]{:S(2)}) collective-permute-start(bf16[128,2048]{1,0:T(8,128)(2,1)S(1)} %get-tuple-element.59), channel_id=1, source_target_pairs={{0,1},{1,0},{2,3},{3,2},{4,5},{5,4},{6,7},{7,6},{8,9},{9,8},{10,11... | collective-permute-start | bytes 1572872 | tf_op jit(solution)/shard_map/ppermute | solution.py:44
  134.6 22.6 %collective-permute-start.20 = (bf16[128,2048]{1,0:T(8,128)(2,1)S(1)}, bf16[128,2048]{1,0:T(8,128)(2,1)S(1)}, u32[]{:S(2)}, u32[]{:S(2)}) collective-permute-start(bf16[128,2048]{1,0:T(8,128)(2,1)S(1)} %add.18), channel_id=1, source_target_pairs={{0,2},{1,3},{2,0},{3,1},{4,6},{5,7},{6,4},{7,5},{8,10},{9,11},{10,... | collective-permute-start | bytes 1572872 | tf_op jit(solution)/shard_map/ppermute | solution.py:44
  157.3 7.3 %collective-permute-start.21 = (bf16[64,2048]{1,0:T(8,128)(2,1)S(1)}, bf16[64,2048]{1,0:T(8,128)(2,1)S(1)}, u32[]{:S(2)}, u32[]{:S(2)}) collective-permute-start(bf16[64,2048]{1,0:T(8,128)(2,1)S(1)} %add_convert_fusion), channel_id=1, source_target_pairs={{0,4},{4,0},{8,12},{12,8},{16,20},{20,16},{24,28},{28,24},{1,5},{5... | collective-permute-start | bytes 786440 | tf_op jit(solution)/shard_map/ppermute | solution.py:44
  162.5 2.1 %copy-start.7 = (bf16[64,4096]{1,0:T(8,128)(2,1)S(1)}, bf16[64,4096]{1,0:T(8,128)(2,1)}, u32[]{:S(2)}) copy-start(bf16[64,4096]{1,0:T(8,128)(2,1)} %tokens.3) | copy-start | bytes 1572868
  (8 other events, 9.2 us)

commit v9 on v7

--- a/solution.py
+++ b/solution.py
@@ -135,8 +135,18 @@
     return pl.multiple_of(((place[0] ^ k) * 2 + which) * block, 128)
 
 
-def prepare_kernel(block, place, grad_out, tokens, gain, grad_keep, normed_keep, send, normed):
+def prepare_kernel(
+    block, place, gain, grad_far, tokens_far, grad_keep, normed_keep, send, normed, grad_out, tokens, arrived
+):
     rows, core = tokens.shape[0], place[1]
+    copies = [
+        pltpu.make_async_copy(tokens_far, tokens, arrived.at[0]),
+        pltpu.make_async_copy(grad_far, grad_out, arrived.at[1]),
+    ]
+    for copy in copies:
+        copy.start()
+    for copy in copies:
+        copy.wait()
     values = tokens[...].astype(jnp.float32)
     root_mean = jnp.sqrt(jnp.mean(values * values, axis=-1, keepdims=True) + epsilon)
     normed[...] = (values / root_mean * gain[...].astype(jnp.float32)).astype(jnp.bfloat16)
@@ -149,48 +159,69 @@
             ]
 
 
-def merge_kernel(out_weight, query_weight, kv_weight, merged):
-    block, start = merged.shape[0], 0
-    for chunk in range(out_weight.shape[0] // block):
-        merged[:, start : start + block] = out_weight[chunk * block : (chunk + 1) * block]
-        start += block
-    for weight in (query_weight, kv_weight):
-        merged[:, start : start + weight.shape[1]] = weight[...]
-        start += weight.shape[1]
-
-
-def products(grads, normed, weights, first, out_width, block, columns):
-    chunks = out_width // block
+def merge_kernel(count, query_weight, kv_weight, out_weight, merged, arrived):
+    block, start, parts = merged.shape[0], 0, [query_weight, kv_weight]
+    parts += [out_weight.at[k * block : (k + 1) * block] for k in range(count)]
+    copies = []
+    for number, part in enumerate(parts):
+        width = part.shape[1]
+        target = merged.at[:, start : start + width]
+        copies.append(pltpu.make_async_copy(part, target, arrived.at[number]))
+        copies[-1].start()
+        start += width
+    for copy in copies:
+        copy.wait()
+
+
+def merge(query_weight, kv_weight, out_weight):
+    block = query_weight.shape[0]
+    count = out_weight.shape[0] // block
+    width = query_weight.shape[1] + kv_weight.shape[1] + out_weight.shape[0]
+    if kv_weight.shape[1] % 128:
+        chunks = jnp.split(out_weight, count, axis=0)
+        return jnp.concatenate([query_weight, kv_weight, *chunks], axis=1)
+    return pl.pallas_call(
+        functools.partial(merge_kernel, count),
+        out_shape=shaped((block, width)),
+        in_specs=[pl.BlockSpec(memory_space=pltpu.HBM)] * 3,
+        out_specs=WHOLE,
+        scratch_shapes=[pltpu.SemaphoreType.DMA((2 + count,))],
+        compiler_params=pltpu.CompilerParams(vmem_limit_bytes=58 * 2**20),
+        cost_estimate=pl.CostEstimate(flops=0, bytes_accessed=4 * block * width, transcendentals=0),
+    )(query_weight, kv_weight, out_weight)
+
+
+def products(grads, normed, weights, first, joint_width, block, columns):
     size = weights[0].shape[0]
-    if columns < out_width:
-        chunk = columns // block
-        for row in range(0, block, min(size, 256)):
-            total = None
-            if size == block:
-                for k, weight in enumerate(weights):
-                    right = weight[row : row + min(size, 256), chunk * block : (chunk + 1) * block]
-                    left = grads[:, first + k * block : first + (k + 1) * block]
-                    term = dot(left, right, CONTRACT_LAST)
-                    total = term if total is None else total + term
-            else:
-                right = weights[row // size][:, chunk * block : (chunk + 1) * block]
-                total = dot(grads[:, first : first + block], right, CONTRACT_LAST)
-            yield slice(columns + row, columns + row + min(size, 256)), total
-    else:
-        width = min(256, weights[0].shape[1] - columns)
+    if columns < joint_width:
+        width = min(256, joint_width - columns)
         total = None
         for k, weight in enumerate(weights):
             left = normed[:, first + k * size : first + (k + 1) * size]
             term = dot(left, weight[:, columns : columns + width])
             total = term if total is None else total + term
         yield slice(columns, columns + width), total
-
-
-def column_steps(out_width, width, block):
-    return [*range(0, out_width, block), *range(out_width, width, 256)]
-
-
-def early_kernel(pieces, weights, size, out_width, place, *refs):
+        return
+    for row in range(0, block, min(size, 256)):
+        place_out = slice(columns + row, columns + row + min(size, 256))
+        total = None
+        if size == block:
+            for k, weight in enumerate(weights):
+                right = weight[row : row + min(size, 256), columns : columns + block]
+                left = grads[:, first + k * block : first + (k + 1) * block]
+                term = dot(left, right, CONTRACT_LAST)
+                total = term if total is None else total + term
+        else:
+            right = weights[row // size][:, columns : columns + block]
+            total = dot(grads[:, first : first + block], right, CONTRACT_LAST)
+        yield place_out, total
+
+
+def column_steps(joint_width, width, block):
+    return [*range(0, joint_width, 256), *range(joint_width, width, block)]
+
+
+def early_kernel(pieces, weights, size, joint_width, place, *refs):
     row_refs, weight_refs = refs[:pieces], refs[pieces : pieces + weights]
     total, grads, normed = refs[pieces + weights :]
     rows = row_refs[0].shape[0] // 2
@@ -203,32 +234,32 @@
                 pair[target : target + rows] = pick(
                     place[2], gathered, size, k, slice(core * rows, (core + 1) * rows)
                 )
-    for columns in column_steps(out_width, total.shape[1], block):
-        for place_out, value in products(grads, normed, weight_refs, 0, out_width, block, columns):
+    for columns in column_steps(joint_width, total.shape[1], block):
+        for place_out, value in products(grads, normed, weight_refs, 0, joint_width, block, columns):
             total[:, place_out] = value
 
 
-def late_kernel(first, out_width, block, total, grads, normed, *refs):
+def late_kernel(first, joint_width, block, total, grads, normed, *refs):
     weight_refs, (keep, send) = refs[:-2], refs[-2:]
     length = keep.shape[0]
     if not weight_refs:
         keep[...] = total[:length]
         send[...] = total[length:].astype(jnp.bfloat16)
-    for columns in column_steps(out_width, keep.shape[1], block) if weight_refs else []:
+    for columns in column_steps(joint_width, keep.shape[1], block) if weight_refs else []:
         for place_out, value in products(
-            grads, normed, weight_refs, first, out_width, block, columns
+            grads, normed, weight_refs, first, joint_width, block, columns
         ):
             keep[:, place_out] = total[:length, place_out] + value[:length]
             send[:, place_out] = (total[length:, place_out] + value[length:]).astype(jnp.bfloat16)
 
 
-def project(place, pieces, early, late, size, out_width):
+def project(place, pieces, early, late, size, joint_width):
     rows = pieces[0].shape[0] // 2 * size
     half = pieces[0].shape[1]
     block, width = early[0].shape
     first = len(early) * block
     total, grads, normed = call(
-        functools.partial(early_kernel, len(pieces), len(early), size, out_width),
+        functools.partial(early_kernel, len(pieces), len(early), size, joint_width),
         [shaped((2 * rows, width), jnp.float32)] + [shaped((2 * rows, half))] * 2,
         [*pieces, *early],
         [place],
@@ -236,7 +267,7 @@
         megabytes=24,
     )
     own, sent = call(
-        functools.partial(late_kernel, first, out_width, block),
+        functools.partial(late_kernel, first, joint_width, block),
         [shaped((rows, width), jnp.float32), shaped((rows, width))],
         [total, grads, normed, *late],
         flops=4 * rows * (half - first) * width,
@@ -270,13 +301,14 @@
     def joined(first, second, columns):
         return (first[:, columns] + second[:, columns].astype(jnp.float32)).astype(jnp.bfloat16)
 
-    keys = joined(own, sent, slice(2 * width, 2 * width + HD))
-    values = joined(own, sent, slice(2 * width + HD, 2 * width + 2 * HD))
+    keys = joined(own, sent, slice(width, width + HD))
+    values = joined(own, sent, slice(width + HD, width + 2 * HD))
     key_total = value_total = None
     for head in range(heads):
         columns = slice(head * HD, (head + 1) * HD)
-        out_grad = joined(own, sent, columns)
-        queries = joined(own, sent, slice(width + head * HD, width + (head + 1) * HD))
+        start = width + 2 * HD + head * HD
+        queries = joined(own, sent, columns)
+        out_grad = joined(own, sent, slice(start, start + HD))
         scores = jnp.where(allowed, dot(keys, queries, CONTRACT_LAST) * scale, -1e30)
         expo = jnp.exp(scores - jnp.max(scores, axis=0, keepdims=True))
         probs = expo * (1 / jnp.sum(expo, axis=0, keepdims=True))
@@ -335,7 +367,7 @@
     )
 
 
-def row_kernel(weights, offset_columns, own, other, *refs):
+def row_kernel(weights, own, other, *refs):
     weight_refs, outs = refs[:weights], refs[weights:]
     length = own.shape[0]
     rows = length // len(outs)
@@ -343,7 +375,7 @@
     for weight in weight_refs:
         tile = min(weight.shape[0], 256)
         for part in range(weight.shape[0] // tile):
-            right = weight[part * tile : (part + 1) * tile, offset_columns:]
+            right = weight[part * tile : (part + 1) * tile]
             for offset, left in ((0, own), (rows, other)):
                 term = dot(left[...], right, CONTRACT_LAST).astype(jnp.bfloat16)
                 for k, out in enumerate(outs):
@@ -353,15 +385,27 @@
             start += tile
 
 
-def row_terms(own, other, weights, size, out_width):
+def row_terms(own, other, weights, size):
     length, width = own.shape
     half = sum(weight.shape[0] for weight in weights)
-    return call(
-        functools.partial(row_kernel, len(weights), out_width),
-        [shaped((2 * length // size, half))] * size,
-        [own, other, *weights],
-        flops=4 * length * width * half,
-    )
+    moved = sum(2 * weight.shape[0] * width for weight in weights) + 4 * length * (width + half)
+    if width % 128 == 0:
+        specs = [pl.BlockSpec((weight.shape[0], width), lambda i: (0, 0)) for weight in weights]
+    else:
+        weights = [weight[:, :width] for weight in weights]
+        specs = [pl.BlockSpec(weight.shape, lambda i: (0, 0)) for weight in weights]
+    part = (2 * length // size, half)
+    return pl.pallas_call(
+        functools.partial(row_kernel, len(weights)),
+        grid=(1,),
+        out_shape=[shaped(part)] * size,
+        in_specs=[pl.BlockSpec(own.shape, lambda i: (0, 0))] * 2 + specs,
+        out_specs=[pl.BlockSpec(part, lambda i: (0, 0))] * size,
+        compiler_params=pltpu.CompilerParams(vmem_limit_bytes=24 * 2**20),
+        cost_estimate=pl.CostEstimate(
+            flops=4 * length * width * half, bytes_accessed=moved, transcendentals=0
+        ),
+    )(own, other, *weights)
 
 
 def finish_kernel(count, share, *refs):
@@ -435,29 +479,30 @@
     query_width = query_weight.shape[1]
     gain = norm_gain.reshape(1, width)
 
-    grad_keep, normed_keep, send = call(
+    merged = merge(query_weight, kv_weight, out_weight)
+    merged, early_tokens, early_grads = tied(merged, tokens, grad_out)
+    row_block = pltpu.VMEM((rows, width), jnp.bfloat16)
+    grad_keep, normed_keep, send = pl.pallas_call(
         functools.partial(prepare_kernel, block),
-        [shaped((rows, width // 2))] * 2 + [shaped((2 * rows, width // 2))],
-        [grad_out, tokens, gain],
-        [place],
-        [pltpu.VMEM((rows, width), jnp.bfloat16)],
-    )
-    out_width = out_weight.shape[0]
-    send, out_weight, query_weight, kv_weight = tied(send, out_weight, query_weight, kv_weight)
+        out_shape=[shaped((rows, width // 2))] * 2 + [shaped((2 * rows, width // 2))],
+        in_specs=[SCALARS, WHOLE] + [pl.BlockSpec(memory_space=pltpu.HBM)] * 2,
+        out_specs=[WHOLE] * 3,
+        scratch_shapes=[row_block] * 3 + [pltpu.SemaphoreType.DMA((2,))],
+        compiler_params=pltpu.CompilerParams(vmem_limit_bytes=56 * 2**20),
+        cost_estimate=pl.CostEstimate(
+            flops=0, bytes_accessed=8 * rows * width, transcendentals=0
+        ),
+    )(place, gain, early_grads, early_tokens)
+    joint_width = query_width + kv_weight.shape[1]
     sent = swap(send, "dp", 1)
+    early, late = gather_chips(merged)
     row_pieces = gather_tensor(jnp.concatenate([grad_keep, sent[:rows]], axis=0))
     row_pieces += gather_tensor(jnp.concatenate([normed_keep, sent[rows:]], axis=0))
-    (merged,) = call(
-        merge_kernel,
-        [shaped((block, out_width + query_width + kv_weight.shape[1]))],
-        [out_weight, query_weight, kv_weight],
-    )
-    early, late = gather_chips(merged)
-    own, sent, normed = project(place, row_pieces, early, late, tensor_size, out_width)
+    own, sent, normed = project(place, row_pieces, early, late, tensor_size, joint_width)
     sent = swap(sent, "dp", 1)
     if levels:
         joined = (own + sent.astype(jnp.float32)).astype(jnp.bfloat16)
-        keyvals = joined[:, out_width + query_width :]
+        keyvals = joined[:, query_width:joint_width]
         for bit_index in range(levels):
             partner = swap(keyvals, "tensor", 2**bit_index)
             upper = tensor_index >> bit_index & 1 == 1
@@ -465,7 +510,7 @@
                 [jnp.where(upper, partner, keyvals), jnp.where(upper, keyvals, partner)], axis=1
             )
         own = jnp.concatenate(
-            [joined[:, : out_width + query_width], keyvals], axis=1
+            [joined[:, :query_width], keyvals, joined[:, joint_width:]], axis=1
         ).astype(jnp.float32)
         sent = jnp.zeros(own.shape, jnp.bfloat16)
     combined, *partial = attention(place, doc_lengths, own, sent, rows, query_width, levels > 0)
@@ -486,7 +531,7 @@
 
     far = weight_terms(normed, combined, other, chips - 1, 1, block)
     near = weight_terms(normed, combined, other, 0, chips - 1, block)
-    row_parts = scatter_tensor(row_terms(combined, other, early + late, tensor_size, out_width))
+    row_parts = scatter_tensor(row_terms(combined, other, early + late, tensor_size))
     weight_parts = scatter_chips([*near, *far])
     handed = sum(part[rows:].astype(jnp.float32) for part in row_parts).astype(jnp.bfloat16)
     handed = swap(handed, "dp", 1)

time: 161 us -> 162 us (level)
  local copies, waits for them, and re-layouts: 8.76 us -> 3.14 us
  Pallas kernels: 26.8 us -> 30.4 us
  starting transfers between devices: 43.8 us -> 45.7 us
    pallas_call x0 -> x3, Pallas kernels: none -> 10.6 us  [the longest x1 4.38 us: row_terms(): pl.pallas_call(functools.partial(row_kernel, len(weights)), grid=(1,), ou...]
    pallas_call x9 -> x6, Pallas kernels: 24.7 us -> 17.6 us  [call(): pl.pallas_call(kernel, out_shape=outs, in_specs=[SCALARS] * len(scalars)...]
    unnamed x20, local copies, waits for them, and re-layouts: 5.24 us -> 0.84 us
    ppermute x14, starting transfers between devices: 20.8 us -> 23.3 us  [swap(): return lax.ppermute(value, axis, pairs)]
  transfers between devices with their start and end apart: 26 -> 26, of which waited for: 14 -> 15; matrix products, arithmetic and copies ran while one was open for 4% -> 3% of each run, Pallas kernels for 11% -> 10%
where the time goes in v9:
time: 162 us; the launch traced here: 161 us
  waiting for transfers between devices  76.6 us (47%)
  starting transfers between devices  45.7 us (28%)
  Pallas kernels  30.4 us (19%)
  other arithmetic  4.57 us (3%)
  local copies, waits for them, and re-layouts  3.14 us (2%)
    ppermute x12, waiting for transfers between devices, along(): return lax.ppermute(value, 'tensor', pairs)  47.6 us
    ppermute x14, waiting for transfers between devices, swap(): return lax.ppermute(value, axis, pairs)  29 us
    ppermute x14, starting transfers between devices, swap(): return lax.ppermute(value, axis, pairs)  23.3 us
    ppermute x12, starting transfers between devices, along(): return lax.ppermute(value, 'tensor', pairs)  22.4 us
    pallas_call x6, Pallas kernels, call(): pl.pallas_call(kernel, out_shape=outs, in_specs=[SCALARS] * len(scalars)...  17.6 us
    pallas_call x1, Pallas kernels, row_terms(): pl.pallas_call(functools.partial(row_kernel, len(weights)), grid=(1,), ou...  4.38 us
  transfers between devices with their start and end apart: 26, of which 15 were waited for; matrix products, arithmetic and copies ran while one was open for 3% of the time, Pallas kernels for 10%

profile of v9, /device:TPU:1, one launch (start us, length us, event | category | flops | bytes accessed | tf_op | source)
XLA Modules:
  0.0 161.4 jit_solution(10078235262125071725)
XLA Ops:
  0.6 3.1 %shard_map.94.refs_12_.refs_0_ = bf16[512,2304]{1,0:T(8,128)(2,1)} custom-call(bf16[512,1024]{1,0:T(8,128)(2,1)} %query_weight.1, bf16[512,256]{1,0:T(8,128)(2,1)} %kv_weight.1, bf16[1024,512]{1,0:T(8,128)(2,1)} %out_weight.1), custom_call_target="tpu_custom_call" | custom-call | bytes 4718592 | tf_op jit(solution)/shard_map/pallas_call | solution.py:183
  4.9 3.2 %shard_map.95 = (bf16[64,2048]{1,0:T(8,128)(2,1)}, bf16[64,2048]{1,0:T(8,128)(2,1)}, bf16[128,2048]{1,0:T(8,128)(2,1)}) custom-call(s32[3]{0:T(128)} %pad_add_fusion.place.refs_0_, bf16[1,4096]{1,0:T(2,128)(2,1)} %reshape.9.gain, bf16[64,4096]{1,0:T(8,128)(2,1)} %grad_out.1, bf16[64,4096]{1,0:T(8,128)(2,1)} %tokens.1), custom_call_target="tpu_custom_call" | custom-call | bytes 2097152 | tf_op jit(solution)/shard_map/pallas_call | solution.py:485
  8.3 2.7 %collective-permute-start.11 = (bf16[512,2304]{1,0:T(8,128)(2,1)}, bf16[512,2304]{1,0:T(8,128)(2,1)S(1)}, u32[]{:S(2)}, u32[]{:S(2)}) collective-permute-start(bf16[512,2304]{1,0:T(8,128)(2,1)} %shard_map.94.refs_12_.refs_0_), channel_id=1, source_target_pairs={{0,8},{4,12},{8,0},{12,4},{16,24},{20,28},{24,16},{28,20},{1,9},{5... | collective-permute-start | bytes 7077896 | tf_op jit(solution)/shard_map/ppermute | solution.py:44
  13.2 3.2 %collective-permute-start.6 = (bf16[128,2048]{1,0:T(8,128)(2,1)S(1)}, bf16[128,2048]{1,0:T(8,128)(2,1)S(1)}, u32[]{:S(2)}, u32[]{:S(2)}) collective-permute-start(bf16[128,2048]{1,0:T(8,128)(2,1)S(1)} %pad_maximum_fusion.3.refs_6_), channel_id=1, source_target_pairs={{0,1},{1,2},{2,3},{4,5},{5,6},{6,7},{8,9},{9,10},{10,11},{12,13},{... | collective-permute-start | bytes 1572872 | tf_op jit(solution)/shard_map/ppermute | solution.py:69
  17.8 4.8 %collective-permute-start.1 = (bf16[128,2048]{1,0:T(8,128)(2,1)S(1)}, bf16[128,2048]{1,0:T(8,128)(2,1)}, u32[]{:S(2)}, u32[]{:S(2)}) collective-permute-start(bf16[128,2048]{1,0:T(8,128)(2,1)S(1)} %pad_maximum_fusion.2.refs_0_), channel_id=1, source_target_pairs={{0,1},{1,2},{2,3},{4,5},{5,6},{6,7},{8,9},{9,10},{10,11},{12,13},{... | collective-permute-start | bytes 1572872 | tf_op jit(solution)/shard_map/ppermute | solution.py:69
  22.7 4.4 %collective-permute-done.6.refs_7_ = bf16[128,2048]{1,0:T(8,128)(2,1)S(1)} collective-permute-done((bf16[128,2048]{1,0:T(8,128)(2,1)S(1)}, bf16[128,2048]{1,0:T(8,128)(2,1)S(1)}, u32[]{:S(2)}, u32[]{:S(2)}) %collective-permute-start.6) | collective-permute-done | bytes 524320 | tf_op jit(solution)/shard_map/ppermute | solution.py:69
  28.4 2.6 %collective-permute-done.7.refs_8_ = bf16[128,2048]{1,0:T(8,128)(2,1)} collective-permute-done((bf16[128,2048]{1,0:T(8,128)(2,1)S(1)}, bf16[128,2048]{1,0:T(8,128)(2,1)}, u32[]{:S(2)}, u32[]{:S(2)}) %collective-permute-start.7) | collective-permute-done | bytes 524320 | tf_op jit(solution)/shard_map/ppermute | solution.py:69
  31.0 1.5 collective-permute-start.8
  33.3 5.0 %collective-permute-done.1.refs_1_ = bf16[128,2048]{1,0:T(8,128)(2,1)} collective-permute-done((bf16[128,2048]{1,0:T(8,128)(2,1)S(1)}, bf16[128,2048]{1,0:T(8,128)(2,1)}, u32[]{:S(2)}, u32[]{:S(2)}) %collective-permute-start.1) | collective-permute-done | bytes 524320 | tf_op jit(solution)/shard_map/ppermute | solution.py:69
  39.6 1.5 collective-permute-done.2.refs_2_
  41.1 1.5 collective-permute-start.3
  43.9 9.6 %collective-permute-done.9.refs_10_ = bf16[128,2048]{1,0:T(8,128)(2,1)} collective-permute-done((bf16[128,2048]{1,0:T(8,128)(2,1)}, bf16[128,2048]{1,0:T(8,128)(2,1)}, u32[]{:S(2)}, u32[]{:S(2)}) %collective-permute-start.9) | collective-permute-done | bytes 524320 | tf_op jit(solution)/shard_map/ppermute | solution.py:69
  55.9 8.8 %collective-permute-done.4.refs_4_ = bf16[128,2048]{1,0:T(8,128)(2,1)} collective-permute-done((bf16[128,2048]{1,0:T(8,128)(2,1)}, bf16[128,2048]{1,0:T(8,128)(2,1)}, u32[]{:S(2)}, u32[]{:S(2)}) %collective-permute-start.4) | collective-permute-done | bytes 524320 | tf_op jit(solution)/shard_map/ppermute | solution.py:69
  64.8 1.5 collective-permute-start.13
  66.3 1.5 slice.45
  70.2 1.5 collective-permute-start.5
  71.6 4.2 %collective-permute-done.10.refs_11_ = bf16[128,2048]{1,0:T(8,128)(2,1)S(1)} collective-permute-done((bf16[128,2048]{1,0:T(8,128)(2,1)S(1)}, bf16[128,2048]{1,0:T(8,128)(2,1)S(1)}, u32[]{:S(2)}, u32[]{:S(2)}) %collective-permute-start.10) | collective-permute-done | bytes 524320 | tf_op jit(solution)/shard_map/ppermute | solution.py:69
  75.8 11.2 %collective-permute-done.5.refs_5_ = bf16[128,2048]{1,0:T(8,128)(2,1)S(1)} collective-permute-done((bf16[128,2048]{1,0:T(8,128)(2,1)S(1)}, bf16[128,2048]{1,0:T(8,128)(2,1)S(1)}, u32[]{:S(2)}, u32[]{:S(2)}) %collective-permute-start.5) | collective-permute-done | bytes 524320 | tf_op jit(solution)/shard_map/ppermute | solution.py:69
  87.1 6.8 %shard_map.96 = (f32[512,2304]{1,0:T(8,128)S(1)}, bf16[512,2048]{1,0:T(8,128)(2,1)S(1)}, bf16[512,2048]{1,0:T(8,128)(2,1)S(1)}) custom-call(s32[3]{0:T(128)S(1)} %copy-done.4, bf16[128,2048]{1,0:T(8,128)(2,1)S(1)} %pad_maximum_fusion.2.refs_0_, bf16[128,2048]{1,0:T(8,128)(2,1)} %collective-permute-done.1.refs_1_, ...), custom_call_target="tpu_custom_call" | custom-call | flops 3623878656 | bytes 22282240 | tf_op jit(solution)/shard_map/pallas_call | solution.py:23
  95.4 2.4 %collective-permute-start.15 = (bf16[256,2304]{1,0:T(8,128)(2,1)S(1)}, bf16[256,2304]{1,0:T(8,128)(2,1)S(1)}, u32[]{:S(2)}, u32[]{:S(2)}) collective-permute-start(bf16[256,2304]{1,0:T(8,128)(2,1)S(1)} %get-tuple-element.60), channel_id=1, source_target_pairs={{0,4},{4,0},{8,12},{12,8},{16,20},{20,16},{24,28},{28,24},{1,5},{5... | collective-permute-start | bytes 3538952 | tf_op jit(solution)/shard_map/ppermute | solution.py:44
  97.7 2.5 %collective-permute-done.15.refs_3_ = bf16[256,2304]{1,0:T(8,128)(2,1)S(1)} collective-permute-done((bf16[256,2304]{1,0:T(8,128)(2,1)S(1)}, bf16[256,2304]{1,0:T(8,128)(2,1)S(1)}, u32[]{:S(2)}, u32[]{:S(2)}) %collective-permute-start.15) | collective-permute-done | bytes 1179680 | tf_op jit(solution)/shard_map/ppermute | solution.py:44
  100.2 4.0 %shard_map.98.own = bf16[256,1280]{1,0:T(8,128)(2,1)S(1)} custom-call(s32[3]{0:T(128)S(1)} %copy-done.4, s32[1,4]{1,0:T(1,128)S(1)} %copy-done.5, f32[256,2304]{1,0:T(8,128)S(1)} %get-tuple-element.59.refs_2_, bf16[256,2304]{1,0:T(8,128)(2,1)S(1)} %collective-permute-done.15.refs_3_), custom_call_target="tpu_custom_call" | custom-call | flops 671088640 | bytes 4194304 | tf_op jit(solution)/shard_map/pallas_call | solution.py:23
  104.7 1.7 %collective-permute-done.16.other = bf16[256,1280]{1,0:T(8,128)(2,1)S(1)} collective-permute-done((bf16[256,1280]{1,0:T(8,128)(2,1)S(1)}, bf16[256,1280]{1,0:T(8,128)(2,1)S(1)}, u32[]{:S(2)}, u32[]{:S(2)}) %collective-permute-start.16) | collective-permute-done | bytes 655392 | tf_op jit(solution)/shard_map/ppermute | solution.py:44
  109.4 4.4 %shard_map.99 = (bf16[128,2048]{1,0:T(8,128)(2,1)S(1)}, bf16[128,2048]{1,0:T(8,128)(2,1)S(1)}, bf16[128,2048]{1,0:T(8,128)(2,1)S(1)}, bf16[128,2048]{1,0:T(8,128)(2,1)S(1)}) custom-call(bf16[256,1280]{1,0:T(8,128)(2,1)S(1)} %shard_map.98.own, bf16[256,1280]{1,0:T(8,128)(2,1)S(1)} %collective-permute-done.16.other, bf16[512,2304]{1,0:T(8,128)(2,1)S(1)} %copy-done, ...), custom_call_target="tpu_custom_call" | custom-call | flops 2684354560 | bytes 8650752 | tf_op jit(solution)/shard_map/pallas_call | solution.py:398
  113.7 2.6 %collective-permute-start.17 = (bf16[128,2048]{1,0:T(8,128)(2,1)S(1)}, bf16[128,2048]{1,0:T(8,128)(2,1)S(1)}, u32[]{:S(2)}, u32[]{:S(2)}) collective-permute-start(bf16[128,2048]{1,0:T(8,128)(2,1)S(1)} %get-tuple-element.63), channel_id=1, source_target_pairs={{3,2},{0,1},{7,6},{4,5},{11,10},{8,9},{15,14},{12,13},{19,18},{16,... | collective-permute-start | bytes 1572872 | tf_op jit(solution)/shard_map/ppermute | solution.py:69
  117.2 2.3 %shard_map.100 = (bf16[512,1280]{1,0:T(8,128)(2,1)S(1)}, bf16[512,1280]{1,0:T(8,128)(2,1)S(1)}, bf16[512,1280]{1,0:T(8,128)(2,1)S(1)}) custom-call(bf16[512,2048]{1,0:T(8,128)(2,1)S(1)} %get-tuple-element.58.normed.pair, bf16[256,1280]{1,0:T(8,128)(2,1)S(1)} %shard_map.98.own, bf16[256,1280]{1,0:T(8,128)(2,1)S(1)} %collective-permute-done.16.other), custom_call_target="tpu_custom_call" | custom-call | flops 2013265920 | bytes 7340032 | tf_op jit(solution)/shard_map/pallas_call | solution.py:23
  119.5 3.9 %collective-permute-done.22 = bf16[256,1280]{1,0:T(8,128)(2,1)S(1)} collective-permute-done((bf16[256,1280]{1,0:T(8,128)(2,1)S(1)}, bf16[256,1280]{1,0:T(8,128)(2,1)S(1)}, u32[]{:S(2)}, u32[]{:S(2)}) %collective-permute-start.22) | collective-permute-done | bytes 655392 | tf_op jit(solution)/shard_map/ppermute | solution.py:44
  126.7 3.6 %collective-permute-start.19 = (bf16[128,2048]{1,0:T(8,128)(2,1)S(1)}, bf16[128,2048]{1,0:T(8,128)(2,1)S(1)}, u32[]{:S(2)}, u32[]{:S(2)}) collective-permute-start(bf16[128,2048]{1,0:T(8,128)(2,1)S(1)} %get-tuple-element.66), channel_id=1, source_target_pairs={{0,1},{1,0},{2,3},{3,2},{4,5},{5,4},{6,7},{7,6},{8,9},{9,8},{10,11... | collective-permute-start | bytes 1572872 | tf_op jit(solution)/shard_map/ppermute | solution.py:44
  130.4 20.4 %collective-permute-done.19.refs_1_ = bf16[128,2048]{1,0:T(8,128)(2,1)S(1)} collective-permute-done((bf16[128,2048]{1,0:T(8,128)(2,1)S(1)}, bf16[128,2048]{1,0:T(8,128)(2,1)S(1)}, u32[]{:S(2)}, u32[]{:S(2)}) %collective-permute-start.19) | collective-permute-done | bytes 524320 | tf_op jit(solution)/shard_map/ppermute | solution.py:44
  151.1 5.9 %collective-permute-start.21 = (bf16[64,2048]{1,0:T(8,128)(2,1)S(1)}, bf16[64,2048]{1,0:T(8,128)(2,1)S(1)}, u32[]{:S(2)}, u32[]{:S(2)}) collective-permute-start(bf16[64,2048]{1,0:T(8,128)(2,1)S(1)} %add_convert_fusion), channel_id=1, source_target_pairs={{0,4},{4,0},{8,12},{12,8},{16,20},{20,16},{24,28},{28,24},{1,5},{5... | collective-permute-start | bytes 786440 | tf_op jit(solution)/shard_map/ppermute | solution.py:44
  157.0 2.1 %shard_map.102 = (f32[512,1024]{1,0:T(8,128)}, f32[512,256]{1,0:T(8,128)}) custom-call(bf16[512,1280]{1,0:T(8,128)(2,1)S(1)} %get-tuple-element.69.refs_0_, bf16[512,1280]{1,0:T(8,128)(2,1)S(1)} %collective-permute-done.23.refs_1_, bf16[512,1280]{1,0:T(8,128)(2,1)S(1)} %collective-permute-done.25.refs_2_), custom_call_target="tpu_custom_call" | custom-call | bytes 6553600 | tf_op jit(solution)/shard_map/pallas_call | solution.py:429
  159.2 2.2 %shard_map.103 = bf16[64,4096]{1,0:T(8,128)(2,1)} custom-call(s32[3]{0:T(128)S(1)} %copy-done.4, bf16[64,4096]{1,0:T(8,128)(2,1)S(1)} %copy-done.1, bf16[1,4096]{1,0:T(2,128)(2,1)S(1)} %copy-done.3, bf16[64,4096]{1,0:T(8,128)(2,1)S(1)} %copy-done.2, bf16[64,2048]{1,0:T(8,128)(2,1)S(1)} %collective-permute-done.21.handed, ...), custom_call_target="tpu_custom_call" | custom-call | bytes 3940352 | tf_op jit(solution)/shard_map/pallas_call | solution.py:23
  (65 shorter events, 23.9 us)
Async XLA Ops:
  0.6 3.1 %copy-start.9 = (bf16[4096]{0:T(1024)(128)(2,1)S(1)}, bf16[4096]{0:T(1024)(128)(2,1)}, u32[]{:S(2)}) copy-start(bf16[4096]{0:T(1024)(128)(2,1)} %param.8) | copy-start | bytes 24580
  8.1 9.6 %copy-start.8 = (bf16[64,2048]{1,0:T(8,128)(2,1)S(1)}, bf16[64,2048]{1,0:T(8,128)(2,1)}, u32[]{:S(2)}) copy-start(bf16[64,2048]{1,0:T(8,128)(2,1)} %get-tuple-element.42) | copy-start | bytes 786436
  8.2 4.0 %collective-permute-start = (bf16[128,2048]{1,0:T(8,128)(2,1)}, bf16[128,2048]{1,0:T(8,128)(2,1)S(1)}, u32[]{:S(2)}, u32[]{:S(2)}) collective-permute-start(bf16[128,2048]{1,0:T(8,128)(2,1)} %get-tuple-element.43), channel_id=1, source_target_pairs={{0,4},{4,0},{8,12},{12,8},{16,20},{20,16},{24,28},{28,24},{1,5},{5... | collective-permute-start | bytes 1572872 | tf_op jit(solution)/shard_map/ppermute | solution.py:44
  8.3 56.4 %collective-permute-start.11 = (bf16[512,2304]{1,0:T(8,128)(2,1)}, bf16[512,2304]{1,0:T(8,128)(2,1)S(1)}, u32[]{:S(2)}, u32[]{:S(2)}) collective-permute-start(bf16[512,2304]{1,0:T(8,128)(2,1)} %shard_map.94.refs_12_.refs_0_), channel_id=1, source_target_pairs={{0,8},{4,12},{8,0},{12,4},{16,24},{20,28},{24,16},{28,20},{1,9},{5... | collective-permute-start | bytes 7077896 | tf_op jit(solution)/shard_map/ppermute | solution.py:44
  11.0 53.8 %collective-permute-start.12 = (bf16[512,2304]{1,0:T(8,128)(2,1)}, bf16[512,2304]{1,0:T(8,128)(2,1)}, u32[]{:S(2)}, u32[]{:S(2)}) collective-permute-start(bf16[512,2304]{1,0:T(8,128)(2,1)} %shard_map.94.refs_12_.refs_0_), channel_id=1, source_target_pairs={{0,16},{4,20},{8,24},{12,28},{16,0},{20,4},{24,8},{28,12},{1,17},{... | collective-permute-start | bytes 7077896 | tf_op jit(solution)/shard_map/ppermute | solution.py:44
  13.2 13.8 %collective-permute-start.6 = (bf16[128,2048]{1,0:T(8,128)(2,1)S(1)}, bf16[128,2048]{1,0:T(8,128)(2,1)S(1)}, u32[]{:S(2)}, u32[]{:S(2)}) collective-permute-start(bf16[128,2048]{1,0:T(8,128)(2,1)S(1)} %pad_maximum_fusion.3.refs_6_), channel_id=1, source_target_pairs={{0,1},{1,2},{2,3},{4,5},{5,6},{6,7},{8,9},{9,10},{10,11},{12,13},{... | collective-permute-start | bytes 1572872 | tf_op jit(solution)/shard_map/ppermute | solution.py:69
  16.5 14.5 %collective-permute-start.7 = (bf16[128,2048]{1,0:T(8,128)(2,1)S(1)}, bf16[128,2048]{1,0:T(8,128)(2,1)}, u32[]{:S(2)}, u32[]{:S(2)}) collective-permute-start(bf16[128,2048]{1,0:T(8,128)(2,1)S(1)} %pad_maximum_fusion.3.refs_6_), channel_id=1, source_target_pairs={{1,0},{2,1},{3,2},{5,4},{6,5},{7,6},{9,8},{10,9},{11,10},{13,12},{... | collective-permute-start | bytes 1572872 | tf_op jit(solution)/shard_map/ppermute | solution.py:69
  17.8 20.5 %collective-permute-start.1 = (bf16[128,2048]{1,0:T(8,128)(2,1)S(1)}, bf16[128,2048]{1,0:T(8,128)(2,1)}, u32[]{:S(2)}, u32[]{:S(2)}) collective-permute-start(bf16[128,2048]{1,0:T(8,128)(2,1)S(1)} %pad_maximum_fusion.2.refs_0_), channel_id=1, source_target_pairs={{0,1},{1,2},{2,3},{4,5},{5,6},{6,7},{8,9},{9,10},{10,11},{12,13},{... | collective-permute-start | bytes 1572872 | tf_op jit(solution)/shard_map/ppermute | solution.py:69
  27.1 14.1 %collective-permute-start.2 = (bf16[128,2048]{1,0:T(8,128)(2,1)S(1)}, bf16[128,2048]{1,0:T(8,128)(2,1)}, u32[]{:S(2)}, u32[]{:S(2)}) collective-permute-start(bf16[128,2048]{1,0:T(8,128)(2,1)S(1)} %pad_maximum_fusion.2.refs_0_), channel_id=1, source_target_pairs={{1,0},{2,1},{3,2},{5,4},{6,5},{7,6},{9,8},{10,9},{11,10},{13,12},{... | collective-permute-start | bytes 1572872 | tf_op jit(solution)/shard_map/ppermute | solution.py:69
  31.0 11.6 %collective-permute-start.8 = (bf16[128,2048]{1,0:T(8,128)(2,1)S(1)}, bf16[128,2048]{1,0:T(8,128)(2,1)}, u32[]{:S(2)}, u32[]{:S(2)}) collective-permute-start(bf16[128,2048]{1,0:T(8,128)(2,1)S(1)} %collective-permute-done.6.refs_7_), channel_id=1, source_target_pairs={{1,2},{2,3},{5,6},{6,7},{9,10},{10,11},{13,14},{14,15},{17,18},{18... | collective-permute-start | bytes 1572872 | tf_op jit(solution)/shard_map/ppermute | solution.py:69
  38.3 15.2 %collective-permute-start.9 = (bf16[128,2048]{1,0:T(8,128)(2,1)}, bf16[128,2048]{1,0:T(8,128)(2,1)}, u32[]{:S(2)}, u32[]{:S(2)}) collective-permute-start(bf16[128,2048]{1,0:T(8,128)(2,1)} %collective-permute-done.7.refs_8_), channel_id=1, source_target_pairs={{1,0},{2,1},{5,4},{6,5},{9,8},{10,9},{13,12},{14,13},{17,16},{18,1... | collective-permute-start | bytes 1572872 | tf_op jit(solution)/shard_map/ppermute | solution.py:69
  41.1 14.8 %collective-permute-start.3 = (bf16[128,2048]{1,0:T(8,128)(2,1)}, bf16[128,2048]{1,0:T(8,128)(2,1)}, u32[]{:S(2)}, u32[]{:S(2)}) collective-permute-start(bf16[128,2048]{1,0:T(8,128)(2,1)} %collective-permute-done.1.refs_1_), channel_id=1, source_target_pairs={{1,2},{2,3},{5,6},{6,7},{9,10},{10,11},{13,14},{14,15},{17,18},{18... | collective-permute-start | bytes 1572872 | tf_op jit(solution)/shard_map/ppermute | solution.py:69
  42.6 22.1 %collective-permute-start.4 = (bf16[128,2048]{1,0:T(8,128)(2,1)}, bf16[128,2048]{1,0:T(8,128)(2,1)}, u32[]{:S(2)}, u32[]{:S(2)}) collective-permute-start(bf16[128,2048]{1,0:T(8,128)(2,1)} %collective-permute-done.2.refs_2_), channel_id=1, source_target_pairs={{1,0},{2,1},{5,4},{6,5},{9,8},{10,9},{13,12},{14,13},{17,16},{18,1... | collective-permute-start | bytes 1572872 | tf_op jit(solution)/shard_map/ppermute | solution.py:69
  54.6 21.3 %collective-permute-start.10 = (bf16[128,2048]{1,0:T(8,128)(2,1)S(1)}, bf16[128,2048]{1,0:T(8,128)(2,1)S(1)}, u32[]{:S(2)}, u32[]{:S(2)}) collective-permute-start(bf16[128,2048]{1,0:T(8,128)(2,1)S(1)} %broadcast_select_fusion), channel_id=1, source_target_pairs={{1,0},{2,3},{5,4},{6,7},{9,8},{10,11},{13,12},{14,15},{17,16},{18,... | collective-permute-start | bytes 1572872 | tf_op jit(solution)/shard_map/ppermute | solution.py:69
  64.8 29.1 %collective-permute-start.13 = (bf16[256,2304]{1,0:T(8,128)(2,1)S(1)}, bf16[256,2304]{1,0:T(8,128)(2,1)S(1)}, u32[]{:S(2)}, u32[]{:S(2)}) collective-permute-start(bf16[256,2304]{1,0:T(8,128)(2,1)S(1)} %slice.44), channel_id=1, source_target_pairs={{0,16},{4,20},{8,24},{12,28},{16,0},{20,4},{24,8},{28,12},{1,17},{... | collective-permute-start | bytes 3538952 | tf_op jit(solution)/shard_map/ppermute | solution.py:44
  66.3 20.8 %copy-start = (bf16[512,2304]{1,0:T(8,128)(2,1)S(1)}, bf16[512,2304]{1,0:T(8,128)(2,1)}, u32[]{:S(2)}) copy-start(bf16[512,2304]{1,0:T(8,128)(2,1)} %shard_map.94.refs_12_.refs_0_) | copy-start | bytes 7077892
  67.8 19.3 %copy-start.4 = (s32[3]{0:T(128)S(1)}, s32[3]{0:T(128)}, u32[]{:S(2)}) copy-start(s32[3]{0:T(128)} %pad_add_fusion.place.refs_0_) | copy-start | bytes 40
  67.8 19.3 %copy-start.7 = (bf16[128,2048]{1,0:T(8,128)(2,1)S(1)}, bf16[128,2048]{1,0:T(8,128)(2,1)}, u32[]{:S(2)}) copy-start(bf16[128,2048]{1,0:T(8,128)(2,1)} %copy-done.6) | copy-start | bytes 1572868
  67.8 26.1 %collective-permute-start.14 = (bf16[256,2304]{1,0:T(8,128)(2,1)S(1)}, bf16[256,2304]{1,0:T(8,128)(2,1)S(1)}, u32[]{:S(2)}, u32[]{:S(2)}) collective-permute-start(bf16[256,2304]{1,0:T(8,128)(2,1)S(1)} %slice.45), channel_id=1, source_target_pairs={{0,8},{4,12},{8,0},{12,4},{16,24},{20,28},{24,16},{28,20},{1,9},{5... | collective-permute-start | bytes 3538952 | tf_op jit(solution)/shard_map/ppermute | solution.py:44
  70.2 16.9 %collective-permute-start.5 = (bf16[128,2048]{1,0:T(8,128)(2,1)S(1)}, bf16[128,2048]{1,0:T(8,128)(2,1)S(1)}, u32[]{:S(2)}, u32[]{:S(2)}) collective-permute-start(bf16[128,2048]{1,0:T(8,128)(2,1)S(1)} %broadcast_select_fusion.1), channel_id=1, source_target_pairs={{1,0},{2,3},{5,4},{6,7},{9,8},{10,11},{13,12},{14,15},{17,16},{18,... | collective-permute-start | bytes 1572872 | tf_op jit(solution)/shard_map/ppermute | solution.py:69
  93.9 6.3 %copy-start.5 = (s32[1,4]{1,0:T(1,128)S(1)}, s32[1,4]{1,0:T(1,128)}, u32[]{:S(2)}) copy-start(s32[1,4]{1,0:T(1,128)} %refs_1_.1) | copy-start | bytes 52
  95.4 4.8 %collective-permute-start.15 = (bf16[256,2304]{1,0:T(8,128)(2,1)S(1)}, bf16[256,2304]{1,0:T(8,128)(2,1)S(1)}, u32[]{:S(2)}, u32[]{:S(2)}) collective-permute-start(bf16[256,2304]{1,0:T(8,128)(2,1)S(1)} %get-tuple-element.60), channel_id=1, source_target_pairs={{0,4},{4,0},{8,12},{12,8},{16,20},{20,16},{24,28},{28,24},{1,5},{5... | collective-permute-start | bytes 3538952 | tf_op jit(solution)/shard_map/ppermute | solution.py:44
  104.2 2.2 %collective-permute-start.16 = (bf16[256,1280]{1,0:T(8,128)(2,1)S(1)}, bf16[256,1280]{1,0:T(8,128)(2,1)S(1)}, u32[]{:S(2)}, u32[]{:S(2)}) collective-permute-start(bf16[256,1280]{1,0:T(8,128)(2,1)S(1)} %shard_map.98.own), channel_id=1, source_target_pairs={{0,4},{4,0},{8,12},{12,8},{16,20},{20,16},{24,28},{28,24},{1,5},{5... | collective-permute-start | bytes 1966088 | tf_op jit(solution)/shard_map/ppermute | solution.py:44
  107.4 16.0 %collective-permute-start.22 = (bf16[256,1280]{1,0:T(8,128)(2,1)S(1)}, bf16[256,1280]{1,0:T(8,128)(2,1)S(1)}, u32[]{:S(2)}, u32[]{:S(2)}) collective-permute-start(bf16[256,1280]{1,0:T(8,128)(2,1)S(1)} %get-tuple-element.80), channel_id=1, source_target_pairs={{0,16},{4,20},{8,24},{12,28},{16,0},{20,4},{24,8},{28,12},{1,17},{... | collective-permute-start | bytes 1966088 | tf_op jit(solution)/shard_map/ppermute | solution.py:44
  108.2 15.6 %collective-permute-start.24 = (bf16[256,1280]{1,0:T(8,128)(2,1)S(1)}, bf16[256,1280]{1,0:T(8,128)(2,1)S(1)}, u32[]{:S(2)}, u32[]{:S(2)}) collective-permute-start(bf16[256,1280]{1,0:T(8,128)(2,1)S(1)} %get-tuple-element.79), channel_id=1, source_target_pairs={{0,8},{4,12},{8,0},{12,4},{16,24},{20,28},{24,16},{28,20},{1,9},{5... | collective-permute-start | bytes 1966088 | tf_op jit(solution)/shard_map/ppermute | solution.py:44
  113.7 12.8 %collective-permute-start.17 = (bf16[128,2048]{1,0:T(8,128)(2,1)S(1)}, bf16[128,2048]{1,0:T(8,128)(2,1)S(1)}, u32[]{:S(2)}, u32[]{:S(2)}) collective-permute-start(bf16[128,2048]{1,0:T(8,128)(2,1)S(1)} %get-tuple-element.63), channel_id=1, source_target_pairs={{3,2},{0,1},{7,6},{4,5},{11,10},{8,9},{15,14},{12,13},{19,18},{16,... | collective-permute-start | bytes 1572872 | tf_op jit(solution)/shard_map/ppermute | solution.py:69
  116.3 10.2 %collective-permute-start.18 = (bf16[128,2048]{1,0:T(8,128)(2,1)S(1)}, bf16[128,2048]{1,0:T(8,128)(2,1)S(1)}, u32[]{:S(2)}, u32[]{:S(2)}) collective-permute-start(bf16[128,2048]{1,0:T(8,128)(2,1)S(1)} %get-tuple-element.63), channel_id=1, source_target_pairs={{1,2},{2,1},{5,6},{6,5},{9,10},{10,9},{13,14},{14,13},{17,18},{18,... | collective-permute-start | bytes 1572872 | tf_op jit(solution)/shard_map/ppermute | solution.py:69
  124.2 32.8 %collective-permute-start.25 = (bf16[512,1280]{1,0:T(8,128)(2,1)S(1)}, bf16[512,1280]{1,0:T(8,128)(2,1)S(1)}, u32[]{:S(2)}, u32[]{:S(2)}) collective-permute-start(bf16[512,1280]{1,0:T(8,128)(2,1)S(1)} %pad_maximum_fusion.1), channel_id=1, source_target_pairs={{0,16},{4,20},{8,24},{12,28},{16,0},{20,4},{24,8},{28,12},{1,17},{... | collective-permute-start | bytes 3932168 | tf_op jit(solution)/shard_map/ppermute | solution.py:44
  125.1 31.9 %collective-permute-start.23 = (bf16[512,1280]{1,0:T(8,128)(2,1)S(1)}, bf16[512,1280]{1,0:T(8,128)(2,1)S(1)}, u32[]{:S(2)}, u32[]{:S(2)}) collective-permute-start(bf16[512,1280]{1,0:T(8,128)(2,1)S(1)} %pad_maximum_fusion), channel_id=1, source_target_pairs={{0,8},{4,12},{8,0},{12,4},{16,24},{20,28},{24,16},{28,20},{1,9},{5... | collective-permute-start | bytes 3932168 | tf_op jit(solution)/shard_map/ppermute | solution.py:44
  126.7 24.1 %collective-permute-start.19 = (bf16[128,2048]{1,0:T(8,128)(2,1)S(1)}, bf16[128,2048]{1,0:T(8,128)(2,1)S(1)}, u32[]{:S(2)}, u32[]{:S(2)}) collective-permute-start(bf16[128,2048]{1,0:T(8,128)(2,1)S(1)} %get-tuple-element.66), channel_id=1, source_target_pairs={{0,1},{1,0},{2,3},{3,2},{4,5},{5,4},{6,7},{7,6},{8,9},{9,8},{10,11... | collective-permute-start | bytes 1572872 | tf_op jit(solution)/shard_map/ppermute | solution.py:44
  130.3 20.7 %collective-permute-start.20 = (bf16[128,2048]{1,0:T(8,128)(2,1)S(1)}, bf16[128,2048]{1,0:T(8,128)(2,1)S(1)}, u32[]{:S(2)}, u32[]{:S(2)}) collective-permute-start(bf16[128,2048]{1,0:T(8,128)(2,1)S(1)} %add.18), channel_id=1, source_target_pairs={{0,2},{1,3},{2,0},{3,1},{4,6},{5,7},{6,4},{7,5},{8,10},{9,11},{10,... | collective-permute-start | bytes 1572872 | tf_op jit(solution)/shard_map/ppermute | solution.py:44
  151.1 8.1 %collective-permute-start.21 = (bf16[64,2048]{1,0:T(8,128)(2,1)S(1)}, bf16[64,2048]{1,0:T(8,128)(2,1)S(1)}, u32[]{:S(2)}, u32[]{:S(2)}) collective-permute-start(bf16[64,2048]{1,0:T(8,128)(2,1)S(1)} %add_convert_fusion), channel_id=1, source_target_pairs={{0,4},{4,0},{8,12},{12,8},{16,20},{20,16},{24,28},{28,24},{1,5},{5... | collective-permute-start | bytes 786440 | tf_op jit(solution)/shard_map/ppermute | solution.py:44
  (4 other events, 7.2 us)

commit v10 on v9

--- a/solution.py
+++ b/solution.py
@@ -53,28 +53,39 @@
     return [value] + [swap(value, axis, unit * k) for k in range(1, size)]
 
 
-def gather_chips(value):
+def gather_chips(top, bottom, after):
     if lax.axis_size("dp") != 8:
-        return everyone(value, "dp", 2), []
-    half = value.shape[0] // 2
-    near_x = swap(value, "dp", 2)
-    near_y = swap(value, "dp", 4)
-    near_x, near_y = tied(near_x, near_y)
-    far_top = swap(near_x[:half], "dp", 4)
-    far_bottom = swap(near_y[half:], "dp", 2)
-    return [value, near_x, near_y], [far_top, far_bottom]
+        halves = zip(everyone(top, "dp", 2), everyone(bottom, "dp", 2))
+        return [half for pair in halves for half in pair], []
+    x_top = swap(top, "dp", 2)
+    y_bottom = swap(bottom, "dp", 4)
+    later, x_top, *_ = tied(bottom, x_top, *after)
+    x_bottom = swap(later, "dp", 2)
+    later, y_bottom, *_ = tied(top, y_bottom, *after)
+    y_top = swap(later, "dp", 4)
+    far_bottom, x_bottom = tied(y_bottom, x_bottom)
+    far_bottom = swap(far_bottom, "dp", 2)
+    far_top, y_top = tied(x_top, y_top)
+    far_top = swap(far_top, "dp", 4)
+    return [top, bottom, x_top, x_bottom, y_top, y_bottom], [far_top, far_bottom]
 
 
 def along(value, pairs):
     return lax.ppermute(value, "tensor", pairs)
 
 
-def gather_tensor(value):
+def first_hops(value):
+    if lax.axis_size("tensor") != 4:
+        return []
+    right_one = along(value, [(0, 1), (1, 2), (2, 3)])
+    left_one = along(value, [(1, 0), (2, 1), (3, 2)])
+    return tied(right_one, left_one)
+
+
+def gather_tensor(value, ones):
     if lax.axis_size("tensor") != 4:
         return everyone(value, "tensor", 1)
-    right_one = along(value, [(0, 1), (1, 2), (2, 3)])
-    left_one = along(value, [(1, 0), (2, 1), (3, 2)])
-    right_one, left_one = tied(right_one, left_one)
+    right_one, left_one = ones
     right_two = along(right_one, [(1, 2), (2, 3)])
     left_two = along(left_one, [(1, 0), (2, 1)])
     right_two, left_two = tied(right_two, left_two)
@@ -135,18 +146,8 @@
     return pl.multiple_of(((place[0] ^ k) * 2 + which) * block, 128)
 
 
-def prepare_kernel(
-    block, place, gain, grad_far, tokens_far, grad_keep, normed_keep, send, normed, grad_out, tokens, arrived
-):
+def prepare_kernel(block, place, grad_out, tokens, gain, grad_keep, normed_keep, send, normed):
     rows, core = tokens.shape[0], place[1]
-    copies = [
-        pltpu.make_async_copy(tokens_far, tokens, arrived.at[0]),
-        pltpu.make_async_copy(grad_far, grad_out, arrived.at[1]),
-    ]
-    for copy in copies:
-        copy.start()
-    for copy in copies:
-        copy.wait()
     values = tokens[...].astype(jnp.float32)
     root_mean = jnp.sqrt(jnp.mean(values * values, axis=-1, keepdims=True) + epsilon)
     normed[...] = (values / root_mean * gain[...].astype(jnp.float32)).astype(jnp.bfloat16)
@@ -159,36 +160,17 @@
             ]
 
 
-def merge_kernel(count, query_weight, kv_weight, out_weight, merged, arrived):
-    block, start, parts = merged.shape[0], 0, [query_weight, kv_weight]
-    parts += [out_weight.at[k * block : (k + 1) * block] for k in range(count)]
-    copies = []
-    for number, part in enumerate(parts):
-        width = part.shape[1]
-        target = merged.at[:, start : start + width]
-        copies.append(pltpu.make_async_copy(part, target, arrived.at[number]))
-        copies[-1].start()
-        start += width
-    for copy in copies:
-        copy.wait()
-
-
-def merge(query_weight, kv_weight, out_weight):
-    block = query_weight.shape[0]
-    count = out_weight.shape[0] // block
-    width = query_weight.shape[1] + kv_weight.shape[1] + out_weight.shape[0]
-    if kv_weight.shape[1] % 128:
-        chunks = jnp.split(out_weight, count, axis=0)
-        return jnp.concatenate([query_weight, kv_weight, *chunks], axis=1)
-    return pl.pallas_call(
-        functools.partial(merge_kernel, count),
-        out_shape=shaped((block, width)),
-        in_specs=[pl.BlockSpec(memory_space=pltpu.HBM)] * 3,
-        out_specs=WHOLE,
-        scratch_shapes=[pltpu.SemaphoreType.DMA((2 + count,))],
-        compiler_params=pltpu.CompilerParams(vmem_limit_bytes=58 * 2**20),
-        cost_estimate=pl.CostEstimate(flops=0, bytes_accessed=4 * block * width, transcendentals=0),
-    )(query_weight, kv_weight, out_weight)
+def merge_kernel(query_weight, kv_weight, out_weight, *halves):
+    half = halves[0].shape[0]
+    for number, merged in enumerate(halves):
+        start = 0
+        for weight in (query_weight, kv_weight):
+            merged[:, start : start + weight.shape[1]] = weight[number * half : (number + 1) * half]
+            start += weight.shape[1]
+        for chunk in range(0, out_weight.shape[0], 2 * half):
+            first = chunk + number * half
+            merged[:, start : start + out_weight.shape[1]] = out_weight[first : first + half]
+            start += out_weight.shape[1]
 
 
 def products(grads, normed, weights, first, joint_width, block, columns):
@@ -202,19 +184,13 @@
             total = term if total is None else total + term
         yield slice(columns, columns + width), total
         return
-    for row in range(0, block, min(size, 256)):
-        place_out = slice(columns + row, columns + row + min(size, 256))
+    for half in range(2):
         total = None
-        if size == block:
-            for k, weight in enumerate(weights):
-                right = weight[row : row + min(size, 256), columns : columns + block]
-                left = grads[:, first + k * block : first + (k + 1) * block]
-                term = dot(left, right, CONTRACT_LAST)
-                total = term if total is None else total + term
-        else:
-            right = weights[row // size][:, columns : columns + block]
-            total = dot(grads[:, first : first + block], right, CONTRACT_LAST)
-        yield place_out, total
+        for k, weight in enumerate(weights[half::2]):
+            left = grads[:, first + k * block : first + (k + 1) * block]
+            term = dot(left, weight[:, columns : columns + block], CONTRACT_LAST)
+            total = term if total is None else total + term
+        yield slice(columns + half * size, columns + (half + 1) * size), total
 
 
 def column_steps(joint_width, width, block):
@@ -225,7 +201,7 @@
     row_refs, weight_refs = refs[:pieces], refs[pieces : pieces + weights]
     total, grads, normed = refs[pieces + weights :]
     rows = row_refs[0].shape[0] // 2
-    block = weight_refs[0].shape[0]
+    block = 2 * weight_refs[0].shape[0]
     halves = row_refs[: pieces // 2], row_refs[pieces // 2 :]
     for pair, gathered in zip((grads, normed), halves):
         for core in range(2):
@@ -256,8 +232,8 @@
 def project(place, pieces, early, late, size, joint_width):
     rows = pieces[0].shape[0] // 2 * size
     half = pieces[0].shape[1]
-    block, width = early[0].shape
-    first = len(early) * block
+    half_block, width = early[0].shape
+    block, first = 2 * half_block, len(early) * half_block
     total, grads, normed = call(
         functools.partial(early_kernel, len(pieces), len(early), size, joint_width),
         [shaped((2 * rows, width), jnp.float32)] + [shaped((2 * rows, half))] * 2,
@@ -479,25 +455,27 @@
     query_width = query_weight.shape[1]
     gain = norm_gain.reshape(1, width)
 
-    merged = merge(query_weight, kv_weight, out_weight)
-    merged, early_tokens, early_grads = tied(merged, tokens, grad_out)
-    row_block = pltpu.VMEM((rows, width), jnp.bfloat16)
-    grad_keep, normed_keep, send = pl.pallas_call(
+    grad_keep, normed_keep, send = call(
         functools.partial(prepare_kernel, block),
-        out_shape=[shaped((rows, width // 2))] * 2 + [shaped((2 * rows, width // 2))],
-        in_specs=[SCALARS, WHOLE] + [pl.BlockSpec(memory_space=pltpu.HBM)] * 2,
-        out_specs=[WHOLE] * 3,
-        scratch_shapes=[row_block] * 3 + [pltpu.SemaphoreType.DMA((2,))],
-        compiler_params=pltpu.CompilerParams(vmem_limit_bytes=56 * 2**20),
-        cost_estimate=pl.CostEstimate(
-            flops=0, bytes_accessed=8 * rows * width, transcendentals=0
-        ),
-    )(place, gain, early_grads, early_tokens)
+        [shaped((rows, width // 2))] * 2 + [shaped((2 * rows, width // 2))],
+        [grad_out, tokens, gain],
+        [place],
+        [pltpu.VMEM((rows, width), jnp.bfloat16)],
+    )
     joint_width = query_width + kv_weight.shape[1]
+    send, out_weight, query_weight, kv_weight = tied(send, out_weight, query_weight, kv_weight)
     sent = swap(send, "dp", 1)
-    early, late = gather_chips(merged)
-    row_pieces = gather_tensor(jnp.concatenate([grad_keep, sent[:rows]], axis=0))
-    row_pieces += gather_tensor(jnp.concatenate([normed_keep, sent[rows:]], axis=0))
+    merged = call(
+        merge_kernel,
+        [shaped((block // 2, joint_width + out_weight.shape[0]))] * 2,
+        [query_weight, kv_weight, out_weight],
+    )
+    grad_pair = jnp.concatenate([grad_keep, sent[:rows]], axis=0)
+    normed_pair = jnp.concatenate([normed_keep, sent[rows:]], axis=0)
+    ones = first_hops(grad_pair)
+    early, late = gather_chips(*merged, ones)
+    row_pieces = gather_tensor(grad_pair, ones)
+    row_pieces += gather_tensor(normed_pair, first_hops(normed_pair))
     own, sent, normed = project(place, row_pieces, early, late, tensor_size, joint_width)
     sent = swap(sent, "dp", 1)
     if levels:

time: 162 us -> 166 us (1.025); the launches traced: 161 us -> 163 us
  waiting for transfers between devices: 76.6 us -> 84.3 us
  Pallas kernels: 30.4 us -> 25.1 us
  local copies, waits for them, and re-layouts: 3.14 us -> 7.89 us
  starting transfers between devices: 45.7 us -> 42 us
    ppermute x14 -> x16, waiting for transfers between devices: 29 us -> 38.1 us  [swap(): return lax.ppermute(value, axis, pairs)]
    pallas_call x2 -> x0, Pallas kernels: 6.27 us -> none  [the longest x1 3.19 us: local(): pl.pallas_call(functools.partial(prepare_kernel, block), out_shape=[shape...]
    unnamed x20 -> x36, local copies, waits for them, and re-layouts: 0.84 us -> 7.06 us
    ppermute x14 -> x16, starting transfers between devices: 23.3 us -> 20.9 us  [swap(): return lax.ppermute(value, axis, pairs)]
    pallas_call x6 -> x8, Pallas kernels: 17.6 us -> 18.7 us  [call(): pl.pallas_call(kernel, out_shape=outs, in_specs=[SCALARS] * len(scalars)...]
  transfers between devices with their start and end apart: 26 -> 28, of which waited for: 15 -> 13; matrix products, arithmetic and copies ran while one was open for 3% -> 2% of each run, Pallas kernels for 10% -> 10%
where the time goes in v10:
time: 166 us; the launch traced here: 163 us
  waiting for transfers between devices  84.3 us (51%)
  starting transfers between devices  42 us (25%)
  Pallas kernels  25.1 us (15%)
  local copies, waits for them, and re-layouts  7.89 us (5%)
  other arithmetic  3 us (2%)
    ppermute x12, waiting for transfers between devices, along(): return lax.ppermute(value, 'tensor', pairs)  46.2 us
    ppermute x16, waiting for transfers between devices, swap(): return lax.ppermute(value, axis, pairs)  38.1 us
    ppermute x12, starting transfers between devices, along(): return lax.ppermute(value, 'tensor', pairs)  21.1 us
    ppermute x16, starting transfers between devices, swap(): return lax.ppermute(value, axis, pairs)  20.9 us
    pallas_call x8, Pallas kernels, call(): pl.pallas_call(kernel, out_shape=outs, in_specs=[SCALARS] * len(scalars)...  18.7 us
    unnamed x36, local copies, waits for them, and re-layouts  7.06 us
    pallas_call x1, Pallas kernels, row_terms(): pl.pallas_call(functools.partial(row_kernel, len(weights)), grid=(1,), ou...  4.3 us
  transfers between devices with their start and end apart: 28, of which 13 were waited for; matrix products, arithmetic and copies ran while one was open for 2% of the time, Pallas kernels for 10%

profile of v10, /device:TPU:1, one launch (start us, length us, event | category | flops | bytes accessed | tf_op | source)
XLA Modules:
  0.0 163.3 jit_solution(12915810494260732109)
XLA Ops:
  7.1 2.6 %collective-permute-start.12 = (bf16[256,2304]{1,0:T(8,128)(2,1)S(1)}, bf16[256,2304]{1,0:T(8,128)(2,1)S(1)}, u32[]{:S(2)}, u32[]{:S(2)}) collective-permute-start(bf16[256,2304]{1,0:T(8,128)(2,1)S(1)} %get-tuple-element.68.refs_13_.refs_1_), channel_id=1, source_target_pairs={{0,16},{4,20},{8,24},{12,28},{16,0},{20,4},{24,8},{28,12},{1,17},{... | collective-permute-start | bytes 3538952 | tf_op jit(solution)/shard_map/ppermute | solution.py:44
  11.0 4.0 %collective-permute-start.1 = (bf16[128,2048]{1,0:T(8,128)(2,1)S(1)}, bf16[128,2048]{1,0:T(8,128)(2,1)}, u32[]{:S(2)}, u32[]{:S(2)}) collective-permute-start(bf16[128,2048]{1,0:T(8,128)(2,1)S(1)} %pad_maximum_fusion.2.refs_0_), channel_id=1, source_target_pairs={{0,1},{1,2},{2,3},{4,5},{5,6},{6,7},{8,9},{9,10},{10,11},{12,13},{... | collective-permute-start | bytes 1572872 | tf_op jit(solution)/shard_map/ppermute | solution.py:74
  15.0 1.3 collective-permute-start.2
  16.3 4.0 %collective-permute-start.6 = (bf16[128,2048]{1,0:T(8,128)(2,1)S(1)}, bf16[128,2048]{1,0:T(8,128)(2,1)S(1)}, u32[]{:S(2)}, u32[]{:S(2)}) collective-permute-start(bf16[128,2048]{1,0:T(8,128)(2,1)S(1)} %pad_maximum_fusion.3.refs_6_), channel_id=1, source_target_pairs={{0,1},{1,2},{2,3},{4,5},{5,6},{6,7},{8,9},{9,10},{10,11},{12,13},{... | collective-permute-start | bytes 1572872 | tf_op jit(solution)/shard_map/ppermute | solution.py:74
  20.3 4.3 %collective-permute-done.1.refs_1_ = bf16[128,2048]{1,0:T(8,128)(2,1)} collective-permute-done((bf16[128,2048]{1,0:T(8,128)(2,1)S(1)}, bf16[128,2048]{1,0:T(8,128)(2,1)}, u32[]{:S(2)}, u32[]{:S(2)}) %collective-permute-start.1) | collective-permute-done | bytes 524320 | tf_op jit(solution)/shard_map/ppermute | solution.py:74
  24.7 1.3 collective-permute-start.7
  26.8 2.6 %collective-permute-done.2.refs_2_ = bf16[128,2048]{1,0:T(8,128)(2,1)} collective-permute-done((bf16[128,2048]{1,0:T(8,128)(2,1)S(1)}, bf16[128,2048]{1,0:T(8,128)(2,1)}, u32[]{:S(2)}, u32[]{:S(2)}) %collective-permute-start.2) | collective-permute-done | bytes 524320 | tf_op jit(solution)/shard_map/ppermute | solution.py:74
  29.3 6.7 %collective-permute-done.12.refs_17_.refs_5_ = bf16[256,2304]{1,0:T(8,128)(2,1)S(1)} collective-permute-done((bf16[256,2304]{1,0:T(8,128)(2,1)S(1)}, bf16[256,2304]{1,0:T(8,128)(2,1)S(1)}, u32[]{:S(2)}, u32[]{:S(2)}) %collective-permute-start.12) | collective-permute-done | bytes 1179680 | tf_op jit(solution)/shard_map/ppermute | solution.py:44
  39.7 1.5 collective-permute-start.8
  43.2 1.5 collective-permute-start.3
  44.7 1.3 collective-permute-start.4
  46.1 11.0 %collective-permute-done.9.refs_10_ = bf16[128,2048]{1,0:T(8,128)(2,1)} collective-permute-done((bf16[128,2048]{1,0:T(8,128)(2,1)}, bf16[128,2048]{1,0:T(8,128)(2,1)}, u32[]{:S(2)}, u32[]{:S(2)}) %collective-permute-start.9) | collective-permute-done | bytes 524320 | tf_op jit(solution)/shard_map/ppermute | solution.py:74
  58.2 1.3 collective-permute-start.10
  59.5 8.8 %collective-permute-done.4.refs_4_ = bf16[128,2048]{1,0:T(8,128)(2,1)} collective-permute-done((bf16[128,2048]{1,0:T(8,128)(2,1)}, bf16[128,2048]{1,0:T(8,128)(2,1)}, u32[]{:S(2)}, u32[]{:S(2)}) %collective-permute-start.4) | collective-permute-done | bytes 524320 | tf_op jit(solution)/shard_map/ppermute | solution.py:74
  70.0 1.5 collective-permute-start.5
  71.4 8.0 %collective-permute-done.10.refs_11_ = bf16[128,2048]{1,0:T(8,128)(2,1)S(1)} collective-permute-done((bf16[128,2048]{1,0:T(8,128)(2,1)S(1)}, bf16[128,2048]{1,0:T(8,128)(2,1)S(1)}, u32[]{:S(2)}, u32[]{:S(2)}) %collective-permute-start.10) | collective-permute-done | bytes 524320 | tf_op jit(solution)/shard_map/ppermute | solution.py:74
  79.4 11.2 %collective-permute-done.5.refs_5_ = bf16[128,2048]{1,0:T(8,128)(2,1)S(1)} collective-permute-done((bf16[128,2048]{1,0:T(8,128)(2,1)S(1)}, bf16[128,2048]{1,0:T(8,128)(2,1)S(1)}, u32[]{:S(2)}, u32[]{:S(2)}) %collective-permute-start.5) | collective-permute-done | bytes 524320 | tf_op jit(solution)/shard_map/ppermute | solution.py:74
  90.7 6.8 %shard_map.96 = (f32[512,2304]{1,0:T(8,128)S(1)}, bf16[512,2048]{1,0:T(8,128)(2,1)S(1)}, bf16[512,2048]{1,0:T(8,128)(2,1)S(1)}) custom-call(s32[3]{0:T(128)S(1)} %copy-done.14, bf16[128,2048]{1,0:T(8,128)(2,1)S(1)} %copy-done.9, bf16[128,2048]{1,0:T(8,128)(2,1)} %collective-permute-done.1.refs_1_, bf16[128,2048]{1,0:T(8,128)(2,1)} %collective-permute-done.2.refs_2_, ...), custom_call_target="tpu_custom_call" | custom-call | flops 3623878656 | bytes 22282240 | tf_op jit(solution)/shard_map/pallas_call | solution.py:23
  97.5 1.4 shard_map.97
  98.9 3.6 %collective-permute-start.17 = (bf16[256,2304]{1,0:T(8,128)(2,1)S(1)}, bf16[256,2304]{1,0:T(8,128)(2,1)S(1)}, u32[]{:S(2)}, u32[]{:S(2)}) collective-permute-start(bf16[256,2304]{1,0:T(8,128)(2,1)S(1)} %get-tuple-element.78), channel_id=1, source_target_pairs={{0,4},{4,0},{8,12},{12,8},{16,20},{20,16},{24,28},{28,24},{1,5},{5... | collective-permute-start | bytes 3538952 | tf_op jit(solution)/shard_map/ppermute | solution.py:44
  102.5 2.5 %collective-permute-done.17.refs_3_ = bf16[256,2304]{1,0:T(8,128)(2,1)S(1)} collective-permute-done((bf16[256,2304]{1,0:T(8,128)(2,1)S(1)}, bf16[256,2304]{1,0:T(8,128)(2,1)S(1)}, u32[]{:S(2)}, u32[]{:S(2)}) %collective-permute-start.17) | collective-permute-done | bytes 1179680 | tf_op jit(solution)/shard_map/ppermute | solution.py:44
  105.0 4.0 %shard_map.98.own = bf16[256,1280]{1,0:T(8,128)(2,1)S(1)} custom-call(s32[3]{0:T(128)S(1)} %copy-done.14, s32[1,4]{1,0:T(1,128)S(1)} %copy-done.15, f32[256,2304]{1,0:T(8,128)S(1)} %get-tuple-element.77.refs_2_, bf16[256,2304]{1,0:T(8,128)(2,1)S(1)} %collective-permute-done.17.refs_3_), custom_call_target="tpu_custom_call" | custom-call | flops 671088640 | bytes 4194304 | tf_op jit(solution)/shard_map/pallas_call | solution.py:23
  109.5 1.7 %collective-permute-done.18.other = bf16[256,1280]{1,0:T(8,128)(2,1)S(1)} collective-permute-done((bf16[256,1280]{1,0:T(8,128)(2,1)S(1)}, bf16[256,1280]{1,0:T(8,128)(2,1)S(1)}, u32[]{:S(2)}, u32[]{:S(2)}) %collective-permute-start.18) | collective-permute-done | bytes 655392 | tf_op jit(solution)/shard_map/ppermute | solution.py:44
  112.7 4.3 %shard_map.99 = (bf16[128,2048]{1,0:T(8,128)(2,1)S(1)}, bf16[128,2048]{1,0:T(8,128)(2,1)S(1)}, bf16[128,2048]{1,0:T(8,128)(2,1)S(1)}, bf16[128,2048]{1,0:T(8,128)(2,1)S(1)}) custom-call(bf16[256,1280]{1,0:T(8,128)(2,1)S(1)} %shard_map.98.own, bf16[256,1280]{1,0:T(8,128)(2,1)S(1)} %collective-permute-done.18.other, ...), custom_call_target="tpu_custom_call" | custom-call | flops 2684354560 | bytes 8650752 | tf_op jit(solution)/shard_map/pallas_call | solution.py:374
  117.0 1.3 collective-permute-start.19
  119.3 2.3 %shard_map.100 = (bf16[512,1280]{1,0:T(8,128)(2,1)S(1)}, bf16[512,1280]{1,0:T(8,128)(2,1)S(1)}, bf16[512,1280]{1,0:T(8,128)(2,1)S(1)}) custom-call(bf16[512,2048]{1,0:T(8,128)(2,1)S(1)} %get-tuple-element.74.normed.pair, bf16[256,1280]{1,0:T(8,128)(2,1)S(1)} %shard_map.98.own, bf16[256,1280]{1,0:T(8,128)(2,1)S(1)} %collective-permute-done.18.other), custom_call_target="tpu_custom_call" | custom-call | flops 2013265920 | bytes 7340032 | tf_op jit(solution)/shard_map/pallas_call | solution.py:23
  121.5 6.6 %collective-permute-done.24 = bf16[256,1280]{1,0:T(8,128)(2,1)S(1)} collective-permute-done((bf16[256,1280]{1,0:T(8,128)(2,1)S(1)}, bf16[256,1280]{1,0:T(8,128)(2,1)S(1)}, u32[]{:S(2)}, u32[]{:S(2)}) %collective-permute-start.24) | collective-permute-done | bytes 655392 | tf_op jit(solution)/shard_map/ppermute | solution.py:44
  130.3 1.9 %collective-permute-start.21 = (bf16[128,2048]{1,0:T(8,128)(2,1)S(1)}, bf16[128,2048]{1,0:T(8,128)(2,1)S(1)}, u32[]{:S(2)}, u32[]{:S(2)}) collective-permute-start(bf16[128,2048]{1,0:T(8,128)(2,1)S(1)} %get-tuple-element.84), channel_id=1, source_target_pairs={{0,1},{1,0},{2,3},{3,2},{4,5},{5,4},{6,7},{7,6},{8,9},{9,8},{10,11... | collective-permute-start | bytes 1572872 | tf_op jit(solution)/shard_map/ppermute | solution.py:44
  132.3 20.3 %collective-permute-done.21.refs_1_ = bf16[128,2048]{1,0:T(8,128)(2,1)S(1)} collective-permute-done((bf16[128,2048]{1,0:T(8,128)(2,1)S(1)}, bf16[128,2048]{1,0:T(8,128)(2,1)S(1)}, u32[]{:S(2)}, u32[]{:S(2)}) %collective-permute-start.21) | collective-permute-done | bytes 524320 | tf_op jit(solution)/shard_map/ppermute | solution.py:44
  152.9 5.9 %collective-permute-start.23 = (bf16[64,2048]{1,0:T(8,128)(2,1)S(1)}, bf16[64,2048]{1,0:T(8,128)(2,1)S(1)}, u32[]{:S(2)}, u32[]{:S(2)}) collective-permute-start(bf16[64,2048]{1,0:T(8,128)(2,1)S(1)} %add_convert_fusion), channel_id=1, source_target_pairs={{0,4},{4,0},{8,12},{12,8},{16,20},{20,16},{24,28},{28,24},{1,5},{5... | collective-permute-start | bytes 786440 | tf_op jit(solution)/shard_map/ppermute | solution.py:44
  158.9 2.1 %shard_map.102 = (f32[512,1024]{1,0:T(8,128)}, f32[512,256]{1,0:T(8,128)}) custom-call(bf16[512,1280]{1,0:T(8,128)(2,1)S(1)} %get-tuple-element.87.refs_0_, bf16[512,1280]{1,0:T(8,128)(2,1)S(1)} %collective-permute-done.25.refs_1_, bf16[512,1280]{1,0:T(8,128)(2,1)S(1)} %collective-permute-done.27.refs_2_), custom_call_target="tpu_custom_call" | custom-call | bytes 6553600 | tf_op jit(solution)/shard_map/pallas_call | solution.py:405
  161.0 2.2 %shard_map.103 = bf16[64,4096]{1,0:T(8,128)(2,1)} custom-call(s32[3]{0:T(128)S(1)} %copy-done.14, bf16[64,4096]{1,0:T(8,128)(2,1)S(1)} %copy-done.1, bf16[1,4096]{1,0:T(2,128)(2,1)S(1)} %reshape.9.gain, bf16[64,4096]{1,0:T(8,128)(2,1)S(1)} %copy-done.3, bf16[64,2048]{1,0:T(8,128)(2,1)S(1)} %collective-permute-done.23.handed, ...), custom_call_target="tpu_custom_call" | custom-call | bytes 3940352 | tf_op jit(solution)/shard_map/pallas_call | solution.py:23
  (83 shorter events, 22.5 us)
Async XLA Ops:
  4.5 6.4 %collective-permute-start = (bf16[128,2048]{1,0:T(8,128)(2,1)S(1)}, bf16[128,2048]{1,0:T(8,128)(2,1)S(1)}, u32[]{:S(2)}, u32[]{:S(2)}) collective-permute-start(bf16[128,2048]{1,0:T(8,128)(2,1)S(1)} %get-tuple-element.51), channel_id=1, source_target_pairs={{0,4},{4,0},{8,12},{12,8},{16,20},{20,16},{24,28},{28,24},{1,5},{5... | collective-permute-start | bytes 1572872 | tf_op jit(solution)/shard_map/ppermute | solution.py:44
  7.1 28.9 %collective-permute-start.12 = (bf16[256,2304]{1,0:T(8,128)(2,1)S(1)}, bf16[256,2304]{1,0:T(8,128)(2,1)S(1)}, u32[]{:S(2)}, u32[]{:S(2)}) collective-permute-start(bf16[256,2304]{1,0:T(8,128)(2,1)S(1)} %get-tuple-element.68.refs_13_.refs_1_), channel_id=1, source_target_pairs={{0,16},{4,20},{8,24},{12,28},{16,0},{20,4},{24,8},{28,12},{1,17},{... | collective-permute-start | bytes 3538952 | tf_op jit(solution)/shard_map/ppermute | solution.py:44
  9.7 27.5 %collective-permute-start.11 = (bf16[256,2304]{1,0:T(8,128)(2,1)S(1)}, bf16[256,2304]{1,0:T(8,128)(2,1)S(1)}, u32[]{:S(2)}, u32[]{:S(2)}) collective-permute-start(bf16[256,2304]{1,0:T(8,128)(2,1)S(1)} %get-tuple-element.70.refs_12_.refs_0_), channel_id=1, source_target_pairs={{0,8},{4,12},{8,0},{12,4},{16,24},{20,28},{24,16},{28,20},{1,9},{5... | collective-permute-start | bytes 3538952 | tf_op jit(solution)/shard_map/ppermute | solution.py:44
  11.0 13.7 %collective-permute-start.1 = (bf16[128,2048]{1,0:T(8,128)(2,1)S(1)}, bf16[128,2048]{1,0:T(8,128)(2,1)}, u32[]{:S(2)}, u32[]{:S(2)}) collective-permute-start(bf16[128,2048]{1,0:T(8,128)(2,1)S(1)} %pad_maximum_fusion.2.refs_0_), channel_id=1, source_target_pairs={{0,1},{1,2},{2,3},{4,5},{5,6},{6,7},{8,9},{9,10},{10,11},{12,13},{... | collective-permute-start | bytes 1572872 | tf_op jit(solution)/shard_map/ppermute | solution.py:74
  15.0 14.4 %collective-permute-start.2 = (bf16[128,2048]{1,0:T(8,128)(2,1)S(1)}, bf16[128,2048]{1,0:T(8,128)(2,1)}, u32[]{:S(2)}, u32[]{:S(2)}) collective-permute-start(bf16[128,2048]{1,0:T(8,128)(2,1)S(1)} %pad_maximum_fusion.2.refs_0_), channel_id=1, source_target_pairs={{1,0},{2,1},{3,2},{5,4},{6,5},{7,6},{9,8},{10,9},{11,10},{13,12},{... | collective-permute-start | bytes 1572872 | tf_op jit(solution)/shard_map/ppermute | solution.py:74
  16.3 23.1 %collective-permute-start.6 = (bf16[128,2048]{1,0:T(8,128)(2,1)S(1)}, bf16[128,2048]{1,0:T(8,128)(2,1)S(1)}, u32[]{:S(2)}, u32[]{:S(2)}) collective-permute-start(bf16[128,2048]{1,0:T(8,128)(2,1)S(1)} %pad_maximum_fusion.3.refs_6_), channel_id=1, source_target_pairs={{0,1},{1,2},{2,3},{4,5},{5,6},{6,7},{8,9},{9,10},{10,11},{12,13},{... | collective-permute-start | bytes 1572872 | tf_op jit(solution)/shard_map/ppermute | solution.py:74
  24.7 15.0 %collective-permute-start.7 = (bf16[128,2048]{1,0:T(8,128)(2,1)S(1)}, bf16[128,2048]{1,0:T(8,128)(2,1)}, u32[]{:S(2)}, u32[]{:S(2)}) collective-permute-start(bf16[128,2048]{1,0:T(8,128)(2,1)S(1)} %pad_maximum_fusion.3.refs_6_), channel_id=1, source_target_pairs={{1,0},{2,1},{3,2},{5,4},{6,5},{7,6},{9,8},{10,9},{11,10},{13,12},{... | collective-permute-start | bytes 1572872 | tf_op jit(solution)/shard_map/ppermute | solution.py:74
  36.0 32.3 %collective-permute-start.14 = (bf16[256,2304]{1,0:T(8,128)(2,1)S(1)}, bf16[256,2304]{1,0:T(8,128)(2,1)}, u32[]{:S(2)}, u32[]{:S(2)}) collective-permute-start(bf16[256,2304]{1,0:T(8,128)(2,1)S(1)} %get-tuple-element.70.refs_12_.refs_0_), channel_id=1, source_target_pairs={{0,16},{4,20},{8,24},{12,28},{16,0},{20,4},{24,8},{28,12},{1,17},{... | collective-permute-start | bytes 3538952 | tf_op jit(solution)/shard_map/ppermute | solution.py:44
  38.2 30.1 %collective-permute-start.13 = (bf16[256,2304]{1,0:T(8,128)(2,1)S(1)}, bf16[256,2304]{1,0:T(8,128)(2,1)}, u32[]{:S(2)}, u32[]{:S(2)}) collective-permute-start(bf16[256,2304]{1,0:T(8,128)(2,1)S(1)} %get-tuple-element.68.refs_13_.refs_1_), channel_id=1, source_target_pairs={{0,8},{4,12},{8,0},{12,4},{16,24},{20,28},{24,16},{28,20},{1,9},{5... | collective-permute-start | bytes 3538952 | tf_op jit(solution)/shard_map/ppermute | solution.py:44
  39.7 5.0 %collective-permute-start.8 = (bf16[128,2048]{1,0:T(8,128)(2,1)S(1)}, bf16[128,2048]{1,0:T(8,128)(2,1)}, u32[]{:S(2)}, u32[]{:S(2)}) collective-permute-start(bf16[128,2048]{1,0:T(8,128)(2,1)S(1)} %collective-permute-done.6.refs_7_), channel_id=1, source_target_pairs={{1,2},{2,3},{5,6},{6,7},{9,10},{10,11},{13,14},{14,15},{17,18},{18... | collective-permute-start | bytes 1572872 | tf_op jit(solution)/shard_map/ppermute | solution.py:74
  42.0 15.1 %collective-permute-start.9 = (bf16[128,2048]{1,0:T(8,128)(2,1)}, bf16[128,2048]{1,0:T(8,128)(2,1)}, u32[]{:S(2)}, u32[]{:S(2)}) collective-permute-start(bf16[128,2048]{1,0:T(8,128)(2,1)} %collective-permute-done.7.refs_8_), channel_id=1, source_target_pairs={{1,0},{2,1},{5,4},{6,5},{9,8},{10,9},{13,12},{14,13},{17,16},{18,1... | collective-permute-start | bytes 1572872 | tf_op jit(solution)/shard_map/ppermute | solution.py:74
  43.2 16.2 %collective-permute-start.3 = (bf16[128,2048]{1,0:T(8,128)(2,1)}, bf16[128,2048]{1,0:T(8,128)(2,1)}, u32[]{:S(2)}, u32[]{:S(2)}) collective-permute-start(bf16[128,2048]{1,0:T(8,128)(2,1)} %collective-permute-done.1.refs_1_), channel_id=1, source_target_pairs={{1,2},{2,3},{5,6},{6,7},{9,10},{10,11},{13,14},{14,15},{17,18},{18... | collective-permute-start | bytes 1572872 | tf_op jit(solution)/shard_map/ppermute | solution.py:74
  44.7 23.6 %collective-permute-start.4 = (bf16[128,2048]{1,0:T(8,128)(2,1)}, bf16[128,2048]{1,0:T(8,128)(2,1)}, u32[]{:S(2)}, u32[]{:S(2)}) collective-permute-start(bf16[128,2048]{1,0:T(8,128)(2,1)} %collective-permute-done.2.refs_2_), channel_id=1, source_target_pairs={{1,0},{2,1},{5,4},{6,5},{9,8},{10,9},{13,12},{14,13},{17,16},{18,1... | collective-permute-start | bytes 1572872 | tf_op jit(solution)/shard_map/ppermute | solution.py:74
  46.0 44.6 %copy-start.9 = (bf16[128,2048]{1,0:T(8,128)(2,1)S(1)}, bf16[128,2048]{1,0:T(8,128)(2,1)}, u32[]{:S(2)}) copy-start(bf16[128,2048]{1,0:T(8,128)(2,1)} %copy-done.8) | copy-start | bytes 1572868
  46.0 44.6 %copy-start.11 = (bf16[128,2048]{1,0:T(8,128)(2,1)S(1)}, bf16[128,2048]{1,0:T(8,128)(2,1)}, u32[]{:S(2)}) copy-start(bf16[128,2048]{1,0:T(8,128)(2,1)} %copy-done.10) | copy-start | bytes 1572868
  46.1 44.6 %copy-start.14 = (s32[3]{0:T(128)S(1)}, s32[3]{0:T(128)}, u32[]{:S(2)}) copy-start(s32[3]{0:T(128)} %copy-done.13) | copy-start | bytes 40
  46.1 44.6 %copy-start.17 = (bf16[128,2048]{1,0:T(8,128)(2,1)S(1)}, bf16[128,2048]{1,0:T(8,128)(2,1)}, u32[]{:S(2)}) copy-start(bf16[128,2048]{1,0:T(8,128)(2,1)} %copy-done.16) | copy-start | bytes 1572868
  58.2 21.3 %collective-permute-start.10 = (bf16[128,2048]{1,0:T(8,128)(2,1)S(1)}, bf16[128,2048]{1,0:T(8,128)(2,1)S(1)}, u32[]{:S(2)}, u32[]{:S(2)}) collective-permute-start(bf16[128,2048]{1,0:T(8,128)(2,1)S(1)} %broadcast_select_fusion), channel_id=1, source_target_pairs={{1,0},{2,3},{5,4},{6,7},{9,8},{10,11},{13,12},{14,15},{17,16},{18,... | collective-permute-start | bytes 1572872 | tf_op jit(solution)/shard_map/ppermute | solution.py:74
  68.3 29.1 %collective-permute-start.15 = (bf16[256,2304]{1,0:T(8,128)(2,1)S(1)}, bf16[256,2304]{1,0:T(8,128)(2,1)S(1)}, u32[]{:S(2)}, u32[]{:S(2)}) collective-permute-start(bf16[256,2304]{1,0:T(8,128)(2,1)S(1)} %copy-done.5), channel_id=1, source_target_pairs={{0,16},{4,20},{8,24},{12,28},{16,0},{20,4},{24,8},{28,12},{1,17},{... | collective-permute-start | bytes 3538952 | tf_op jit(solution)/shard_map/ppermute | solution.py:44
  68.6 28.9 %collective-permute-start.16 = (bf16[256,2304]{1,0:T(8,128)(2,1)S(1)}, bf16[256,2304]{1,0:T(8,128)(2,1)S(1)}, u32[]{:S(2)}, u32[]{:S(2)}) collective-permute-start(bf16[256,2304]{1,0:T(8,128)(2,1)S(1)} %collective-permute-done.12.refs_17_.refs_5_), channel_id=1, source_target_pairs={{0,8},{4,12},{8,0},{12,4},{16,24},{20,28},{24,16},{28,20},{1,9},{5... | collective-permute-start | bytes 3538952 | tf_op jit(solution)/shard_map/ppermute | solution.py:44
  70.0 20.7 %collective-permute-start.5 = (bf16[128,2048]{1,0:T(8,128)(2,1)S(1)}, bf16[128,2048]{1,0:T(8,128)(2,1)S(1)}, u32[]{:S(2)}, u32[]{:S(2)}) collective-permute-start(bf16[128,2048]{1,0:T(8,128)(2,1)S(1)} %broadcast_select_fusion.1), channel_id=1, source_target_pairs={{1,0},{2,3},{5,4},{6,7},{9,8},{10,11},{13,12},{14,15},{17,16},{18,... | collective-permute-start | bytes 1572872 | tf_op jit(solution)/shard_map/ppermute | solution.py:74
  98.9 6.1 %collective-permute-start.17 = (bf16[256,2304]{1,0:T(8,128)(2,1)S(1)}, bf16[256,2304]{1,0:T(8,128)(2,1)S(1)}, u32[]{:S(2)}, u32[]{:S(2)}) collective-permute-start(bf16[256,2304]{1,0:T(8,128)(2,1)S(1)} %get-tuple-element.78), channel_id=1, source_target_pairs={{0,4},{4,0},{8,12},{12,8},{16,20},{20,16},{24,28},{28,24},{1,5},{5... | collective-permute-start | bytes 3538952 | tf_op jit(solution)/shard_map/ppermute | solution.py:44
  109.0 2.2 %collective-permute-start.18 = (bf16[256,1280]{1,0:T(8,128)(2,1)S(1)}, bf16[256,1280]{1,0:T(8,128)(2,1)S(1)}, u32[]{:S(2)}, u32[]{:S(2)}) collective-permute-start(bf16[256,1280]{1,0:T(8,128)(2,1)S(1)} %shard_map.98.own), channel_id=1, source_target_pairs={{0,4},{4,0},{8,12},{12,8},{16,20},{20,16},{24,28},{28,24},{1,5},{5... | collective-permute-start | bytes 1966088 | tf_op jit(solution)/shard_map/ppermute | solution.py:44
  112.2 16.0 %collective-permute-start.24 = (bf16[256,1280]{1,0:T(8,128)(2,1)S(1)}, bf16[256,1280]{1,0:T(8,128)(2,1)S(1)}, u32[]{:S(2)}, u32[]{:S(2)}) collective-permute-start(bf16[256,1280]{1,0:T(8,128)(2,1)S(1)} %get-tuple-element.98), channel_id=1, source_target_pairs={{0,16},{4,20},{8,24},{12,28},{16,0},{20,4},{24,8},{28,12},{1,17},{... | collective-permute-start | bytes 1966088 | tf_op jit(solution)/shard_map/ppermute | solution.py:44
  112.4 15.7 %collective-permute-start.26 = (bf16[256,1280]{1,0:T(8,128)(2,1)S(1)}, bf16[256,1280]{1,0:T(8,128)(2,1)S(1)}, u32[]{:S(2)}, u32[]{:S(2)}) collective-permute-start(bf16[256,1280]{1,0:T(8,128)(2,1)S(1)} %get-tuple-element.97), channel_id=1, source_target_pairs={{0,8},{4,12},{8,0},{12,4},{16,24},{20,28},{24,16},{28,20},{1,9},{5... | collective-permute-start | bytes 1966088 | tf_op jit(solution)/shard_map/ppermute | solution.py:44
  117.0 13.1 %collective-permute-start.19 = (bf16[128,2048]{1,0:T(8,128)(2,1)S(1)}, bf16[128,2048]{1,0:T(8,128)(2,1)S(1)}, u32[]{:S(2)}, u32[]{:S(2)}) collective-permute-start(bf16[128,2048]{1,0:T(8,128)(2,1)S(1)} %get-tuple-element.81), channel_id=1, source_target_pairs={{3,2},{0,1},{7,6},{4,5},{11,10},{8,9},{15,14},{12,13},{19,18},{16,... | collective-permute-start | bytes 1572872 | tf_op jit(solution)/shard_map/ppermute | solution.py:74
  118.3 11.8 %collective-permute-start.20 = (bf16[128,2048]{1,0:T(8,128)(2,1)S(1)}, bf16[128,2048]{1,0:T(8,128)(2,1)S(1)}, u32[]{:S(2)}, u32[]{:S(2)}) collective-permute-start(bf16[128,2048]{1,0:T(8,128)(2,1)S(1)} %get-tuple-element.81), channel_id=1, source_target_pairs={{1,2},{2,1},{5,6},{6,5},{9,10},{10,9},{13,14},{14,13},{17,18},{18,... | collective-permute-start | bytes 1572872 | tf_op jit(solution)/shard_map/ppermute | solution.py:74
  128.5 30.4 %collective-permute-start.27 = (bf16[512,1280]{1,0:T(8,128)(2,1)S(1)}, bf16[512,1280]{1,0:T(8,128)(2,1)S(1)}, u32[]{:S(2)}, u32[]{:S(2)}) collective-permute-start(bf16[512,1280]{1,0:T(8,128)(2,1)S(1)} %pad_maximum_fusion.1), channel_id=1, source_target_pairs={{0,16},{4,20},{8,24},{12,28},{16,0},{20,4},{24,8},{28,12},{1,17},{... | collective-permute-start | bytes 3932168 | tf_op jit(solution)/shard_map/ppermute | solution.py:44
  129.8 29.1 %collective-permute-start.25 = (bf16[512,1280]{1,0:T(8,128)(2,1)S(1)}, bf16[512,1280]{1,0:T(8,128)(2,1)S(1)}, u32[]{:S(2)}, u32[]{:S(2)}) collective-permute-start(bf16[512,1280]{1,0:T(8,128)(2,1)S(1)} %pad_maximum_fusion), channel_id=1, source_target_pairs={{0,8},{4,12},{8,0},{12,4},{16,24},{20,28},{24,16},{28,20},{1,9},{5... | collective-permute-start | bytes 3932168 | tf_op jit(solution)/shard_map/ppermute | solution.py:44
  130.3 22.3 %collective-permute-start.21 = (bf16[128,2048]{1,0:T(8,128)(2,1)S(1)}, bf16[128,2048]{1,0:T(8,128)(2,1)S(1)}, u32[]{:S(2)}, u32[]{:S(2)}) collective-permute-start(bf16[128,2048]{1,0:T(8,128)(2,1)S(1)} %get-tuple-element.84), channel_id=1, source_target_pairs={{0,1},{1,0},{2,3},{3,2},{4,5},{5,4},{6,7},{7,6},{8,9},{9,8},{10,11... | collective-permute-start | bytes 1572872 | tf_op jit(solution)/shard_map/ppermute | solution.py:44
  132.2 20.7 %collective-permute-start.22 = (bf16[128,2048]{1,0:T(8,128)(2,1)S(1)}, bf16[128,2048]{1,0:T(8,128)(2,1)S(1)}, u32[]{:S(2)}, u32[]{:S(2)}) collective-permute-start(bf16[128,2048]{1,0:T(8,128)(2,1)S(1)} %add.18), channel_id=1, source_target_pairs={{0,2},{1,3},{2,0},{3,1},{4,6},{5,7},{6,4},{7,5},{8,10},{9,11},{10,... | collective-permute-start | bytes 1572872 | tf_op jit(solution)/shard_map/ppermute | solution.py:44
  152.9 8.1 %collective-permute-start.23 = (bf16[64,2048]{1,0:T(8,128)(2,1)S(1)}, bf16[64,2048]{1,0:T(8,128)(2,1)S(1)}, u32[]{:S(2)}, u32[]{:S(2)}) collective-permute-start(bf16[64,2048]{1,0:T(8,128)(2,1)S(1)} %add_convert_fusion), channel_id=1, source_target_pairs={{0,4},{4,0},{8,12},{12,8},{16,20},{20,16},{24,28},{28,24},{1,5},{5... | collective-permute-start | bytes 786440 | tf_op jit(solution)/shard_map/ppermute | solution.py:44
  (14 other events, 71.5 us)

commit v11 on v9

--- a/solution.py
+++ b/solution.py
@@ -135,18 +135,8 @@
     return pl.multiple_of(((place[0] ^ k) * 2 + which) * block, 128)
 
 
-def prepare_kernel(
-    block, place, gain, grad_far, tokens_far, grad_keep, normed_keep, send, normed, grad_out, tokens, arrived
-):
+def prepare_kernel(block, place, grad_out, tokens, gain, grad_keep, normed_keep, send, normed):
     rows, core = tokens.shape[0], place[1]
-    copies = [
-        pltpu.make_async_copy(tokens_far, tokens, arrived.at[0]),
-        pltpu.make_async_copy(grad_far, grad_out, arrived.at[1]),
-    ]
-    for copy in copies:
-        copy.start()
-    for copy in copies:
-        copy.wait()
     values = tokens[...].astype(jnp.float32)
     root_mean = jnp.sqrt(jnp.mean(values * values, axis=-1, keepdims=True) + epsilon)
     normed[...] = (values / root_mean * gain[...].astype(jnp.float32)).astype(jnp.bfloat16)
@@ -159,36 +149,13 @@
             ]
 
 
-def merge_kernel(count, query_weight, kv_weight, out_weight, merged, arrived):
-    block, start, parts = merged.shape[0], 0, [query_weight, kv_weight]
-    parts += [out_weight.at[k * block : (k + 1) * block] for k in range(count)]
-    copies = []
-    for number, part in enumerate(parts):
-        width = part.shape[1]
-        target = merged.at[:, start : start + width]
-        copies.append(pltpu.make_async_copy(part, target, arrived.at[number]))
-        copies[-1].start()
-        start += width
-    for copy in copies:
-        copy.wait()
-
-
-def merge(query_weight, kv_weight, out_weight):
-    block = query_weight.shape[0]
-    count = out_weight.shape[0] // block
-    width = query_weight.shape[1] + kv_weight.shape[1] + out_weight.shape[0]
-    if kv_weight.shape[1] % 128:
-        chunks = jnp.split(out_weight, count, axis=0)
-        return jnp.concatenate([query_weight, kv_weight, *chunks], axis=1)
-    return pl.pallas_call(
-        functools.partial(merge_kernel, count),
-        out_shape=shaped((block, width)),
-        in_specs=[pl.BlockSpec(memory_space=pltpu.HBM)] * 3,
-        out_specs=WHOLE,
-        scratch_shapes=[pltpu.SemaphoreType.DMA((2 + count,))],
-        compiler_params=pltpu.CompilerParams(vmem_limit_bytes=58 * 2**20),
-        cost_estimate=pl.CostEstimate(flops=0, bytes_accessed=4 * block * width, transcendentals=0),
-    )(query_weight, kv_weight, out_weight)
+def merge_kernel(query_weight, kv_weight, out_weight, merged):
+    block, start = merged.shape[0], 0
+    parts = [query_weight, kv_weight]
+    parts += [out_weight.at[k : k + block] for k in range(0, out_weight.shape[0], block)]
+    for part in parts:
+        merged[:, start : start + part.shape[1]] = part[...]
+        start += part.shape[1]
 
 
 def products(grads, normed, weights, first, joint_width, block, columns):
@@ -479,22 +446,21 @@
     query_width = query_weight.shape[1]
     gain = norm_gain.reshape(1, width)
 
-    merged = merge(query_weight, kv_weight, out_weight)
-    merged, early_tokens, early_grads = tied(merged, tokens, grad_out)
-    row_block = pltpu.VMEM((rows, width), jnp.bfloat16)
-    grad_keep, normed_keep, send = pl.pallas_call(
+    grad_keep, normed_keep, send = call(
         functools.partial(prepare_kernel, block),
-        out_shape=[shaped((rows, width // 2))] * 2 + [shaped((2 * rows, width // 2))],
-        in_specs=[SCALARS, WHOLE] + [pl.BlockSpec(memory_space=pltpu.HBM)] * 2,
-        out_specs=[WHOLE] * 3,
-        scratch_shapes=[row_block] * 3 + [pltpu.SemaphoreType.DMA((2,))],
-        compiler_params=pltpu.CompilerParams(vmem_limit_bytes=56 * 2**20),
-        cost_estimate=pl.CostEstimate(
-            flops=0, bytes_accessed=8 * rows * width, transcendentals=0
-        ),
-    )(place, gain, early_grads, early_tokens)
+        [shaped((rows, width // 2))] * 2 + [shaped((2 * rows, width // 2))],
+        [grad_out, tokens, gain],
+        [place],
+        [pltpu.VMEM((rows, width), jnp.bfloat16)],
+    )
     joint_width = query_width + kv_weight.shape[1]
+    send, out_weight, query_weight, kv_weight = tied(send, out_weight, query_weight, kv_weight)
     sent = swap(send, "dp", 1)
+    (merged,) = call(
+        merge_kernel,
+        [shaped((block, joint_width + out_weight.shape[0]))],
+        [query_weight, kv_weight, out_weight],
+    )
     early, late = gather_chips(merged)
     row_pieces = gather_tensor(jnp.concatenate([grad_keep, sent[:rows]], axis=0))
     row_pieces += gather_tensor(jnp.concatenate([normed_keep, sent[rows:]], axis=0))

time: 162 us -> 160 us (0.988)
  local copies, waits for them, and re-layouts: 3.14 us -> 8.76 us
  Pallas kernels: 30.4 us -> 26.2 us
  starting transfers between devices: 45.7 us -> 43.8 us
    pallas_call x2 -> x0, Pallas kernels: 6.27 us -> none  [the longest x1 3.19 us: local(): pl.pallas_call(functools.partial(prepare_kernel, block), out_shape=[shape...]
    unnamed x20, local copies, waits for them, and re-layouts: 0.84 us -> 5.24 us
    ppermute x14, starting transfers between devices: 23.3 us -> 20.8 us  [swap(): return lax.ppermute(value, axis, pairs)]
    pallas_call x6 -> x8, Pallas kernels: 17.6 us -> 19.4 us  [call(): pl.pallas_call(kernel, out_shape=outs, in_specs=[SCALARS] * len(scalars)...]
  transfers between devices with their start and end apart: 26 -> 26, of which waited for: 15 -> 14; matrix products, arithmetic and copies ran while one was open for 3% -> 4% of each run, Pallas kernels for 10% -> 10%
where the time goes in v11:
time: 160 us; the launch traced here: 159 us
  waiting for transfers between devices  76.6 us (48%)
  starting transfers between devices  43.8 us (27%)
  Pallas kernels  26.2 us (16%)
  local copies, waits for them, and re-layouts  8.76 us (5%)
  other arithmetic  3 us (2%)
    ppermute x12, waiting for transfers between devices, along(): return lax.ppermute(value, 'tensor', pairs)  47.5 us
    ppermute x14, waiting for transfers between devices, swap(): return lax.ppermute(value, axis, pairs)  29 us
    ppermute x12, starting transfers between devices, along(): return lax.ppermute(value, 'tensor', pairs)  23 us
    ppermute x14, starting transfers between devices, swap(): return lax.ppermute(value, axis, pairs)  20.8 us
    pallas_call x8, Pallas kernels, call(): pl.pallas_call(kernel, out_shape=outs, in_specs=[SCALARS] * len(scalars)...  19.4 us
    unnamed x20, local copies, waits for them, and re-layouts  5.24 us
    pallas_call x1, Pallas kernels, row_terms(): pl.pallas_call(functools.partial(row_kernel, len(weights)), grid=(1,), ou...  4.69 us
  transfers between devices with their start and end apart: 26, of which 14 were waited for; matrix products, arithmetic and copies ran while one was open for 4% of the time, Pallas kernels for 10%

profile of v11, /device:TPU:1, one launch (start us, length us, event | category | flops | bytes accessed | tf_op | source)
XLA Modules:
  0.0 159.3 jit_solution(3321141644276618729)
XLA Ops:
  7.1 2.6 %collective-permute-start.11 = (bf16[512,2304]{1,0:T(8,128)(2,1)S(1)}, bf16[512,2304]{1,0:T(8,128)(2,1)}, u32[]{:S(2)}, u32[]{:S(2)}) collective-permute-start(bf16[512,2304]{1,0:T(8,128)(2,1)S(1)} %shard_map.95.refs_12_.refs_0_), channel_id=1, source_target_pairs={{0,8},{4,12},{8,0},{12,4},{16,24},{20,28},{24,16},{28,20},{1,9},{5... | collective-permute-start | bytes 7077896 | tf_op jit(solution)/shard_map/ppermute | solution.py:44
  11.0 3.2 %collective-permute-start.6 = (bf16[128,2048]{1,0:T(8,128)(2,1)S(1)}, bf16[128,2048]{1,0:T(8,128)(2,1)S(1)}, u32[]{:S(2)}, u32[]{:S(2)}) collective-permute-start(bf16[128,2048]{1,0:T(8,128)(2,1)S(1)} %pad_maximum_fusion.3.refs_6_), channel_id=1, source_target_pairs={{0,1},{1,2},{2,3},{4,5},{5,6},{6,7},{8,9},{9,10},{10,11},{12,13},{... | collective-permute-start | bytes 1572872 | tf_op jit(solution)/shard_map/ppermute | solution.py:69
  14.2 1.3 collective-permute-start.7
  15.6 4.8 %collective-permute-start.1 = (bf16[128,2048]{1,0:T(8,128)(2,1)S(1)}, bf16[128,2048]{1,0:T(8,128)(2,1)}, u32[]{:S(2)}, u32[]{:S(2)}) collective-permute-start(bf16[128,2048]{1,0:T(8,128)(2,1)S(1)} %pad_maximum_fusion.2.refs_0_), channel_id=1, source_target_pairs={{0,1},{1,2},{2,3},{4,5},{5,6},{6,7},{8,9},{9,10},{10,11},{12,13},{... | collective-permute-start | bytes 1572872 | tf_op jit(solution)/shard_map/ppermute | solution.py:69
  20.4 4.2 %collective-permute-done.6.refs_7_ = bf16[128,2048]{1,0:T(8,128)(2,1)S(1)} collective-permute-done((bf16[128,2048]{1,0:T(8,128)(2,1)S(1)}, bf16[128,2048]{1,0:T(8,128)(2,1)S(1)}, u32[]{:S(2)}, u32[]{:S(2)}) %collective-permute-start.6) | collective-permute-done | bytes 524320 | tf_op jit(solution)/shard_map/ppermute | solution.py:69
  25.9 2.6 %collective-permute-done.7.refs_8_ = bf16[128,2048]{1,0:T(8,128)(2,1)} collective-permute-done((bf16[128,2048]{1,0:T(8,128)(2,1)S(1)}, bf16[128,2048]{1,0:T(8,128)(2,1)}, u32[]{:S(2)}, u32[]{:S(2)}) %collective-permute-start.7) | collective-permute-done | bytes 524320 | tf_op jit(solution)/shard_map/ppermute | solution.py:69
  28.6 1.5 collective-permute-start.8
  30.9 5.0 %collective-permute-done.1.refs_1_ = bf16[128,2048]{1,0:T(8,128)(2,1)} collective-permute-done((bf16[128,2048]{1,0:T(8,128)(2,1)S(1)}, bf16[128,2048]{1,0:T(8,128)(2,1)}, u32[]{:S(2)}, u32[]{:S(2)}) %collective-permute-start.1) | collective-permute-done | bytes 524320 | tf_op jit(solution)/shard_map/ppermute | solution.py:69
  38.4 1.5 collective-permute-start.3
  41.1 9.6 %collective-permute-done.9.refs_10_ = bf16[128,2048]{1,0:T(8,128)(2,1)} collective-permute-done((bf16[128,2048]{1,0:T(8,128)(2,1)}, bf16[128,2048]{1,0:T(8,128)(2,1)}, u32[]{:S(2)}, u32[]{:S(2)}) %collective-permute-start.9) | collective-permute-done | bytes 524320 | tf_op jit(solution)/shard_map/ppermute | solution.py:69
  53.1 8.8 %collective-permute-done.4.refs_4_ = bf16[128,2048]{1,0:T(8,128)(2,1)} collective-permute-done((bf16[128,2048]{1,0:T(8,128)(2,1)}, bf16[128,2048]{1,0:T(8,128)(2,1)}, u32[]{:S(2)}, u32[]{:S(2)}) %collective-permute-start.4) | collective-permute-done | bytes 524320 | tf_op jit(solution)/shard_map/ppermute | solution.py:69
  62.1 1.3 slice.44
  63.4 1.3 collective-permute-start.13
  64.7 1.3 slice.45
  67.6 1.5 collective-permute-start.5
  69.1 4.0 %collective-permute-done.10.refs_11_ = bf16[128,2048]{1,0:T(8,128)(2,1)S(1)} collective-permute-done((bf16[128,2048]{1,0:T(8,128)(2,1)S(1)}, bf16[128,2048]{1,0:T(8,128)(2,1)S(1)}, u32[]{:S(2)}, u32[]{:S(2)}) %collective-permute-start.10) | collective-permute-done | bytes 524320 | tf_op jit(solution)/shard_map/ppermute | solution.py:69
  73.1 11.2 %collective-permute-done.5.refs_5_ = bf16[128,2048]{1,0:T(8,128)(2,1)S(1)} collective-permute-done((bf16[128,2048]{1,0:T(8,128)(2,1)S(1)}, bf16[128,2048]{1,0:T(8,128)(2,1)S(1)}, u32[]{:S(2)}, u32[]{:S(2)}) %collective-permute-start.5) | collective-permute-done | bytes 524320 | tf_op jit(solution)/shard_map/ppermute | solution.py:69
  84.3 7.5 %shard_map.96 = (f32[512,2304]{1,0:T(8,128)S(1)}, bf16[512,2048]{1,0:T(8,128)(2,1)S(1)}, bf16[512,2048]{1,0:T(8,128)(2,1)S(1)}) custom-call(s32[3]{0:T(128)S(1)} %pad_add_fusion.place.refs_0_, bf16[128,2048]{1,0:T(8,128)(2,1)S(1)} %pad_maximum_fusion.2.refs_0_, bf16[128,2048]{1,0:T(8,128)(2,1)} %collective-permute-done.1.refs_1_, ...), custom_call_target="tpu_custom_call" | custom-call | flops 3623878656 | bytes 22282240 | tf_op jit(solution)/shard_map/pallas_call | solution.py:23
  91.9 1.4 shard_map.97
  93.3 2.7 %collective-permute-start.15 = (bf16[256,2304]{1,0:T(8,128)(2,1)S(1)}, bf16[256,2304]{1,0:T(8,128)(2,1)S(1)}, u32[]{:S(2)}, u32[]{:S(2)}) collective-permute-start(bf16[256,2304]{1,0:T(8,128)(2,1)S(1)} %get-tuple-element.62), channel_id=1, source_target_pairs={{0,4},{4,0},{8,12},{12,8},{16,20},{20,16},{24,28},{28,24},{1,5},{5... | collective-permute-start | bytes 3538952 | tf_op jit(solution)/shard_map/ppermute | solution.py:44
  96.0 2.5 %collective-permute-done.15.refs_3_ = bf16[256,2304]{1,0:T(8,128)(2,1)S(1)} collective-permute-done((bf16[256,2304]{1,0:T(8,128)(2,1)S(1)}, bf16[256,2304]{1,0:T(8,128)(2,1)S(1)}, u32[]{:S(2)}, u32[]{:S(2)}) %collective-permute-start.15) | collective-permute-done | bytes 1179680 | tf_op jit(solution)/shard_map/ppermute | solution.py:44
  98.5 4.0 %shard_map.98.own = bf16[256,1280]{1,0:T(8,128)(2,1)S(1)} custom-call(s32[3]{0:T(128)S(1)} %pad_add_fusion.place.refs_0_, s32[1,4]{1,0:T(1,128)S(1)} %copy-done.7, f32[256,2304]{1,0:T(8,128)S(1)} %get-tuple-element.61.refs_2_, bf16[256,2304]{1,0:T(8,128)(2,1)S(1)} %collective-permute-done.15.refs_3_), custom_call_target="tpu_custom_call" | custom-call | flops 671088640 | bytes 4194304 | tf_op jit(solution)/shard_map/pallas_call | solution.py:23
  103.0 1.7 %collective-permute-done.16.other = bf16[256,1280]{1,0:T(8,128)(2,1)S(1)} collective-permute-done((bf16[256,1280]{1,0:T(8,128)(2,1)S(1)}, bf16[256,1280]{1,0:T(8,128)(2,1)S(1)}, u32[]{:S(2)}, u32[]{:S(2)}) %collective-permute-start.16) | collective-permute-done | bytes 655392 | tf_op jit(solution)/shard_map/ppermute | solution.py:44
  106.4 4.7 %shard_map.99 = (bf16[128,2048]{1,0:T(8,128)(2,1)S(1)}, bf16[128,2048]{1,0:T(8,128)(2,1)S(1)}, bf16[128,2048]{1,0:T(8,128)(2,1)S(1)}, bf16[128,2048]{1,0:T(8,128)(2,1)S(1)}) custom-call(bf16[256,1280]{1,0:T(8,128)(2,1)S(1)} %shard_map.98.own, bf16[256,1280]{1,0:T(8,128)(2,1)S(1)} %collective-permute-done.16.other, ...), custom_call_target="tpu_custom_call" | custom-call | flops 2684354560 | bytes 8650752 | tf_op jit(solution)/shard_map/pallas_call | solution.py:365
  111.1 3.2 %collective-permute-start.17 = (bf16[128,2048]{1,0:T(8,128)(2,1)S(1)}, bf16[128,2048]{1,0:T(8,128)(2,1)S(1)}, u32[]{:S(2)}, u32[]{:S(2)}) collective-permute-start(bf16[128,2048]{1,0:T(8,128)(2,1)S(1)} %get-tuple-element.65), channel_id=1, source_target_pairs={{3,2},{0,1},{7,6},{4,5},{11,10},{8,9},{15,14},{12,13},{19,18},{16,... | collective-permute-start | bytes 1572872 | tf_op jit(solution)/shard_map/ppermute | solution.py:69
  115.2 2.3 %shard_map.100 = (bf16[512,1280]{1,0:T(8,128)(2,1)S(1)}, bf16[512,1280]{1,0:T(8,128)(2,1)S(1)}, bf16[512,1280]{1,0:T(8,128)(2,1)S(1)}) custom-call(bf16[512,2048]{1,0:T(8,128)(2,1)S(1)} %get-tuple-element.60.normed.pair, bf16[256,1280]{1,0:T(8,128)(2,1)S(1)} %shard_map.98.own, bf16[256,1280]{1,0:T(8,128)(2,1)S(1)} %collective-permute-done.16.other), custom_call_target="tpu_custom_call" | custom-call | flops 2013265920 | bytes 7340032 | tf_op jit(solution)/shard_map/pallas_call | solution.py:23
  117.4 4.3 %collective-permute-done.22 = bf16[256,1280]{1,0:T(8,128)(2,1)S(1)} collective-permute-done((bf16[256,1280]{1,0:T(8,128)(2,1)S(1)}, bf16[256,1280]{1,0:T(8,128)(2,1)S(1)}, u32[]{:S(2)}, u32[]{:S(2)}) %collective-permute-start.22) | collective-permute-done | bytes 655392 | tf_op jit(solution)/shard_map/ppermute | solution.py:44
  124.6 3.6 %collective-permute-start.19 = (bf16[128,2048]{1,0:T(8,128)(2,1)S(1)}, bf16[128,2048]{1,0:T(8,128)(2,1)S(1)}, u32[]{:S(2)}, u32[]{:S(2)}) collective-permute-start(bf16[128,2048]{1,0:T(8,128)(2,1)S(1)} %get-tuple-element.68), channel_id=1, source_target_pairs={{0,1},{1,0},{2,3},{3,2},{4,5},{5,4},{6,7},{7,6},{8,9},{9,8},{10,11... | collective-permute-start | bytes 1572872 | tf_op jit(solution)/shard_map/ppermute | solution.py:44
  129.2 20.4 %collective-permute-done.19.refs_1_ = bf16[128,2048]{1,0:T(8,128)(2,1)S(1)} collective-permute-done((bf16[128,2048]{1,0:T(8,128)(2,1)S(1)}, bf16[128,2048]{1,0:T(8,128)(2,1)S(1)}, u32[]{:S(2)}, u32[]{:S(2)}) %collective-permute-start.19) | collective-permute-done | bytes 524320 | tf_op jit(solution)/shard_map/ppermute | solution.py:44
  149.8 5.1 %collective-permute-start.21 = (bf16[64,2048]{1,0:T(8,128)(2,1)S(1)}, bf16[64,2048]{1,0:T(8,128)(2,1)S(1)}, u32[]{:S(2)}, u32[]{:S(2)}) collective-permute-start(bf16[64,2048]{1,0:T(8,128)(2,1)S(1)} %add_convert_fusion), channel_id=1, source_target_pairs={{0,4},{4,0},{8,12},{12,8},{16,20},{20,16},{24,28},{28,24},{1,5},{5... | collective-permute-start | bytes 786440 | tf_op jit(solution)/shard_map/ppermute | solution.py:44
  154.9 2.1 %shard_map.102 = (f32[512,1024]{1,0:T(8,128)}, f32[512,256]{1,0:T(8,128)}) custom-call(bf16[512,1280]{1,0:T(8,128)(2,1)S(1)} %get-tuple-element.71.refs_0_, bf16[512,1280]{1,0:T(8,128)(2,1)S(1)} %collective-permute-done.23.refs_1_, bf16[512,1280]{1,0:T(8,128)(2,1)S(1)} %collective-permute-done.25.refs_2_), custom_call_target="tpu_custom_call" | custom-call | bytes 6553600 | tf_op jit(solution)/shard_map/pallas_call | solution.py:396
  157.1 2.2 %shard_map.103 = bf16[64,4096]{1,0:T(8,128)(2,1)} custom-call(s32[3]{0:T(128)S(1)} %pad_add_fusion.place.refs_0_, bf16[64,4096]{1,0:T(8,128)(2,1)S(1)} %copy-done.1, bf16[1,4096]{1,0:T(2,128)(2,1)S(1)} %reshape.9.gain, bf16[64,4096]{1,0:T(8,128)(2,1)S(1)} %copy-done.3, bf16[64,2048]{1,0:T(8,128)(2,1)S(1)} %collective-permute-done.21.handed, ...), custom_call_target="tpu_custom_call" | custom-call | bytes 3940352 | tf_op jit(solution)/shard_map/pallas_call | solution.py:23
  (65 shorter events, 24.7 us)
Async XLA Ops:
  3.5 1.2 copy-start.4
  4.5 6.4 %collective-permute-start = (bf16[128,2048]{1,0:T(8,128)(2,1)S(1)}, bf16[128,2048]{1,0:T(8,128)(2,1)S(1)}, u32[]{:S(2)}, u32[]{:S(2)}) collective-permute-start(bf16[128,2048]{1,0:T(8,128)(2,1)S(1)} %get-tuple-element.43), channel_id=1, source_target_pairs={{0,4},{4,0},{8,12},{12,8},{16,20},{20,16},{24,28},{28,24},{1,5},{5... | collective-permute-start | bytes 1572872 | tf_op jit(solution)/shard_map/ppermute | solution.py:44
  4.7 1.2 copy-start.5
  7.1 54.9 %collective-permute-start.11 = (bf16[512,2304]{1,0:T(8,128)(2,1)S(1)}, bf16[512,2304]{1,0:T(8,128)(2,1)}, u32[]{:S(2)}, u32[]{:S(2)}) collective-permute-start(bf16[512,2304]{1,0:T(8,128)(2,1)S(1)} %shard_map.95.refs_12_.refs_0_), channel_id=1, source_target_pairs={{0,8},{4,12},{8,0},{12,4},{16,24},{20,28},{24,16},{28,20},{1,9},{5... | collective-permute-start | bytes 7077896 | tf_op jit(solution)/shard_map/ppermute | solution.py:44
  9.6 52.4 %collective-permute-start.12 = (bf16[512,2304]{1,0:T(8,128)(2,1)S(1)}, bf16[512,2304]{1,0:T(8,128)(2,1)}, u32[]{:S(2)}, u32[]{:S(2)}) collective-permute-start(bf16[512,2304]{1,0:T(8,128)(2,1)S(1)} %shard_map.95.refs_12_.refs_0_), channel_id=1, source_target_pairs={{0,16},{4,20},{8,24},{12,28},{16,0},{20,4},{24,8},{28,12},{1,17},{... | collective-permute-start | bytes 7077896 | tf_op jit(solution)/shard_map/ppermute | solution.py:44
  11.0 13.7 %collective-permute-start.6 = (bf16[128,2048]{1,0:T(8,128)(2,1)S(1)}, bf16[128,2048]{1,0:T(8,128)(2,1)S(1)}, u32[]{:S(2)}, u32[]{:S(2)}) collective-permute-start(bf16[128,2048]{1,0:T(8,128)(2,1)S(1)} %pad_maximum_fusion.3.refs_6_), channel_id=1, source_target_pairs={{0,1},{1,2},{2,3},{4,5},{5,6},{6,7},{8,9},{9,10},{10,11},{12,13},{... | collective-permute-start | bytes 1572872 | tf_op jit(solution)/shard_map/ppermute | solution.py:69
  14.2 14.4 %collective-permute-start.7 = (bf16[128,2048]{1,0:T(8,128)(2,1)S(1)}, bf16[128,2048]{1,0:T(8,128)(2,1)}, u32[]{:S(2)}, u32[]{:S(2)}) collective-permute-start(bf16[128,2048]{1,0:T(8,128)(2,1)S(1)} %pad_maximum_fusion.3.refs_6_), channel_id=1, source_target_pairs={{1,0},{2,1},{3,2},{5,4},{6,5},{7,6},{9,8},{10,9},{11,10},{13,12},{... | collective-permute-start | bytes 1572872 | tf_op jit(solution)/shard_map/ppermute | solution.py:69
  15.6 20.3 %collective-permute-start.1 = (bf16[128,2048]{1,0:T(8,128)(2,1)S(1)}, bf16[128,2048]{1,0:T(8,128)(2,1)}, u32[]{:S(2)}, u32[]{:S(2)}) collective-permute-start(bf16[128,2048]{1,0:T(8,128)(2,1)S(1)} %pad_maximum_fusion.2.refs_0_), channel_id=1, source_target_pairs={{0,1},{1,2},{2,3},{4,5},{5,6},{6,7},{8,9},{9,10},{10,11},{12,13},{... | collective-permute-start | bytes 1572872 | tf_op jit(solution)/shard_map/ppermute | solution.py:69
  24.6 13.7 %collective-permute-start.2 = (bf16[128,2048]{1,0:T(8,128)(2,1)S(1)}, bf16[128,2048]{1,0:T(8,128)(2,1)}, u32[]{:S(2)}, u32[]{:S(2)}) collective-permute-start(bf16[128,2048]{1,0:T(8,128)(2,1)S(1)} %pad_maximum_fusion.2.refs_0_), channel_id=1, source_target_pairs={{1,0},{2,1},{3,2},{5,4},{6,5},{7,6},{9,8},{10,9},{11,10},{13,12},{... | collective-permute-start | bytes 1572872 | tf_op jit(solution)/shard_map/ppermute | solution.py:69
  28.6 11.2 %collective-permute-start.8 = (bf16[128,2048]{1,0:T(8,128)(2,1)S(1)}, bf16[128,2048]{1,0:T(8,128)(2,1)}, u32[]{:S(2)}, u32[]{:S(2)}) collective-permute-start(bf16[128,2048]{1,0:T(8,128)(2,1)S(1)} %collective-permute-done.6.refs_7_), channel_id=1, source_target_pairs={{1,2},{2,3},{5,6},{6,7},{9,10},{10,11},{13,14},{14,15},{17,18},{18... | collective-permute-start | bytes 1572872 | tf_op jit(solution)/shard_map/ppermute | solution.py:69
  35.9 14.8 %collective-permute-start.9 = (bf16[128,2048]{1,0:T(8,128)(2,1)}, bf16[128,2048]{1,0:T(8,128)(2,1)}, u32[]{:S(2)}, u32[]{:S(2)}) collective-permute-start(bf16[128,2048]{1,0:T(8,128)(2,1)} %collective-permute-done.7.refs_8_), channel_id=1, source_target_pairs={{1,0},{2,1},{5,4},{6,5},{9,8},{10,9},{13,12},{14,13},{17,16},{18,1... | collective-permute-start | bytes 1572872 | tf_op jit(solution)/shard_map/ppermute | solution.py:69
  38.4 14.8 %collective-permute-start.3 = (bf16[128,2048]{1,0:T(8,128)(2,1)}, bf16[128,2048]{1,0:T(8,128)(2,1)}, u32[]{:S(2)}, u32[]{:S(2)}) collective-permute-start(bf16[128,2048]{1,0:T(8,128)(2,1)} %collective-permute-done.1.refs_1_), channel_id=1, source_target_pairs={{1,2},{2,3},{5,6},{6,7},{9,10},{10,11},{13,14},{14,15},{17,18},{18... | collective-permute-start | bytes 1572872 | tf_op jit(solution)/shard_map/ppermute | solution.py:69
  39.8 22.1 %collective-permute-start.4 = (bf16[128,2048]{1,0:T(8,128)(2,1)}, bf16[128,2048]{1,0:T(8,128)(2,1)}, u32[]{:S(2)}, u32[]{:S(2)}) collective-permute-start(bf16[128,2048]{1,0:T(8,128)(2,1)} %collective-permute-done.2.refs_2_), channel_id=1, source_target_pairs={{1,0},{2,1},{5,4},{6,5},{9,8},{10,9},{13,12},{14,13},{17,16},{18,1... | collective-permute-start | bytes 1572872 | tf_op jit(solution)/shard_map/ppermute | solution.py:69
  51.8 21.3 %collective-permute-start.10 = (bf16[128,2048]{1,0:T(8,128)(2,1)S(1)}, bf16[128,2048]{1,0:T(8,128)(2,1)S(1)}, u32[]{:S(2)}, u32[]{:S(2)}) collective-permute-start(bf16[128,2048]{1,0:T(8,128)(2,1)S(1)} %broadcast_select_fusion), channel_id=1, source_target_pairs={{1,0},{2,3},{5,4},{6,7},{9,8},{10,11},{13,12},{14,15},{17,16},{18,... | collective-permute-start | bytes 1572872 | tf_op jit(solution)/shard_map/ppermute | solution.py:69
  63.4 28.4 %collective-permute-start.13 = (bf16[256,2304]{1,0:T(8,128)(2,1)S(1)}, bf16[256,2304]{1,0:T(8,128)(2,1)S(1)}, u32[]{:S(2)}, u32[]{:S(2)}) collective-permute-start(bf16[256,2304]{1,0:T(8,128)(2,1)S(1)} %slice.44), channel_id=1, source_target_pairs={{0,16},{4,20},{8,24},{12,28},{16,0},{20,4},{24,8},{28,12},{1,17},{... | collective-permute-start | bytes 3538952 | tf_op jit(solution)/shard_map/ppermute | solution.py:44
  66.1 18.2 %copy-start.9 = (bf16[128,2048]{1,0:T(8,128)(2,1)S(1)}, bf16[128,2048]{1,0:T(8,128)(2,1)}, u32[]{:S(2)}) copy-start(bf16[128,2048]{1,0:T(8,128)(2,1)} %copy-done.8) | copy-start | bytes 1572868
  66.1 25.8 %collective-permute-start.14 = (bf16[256,2304]{1,0:T(8,128)(2,1)S(1)}, bf16[256,2304]{1,0:T(8,128)(2,1)S(1)}, u32[]{:S(2)}, u32[]{:S(2)}) collective-permute-start(bf16[256,2304]{1,0:T(8,128)(2,1)S(1)} %slice.45), channel_id=1, source_target_pairs={{0,8},{4,12},{8,0},{12,4},{16,24},{20,28},{24,16},{28,20},{1,9},{5... | collective-permute-start | bytes 3538952 | tf_op jit(solution)/shard_map/ppermute | solution.py:44
  67.6 16.7 %collective-permute-start.5 = (bf16[128,2048]{1,0:T(8,128)(2,1)S(1)}, bf16[128,2048]{1,0:T(8,128)(2,1)S(1)}, u32[]{:S(2)}, u32[]{:S(2)}) collective-permute-start(bf16[128,2048]{1,0:T(8,128)(2,1)S(1)} %broadcast_select_fusion.1), channel_id=1, source_target_pairs={{1,0},{2,3},{5,4},{6,7},{9,8},{10,11},{13,12},{14,15},{17,16},{18,... | collective-permute-start | bytes 1572872 | tf_op jit(solution)/shard_map/ppermute | solution.py:69
  91.8 6.7 %copy-start.7 = (s32[1,4]{1,0:T(1,128)S(1)}, s32[1,4]{1,0:T(1,128)}, u32[]{:S(2)}) copy-start(s32[1,4]{1,0:T(1,128)} %refs_1_.1) | copy-start | bytes 52
  93.3 5.2 %collective-permute-start.15 = (bf16[256,2304]{1,0:T(8,128)(2,1)S(1)}, bf16[256,2304]{1,0:T(8,128)(2,1)S(1)}, u32[]{:S(2)}, u32[]{:S(2)}) collective-permute-start(bf16[256,2304]{1,0:T(8,128)(2,1)S(1)} %get-tuple-element.62), channel_id=1, source_target_pairs={{0,4},{4,0},{8,12},{12,8},{16,20},{20,16},{24,28},{28,24},{1,5},{5... | collective-permute-start | bytes 3538952 | tf_op jit(solution)/shard_map/ppermute | solution.py:44
  102.5 2.2 %collective-permute-start.16 = (bf16[256,1280]{1,0:T(8,128)(2,1)S(1)}, bf16[256,1280]{1,0:T(8,128)(2,1)S(1)}, u32[]{:S(2)}, u32[]{:S(2)}) collective-permute-start(bf16[256,1280]{1,0:T(8,128)(2,1)S(1)} %shard_map.98.own), channel_id=1, source_target_pairs={{0,4},{4,0},{8,12},{12,8},{16,20},{20,16},{24,28},{28,24},{1,5},{5... | collective-permute-start | bytes 1966088 | tf_op jit(solution)/shard_map/ppermute | solution.py:44
  105.7 16.0 %collective-permute-start.22 = (bf16[256,1280]{1,0:T(8,128)(2,1)S(1)}, bf16[256,1280]{1,0:T(8,128)(2,1)S(1)}, u32[]{:S(2)}, u32[]{:S(2)}) collective-permute-start(bf16[256,1280]{1,0:T(8,128)(2,1)S(1)} %get-tuple-element.82), channel_id=1, source_target_pairs={{0,16},{4,20},{8,24},{12,28},{16,0},{20,4},{24,8},{28,12},{1,17},{... | collective-permute-start | bytes 1966088 | tf_op jit(solution)/shard_map/ppermute | solution.py:44
  106.0 15.7 %collective-permute-start.24 = (bf16[256,1280]{1,0:T(8,128)(2,1)S(1)}, bf16[256,1280]{1,0:T(8,128)(2,1)S(1)}, u32[]{:S(2)}, u32[]{:S(2)}) collective-permute-start(bf16[256,1280]{1,0:T(8,128)(2,1)S(1)} %get-tuple-element.81), channel_id=1, source_target_pairs={{0,8},{4,12},{8,0},{12,4},{16,24},{20,28},{24,16},{28,20},{1,9},{5... | collective-permute-start | bytes 1966088 | tf_op jit(solution)/shard_map/ppermute | solution.py:44
  111.1 13.4 %collective-permute-start.17 = (bf16[128,2048]{1,0:T(8,128)(2,1)S(1)}, bf16[128,2048]{1,0:T(8,128)(2,1)S(1)}, u32[]{:S(2)}, u32[]{:S(2)}) collective-permute-start(bf16[128,2048]{1,0:T(8,128)(2,1)S(1)} %get-tuple-element.65), channel_id=1, source_target_pairs={{3,2},{0,1},{7,6},{4,5},{11,10},{8,9},{15,14},{12,13},{19,18},{16,... | collective-permute-start | bytes 1572872 | tf_op jit(solution)/shard_map/ppermute | solution.py:69
  114.2 10.2 %collective-permute-start.18 = (bf16[128,2048]{1,0:T(8,128)(2,1)S(1)}, bf16[128,2048]{1,0:T(8,128)(2,1)S(1)}, u32[]{:S(2)}, u32[]{:S(2)}) collective-permute-start(bf16[128,2048]{1,0:T(8,128)(2,1)S(1)} %get-tuple-element.65), channel_id=1, source_target_pairs={{1,2},{2,1},{5,6},{6,5},{9,10},{10,9},{13,14},{14,13},{17,18},{18,... | collective-permute-start | bytes 1572872 | tf_op jit(solution)/shard_map/ppermute | solution.py:69
  122.0 32.9 %collective-permute-start.25 = (bf16[512,1280]{1,0:T(8,128)(2,1)S(1)}, bf16[512,1280]{1,0:T(8,128)(2,1)S(1)}, u32[]{:S(2)}, u32[]{:S(2)}) collective-permute-start(bf16[512,1280]{1,0:T(8,128)(2,1)S(1)} %pad_maximum_fusion.1), channel_id=1, source_target_pairs={{0,16},{4,20},{8,24},{12,28},{16,0},{20,4},{24,8},{28,12},{1,17},{... | collective-permute-start | bytes 3932168 | tf_op jit(solution)/shard_map/ppermute | solution.py:44
  123.3 31.6 %collective-permute-start.23 = (bf16[512,1280]{1,0:T(8,128)(2,1)S(1)}, bf16[512,1280]{1,0:T(8,128)(2,1)S(1)}, u32[]{:S(2)}, u32[]{:S(2)}) collective-permute-start(bf16[512,1280]{1,0:T(8,128)(2,1)S(1)} %pad_maximum_fusion), channel_id=1, source_target_pairs={{0,8},{4,12},{8,0},{12,4},{16,24},{20,28},{24,16},{28,20},{1,9},{5... | collective-permute-start | bytes 3932168 | tf_op jit(solution)/shard_map/ppermute | solution.py:44
  124.6 25.0 %collective-permute-start.19 = (bf16[128,2048]{1,0:T(8,128)(2,1)S(1)}, bf16[128,2048]{1,0:T(8,128)(2,1)S(1)}, u32[]{:S(2)}, u32[]{:S(2)}) collective-permute-start(bf16[128,2048]{1,0:T(8,128)(2,1)S(1)} %get-tuple-element.68), channel_id=1, source_target_pairs={{0,1},{1,0},{2,3},{3,2},{4,5},{5,4},{6,7},{7,6},{8,9},{9,8},{10,11... | collective-permute-start | bytes 1572872 | tf_op jit(solution)/shard_map/ppermute | solution.py:44
  128.2 21.5 %collective-permute-start.20 = (bf16[128,2048]{1,0:T(8,128)(2,1)S(1)}, bf16[128,2048]{1,0:T(8,128)(2,1)S(1)}, u32[]{:S(2)}, u32[]{:S(2)}) collective-permute-start(bf16[128,2048]{1,0:T(8,128)(2,1)S(1)} %add.18), channel_id=1, source_target_pairs={{0,2},{1,3},{2,0},{3,1},{4,6},{5,7},{6,4},{7,5},{8,10},{9,11},{10,... | collective-permute-start | bytes 1572872 | tf_op jit(solution)/shard_map/ppermute | solution.py:44
  149.8 7.2 %collective-permute-start.21 = (bf16[64,2048]{1,0:T(8,128)(2,1)S(1)}, bf16[64,2048]{1,0:T(8,128)(2,1)S(1)}, u32[]{:S(2)}, u32[]{:S(2)}) collective-permute-start(bf16[64,2048]{1,0:T(8,128)(2,1)S(1)} %add_convert_fusion), channel_id=1, source_target_pairs={{0,4},{4,0},{8,12},{12,8},{16,20},{20,16},{24,28},{28,24},{1,5},{5... | collective-permute-start | bytes 786440 | tf_op jit(solution)/shard_map/ppermute | solution.py:44
  154.9 2.1 %copy-start.1 = (bf16[64,4096]{1,0:T(8,128)(2,1)S(1)}, bf16[64,4096]{1,0:T(8,128)(2,1)}, u32[]{:S(2)}) copy-start(bf16[64,4096]{1,0:T(8,128)(2,1)} %tokens.3) | copy-start | bytes 1572868
  154.9 2.1 %copy-start.3 = (bf16[64,4096]{1,0:T(8,128)(2,1)S(1)}, bf16[64,4096]{1,0:T(8,128)(2,1)}, u32[]{:S(2)}) copy-start(bf16[64,4096]{1,0:T(8,128)(2,1)} %grad_out.3) | copy-start | bytes 1572868
  (4 other events, 3.8 us)

commit v12 on v11

--- a/solution.py
+++ b/solution.py
@@ -53,23 +53,25 @@
     return [value] + [swap(value, axis, unit * k) for k in range(1, size)]
 
 
-def gather_chips(value):
+def gather_near(value):
     if lax.axis_size("dp") != 8:
         return everyone(value, "dp", 2), []
     half = value.shape[0] // 2
     near_x = swap(value, "dp", 2)
     near_y = swap(value, "dp", 4)
     near_x, near_y = tied(near_x, near_y)
-    far_top = swap(near_x[:half], "dp", 4)
-    far_bottom = swap(near_y[half:], "dp", 2)
-    return [value, near_x, near_y], [far_top, far_bottom]
+    return [value, near_x, near_y], [near_x[:half], near_y[half:]]
+
+
+def gather_far(parts):
+    return [swap(part, "dp", mask) for part, mask in zip(parts, (4, 2))]
 
 
 def along(value, pairs):
     return lax.ppermute(value, "tensor", pairs)
 
 
-def gather_tensor(value):
+def gather_tensor(value, after=()):
     if lax.axis_size("tensor") != 4:
         return everyone(value, "tensor", 1)
     right_one = along(value, [(0, 1), (1, 2), (2, 3)])
@@ -77,7 +79,7 @@
     right_one, left_one = tied(right_one, left_one)
     right_two = along(right_one, [(1, 2), (2, 3)])
     left_two = along(left_one, [(1, 0), (2, 1)])
-    right_two, left_two = tied(right_two, left_two)
+    right_two, left_two, *_ = tied(right_two, left_two, *after)
     last = along(
         jnp.where(lax.axis_index("tensor") == 1, left_two, right_two), [(1, 0), (2, 3)]
     )
@@ -388,7 +390,7 @@
 
 def finish(parts, query_width, share):
     block, width = parts[0].shape
-    step = min(block, 128)
+    step = min(block, 256)
 
     def spec(columns):
         return pl.BlockSpec((step, columns), lambda i: (i, 0))
@@ -461,9 +463,12 @@
         [shaped((block, joint_width + out_weight.shape[0]))],
         [query_weight, kv_weight, out_weight],
     )
-    early, late = gather_chips(merged)
+    early, parts = gather_near(merged)
+    late = gather_far(parts)
     row_pieces = gather_tensor(jnp.concatenate([grad_keep, sent[:rows]], axis=0))
-    row_pieces += gather_tensor(jnp.concatenate([normed_keep, sent[rows:]], axis=0))
+    row_pieces += gather_tensor(
+        jnp.concatenate([normed_keep, sent[rows:]], axis=0), (*parts, *row_pieces[3:4])
+    )
     own, sent, normed = project(place, row_pieces, early, late, tensor_size, joint_width)
     sent = swap(sent, "dp", 1)
     if levels:

time: 160 us -> 161 us (level)
    ppermute x14, waiting for transfers between devices: 29 us -> 36.3 us  [swap(): return lax.ppermute(value, axis, pairs)]
    ppermute x12, waiting for transfers between devices: 47.5 us -> 40.9 us  [along(): return lax.ppermute(value, 'tensor', pairs)]
    ppermute x12, starting transfers between devices: 23 us -> 25.4 us  [along(): return lax.ppermute(value, 'tensor', pairs)]
where the time goes in v12:
time: 161 us; the launch traced here: 160 us
  waiting for transfers between devices  77.2 us (48%)
  starting transfers between devices  44.8 us (28%)
  Pallas kernels  25.8 us (16%)
  local copies, waits for them, and re-layouts  8.76 us (5%)
  other arithmetic  3.01 us (2%)
    ppermute x12, waiting for transfers between devices, along(): return lax.ppermute(value, 'tensor', pairs)  40.9 us
    ppermute x14, waiting for transfers between devices, swap(): return lax.ppermute(value, axis, pairs)  36.3 us
    ppermute x12, starting transfers between devices, along(): return lax.ppermute(value, 'tensor', pairs)  25.4 us
    pallas_call x8, Pallas kernels, call(): pl.pallas_call(kernel, out_shape=outs, in_specs=[SCALARS] * len(scalars)...  19.4 us
    ppermute x14, starting transfers between devices, swap(): return lax.ppermute(value, axis, pairs)  19.4 us
    unnamed x20, local copies, waits for them, and re-layouts  5.23 us
    pallas_call x1, Pallas kernels, row_terms(): pl.pallas_call(functools.partial(row_kernel, len(weights)), grid=(1,), ou...  4.69 us
  transfers between devices with their start and end apart: 26, of which 14 were waited for; matrix products, arithmetic and copies ran while one was open for 4% of the time, Pallas kernels for 10%

profile of v12, /device:TPU:1, one launch (start us, length us, event | category | flops | bytes accessed | tf_op | source)
XLA Modules:
  0.0 160.5 jit_solution(13741029154443256580)
XLA Ops:
  7.1 2.6 %collective-permute-start.11 = (bf16[512,2304]{1,0:T(8,128)(2,1)S(1)}, bf16[512,2304]{1,0:T(8,128)(2,1)}, u32[]{:S(2)}, u32[]{:S(2)}) collective-permute-start(bf16[512,2304]{1,0:T(8,128)(2,1)S(1)} %shard_map.95.refs_12_.refs_0_), channel_id=1, source_target_pairs={{0,16},{4,20},{8,24},{12,28},{16,0},{20,4},{24,8},{28,12},{1,17},{... | collective-permute-start | bytes 7077896 | tf_op jit(solution)/shard_map/ppermute | solution.py:44
  11.0 1.3 collective-permute-start.2
  12.3 4.0 %collective-permute-start.1 = (bf16[128,2048]{1,0:T(8,128)(2,1)S(1)}, bf16[128,2048]{1,0:T(8,128)(2,1)S(1)}, u32[]{:S(2)}, u32[]{:S(2)}) collective-permute-start(bf16[128,2048]{1,0:T(8,128)(2,1)S(1)} %pad_maximum_fusion.2.refs_0_), channel_id=1, source_target_pairs={{0,1},{1,2},{2,3},{4,5},{5,6},{6,7},{8,9},{9,10},{10,11},{12,13},{... | collective-permute-start | bytes 1572872 | tf_op jit(solution)/shard_map/ppermute | solution.py:71
  16.4 1.3 collective-permute-start.7
  17.7 8.0 %collective-permute-done.2.refs_2_ = bf16[128,2048]{1,0:T(8,128)(2,1)} collective-permute-done((bf16[128,2048]{1,0:T(8,128)(2,1)S(1)}, bf16[128,2048]{1,0:T(8,128)(2,1)}, u32[]{:S(2)}, u32[]{:S(2)}) %collective-permute-start.2) | collective-permute-done | bytes 524320 | tf_op jit(solution)/shard_map/ppermute | solution.py:71
  25.7 4.0 %collective-permute-start.6 = (bf16[128,2048]{1,0:T(8,128)(2,1)S(1)}, bf16[128,2048]{1,0:T(8,128)(2,1)}, u32[]{:S(2)}, u32[]{:S(2)}) collective-permute-start(bf16[128,2048]{1,0:T(8,128)(2,1)S(1)} %pad_maximum_fusion.3.refs_6_), channel_id=1, source_target_pairs={{0,1},{1,2},{2,3},{4,5},{5,6},{6,7},{8,9},{9,10},{10,11},{12,13},{... | collective-permute-start | bytes 1572872 | tf_op jit(solution)/shard_map/ppermute | solution.py:71
  29.6 1.5 collective-permute-start.3
  31.9 5.0 %collective-permute-done.7.refs_8_ = bf16[128,2048]{1,0:T(8,128)(2,1)} collective-permute-done((bf16[128,2048]{1,0:T(8,128)(2,1)S(1)}, bf16[128,2048]{1,0:T(8,128)(2,1)}, u32[]{:S(2)}, u32[]{:S(2)}) %collective-permute-start.7) | collective-permute-done | bytes 524320 | tf_op jit(solution)/shard_map/ppermute | solution.py:71
  38.2 1.5 collective-permute-start.8
  41.0 9.8 %collective-permute-done.4.refs_4_ = bf16[128,2048]{1,0:T(8,128)(2,1)} collective-permute-done((bf16[128,2048]{1,0:T(8,128)(2,1)}, bf16[128,2048]{1,0:T(8,128)(2,1)}, u32[]{:S(2)}, u32[]{:S(2)}) %collective-permute-start.4) | collective-permute-done | bytes 524320 | tf_op jit(solution)/shard_map/ppermute | solution.py:71
  52.0 1.3 collective-permute-start.5
  53.2 8.0 %collective-permute-done.11.refs_14_.refs_2_ = bf16[512,2304]{1,0:T(8,128)(2,1)} collective-permute-done((bf16[512,2304]{1,0:T(8,128)(2,1)S(1)}, bf16[512,2304]{1,0:T(8,128)(2,1)}, u32[]{:S(2)}, u32[]{:S(2)}) %collective-permute-start.11) | collective-permute-done | bytes 2359328 | tf_op jit(solution)/shard_map/ppermute | solution.py:44
  62.1 1.3 slice.44
  63.5 1.3 slice.45
  67.5 1.5 collective-permute-start.12
  69.0 14.4 %collective-permute-done.12.refs_11_ = bf16[128,2048]{1,0:T(8,128)(2,1)S(1)} collective-permute-done((bf16[128,2048]{1,0:T(8,128)(2,1)S(1)}, bf16[128,2048]{1,0:T(8,128)(2,1)S(1)}, u32[]{:S(2)}, u32[]{:S(2)}) %collective-permute-start.12) | collective-permute-done | bytes 524320 | tf_op jit(solution)/shard_map/ppermute | solution.py:71
  83.4 7.5 %shard_map.96 = (f32[512,2304]{1,0:T(8,128)S(1)}, bf16[512,2048]{1,0:T(8,128)(2,1)S(1)}, bf16[512,2048]{1,0:T(8,128)(2,1)S(1)}) custom-call(s32[3]{0:T(128)S(1)} %pad_add_fusion.place.refs_0_, bf16[128,2048]{1,0:T(8,128)(2,1)S(1)} %pad_maximum_fusion.2.refs_0_, bf16[128,2048]{1,0:T(8,128)(2,1)S(1)} %copy-done.9, ...), custom_call_target="tpu_custom_call" | custom-call | flops 3623878656 | bytes 22282240 | tf_op jit(solution)/shard_map/pallas_call | solution.py:23
  91.9 1.4 shard_map.97
  93.4 2.8 %collective-permute-start.15 = (bf16[256,2304]{1,0:T(8,128)(2,1)S(1)}, bf16[256,2304]{1,0:T(8,128)(2,1)S(1)}, u32[]{:S(2)}, u32[]{:S(2)}) collective-permute-start(bf16[256,2304]{1,0:T(8,128)(2,1)S(1)} %get-tuple-element.62), channel_id=1, source_target_pairs={{0,4},{4,0},{8,12},{12,8},{16,20},{20,16},{24,28},{28,24},{1,5},{5... | collective-permute-start | bytes 3538952 | tf_op jit(solution)/shard_map/ppermute | solution.py:44
  96.2 2.5 %collective-permute-done.15.refs_3_ = bf16[256,2304]{1,0:T(8,128)(2,1)S(1)} collective-permute-done((bf16[256,2304]{1,0:T(8,128)(2,1)S(1)}, bf16[256,2304]{1,0:T(8,128)(2,1)S(1)}, u32[]{:S(2)}, u32[]{:S(2)}) %collective-permute-start.15) | collective-permute-done | bytes 1179680 | tf_op jit(solution)/shard_map/ppermute | solution.py:44
  98.6 4.0 %shard_map.98.own = bf16[256,1280]{1,0:T(8,128)(2,1)S(1)} custom-call(s32[3]{0:T(128)S(1)} %pad_add_fusion.place.refs_0_, s32[1,4]{1,0:T(1,128)S(1)} %copy-done.7, f32[256,2304]{1,0:T(8,128)S(1)} %get-tuple-element.61.refs_2_, bf16[256,2304]{1,0:T(8,128)(2,1)S(1)} %collective-permute-done.15.refs_3_), custom_call_target="tpu_custom_call" | custom-call | flops 671088640 | bytes 4194304 | tf_op jit(solution)/shard_map/pallas_call | solution.py:23
  103.1 1.7 %collective-permute-done.16.other = bf16[256,1280]{1,0:T(8,128)(2,1)S(1)} collective-permute-done((bf16[256,1280]{1,0:T(8,128)(2,1)S(1)}, bf16[256,1280]{1,0:T(8,128)(2,1)S(1)}, u32[]{:S(2)}, u32[]{:S(2)}) %collective-permute-start.16) | collective-permute-done | bytes 655392 | tf_op jit(solution)/shard_map/ppermute | solution.py:44
  106.5 4.7 %shard_map.99 = (bf16[128,2048]{1,0:T(8,128)(2,1)S(1)}, bf16[128,2048]{1,0:T(8,128)(2,1)S(1)}, bf16[128,2048]{1,0:T(8,128)(2,1)S(1)}, bf16[128,2048]{1,0:T(8,128)(2,1)S(1)}) custom-call(bf16[256,1280]{1,0:T(8,128)(2,1)S(1)} %shard_map.98.own, bf16[256,1280]{1,0:T(8,128)(2,1)S(1)} %collective-permute-done.16.other, ...), custom_call_target="tpu_custom_call" | custom-call | flops 2684354560 | bytes 8650752 | tf_op jit(solution)/shard_map/pallas_call | solution.py:367
  111.8 5.8 %collective-permute-start.17 = (bf16[128,2048]{1,0:T(8,128)(2,1)S(1)}, bf16[128,2048]{1,0:T(8,128)(2,1)S(1)}, u32[]{:S(2)}, u32[]{:S(2)}) collective-permute-start(bf16[128,2048]{1,0:T(8,128)(2,1)S(1)} %get-tuple-element.65), channel_id=1, source_target_pairs={{3,2},{0,1},{7,6},{4,5},{11,10},{8,9},{15,14},{12,13},{19,18},{16,... | collective-permute-start | bytes 1572872 | tf_op jit(solution)/shard_map/ppermute | solution.py:71
  117.6 2.3 %shard_map.100 = (bf16[512,1280]{1,0:T(8,128)(2,1)S(1)}, bf16[512,1280]{1,0:T(8,128)(2,1)S(1)}, bf16[512,1280]{1,0:T(8,128)(2,1)S(1)}) custom-call(bf16[512,2048]{1,0:T(8,128)(2,1)S(1)} %get-tuple-element.60.normed.pair, bf16[256,1280]{1,0:T(8,128)(2,1)S(1)} %shard_map.98.own, bf16[256,1280]{1,0:T(8,128)(2,1)S(1)} %collective-permute-done.16.other), custom_call_target="tpu_custom_call" | custom-call | flops 2013265920 | bytes 7340032 | tf_op jit(solution)/shard_map/pallas_call | solution.py:23
  119.9 1.9 %collective-permute-done.24 = bf16[256,1280]{1,0:T(8,128)(2,1)S(1)} collective-permute-done((bf16[256,1280]{1,0:T(8,128)(2,1)S(1)}, bf16[256,1280]{1,0:T(8,128)(2,1)S(1)}, u32[]{:S(2)}, u32[]{:S(2)}) %collective-permute-start.24) | collective-permute-done | bytes 655392 | tf_op jit(solution)/shard_map/ppermute | solution.py:44
  123.7 3.6 %collective-permute-done.17 = bf16[128,2048]{1,0:T(8,128)(2,1)S(1)} collective-permute-done((bf16[128,2048]{1,0:T(8,128)(2,1)S(1)}, bf16[128,2048]{1,0:T(8,128)(2,1)S(1)}, u32[]{:S(2)}, u32[]{:S(2)}) %collective-permute-start.17) | collective-permute-done | bytes 524320 | tf_op jit(solution)/shard_map/ppermute | solution.py:71
  127.5 2.3 %collective-permute-start.19 = (bf16[128,2048]{1,0:T(8,128)(2,1)S(1)}, bf16[128,2048]{1,0:T(8,128)(2,1)S(1)}, u32[]{:S(2)}, u32[]{:S(2)}) collective-permute-start(bf16[128,2048]{1,0:T(8,128)(2,1)S(1)} %get-tuple-element.68), channel_id=1, source_target_pairs={{0,1},{1,0},{2,3},{3,2},{4,5},{5,4},{6,7},{7,6},{8,9},{9,8},{10,11... | collective-permute-start | bytes 1572872 | tf_op jit(solution)/shard_map/ppermute | solution.py:44
  129.8 20.1 %collective-permute-done.19.refs_1_ = bf16[128,2048]{1,0:T(8,128)(2,1)S(1)} collective-permute-done((bf16[128,2048]{1,0:T(8,128)(2,1)S(1)}, bf16[128,2048]{1,0:T(8,128)(2,1)S(1)}, u32[]{:S(2)}, u32[]{:S(2)}) %collective-permute-start.19) | collective-permute-done | bytes 524320 | tf_op jit(solution)/shard_map/ppermute | solution.py:44
  150.2 6.3 %collective-permute-start.21 = (bf16[64,2048]{1,0:T(8,128)(2,1)S(1)}, bf16[64,2048]{1,0:T(8,128)(2,1)S(1)}, u32[]{:S(2)}, u32[]{:S(2)}) collective-permute-start(bf16[64,2048]{1,0:T(8,128)(2,1)S(1)} %add_convert_fusion), channel_id=1, source_target_pairs={{0,4},{4,0},{8,12},{12,8},{16,20},{20,16},{24,28},{28,24},{1,5},{5... | collective-permute-start | bytes 786440 | tf_op jit(solution)/shard_map/ppermute | solution.py:44
  156.5 1.7 %shard_map.102 = (f32[512,1024]{1,0:T(8,128)}, f32[512,256]{1,0:T(8,128)}) custom-call(bf16[512,1280]{1,0:T(8,128)(2,1)S(1)} %get-tuple-element.71.refs_0_, bf16[512,1280]{1,0:T(8,128)(2,1)S(1)} %collective-permute-done.23.refs_1_, bf16[512,1280]{1,0:T(8,128)(2,1)S(1)} %collective-permute-done.25.refs_2_), custom_call_target="tpu_custom_call" | custom-call | bytes 6553600 | tf_op jit(solution)/shard_map/pallas_call | solution.py:398
  158.2 2.2 %shard_map.103 = bf16[64,4096]{1,0:T(8,128)(2,1)} custom-call(s32[3]{0:T(128)S(1)} %pad_add_fusion.place.refs_0_, bf16[64,4096]{1,0:T(8,128)(2,1)S(1)} %copy-done.1, bf16[1,4096]{1,0:T(2,128)(2,1)S(1)} %reshape.9.gain, bf16[64,4096]{1,0:T(8,128)(2,1)S(1)} %copy-done.3, bf16[64,2048]{1,0:T(8,128)(2,1)S(1)} %collective-permute-done.21.handed, ...), custom_call_target="tpu_custom_call" | custom-call | bytes 3940352 | tf_op jit(solution)/shard_map/pallas_call | solution.py:23
  (65 shorter events, 21.9 us)
Async XLA Ops:
  3.5 1.2 copy-start.4
  4.5 6.4 %collective-permute-start = (bf16[128,2048]{1,0:T(8,128)(2,1)S(1)}, bf16[128,2048]{1,0:T(8,128)(2,1)S(1)}, u32[]{:S(2)}, u32[]{:S(2)}) collective-permute-start(bf16[128,2048]{1,0:T(8,128)(2,1)S(1)} %get-tuple-element.43), channel_id=1, source_target_pairs={{0,4},{4,0},{8,12},{12,8},{16,20},{20,16},{24,28},{28,24},{1,5},{5... | collective-permute-start | bytes 1572872 | tf_op jit(solution)/shard_map/ppermute | solution.py:44
  4.7 1.2 copy-start.5
  7.1 54.2 %collective-permute-start.11 = (bf16[512,2304]{1,0:T(8,128)(2,1)S(1)}, bf16[512,2304]{1,0:T(8,128)(2,1)}, u32[]{:S(2)}, u32[]{:S(2)}) collective-permute-start(bf16[512,2304]{1,0:T(8,128)(2,1)S(1)} %shard_map.95.refs_12_.refs_0_), channel_id=1, source_target_pairs={{0,16},{4,20},{8,24},{12,28},{16,0},{20,4},{24,8},{28,12},{1,17},{... | collective-permute-start | bytes 7077896 | tf_op jit(solution)/shard_map/ppermute | solution.py:44
  9.7 52.4 %collective-permute-start.10 = (bf16[512,2304]{1,0:T(8,128)(2,1)S(1)}, bf16[512,2304]{1,0:T(8,128)(2,1)}, u32[]{:S(2)}, u32[]{:S(2)}) collective-permute-start(bf16[512,2304]{1,0:T(8,128)(2,1)S(1)} %shard_map.95.refs_12_.refs_0_), channel_id=1, source_target_pairs={{0,8},{4,12},{8,0},{12,4},{16,24},{20,28},{24,16},{28,20},{1,9},{5... | collective-permute-start | bytes 7077896 | tf_op jit(solution)/shard_map/ppermute | solution.py:44
  11.0 14.7 %collective-permute-start.2 = (bf16[128,2048]{1,0:T(8,128)(2,1)S(1)}, bf16[128,2048]{1,0:T(8,128)(2,1)}, u32[]{:S(2)}, u32[]{:S(2)}) collective-permute-start(bf16[128,2048]{1,0:T(8,128)(2,1)S(1)} %pad_maximum_fusion.2.refs_0_), channel_id=1, source_target_pairs={{1,0},{2,1},{3,2},{5,4},{6,5},{7,6},{9,8},{10,9},{11,10},{13,12},{... | collective-permute-start | bytes 1572872 | tf_op jit(solution)/shard_map/ppermute | solution.py:71
  12.3 17.4 %collective-permute-start.1 = (bf16[128,2048]{1,0:T(8,128)(2,1)S(1)}, bf16[128,2048]{1,0:T(8,128)(2,1)S(1)}, u32[]{:S(2)}, u32[]{:S(2)}) collective-permute-start(bf16[128,2048]{1,0:T(8,128)(2,1)S(1)} %pad_maximum_fusion.2.refs_0_), channel_id=1, source_target_pairs={{0,1},{1,2},{2,3},{4,5},{5,6},{6,7},{8,9},{9,10},{10,11},{12,13},{... | collective-permute-start | bytes 1572872 | tf_op jit(solution)/shard_map/ppermute | solution.py:71
  16.4 20.5 %collective-permute-start.7 = (bf16[128,2048]{1,0:T(8,128)(2,1)S(1)}, bf16[128,2048]{1,0:T(8,128)(2,1)}, u32[]{:S(2)}, u32[]{:S(2)}) collective-permute-start(bf16[128,2048]{1,0:T(8,128)(2,1)S(1)} %pad_maximum_fusion.3.refs_6_), channel_id=1, source_target_pairs={{1,0},{2,1},{3,2},{5,4},{6,5},{7,6},{9,8},{10,9},{11,10},{13,12},{... | collective-permute-start | bytes 1572872 | tf_op jit(solution)/shard_map/ppermute | solution.py:71
  25.7 12.5 %collective-permute-start.6 = (bf16[128,2048]{1,0:T(8,128)(2,1)S(1)}, bf16[128,2048]{1,0:T(8,128)(2,1)}, u32[]{:S(2)}, u32[]{:S(2)}) collective-permute-start(bf16[128,2048]{1,0:T(8,128)(2,1)S(1)} %pad_maximum_fusion.3.refs_6_), channel_id=1, source_target_pairs={{0,1},{1,2},{2,3},{4,5},{5,6},{6,7},{8,9},{9,10},{10,11},{12,13},{... | collective-permute-start | bytes 1572872 | tf_op jit(solution)/shard_map/ppermute | solution.py:71
  29.6 10.1 %collective-permute-start.3 = (bf16[128,2048]{1,0:T(8,128)(2,1)S(1)}, bf16[128,2048]{1,0:T(8,128)(2,1)}, u32[]{:S(2)}, u32[]{:S(2)}) collective-permute-start(bf16[128,2048]{1,0:T(8,128)(2,1)S(1)} %collective-permute-done.1.refs_1_), channel_id=1, source_target_pairs={{1,2},{2,3},{5,6},{6,7},{9,10},{10,11},{13,14},{14,15},{17,18},{18... | collective-permute-start | bytes 1572872 | tf_op jit(solution)/shard_map/ppermute | solution.py:71
  36.9 14.0 %collective-permute-start.4 = (bf16[128,2048]{1,0:T(8,128)(2,1)}, bf16[128,2048]{1,0:T(8,128)(2,1)}, u32[]{:S(2)}, u32[]{:S(2)}) collective-permute-start(bf16[128,2048]{1,0:T(8,128)(2,1)} %collective-permute-done.2.refs_2_), channel_id=1, source_target_pairs={{1,0},{2,1},{5,4},{6,5},{9,8},{10,9},{13,12},{14,13},{17,16},{18,1... | collective-permute-start | bytes 1572872 | tf_op jit(solution)/shard_map/ppermute | solution.py:71
  38.2 28.2 %collective-permute-start.8 = (bf16[128,2048]{1,0:T(8,128)(2,1)}, bf16[128,2048]{1,0:T(8,128)(2,1)}, u32[]{:S(2)}, u32[]{:S(2)}) collective-permute-start(bf16[128,2048]{1,0:T(8,128)(2,1)} %collective-permute-done.6.refs_7_), channel_id=1, source_target_pairs={{1,2},{2,3},{5,6},{6,7},{9,10},{10,11},{13,14},{14,15},{17,18},{18... | collective-permute-start | bytes 1572872 | tf_op jit(solution)/shard_map/ppermute | solution.py:71
  39.7 26.7 %collective-permute-start.9 = (bf16[128,2048]{1,0:T(8,128)(2,1)}, bf16[128,2048]{1,0:T(8,128)(2,1)}, u32[]{:S(2)}, u32[]{:S(2)}) collective-permute-start(bf16[128,2048]{1,0:T(8,128)(2,1)} %collective-permute-done.7.refs_8_), channel_id=1, source_target_pairs={{1,0},{2,1},{5,4},{6,5},{9,8},{10,9},{13,12},{14,13},{17,16},{18,1... | collective-permute-start | bytes 1572872 | tf_op jit(solution)/shard_map/ppermute | solution.py:71
  52.0 17.1 %collective-permute-start.5 = (bf16[128,2048]{1,0:T(8,128)(2,1)S(1)}, bf16[128,2048]{1,0:T(8,128)(2,1)S(1)}, u32[]{:S(2)}, u32[]{:S(2)}) collective-permute-start(bf16[128,2048]{1,0:T(8,128)(2,1)S(1)} %broadcast_select_fusion.1), channel_id=1, source_target_pairs={{1,0},{2,3},{5,4},{6,7},{9,8},{10,11},{13,12},{14,15},{17,16},{18,... | collective-permute-start | bytes 1572872 | tf_op jit(solution)/shard_map/ppermute | solution.py:71
  64.8 18.6 %copy-start.9 = (bf16[128,2048]{1,0:T(8,128)(2,1)S(1)}, bf16[128,2048]{1,0:T(8,128)(2,1)}, u32[]{:S(2)}) copy-start(bf16[128,2048]{1,0:T(8,128)(2,1)} %copy-done.8) | copy-start | bytes 1572868
  64.8 26.2 %collective-permute-start.14 = (bf16[256,2304]{1,0:T(8,128)(2,1)S(1)}, bf16[256,2304]{1,0:T(8,128)(2,1)S(1)}, u32[]{:S(2)}, u32[]{:S(2)}) collective-permute-start(bf16[256,2304]{1,0:T(8,128)(2,1)S(1)} %slice.45), channel_id=1, source_target_pairs={{0,8},{4,12},{8,0},{12,4},{16,24},{20,28},{24,16},{28,20},{1,9},{5... | collective-permute-start | bytes 3538952 | tf_op jit(solution)/shard_map/ppermute | solution.py:44
  66.1 25.8 %collective-permute-start.13 = (bf16[256,2304]{1,0:T(8,128)(2,1)S(1)}, bf16[256,2304]{1,0:T(8,128)(2,1)S(1)}, u32[]{:S(2)}, u32[]{:S(2)}) collective-permute-start(bf16[256,2304]{1,0:T(8,128)(2,1)S(1)} %slice.44), channel_id=1, source_target_pairs={{0,16},{4,20},{8,24},{12,28},{16,0},{20,4},{24,8},{28,12},{1,17},{... | collective-permute-start | bytes 3538952 | tf_op jit(solution)/shard_map/ppermute | solution.py:44
  67.5 15.9 %collective-permute-start.12 = (bf16[128,2048]{1,0:T(8,128)(2,1)S(1)}, bf16[128,2048]{1,0:T(8,128)(2,1)S(1)}, u32[]{:S(2)}, u32[]{:S(2)}) collective-permute-start(bf16[128,2048]{1,0:T(8,128)(2,1)S(1)} %broadcast_select_fusion), channel_id=1, source_target_pairs={{1,0},{2,3},{5,4},{6,7},{9,8},{10,11},{13,12},{14,15},{17,16},{18,... | collective-permute-start | bytes 1572872 | tf_op jit(solution)/shard_map/ppermute | solution.py:71
  91.9 6.7 %copy-start.7 = (s32[1,4]{1,0:T(1,128)S(1)}, s32[1,4]{1,0:T(1,128)}, u32[]{:S(2)}) copy-start(s32[1,4]{1,0:T(1,128)} %refs_1_.1) | copy-start | bytes 52
  93.4 5.3 %collective-permute-start.15 = (bf16[256,2304]{1,0:T(8,128)(2,1)S(1)}, bf16[256,2304]{1,0:T(8,128)(2,1)S(1)}, u32[]{:S(2)}, u32[]{:S(2)}) collective-permute-start(bf16[256,2304]{1,0:T(8,128)(2,1)S(1)} %get-tuple-element.62), channel_id=1, source_target_pairs={{0,4},{4,0},{8,12},{12,8},{16,20},{20,16},{24,28},{28,24},{1,5},{5... | collective-permute-start | bytes 3538952 | tf_op jit(solution)/shard_map/ppermute | solution.py:44
  102.7 2.2 %collective-permute-start.16 = (bf16[256,1280]{1,0:T(8,128)(2,1)S(1)}, bf16[256,1280]{1,0:T(8,128)(2,1)S(1)}, u32[]{:S(2)}, u32[]{:S(2)}) collective-permute-start(bf16[256,1280]{1,0:T(8,128)(2,1)S(1)} %shard_map.98.own), channel_id=1, source_target_pairs={{0,4},{4,0},{8,12},{12,8},{16,20},{20,16},{24,28},{28,24},{1,5},{5... | collective-permute-start | bytes 1966088 | tf_op jit(solution)/shard_map/ppermute | solution.py:44
  105.8 16.0 %collective-permute-start.24 = (bf16[256,1280]{1,0:T(8,128)(2,1)S(1)}, bf16[256,1280]{1,0:T(8,128)(2,1)S(1)}, u32[]{:S(2)}, u32[]{:S(2)}) collective-permute-start(bf16[256,1280]{1,0:T(8,128)(2,1)S(1)} %get-tuple-element.81), channel_id=1, source_target_pairs={{0,8},{4,12},{8,0},{12,4},{16,24},{20,28},{24,16},{28,20},{1,9},{5... | collective-permute-start | bytes 1966088 | tf_op jit(solution)/shard_map/ppermute | solution.py:44
  106.1 15.7 %collective-permute-start.22 = (bf16[256,1280]{1,0:T(8,128)(2,1)S(1)}, bf16[256,1280]{1,0:T(8,128)(2,1)S(1)}, u32[]{:S(2)}, u32[]{:S(2)}) collective-permute-start(bf16[256,1280]{1,0:T(8,128)(2,1)S(1)} %get-tuple-element.82), channel_id=1, source_target_pairs={{0,16},{4,20},{8,24},{12,28},{16,0},{20,4},{24,8},{28,12},{1,17},{... | collective-permute-start | bytes 1966088 | tf_op jit(solution)/shard_map/ppermute | solution.py:44
  111.1 12.6 %collective-permute-start.18 = (bf16[128,2048]{1,0:T(8,128)(2,1)S(1)}, bf16[128,2048]{1,0:T(8,128)(2,1)S(1)}, u32[]{:S(2)}, u32[]{:S(2)}) collective-permute-start(bf16[128,2048]{1,0:T(8,128)(2,1)S(1)} %get-tuple-element.65), channel_id=1, source_target_pairs={{1,2},{2,1},{5,6},{6,5},{9,10},{10,9},{13,14},{14,13},{17,18},{18,... | collective-permute-start | bytes 1572872 | tf_op jit(solution)/shard_map/ppermute | solution.py:71
  111.8 15.5 %collective-permute-start.17 = (bf16[128,2048]{1,0:T(8,128)(2,1)S(1)}, bf16[128,2048]{1,0:T(8,128)(2,1)S(1)}, u32[]{:S(2)}, u32[]{:S(2)}) collective-permute-start(bf16[128,2048]{1,0:T(8,128)(2,1)S(1)} %get-tuple-element.65), channel_id=1, source_target_pairs={{3,2},{0,1},{7,6},{4,5},{11,10},{8,9},{15,14},{12,13},{19,18},{16,... | collective-permute-start | bytes 1572872 | tf_op jit(solution)/shard_map/ppermute | solution.py:71
  122.1 34.3 %collective-permute-start.25 = (bf16[512,1280]{1,0:T(8,128)(2,1)S(1)}, bf16[512,1280]{1,0:T(8,128)(2,1)S(1)}, u32[]{:S(2)}, u32[]{:S(2)}) collective-permute-start(bf16[512,1280]{1,0:T(8,128)(2,1)S(1)} %pad_maximum_fusion.1), channel_id=1, source_target_pairs={{0,16},{4,20},{8,24},{12,28},{16,0},{20,4},{24,8},{28,12},{1,17},{... | collective-permute-start | bytes 3932168 | tf_op jit(solution)/shard_map/ppermute | solution.py:44
  122.5 33.9 %collective-permute-start.23 = (bf16[512,1280]{1,0:T(8,128)(2,1)S(1)}, bf16[512,1280]{1,0:T(8,128)(2,1)S(1)}, u32[]{:S(2)}, u32[]{:S(2)}) collective-permute-start(bf16[512,1280]{1,0:T(8,128)(2,1)S(1)} %pad_maximum_fusion), channel_id=1, source_target_pairs={{0,8},{4,12},{8,0},{12,4},{16,24},{20,28},{24,16},{28,20},{1,9},{5... | collective-permute-start | bytes 3932168 | tf_op jit(solution)/shard_map/ppermute | solution.py:44
  127.5 22.4 %collective-permute-start.19 = (bf16[128,2048]{1,0:T(8,128)(2,1)S(1)}, bf16[128,2048]{1,0:T(8,128)(2,1)S(1)}, u32[]{:S(2)}, u32[]{:S(2)}) collective-permute-start(bf16[128,2048]{1,0:T(8,128)(2,1)S(1)} %get-tuple-element.68), channel_id=1, source_target_pairs={{0,1},{1,0},{2,3},{3,2},{4,5},{5,4},{6,7},{7,6},{8,9},{9,8},{10,11... | collective-permute-start | bytes 1572872 | tf_op jit(solution)/shard_map/ppermute | solution.py:44
  129.7 20.3 %collective-permute-start.20 = (bf16[128,2048]{1,0:T(8,128)(2,1)S(1)}, bf16[128,2048]{1,0:T(8,128)(2,1)S(1)}, u32[]{:S(2)}, u32[]{:S(2)}) collective-permute-start(bf16[128,2048]{1,0:T(8,128)(2,1)S(1)} %add.18), channel_id=1, source_target_pairs={{0,2},{1,3},{2,0},{3,1},{4,6},{5,7},{6,4},{7,5},{8,10},{9,11},{10,... | collective-permute-start | bytes 1572872 | tf_op jit(solution)/shard_map/ppermute | solution.py:44
  150.2 8.0 %collective-permute-start.21 = (bf16[64,2048]{1,0:T(8,128)(2,1)S(1)}, bf16[64,2048]{1,0:T(8,128)(2,1)S(1)}, u32[]{:S(2)}, u32[]{:S(2)}) collective-permute-start(bf16[64,2048]{1,0:T(8,128)(2,1)S(1)} %add_convert_fusion), channel_id=1, source_target_pairs={{0,4},{4,0},{8,12},{12,8},{16,20},{20,16},{24,28},{28,24},{1,5},{5... | collective-permute-start | bytes 786440 | tf_op jit(solution)/shard_map/ppermute | solution.py:44
  156.5 1.7 %copy-start.1 = (bf16[64,4096]{1,0:T(8,128)(2,1)S(1)}, bf16[64,4096]{1,0:T(8,128)(2,1)}, u32[]{:S(2)}) copy-start(bf16[64,4096]{1,0:T(8,128)(2,1)} %tokens.3) | copy-start | bytes 1572868
  156.5 1.7 %copy-start.3 = (bf16[64,4096]{1,0:T(8,128)(2,1)S(1)}, bf16[64,4096]{1,0:T(8,128)(2,1)}, u32[]{:S(2)}) copy-start(bf16[64,4096]{1,0:T(8,128)(2,1)} %grad_out.3) | copy-start | bytes 1572868
  (4 other events, 3.8 us)

commit v13 on v12

--- a/solution.py
+++ b/solution.py
@@ -190,57 +190,66 @@
     return [*range(0, joint_width, 256), *range(joint_width, width, block)]
 
 
-def early_kernel(pieces, weights, size, joint_width, place, *refs):
+def early_kernel(pieces, weights, size, joint_width, outward, place, *refs):
     row_refs, weight_refs = refs[:pieces], refs[pieces : pieces + weights]
-    total, grads, normed = refs[pieces + weights :]
+    total, pair = refs[pieces + weights :]
     rows = row_refs[0].shape[0] // 2
-    block = weight_refs[0].shape[0]
-    halves = row_refs[: pieces // 2], row_refs[pieces // 2 :]
-    for pair, gathered in zip((grads, normed), halves):
-        for core in range(2):
-            for k in range(size):
-                target = (core * size + k) * rows
-                pair[target : target + rows] = pick(
-                    place[2], gathered, size, k, slice(core * rows, (core + 1) * rows)
-                )
-    for columns in column_steps(joint_width, total.shape[1], block):
-        for place_out, value in products(grads, normed, weight_refs, 0, joint_width, block, columns):
-            total[:, place_out] = value
-
-
-def late_kernel(first, joint_width, block, total, grads, normed, *refs):
+    block, width = weight_refs[0].shape
+    for core in range(2):
+        for k in range(size):
+            target = (core * size + k) * rows
+            pair[target : target + rows] = pick(
+                place[2], row_refs, size, k, slice(core * rows, (core + 1) * rows)
+            )
+    base = joint_width if outward else 0
+    for columns in range(joint_width, width, block) if outward else range(0, joint_width, 256):
+        for place_out, value in products(pair, pair, weight_refs, 0, joint_width, block, columns):
+            total[:, place_out.start - base : place_out.stop - base] = value
+
+
+def late_kernel(first, joint_width, block, joint_total, out_total, grads, normed, *refs):
     weight_refs, (keep, send) = refs[:-2], refs[-2:]
     length = keep.shape[0]
-    if not weight_refs:
-        keep[...] = total[:length]
-        send[...] = total[length:].astype(jnp.bfloat16)
+    for total, base in ((joint_total, 0), (out_total, joint_width)):
+        if not weight_refs:
+            columns = slice(base, base + total.shape[1])
+            keep[:, columns] = total[:length]
+            send[:, columns] = total[length:].astype(jnp.bfloat16)
     for columns in column_steps(joint_width, keep.shape[1], block) if weight_refs else []:
+        total, base = (joint_total, 0) if columns < joint_width else (out_total, joint_width)
         for place_out, value in products(
             grads, normed, weight_refs, first, joint_width, block, columns
         ):
-            keep[:, place_out] = total[:length, place_out] + value[:length]
-            send[:, place_out] = (total[length:, place_out] + value[length:]).astype(jnp.bfloat16)
-
-
-def project(place, pieces, early, late, size, joint_width):
-    rows = pieces[0].shape[0] // 2 * size
-    half = pieces[0].shape[1]
+            value = value + total[:, place_out.start - base : place_out.stop - base]
+            keep[:, place_out] = value[:length]
+            send[:, place_out] = value[length:].astype(jnp.bfloat16)
+
+
+def project(place, grad_pieces, normed_pieces, early, late, size, joint_width):
+    pair_rows, half = grad_pieces[0].shape
+    rows = pair_rows // 2 * size
     block, width = early[0].shape
     first = len(early) * block
-    total, grads, normed = call(
-        functools.partial(early_kernel, len(pieces), len(early), size, joint_width),
-        [shaped((2 * rows, width), jnp.float32)] + [shaped((2 * rows, half))] * 2,
-        [*pieces, *early],
-        [place],
-        flops=4 * rows * first * width,
-        megabytes=24,
-    )
+    totals, pairs = [], []
+    for pieces, outward in ((normed_pieces, False), (grad_pieces, True)):
+        columns = width - joint_width if outward else joint_width
+        total, pair = call(
+            functools.partial(
+                early_kernel, len(pieces), len(early), size, joint_width, outward
+            ),
+            [shaped((2 * rows, columns), jnp.float32), shaped((2 * rows, half))],
+            [*pieces, *early],
+            [place],
+            flops=4 * rows * first * columns,
+        )
+        totals.append(total)
+        pairs.append(pair)
+    normed, grads = pairs
     own, sent = call(
         functools.partial(late_kernel, first, joint_width, block),
         [shaped((rows, width), jnp.float32), shaped((rows, width))],
-        [total, grads, normed, *late],
+        [*totals, grads, normed, *late],
         flops=4 * rows * (half - first) * width,
-        megabytes=24,
     )
     return own, sent, normed
 
@@ -465,11 +474,13 @@
     )
     early, parts = gather_near(merged)
     late = gather_far(parts)
-    row_pieces = gather_tensor(jnp.concatenate([grad_keep, sent[:rows]], axis=0))
-    row_pieces += gather_tensor(
-        jnp.concatenate([normed_keep, sent[rows:]], axis=0), (*parts, *row_pieces[3:4])
-    )
-    own, sent, normed = project(place, row_pieces, early, late, tensor_size, joint_width)
+    grad_pieces = gather_tensor(jnp.concatenate([grad_keep, sent[:rows]], axis=0))
+    normed_pieces = gather_tensor(
+        jnp.concatenate([normed_keep, sent[rows:]], axis=0), (*parts, *grad_pieces[3:4])
+    )
+    own, sent, normed = project(
+        place, grad_pieces, normed_pieces, early, late, tensor_size, joint_width
+    )
     sent = swap(sent, "dp", 1)
     if levels:
         joined = (own + sent.astype(jnp.float32)).astype(jnp.bfloat16)

time: 161 us -> 161 us (level)
  waiting for transfers between devices: 77.2 us -> 74.5 us
  Pallas kernels: 25.8 us -> 28.4 us
    ppermute x12, waiting for transfers between devices: 40.9 us -> 36.2 us  [along(): return lax.ppermute(value, 'tensor', pairs)]
    pallas_call x8 -> x9, Pallas kernels: 19.4 us -> 22 us  [call(): pl.pallas_call(kernel, out_shape=outs, in_specs=[SCALARS] * len(scalars)...]
    ppermute x14, waiting for transfers between devices: 36.3 us -> 38.3 us  [swap(): return lax.ppermute(value, axis, pairs)]
  transfers between devices with their start and end apart: 26 -> 26, of which waited for: 14 -> 14; matrix products, arithmetic and copies ran while one was open for 4% -> 4% of each run, Pallas kernels for 10% -> 12%
where the time goes in v13:
time: 161 us; the launch traced here: 160 us
  waiting for transfers between devices  74.5 us (46%)
  starting transfers between devices  44.9 us (28%)
  Pallas kernels  28.4 us (18%)
  local copies, waits for them, and re-layouts  8.76 us (5%)
  other arithmetic  3.01 us (2%)
    ppermute x14, waiting for transfers between devices, swap(): return lax.ppermute(value, axis, pairs)  38.3 us
    ppermute x12, waiting for transfers between devices, along(): return lax.ppermute(value, 'tensor', pairs)  36.2 us
    ppermute x12, starting transfers between devices, along(): return lax.ppermute(value, 'tensor', pairs)  25.5 us
    pallas_call x9, Pallas kernels, call(): pl.pallas_call(kernel, out_shape=outs, in_specs=[SCALARS] * len(scalars)...  22 us
    ppermute x14, starting transfers between devices, swap(): return lax.ppermute(value, axis, pairs)  19.4 us
    unnamed x20, local copies, waits for them, and re-layouts  5.23 us
    pallas_call x1, Pallas kernels, row_terms(): pl.pallas_call(functools.partial(row_kernel, len(weights)), grid=(1,), ou...  4.69 us
  transfers between devices with their start and end apart: 26, of which 14 were waited for; matrix products, arithmetic and copies ran while one was open for 4% of the time, Pallas kernels for 12%

profile of v13, /device:TPU:1, one launch (start us, length us, event | category | flops | bytes accessed | tf_op | source)
XLA Modules:
  0.0 160.4 jit_solution(16690221248254782270)
XLA Ops:
  7.1 2.6 %collective-permute-start.6 = (bf16[512,2304]{1,0:T(8,128)(2,1)S(1)}, bf16[512,2304]{1,0:T(8,128)(2,1)}, u32[]{:S(2)}, u32[]{:S(2)}) collective-permute-start(bf16[512,2304]{1,0:T(8,128)(2,1)S(1)} %shard_map.95.refs_6_.refs_0_), channel_id=1, source_target_pairs={{0,16},{4,20},{8,24},{12,28},{16,0},{20,4},{24,8},{28,12},{1,17},{... | collective-permute-start | bytes 7077896 | tf_op jit(solution)/shard_map/ppermute | solution.py:44
  12.3 4.0 %collective-permute-start.7 = (bf16[128,2048]{1,0:T(8,128)(2,1)S(1)}, bf16[128,2048]{1,0:T(8,128)(2,1)S(1)}, u32[]{:S(2)}, u32[]{:S(2)}) collective-permute-start(bf16[128,2048]{1,0:T(8,128)(2,1)S(1)} %pad_maximum_fusion.3.refs_0_), channel_id=1, source_target_pairs={{0,1},{1,2},{2,3},{4,5},{5,6},{6,7},{8,9},{9,10},{10,11},{12,13},{... | collective-permute-start | bytes 1572872 | tf_op jit(solution)/shard_map/ppermute | solution.py:71
  16.4 1.3 collective-permute-start.2
  17.7 8.0 %collective-permute-done.8.refs_2_ = bf16[128,2048]{1,0:T(8,128)(2,1)} collective-permute-done((bf16[128,2048]{1,0:T(8,128)(2,1)S(1)}, bf16[128,2048]{1,0:T(8,128)(2,1)}, u32[]{:S(2)}, u32[]{:S(2)}) %collective-permute-start.8) | collective-permute-done | bytes 524320 | tf_op jit(solution)/shard_map/ppermute | solution.py:71
  25.7 4.0 %collective-permute-start.1 = (bf16[128,2048]{1,0:T(8,128)(2,1)S(1)}, bf16[128,2048]{1,0:T(8,128)(2,1)}, u32[]{:S(2)}, u32[]{:S(2)}) collective-permute-start(bf16[128,2048]{1,0:T(8,128)(2,1)S(1)} %pad_maximum_fusion.2.refs_0_), channel_id=1, source_target_pairs={{0,1},{1,2},{2,3},{4,5},{5,6},{6,7},{8,9},{9,10},{10,11},{12,13},{... | collective-permute-start | bytes 1572872 | tf_op jit(solution)/shard_map/ppermute | solution.py:71
  29.7 1.5 collective-permute-start.9
  32.0 4.9 %collective-permute-done.2.refs_2_ = bf16[128,2048]{1,0:T(8,128)(2,1)} collective-permute-done((bf16[128,2048]{1,0:T(8,128)(2,1)S(1)}, bf16[128,2048]{1,0:T(8,128)(2,1)}, u32[]{:S(2)}, u32[]{:S(2)}) %collective-permute-start.2) | collective-permute-done | bytes 524320 | tf_op jit(solution)/shard_map/ppermute | solution.py:71
  38.2 1.5 collective-permute-start.3
  41.0 9.9 %collective-permute-done.10.refs_4_ = bf16[128,2048]{1,0:T(8,128)(2,1)} collective-permute-done((bf16[128,2048]{1,0:T(8,128)(2,1)}, bf16[128,2048]{1,0:T(8,128)(2,1)}, u32[]{:S(2)}, u32[]{:S(2)}) %collective-permute-start.10) | collective-permute-done | bytes 524320 | tf_op jit(solution)/shard_map/ppermute | solution.py:71
  53.2 8.0 %collective-permute-done.6.refs_8_.refs_2_ = bf16[512,2304]{1,0:T(8,128)(2,1)} collective-permute-done((bf16[512,2304]{1,0:T(8,128)(2,1)S(1)}, bf16[512,2304]{1,0:T(8,128)(2,1)}, u32[]{:S(2)}, u32[]{:S(2)}) %collective-permute-start.6) | collective-permute-done | bytes 2359328 | tf_op jit(solution)/shard_map/ppermute | solution.py:44
  62.1 1.3 slice.43
  63.5 1.3 slice.44
  67.5 1.5 collective-permute-start.11
  69.0 4.8 %shard_map.97 = (f32[512,1024]{1,0:T(8,128)S(1)}, bf16[512,2048]{1,0:T(8,128)(2,1)S(1)}) custom-call(s32[3]{0:T(128)S(1)} %pad_add_fusion.place.refs_0_, bf16[128,2048]{1,0:T(8,128)(2,1)S(1)} %pad_maximum_fusion.3.refs_0_, bf16[128,2048]{1,0:T(8,128)(2,1)S(1)} %copy-done.7, bf16[128,2048]{1,0:T(8,128)(2,1)} %collective-permute-done.8.refs_2_, ...), custom_call_target="tpu_custom_call" | custom-call | flops 1610612736 | bytes 14417920 | tf_op jit(solution)/shard_map/pallas_call | solution.py:23
  73.8 9.6 %collective-permute-done.11.refs_5_ = bf16[128,2048]{1,0:T(8,128)(2,1)S(1)} collective-permute-done((bf16[128,2048]{1,0:T(8,128)(2,1)S(1)}, bf16[128,2048]{1,0:T(8,128)(2,1)S(1)}, u32[]{:S(2)}, u32[]{:S(2)}) %collective-permute-start.11) | collective-permute-done | bytes 524320 | tf_op jit(solution)/shard_map/ppermute | solution.py:71
  83.4 5.4 %shard_map.96 = (f32[512,1280]{1,0:T(8,128)S(1)}, bf16[512,2048]{1,0:T(8,128)(2,1)S(1)}) custom-call(s32[3]{0:T(128)S(1)} %pad_add_fusion.place.refs_0_, bf16[128,2048]{1,0:T(8,128)(2,1)S(1)} %pad_maximum_fusion.2.refs_0_, bf16[128,2048]{1,0:T(8,128)(2,1)} %collective-permute-done.1.refs_1_, bf16[128,2048]{1,0:T(8,128)(2,1)} %collective-permute-done.2.refs_2_, ...), custom_call_target="tpu_custom_call" | custom-call | flops 2013265920 | bytes 14942208 | tf_op jit(solution)/shard_map/pallas_call | solution.py:23
  88.8 2.2 %collective-permute-done.14.refs_1_.refs_4_ = bf16[256,2304]{1,0:T(8,128)(2,1)S(1)} collective-permute-done((bf16[256,2304]{1,0:T(8,128)(2,1)S(1)}, bf16[256,2304]{1,0:T(8,128)(2,1)S(1)}, u32[]{:S(2)}, u32[]{:S(2)}) %collective-permute-start.14) | collective-permute-done | bytes 1179680 | tf_op jit(solution)/shard_map/ppermute | solution.py:44
  91.9 1.4 shard_map.98
  93.3 2.6 %collective-permute-start.15 = (bf16[256,2304]{1,0:T(8,128)(2,1)S(1)}, bf16[256,2304]{1,0:T(8,128)(2,1)S(1)}, u32[]{:S(2)}, u32[]{:S(2)}) collective-permute-start(bf16[256,2304]{1,0:T(8,128)(2,1)S(1)} %get-tuple-element.64), channel_id=1, source_target_pairs={{0,4},{4,0},{8,12},{12,8},{16,20},{20,16},{24,28},{28,24},{1,5},{5... | collective-permute-start | bytes 3538952 | tf_op jit(solution)/shard_map/ppermute | solution.py:44
  95.9 2.5 %collective-permute-done.15.refs_3_ = bf16[256,2304]{1,0:T(8,128)(2,1)S(1)} collective-permute-done((bf16[256,2304]{1,0:T(8,128)(2,1)S(1)}, bf16[256,2304]{1,0:T(8,128)(2,1)S(1)}, u32[]{:S(2)}, u32[]{:S(2)}) %collective-permute-start.15) | collective-permute-done | bytes 1179680 | tf_op jit(solution)/shard_map/ppermute | solution.py:44
  98.4 4.0 %shard_map.99.own = bf16[256,1280]{1,0:T(8,128)(2,1)S(1)} custom-call(s32[3]{0:T(128)S(1)} %pad_add_fusion.place.refs_0_, s32[1,4]{1,0:T(1,128)S(1)} %copy-done.9, f32[256,2304]{1,0:T(8,128)S(1)} %get-tuple-element.63.refs_2_, bf16[256,2304]{1,0:T(8,128)(2,1)S(1)} %collective-permute-done.15.refs_3_), custom_call_target="tpu_custom_call" | custom-call | flops 671088640 | bytes 4194304 | tf_op jit(solution)/shard_map/pallas_call | solution.py:23
  102.9 1.7 %collective-permute-done.16.other = bf16[256,1280]{1,0:T(8,128)(2,1)S(1)} collective-permute-done((bf16[256,1280]{1,0:T(8,128)(2,1)S(1)}, bf16[256,1280]{1,0:T(8,128)(2,1)S(1)}, u32[]{:S(2)}, u32[]{:S(2)}) %collective-permute-start.16) | collective-permute-done | bytes 655392 | tf_op jit(solution)/shard_map/ppermute | solution.py:44
  106.3 4.7 %shard_map.100 = (bf16[128,2048]{1,0:T(8,128)(2,1)S(1)}, bf16[128,2048]{1,0:T(8,128)(2,1)S(1)}, bf16[128,2048]{1,0:T(8,128)(2,1)S(1)}, bf16[128,2048]{1,0:T(8,128)(2,1)S(1)}) custom-call(bf16[256,1280]{1,0:T(8,128)(2,1)S(1)} %shard_map.99.own, bf16[256,1280]{1,0:T(8,128)(2,1)S(1)} %collective-permute-done.16.other, ...), custom_call_target="tpu_custom_call" | custom-call | flops 2684354560 | bytes 8650752 | tf_op jit(solution)/shard_map/pallas_call | solution.py:376
  111.7 5.9 %collective-permute-start.17 = (bf16[128,2048]{1,0:T(8,128)(2,1)S(1)}, bf16[128,2048]{1,0:T(8,128)(2,1)S(1)}, u32[]{:S(2)}, u32[]{:S(2)}) collective-permute-start(bf16[128,2048]{1,0:T(8,128)(2,1)S(1)} %get-tuple-element.67), channel_id=1, source_target_pairs={{3,2},{0,1},{7,6},{4,5},{11,10},{8,9},{15,14},{12,13},{19,18},{16,... | collective-permute-start | bytes 1572872 | tf_op jit(solution)/shard_map/ppermute | solution.py:71
  117.6 2.2 %shard_map.101 = (bf16[512,1280]{1,0:T(8,128)(2,1)S(1)}, bf16[512,1280]{1,0:T(8,128)(2,1)S(1)}, bf16[512,1280]{1,0:T(8,128)(2,1)S(1)}) custom-call(bf16[512,2048]{1,0:T(8,128)(2,1)S(1)} %get-tuple-element.62.normed.pair, bf16[256,1280]{1,0:T(8,128)(2,1)S(1)} %shard_map.99.own, bf16[256,1280]{1,0:T(8,128)(2,1)S(1)} %collective-permute-done.16.other), custom_call_target="tpu_custom_call" | custom-call | flops 2013265920 | bytes 7340032 | tf_op jit(solution)/shard_map/pallas_call | solution.py:23
  119.8 1.7 %collective-permute-done.24 = bf16[256,1280]{1,0:T(8,128)(2,1)S(1)} collective-permute-done((bf16[256,1280]{1,0:T(8,128)(2,1)S(1)}, bf16[256,1280]{1,0:T(8,128)(2,1)S(1)}, u32[]{:S(2)}, u32[]{:S(2)}) %collective-permute-start.24) | collective-permute-done | bytes 655392 | tf_op jit(solution)/shard_map/ppermute | solution.py:44
  123.6 3.7 %collective-permute-done.17 = bf16[128,2048]{1,0:T(8,128)(2,1)S(1)} collective-permute-done((bf16[128,2048]{1,0:T(8,128)(2,1)S(1)}, bf16[128,2048]{1,0:T(8,128)(2,1)S(1)}, u32[]{:S(2)}, u32[]{:S(2)}) %collective-permute-start.17) | collective-permute-done | bytes 524320 | tf_op jit(solution)/shard_map/ppermute | solution.py:71
  127.4 2.3 %collective-permute-start.19 = (bf16[128,2048]{1,0:T(8,128)(2,1)S(1)}, bf16[128,2048]{1,0:T(8,128)(2,1)S(1)}, u32[]{:S(2)}, u32[]{:S(2)}) collective-permute-start(bf16[128,2048]{1,0:T(8,128)(2,1)S(1)} %get-tuple-element.70), channel_id=1, source_target_pairs={{0,1},{1,0},{2,3},{3,2},{4,5},{5,4},{6,7},{7,6},{8,9},{9,8},{10,11... | collective-permute-start | bytes 1572872 | tf_op jit(solution)/shard_map/ppermute | solution.py:44
  129.7 20.1 %collective-permute-done.19.refs_1_ = bf16[128,2048]{1,0:T(8,128)(2,1)S(1)} collective-permute-done((bf16[128,2048]{1,0:T(8,128)(2,1)S(1)}, bf16[128,2048]{1,0:T(8,128)(2,1)S(1)}, u32[]{:S(2)}, u32[]{:S(2)}) %collective-permute-start.19) | collective-permute-done | bytes 524320 | tf_op jit(solution)/shard_map/ppermute | solution.py:44
  150.2 6.3 %collective-permute-start.21 = (bf16[64,2048]{1,0:T(8,128)(2,1)S(1)}, bf16[64,2048]{1,0:T(8,128)(2,1)S(1)}, u32[]{:S(2)}, u32[]{:S(2)}) collective-permute-start(bf16[64,2048]{1,0:T(8,128)(2,1)S(1)} %add_convert_fusion), channel_id=1, source_target_pairs={{0,4},{4,0},{8,12},{12,8},{16,20},{20,16},{24,28},{28,24},{1,5},{5... | collective-permute-start | bytes 786440 | tf_op jit(solution)/shard_map/ppermute | solution.py:44
  156.5 1.7 %shard_map.103 = (f32[512,1024]{1,0:T(8,128)}, f32[512,256]{1,0:T(8,128)}) custom-call(bf16[512,1280]{1,0:T(8,128)(2,1)S(1)} %get-tuple-element.73.refs_0_, bf16[512,1280]{1,0:T(8,128)(2,1)S(1)} %collective-permute-done.23.refs_1_, bf16[512,1280]{1,0:T(8,128)(2,1)S(1)} %collective-permute-done.25.refs_2_), custom_call_target="tpu_custom_call" | custom-call | bytes 6553600 | tf_op jit(solution)/shard_map/pallas_call | solution.py:407
  158.2 2.2 %shard_map.104 = bf16[64,4096]{1,0:T(8,128)(2,1)} custom-call(s32[3]{0:T(128)S(1)} %pad_add_fusion.place.refs_0_, bf16[64,4096]{1,0:T(8,128)(2,1)S(1)} %copy-done.1, bf16[1,4096]{1,0:T(2,128)(2,1)S(1)} %reshape.9.gain, bf16[64,4096]{1,0:T(8,128)(2,1)S(1)} %copy-done.3, bf16[64,2048]{1,0:T(8,128)(2,1)S(1)} %collective-permute-done.21.handed, ...), custom_call_target="tpu_custom_call" | custom-call | bytes 3940352 | tf_op jit(solution)/shard_map/pallas_call | solution.py:23
  (66 shorter events, 24.6 us)
Async XLA Ops:
  3.5 1.2 copy-start.4
  4.5 6.4 %collective-permute-start = (bf16[128,2048]{1,0:T(8,128)(2,1)S(1)}, bf16[128,2048]{1,0:T(8,128)(2,1)S(1)}, u32[]{:S(2)}, u32[]{:S(2)}) collective-permute-start(bf16[128,2048]{1,0:T(8,128)(2,1)S(1)} %get-tuple-element.44), channel_id=1, source_target_pairs={{0,4},{4,0},{8,12},{12,8},{16,20},{20,16},{24,28},{28,24},{1,5},{5... | collective-permute-start | bytes 1572872 | tf_op jit(solution)/shard_map/ppermute | solution.py:44
  4.7 1.2 copy-start.5
  7.1 54.2 %collective-permute-start.6 = (bf16[512,2304]{1,0:T(8,128)(2,1)S(1)}, bf16[512,2304]{1,0:T(8,128)(2,1)}, u32[]{:S(2)}, u32[]{:S(2)}) collective-permute-start(bf16[512,2304]{1,0:T(8,128)(2,1)S(1)} %shard_map.95.refs_6_.refs_0_), channel_id=1, source_target_pairs={{0,16},{4,20},{8,24},{12,28},{16,0},{20,4},{24,8},{28,12},{1,17},{... | collective-permute-start | bytes 7077896 | tf_op jit(solution)/shard_map/ppermute | solution.py:44
  9.7 52.4 %collective-permute-start.5 = (bf16[512,2304]{1,0:T(8,128)(2,1)S(1)}, bf16[512,2304]{1,0:T(8,128)(2,1)}, u32[]{:S(2)}, u32[]{:S(2)}) collective-permute-start(bf16[512,2304]{1,0:T(8,128)(2,1)S(1)} %shard_map.95.refs_6_.refs_0_), channel_id=1, source_target_pairs={{0,8},{4,12},{8,0},{12,4},{16,24},{20,28},{24,16},{28,20},{1,9},{5... | collective-permute-start | bytes 7077896 | tf_op jit(solution)/shard_map/ppermute | solution.py:44
  11.0 14.7 %collective-permute-start.8 = (bf16[128,2048]{1,0:T(8,128)(2,1)S(1)}, bf16[128,2048]{1,0:T(8,128)(2,1)}, u32[]{:S(2)}, u32[]{:S(2)}) collective-permute-start(bf16[128,2048]{1,0:T(8,128)(2,1)S(1)} %pad_maximum_fusion.3.refs_0_), channel_id=1, source_target_pairs={{1,0},{2,1},{3,2},{5,4},{6,5},{7,6},{9,8},{10,9},{11,10},{13,12},{... | collective-permute-start | bytes 1572872 | tf_op jit(solution)/shard_map/ppermute | solution.py:71
  12.3 17.4 %collective-permute-start.7 = (bf16[128,2048]{1,0:T(8,128)(2,1)S(1)}, bf16[128,2048]{1,0:T(8,128)(2,1)S(1)}, u32[]{:S(2)}, u32[]{:S(2)}) collective-permute-start(bf16[128,2048]{1,0:T(8,128)(2,1)S(1)} %pad_maximum_fusion.3.refs_0_), channel_id=1, source_target_pairs={{0,1},{1,2},{2,3},{4,5},{5,6},{6,7},{8,9},{9,10},{10,11},{12,13},{... | collective-permute-start | bytes 1572872 | tf_op jit(solution)/shard_map/ppermute | solution.py:71
  16.4 20.5 %collective-permute-start.2 = (bf16[128,2048]{1,0:T(8,128)(2,1)S(1)}, bf16[128,2048]{1,0:T(8,128)(2,1)}, u32[]{:S(2)}, u32[]{:S(2)}) collective-permute-start(bf16[128,2048]{1,0:T(8,128)(2,1)S(1)} %pad_maximum_fusion.2.refs_0_), channel_id=1, source_target_pairs={{1,0},{2,1},{3,2},{5,4},{6,5},{7,6},{9,8},{10,9},{11,10},{13,12},{... | collective-permute-start | bytes 1572872 | tf_op jit(solution)/shard_map/ppermute | solution.py:71
  25.7 12.5 %collective-permute-start.1 = (bf16[128,2048]{1,0:T(8,128)(2,1)S(1)}, bf16[128,2048]{1,0:T(8,128)(2,1)}, u32[]{:S(2)}, u32[]{:S(2)}) collective-permute-start(bf16[128,2048]{1,0:T(8,128)(2,1)S(1)} %pad_maximum_fusion.2.refs_0_), channel_id=1, source_target_pairs={{0,1},{1,2},{2,3},{4,5},{5,6},{6,7},{8,9},{9,10},{10,11},{12,13},{... | collective-permute-start | bytes 1572872 | tf_op jit(solution)/shard_map/ppermute | solution.py:71
  29.7 10.0 %collective-permute-start.9 = (bf16[128,2048]{1,0:T(8,128)(2,1)S(1)}, bf16[128,2048]{1,0:T(8,128)(2,1)}, u32[]{:S(2)}, u32[]{:S(2)}) collective-permute-start(bf16[128,2048]{1,0:T(8,128)(2,1)S(1)} %collective-permute-done.7.refs_1_), channel_id=1, source_target_pairs={{1,2},{2,3},{5,6},{6,7},{9,10},{10,11},{13,14},{14,15},{17,18},{18... | collective-permute-start | bytes 1572872 | tf_op jit(solution)/shard_map/ppermute | solution.py:71
  36.9 14.0 %collective-permute-start.10 = (bf16[128,2048]{1,0:T(8,128)(2,1)}, bf16[128,2048]{1,0:T(8,128)(2,1)}, u32[]{:S(2)}, u32[]{:S(2)}) collective-permute-start(bf16[128,2048]{1,0:T(8,128)(2,1)} %collective-permute-done.8.refs_2_), channel_id=1, source_target_pairs={{1,0},{2,1},{5,4},{6,5},{9,8},{10,9},{13,12},{14,13},{17,16},{18,1... | collective-permute-start | bytes 1572872 | tf_op jit(solution)/shard_map/ppermute | solution.py:71
  38.2 28.2 %collective-permute-start.3 = (bf16[128,2048]{1,0:T(8,128)(2,1)}, bf16[128,2048]{1,0:T(8,128)(2,1)}, u32[]{:S(2)}, u32[]{:S(2)}) collective-permute-start(bf16[128,2048]{1,0:T(8,128)(2,1)} %collective-permute-done.1.refs_1_), channel_id=1, source_target_pairs={{1,2},{2,3},{5,6},{6,7},{9,10},{10,11},{13,14},{14,15},{17,18},{18... | collective-permute-start | bytes 1572872 | tf_op jit(solution)/shard_map/ppermute | solution.py:71
  39.7 26.8 %collective-permute-start.4 = (bf16[128,2048]{1,0:T(8,128)(2,1)}, bf16[128,2048]{1,0:T(8,128)(2,1)}, u32[]{:S(2)}, u32[]{:S(2)}) collective-permute-start(bf16[128,2048]{1,0:T(8,128)(2,1)} %collective-permute-done.2.refs_2_), channel_id=1, source_target_pairs={{1,0},{2,1},{5,4},{6,5},{9,8},{10,9},{13,12},{14,13},{17,16},{18,1... | collective-permute-start | bytes 1572872 | tf_op jit(solution)/shard_map/ppermute | solution.py:71
  52.0 17.1 %collective-permute-start.12 = (bf16[128,2048]{1,0:T(8,128)(2,1)S(1)}, bf16[128,2048]{1,0:T(8,128)(2,1)S(1)}, u32[]{:S(2)}, u32[]{:S(2)}) collective-permute-start(bf16[128,2048]{1,0:T(8,128)(2,1)S(1)} %broadcast_select_fusion), channel_id=1, source_target_pairs={{1,0},{2,3},{5,4},{6,7},{9,8},{10,11},{13,12},{14,15},{17,16},{18,... | collective-permute-start | bytes 1572872 | tf_op jit(solution)/shard_map/ppermute | solution.py:71
  64.8 4.2 %copy-start.7 = (bf16[128,2048]{1,0:T(8,128)(2,1)S(1)}, bf16[128,2048]{1,0:T(8,128)(2,1)}, u32[]{:S(2)}) copy-start(bf16[128,2048]{1,0:T(8,128)(2,1)} %copy-done.6) | copy-start | bytes 1572868
  64.8 26.2 %collective-permute-start.14 = (bf16[256,2304]{1,0:T(8,128)(2,1)S(1)}, bf16[256,2304]{1,0:T(8,128)(2,1)S(1)}, u32[]{:S(2)}, u32[]{:S(2)}) collective-permute-start(bf16[256,2304]{1,0:T(8,128)(2,1)S(1)} %slice.44), channel_id=1, source_target_pairs={{0,8},{4,12},{8,0},{12,4},{16,24},{20,28},{24,16},{28,20},{1,9},{5... | collective-permute-start | bytes 3538952 | tf_op jit(solution)/shard_map/ppermute | solution.py:44
  66.1 25.8 %collective-permute-start.13 = (bf16[256,2304]{1,0:T(8,128)(2,1)S(1)}, bf16[256,2304]{1,0:T(8,128)(2,1)S(1)}, u32[]{:S(2)}, u32[]{:S(2)}) collective-permute-start(bf16[256,2304]{1,0:T(8,128)(2,1)S(1)} %slice.43), channel_id=1, source_target_pairs={{0,16},{4,20},{8,24},{12,28},{16,0},{20,4},{24,8},{28,12},{1,17},{... | collective-permute-start | bytes 3538952 | tf_op jit(solution)/shard_map/ppermute | solution.py:44
  67.5 15.9 %collective-permute-start.11 = (bf16[128,2048]{1,0:T(8,128)(2,1)S(1)}, bf16[128,2048]{1,0:T(8,128)(2,1)S(1)}, u32[]{:S(2)}, u32[]{:S(2)}) collective-permute-start(bf16[128,2048]{1,0:T(8,128)(2,1)S(1)} %broadcast_select_fusion.1), channel_id=1, source_target_pairs={{1,0},{2,3},{5,4},{6,7},{9,8},{10,11},{13,12},{14,15},{17,16},{18,... | collective-permute-start | bytes 1572872 | tf_op jit(solution)/shard_map/ppermute | solution.py:71
  91.9 6.5 %copy-start.9 = (s32[1,4]{1,0:T(1,128)S(1)}, s32[1,4]{1,0:T(1,128)}, u32[]{:S(2)}) copy-start(s32[1,4]{1,0:T(1,128)} %refs_1_.1) | copy-start | bytes 52
  93.3 5.1 %collective-permute-start.15 = (bf16[256,2304]{1,0:T(8,128)(2,1)S(1)}, bf16[256,2304]{1,0:T(8,128)(2,1)S(1)}, u32[]{:S(2)}, u32[]{:S(2)}) collective-permute-start(bf16[256,2304]{1,0:T(8,128)(2,1)S(1)} %get-tuple-element.64), channel_id=1, source_target_pairs={{0,4},{4,0},{8,12},{12,8},{16,20},{20,16},{24,28},{28,24},{1,5},{5... | collective-permute-start | bytes 3538952 | tf_op jit(solution)/shard_map/ppermute | solution.py:44
  102.4 2.2 %collective-permute-start.16 = (bf16[256,1280]{1,0:T(8,128)(2,1)S(1)}, bf16[256,1280]{1,0:T(8,128)(2,1)S(1)}, u32[]{:S(2)}, u32[]{:S(2)}) collective-permute-start(bf16[256,1280]{1,0:T(8,128)(2,1)S(1)} %shard_map.99.own), channel_id=1, source_target_pairs={{0,4},{4,0},{8,12},{12,8},{16,20},{20,16},{24,28},{28,24},{1,5},{5... | collective-permute-start | bytes 1966088 | tf_op jit(solution)/shard_map/ppermute | solution.py:44
  105.6 16.0 %collective-permute-start.24 = (bf16[256,1280]{1,0:T(8,128)(2,1)S(1)}, bf16[256,1280]{1,0:T(8,128)(2,1)S(1)}, u32[]{:S(2)}, u32[]{:S(2)}) collective-permute-start(bf16[256,1280]{1,0:T(8,128)(2,1)S(1)} %get-tuple-element.83), channel_id=1, source_target_pairs={{0,8},{4,12},{8,0},{12,4},{16,24},{20,28},{24,16},{28,20},{1,9},{5... | collective-permute-start | bytes 1966088 | tf_op jit(solution)/shard_map/ppermute | solution.py:44
  105.9 15.7 %collective-permute-start.22 = (bf16[256,1280]{1,0:T(8,128)(2,1)S(1)}, bf16[256,1280]{1,0:T(8,128)(2,1)S(1)}, u32[]{:S(2)}, u32[]{:S(2)}) collective-permute-start(bf16[256,1280]{1,0:T(8,128)(2,1)S(1)} %get-tuple-element.84), channel_id=1, source_target_pairs={{0,16},{4,20},{8,24},{12,28},{16,0},{20,4},{24,8},{28,12},{1,17},{... | collective-permute-start | bytes 1966088 | tf_op jit(solution)/shard_map/ppermute | solution.py:44
  111.0 12.6 %collective-permute-start.18 = (bf16[128,2048]{1,0:T(8,128)(2,1)S(1)}, bf16[128,2048]{1,0:T(8,128)(2,1)S(1)}, u32[]{:S(2)}, u32[]{:S(2)}) collective-permute-start(bf16[128,2048]{1,0:T(8,128)(2,1)S(1)} %get-tuple-element.67), channel_id=1, source_target_pairs={{1,2},{2,1},{5,6},{6,5},{9,10},{10,9},{13,14},{14,13},{17,18},{18,... | collective-permute-start | bytes 1572872 | tf_op jit(solution)/shard_map/ppermute | solution.py:71
  111.7 15.6 %collective-permute-start.17 = (bf16[128,2048]{1,0:T(8,128)(2,1)S(1)}, bf16[128,2048]{1,0:T(8,128)(2,1)S(1)}, u32[]{:S(2)}, u32[]{:S(2)}) collective-permute-start(bf16[128,2048]{1,0:T(8,128)(2,1)S(1)} %get-tuple-element.67), channel_id=1, source_target_pairs={{3,2},{0,1},{7,6},{4,5},{11,10},{8,9},{15,14},{12,13},{19,18},{16,... | collective-permute-start | bytes 1572872 | tf_op jit(solution)/shard_map/ppermute | solution.py:71
  121.9 34.5 %collective-permute-start.25 = (bf16[512,1280]{1,0:T(8,128)(2,1)S(1)}, bf16[512,1280]{1,0:T(8,128)(2,1)S(1)}, u32[]{:S(2)}, u32[]{:S(2)}) collective-permute-start(bf16[512,1280]{1,0:T(8,128)(2,1)S(1)} %pad_maximum_fusion.1), channel_id=1, source_target_pairs={{0,16},{4,20},{8,24},{12,28},{16,0},{20,4},{24,8},{28,12},{1,17},{... | collective-permute-start | bytes 3932168 | tf_op jit(solution)/shard_map/ppermute | solution.py:44
  122.4 34.0 %collective-permute-start.23 = (bf16[512,1280]{1,0:T(8,128)(2,1)S(1)}, bf16[512,1280]{1,0:T(8,128)(2,1)S(1)}, u32[]{:S(2)}, u32[]{:S(2)}) collective-permute-start(bf16[512,1280]{1,0:T(8,128)(2,1)S(1)} %pad_maximum_fusion), channel_id=1, source_target_pairs={{0,8},{4,12},{8,0},{12,4},{16,24},{20,28},{24,16},{28,20},{1,9},{5... | collective-permute-start | bytes 3932168 | tf_op jit(solution)/shard_map/ppermute | solution.py:44
  127.4 22.3 %collective-permute-start.19 = (bf16[128,2048]{1,0:T(8,128)(2,1)S(1)}, bf16[128,2048]{1,0:T(8,128)(2,1)S(1)}, u32[]{:S(2)}, u32[]{:S(2)}) collective-permute-start(bf16[128,2048]{1,0:T(8,128)(2,1)S(1)} %get-tuple-element.70), channel_id=1, source_target_pairs={{0,1},{1,0},{2,3},{3,2},{4,5},{5,4},{6,7},{7,6},{8,9},{9,8},{10,11... | collective-permute-start | bytes 1572872 | tf_op jit(solution)/shard_map/ppermute | solution.py:44
  129.7 20.3 %collective-permute-start.20 = (bf16[128,2048]{1,0:T(8,128)(2,1)S(1)}, bf16[128,2048]{1,0:T(8,128)(2,1)S(1)}, u32[]{:S(2)}, u32[]{:S(2)}) collective-permute-start(bf16[128,2048]{1,0:T(8,128)(2,1)S(1)} %add.18), channel_id=1, source_target_pairs={{0,2},{1,3},{2,0},{3,1},{4,6},{5,7},{6,4},{7,5},{8,10},{9,11},{10,... | collective-permute-start | bytes 1572872 | tf_op jit(solution)/shard_map/ppermute | solution.py:44
  150.2 8.0 %collective-permute-start.21 = (bf16[64,2048]{1,0:T(8,128)(2,1)S(1)}, bf16[64,2048]{1,0:T(8,128)(2,1)S(1)}, u32[]{:S(2)}, u32[]{:S(2)}) collective-permute-start(bf16[64,2048]{1,0:T(8,128)(2,1)S(1)} %add_convert_fusion), channel_id=1, source_target_pairs={{0,4},{4,0},{8,12},{12,8},{16,20},{20,16},{24,28},{28,24},{1,5},{5... | collective-permute-start | bytes 786440 | tf_op jit(solution)/shard_map/ppermute | solution.py:44
  156.4 1.7 %copy-start.1 = (bf16[64,4096]{1,0:T(8,128)(2,1)S(1)}, bf16[64,4096]{1,0:T(8,128)(2,1)}, u32[]{:S(2)}) copy-start(bf16[64,4096]{1,0:T(8,128)(2,1)} %tokens.3) | copy-start | bytes 1572868
  156.4 1.7 %copy-start.3 = (bf16[64,4096]{1,0:T(8,128)(2,1)S(1)}, bf16[64,4096]{1,0:T(8,128)(2,1)}, u32[]{:S(2)}) copy-start(bf16[64,4096]{1,0:T(8,128)(2,1)} %grad_out.3) | copy-start | bytes 1572868
  (4 other events, 3.8 us)

commit v14 on v13

--- a/solution.py
+++ b/solution.py
@@ -126,8 +126,8 @@
 def scatter_tensor(blocks):
     if len(blocks) != 4:
         return [blocks[0]] + [swap(blocks[k], "tensor", k) for k in range(1, len(blocks))]
-    outer, inner = outer_pair(blocks[3]), inner_pair(blocks[3])
-    outer, inner = tied(outer, inner)
+    inner, outer = inner_pair(blocks[3]), outer_pair(blocks[3])
+    inner, outer = tied(inner, outer)
     carried, adjacent = tied(blocks[2] + outer, blocks[1])
     two, one = swap(carried, "tensor", 2), swap(adjacent, "tensor", 1)
     return [blocks[0], one, inner, two]

time: 161 us -> 160 us (level)
    ppermute x12, waiting for transfers between devices: 36.2 us -> 33.3 us  [along(): return lax.ppermute(value, 'tensor', pairs)]
    ppermute x14, waiting for transfers between devices: 38.3 us -> 40.9 us  [swap(): return lax.ppermute(value, axis, pairs)]
    ppermute x12, starting transfers between devices: 25.5 us -> 23 us  [along(): return lax.ppermute(value, 'tensor', pairs)]
  transfers between devices with their start and end apart: 26 -> 26, of which waited for: 14 -> 13; matrix products, arithmetic and copies ran while one was open for 4% -> 4% of each run, Pallas kernels for 12% -> 12%
where the time goes in v14:
time: 160 us; the launch traced here: 159 us
  waiting for transfers between devices  74.1 us (46%)
  starting transfers between devices  43.6 us (27%)
  Pallas kernels  28.4 us (18%)
  local copies, waits for them, and re-layouts  8.76 us (5%)
  other arithmetic  3.01 us (2%)
    ppermute x14, waiting for transfers between devices, swap(): return lax.ppermute(value, axis, pairs)  40.9 us
    ppermute x12, waiting for transfers between devices, along(): return lax.ppermute(value, 'tensor', pairs)  33.3 us
    ppermute x12, starting transfers between devices, along(): return lax.ppermute(value, 'tensor', pairs)  23 us
    pallas_call x9, Pallas kernels, call(): pl.pallas_call(kernel, out_shape=outs, in_specs=[SCALARS] * len(scalars)...  22 us
    ppermute x14, starting transfers between devices, swap(): return lax.ppermute(value, axis, pairs)  20.6 us
    unnamed x20, local copies, waits for them, and re-layouts  5.23 us
    pallas_call x1, Pallas kernels, row_terms(): pl.pallas_call(functools.partial(row_kernel, len(weights)), grid=(1,), ou...  4.69 us
  transfers between devices with their start and end apart: 26, of which 13 were waited for; matrix products, arithmetic and copies ran while one was open for 4% of the time, Pallas kernels for 12%

profile of v14, /device:TPU:1, one launch (start us, length us, event | category | flops | bytes accessed | tf_op | source)
XLA Modules:
  0.0 158.8 jit_solution(13747278904653184349)
XLA Ops:
  7.1 2.6 %collective-permute-start.6 = (bf16[512,2304]{1,0:T(8,128)(2,1)S(1)}, bf16[512,2304]{1,0:T(8,128)(2,1)}, u32[]{:S(2)}, u32[]{:S(2)}) collective-permute-start(bf16[512,2304]{1,0:T(8,128)(2,1)S(1)} %shard_map.95.refs_6_.refs_0_), channel_id=1, source_target_pairs={{0,16},{4,20},{8,24},{12,28},{16,0},{20,4},{24,8},{28,12},{1,17},{... | collective-permute-start | bytes 7077896 | tf_op jit(solution)/shard_map/ppermute | solution.py:44
  11.0 1.3 collective-permute-start.8
  12.3 4.0 %collective-permute-start.7 = (bf16[128,2048]{1,0:T(8,128)(2,1)S(1)}, bf16[128,2048]{1,0:T(8,128)(2,1)S(1)}, u32[]{:S(2)}, u32[]{:S(2)}) collective-permute-start(bf16[128,2048]{1,0:T(8,128)(2,1)S(1)} %pad_maximum_fusion.3.refs_0_), channel_id=1, source_target_pairs={{0,1},{1,2},{2,3},{4,5},{5,6},{6,7},{8,9},{9,10},{10,11},{12,13},{... | collective-permute-start | bytes 1572872 | tf_op jit(solution)/shard_map/ppermute | solution.py:71
  16.4 1.3 collective-permute-start.2
  17.7 8.0 %collective-permute-done.8.refs_2_ = bf16[128,2048]{1,0:T(8,128)(2,1)} collective-permute-done((bf16[128,2048]{1,0:T(8,128)(2,1)S(1)}, bf16[128,2048]{1,0:T(8,128)(2,1)}, u32[]{:S(2)}, u32[]{:S(2)}) %collective-permute-start.8) | collective-permute-done | bytes 524320 | tf_op jit(solution)/shard_map/ppermute | solution.py:71
  25.7 4.0 %collective-permute-start.1 = (bf16[128,2048]{1,0:T(8,128)(2,1)S(1)}, bf16[128,2048]{1,0:T(8,128)(2,1)}, u32[]{:S(2)}, u32[]{:S(2)}) collective-permute-start(bf16[128,2048]{1,0:T(8,128)(2,1)S(1)} %pad_maximum_fusion.2.refs_0_), channel_id=1, source_target_pairs={{0,1},{1,2},{2,3},{4,5},{5,6},{6,7},{8,9},{9,10},{10,11},{12,13},{... | collective-permute-start | bytes 1572872 | tf_op jit(solution)/shard_map/ppermute | solution.py:71
  29.7 1.5 collective-permute-start.9
  32.0 4.9 %collective-permute-done.2.refs_2_ = bf16[128,2048]{1,0:T(8,128)(2,1)} collective-permute-done((bf16[128,2048]{1,0:T(8,128)(2,1)S(1)}, bf16[128,2048]{1,0:T(8,128)(2,1)}, u32[]{:S(2)}, u32[]{:S(2)}) %collective-permute-start.2) | collective-permute-done | bytes 524320 | tf_op jit(solution)/shard_map/ppermute | solution.py:71
  38.2 1.5 collective-permute-start.3
  41.0 9.9 %collective-permute-done.10.refs_4_ = bf16[128,2048]{1,0:T(8,128)(2,1)} collective-permute-done((bf16[128,2048]{1,0:T(8,128)(2,1)}, bf16[128,2048]{1,0:T(8,128)(2,1)}, u32[]{:S(2)}, u32[]{:S(2)}) %collective-permute-start.10) | collective-permute-done | bytes 524320 | tf_op jit(solution)/shard_map/ppermute | solution.py:71
  53.2 8.0 %collective-permute-done.6.refs_8_.refs_2_ = bf16[512,2304]{1,0:T(8,128)(2,1)} collective-permute-done((bf16[512,2304]{1,0:T(8,128)(2,1)S(1)}, bf16[512,2304]{1,0:T(8,128)(2,1)}, u32[]{:S(2)}, u32[]{:S(2)}) %collective-permute-start.6) | collective-permute-done | bytes 2359328 | tf_op jit(solution)/shard_map/ppermute | solution.py:44
  62.1 1.3 slice.43
  63.5 1.3 slice.44
  67.5 1.5 collective-permute-start.11
  69.0 4.8 %shard_map.97 = (f32[512,1024]{1,0:T(8,128)S(1)}, bf16[512,2048]{1,0:T(8,128)(2,1)S(1)}) custom-call(s32[3]{0:T(128)S(1)} %pad_add_fusion.place.refs_0_, bf16[128,2048]{1,0:T(8,128)(2,1)S(1)} %pad_maximum_fusion.3.refs_0_, bf16[128,2048]{1,0:T(8,128)(2,1)S(1)} %copy-done.7, bf16[128,2048]{1,0:T(8,128)(2,1)} %collective-permute-done.8.refs_2_, ...), custom_call_target="tpu_custom_call" | custom-call | flops 1610612736 | bytes 14417920 | tf_op jit(solution)/shard_map/pallas_call | solution.py:23
  73.8 9.6 %collective-permute-done.11.refs_5_ = bf16[128,2048]{1,0:T(8,128)(2,1)S(1)} collective-permute-done((bf16[128,2048]{1,0:T(8,128)(2,1)S(1)}, bf16[128,2048]{1,0:T(8,128)(2,1)S(1)}, u32[]{:S(2)}, u32[]{:S(2)}) %collective-permute-start.11) | collective-permute-done | bytes 524320 | tf_op jit(solution)/shard_map/ppermute | solution.py:71
  83.4 5.4 %shard_map.96 = (f32[512,1280]{1,0:T(8,128)S(1)}, bf16[512,2048]{1,0:T(8,128)(2,1)S(1)}) custom-call(s32[3]{0:T(128)S(1)} %pad_add_fusion.place.refs_0_, bf16[128,2048]{1,0:T(8,128)(2,1)S(1)} %pad_maximum_fusion.2.refs_0_, bf16[128,2048]{1,0:T(8,128)(2,1)} %collective-permute-done.1.refs_1_, bf16[128,2048]{1,0:T(8,128)(2,1)} %collective-permute-done.2.refs_2_, ...), custom_call_target="tpu_custom_call" | custom-call | flops 2013265920 | bytes 14942208 | tf_op jit(solution)/shard_map/pallas_call | solution.py:23
  88.8 2.2 %collective-permute-done.14.refs_1_.refs_4_ = bf16[256,2304]{1,0:T(8,128)(2,1)S(1)} collective-permute-done((bf16[256,2304]{1,0:T(8,128)(2,1)S(1)}, bf16[256,2304]{1,0:T(8,128)(2,1)S(1)}, u32[]{:S(2)}, u32[]{:S(2)}) %collective-permute-start.14) | collective-permute-done | bytes 1179680 | tf_op jit(solution)/shard_map/ppermute | solution.py:44
  91.9 1.4 shard_map.98
  93.3 2.6 %collective-permute-start.15 = (bf16[256,2304]{1,0:T(8,128)(2,1)S(1)}, bf16[256,2304]{1,0:T(8,128)(2,1)S(1)}, u32[]{:S(2)}, u32[]{:S(2)}) collective-permute-start(bf16[256,2304]{1,0:T(8,128)(2,1)S(1)} %get-tuple-element.64), channel_id=1, source_target_pairs={{0,4},{4,0},{8,12},{12,8},{16,20},{20,16},{24,28},{28,24},{1,5},{5... | collective-permute-start | bytes 3538952 | tf_op jit(solution)/shard_map/ppermute | solution.py:44
  95.9 2.5 %collective-permute-done.15.refs_3_ = bf16[256,2304]{1,0:T(8,128)(2,1)S(1)} collective-permute-done((bf16[256,2304]{1,0:T(8,128)(2,1)S(1)}, bf16[256,2304]{1,0:T(8,128)(2,1)S(1)}, u32[]{:S(2)}, u32[]{:S(2)}) %collective-permute-start.15) | collective-permute-done | bytes 1179680 | tf_op jit(solution)/shard_map/ppermute | solution.py:44
  98.4 4.0 %shard_map.99.own = bf16[256,1280]{1,0:T(8,128)(2,1)S(1)} custom-call(s32[3]{0:T(128)S(1)} %pad_add_fusion.place.refs_0_, s32[1,4]{1,0:T(1,128)S(1)} %copy-done.9, f32[256,2304]{1,0:T(8,128)S(1)} %get-tuple-element.63.refs_2_, bf16[256,2304]{1,0:T(8,128)(2,1)S(1)} %collective-permute-done.15.refs_3_), custom_call_target="tpu_custom_call" | custom-call | flops 671088640 | bytes 4194304 | tf_op jit(solution)/shard_map/pallas_call | solution.py:23
  102.9 1.7 %collective-permute-done.16.other = bf16[256,1280]{1,0:T(8,128)(2,1)S(1)} collective-permute-done((bf16[256,1280]{1,0:T(8,128)(2,1)S(1)}, bf16[256,1280]{1,0:T(8,128)(2,1)S(1)}, u32[]{:S(2)}, u32[]{:S(2)}) %collective-permute-start.16) | collective-permute-done | bytes 655392 | tf_op jit(solution)/shard_map/ppermute | solution.py:44
  106.3 4.7 %shard_map.100 = (bf16[128,2048]{1,0:T(8,128)(2,1)S(1)}, bf16[128,2048]{1,0:T(8,128)(2,1)S(1)}, bf16[128,2048]{1,0:T(8,128)(2,1)S(1)}, bf16[128,2048]{1,0:T(8,128)(2,1)S(1)}) custom-call(bf16[256,1280]{1,0:T(8,128)(2,1)S(1)} %shard_map.99.own, bf16[256,1280]{1,0:T(8,128)(2,1)S(1)} %collective-permute-done.16.other, ...), custom_call_target="tpu_custom_call" | custom-call | flops 2684354560 | bytes 8650752 | tf_op jit(solution)/shard_map/pallas_call | solution.py:376
  111.0 3.2 %collective-permute-start.18 = (bf16[128,2048]{1,0:T(8,128)(2,1)S(1)}, bf16[128,2048]{1,0:T(8,128)(2,1)S(1)}, u32[]{:S(2)}, u32[]{:S(2)}) collective-permute-start(bf16[128,2048]{1,0:T(8,128)(2,1)S(1)} %get-tuple-element.67), channel_id=1, source_target_pairs={{3,2},{0,1},{7,6},{4,5},{11,10},{8,9},{15,14},{12,13},{19,18},{16,... | collective-permute-start | bytes 1572872 | tf_op jit(solution)/shard_map/ppermute | solution.py:71
  115.1 2.2 %shard_map.101 = (bf16[512,1280]{1,0:T(8,128)(2,1)S(1)}, bf16[512,1280]{1,0:T(8,128)(2,1)S(1)}, bf16[512,1280]{1,0:T(8,128)(2,1)S(1)}) custom-call(bf16[512,2048]{1,0:T(8,128)(2,1)S(1)} %get-tuple-element.62.normed.pair, bf16[256,1280]{1,0:T(8,128)(2,1)S(1)} %shard_map.99.own, bf16[256,1280]{1,0:T(8,128)(2,1)S(1)} %collective-permute-done.16.other), custom_call_target="tpu_custom_call" | custom-call | flops 2013265920 | bytes 7340032 | tf_op jit(solution)/shard_map/pallas_call | solution.py:23
  117.3 4.3 %collective-permute-done.24 = bf16[256,1280]{1,0:T(8,128)(2,1)S(1)} collective-permute-done((bf16[256,1280]{1,0:T(8,128)(2,1)S(1)}, bf16[256,1280]{1,0:T(8,128)(2,1)S(1)}, u32[]{:S(2)}, u32[]{:S(2)}) %collective-permute-start.24) | collective-permute-done | bytes 655392 | tf_op jit(solution)/shard_map/ppermute | solution.py:44
  124.5 3.6 %collective-permute-start.19 = (bf16[128,2048]{1,0:T(8,128)(2,1)S(1)}, bf16[128,2048]{1,0:T(8,128)(2,1)S(1)}, u32[]{:S(2)}, u32[]{:S(2)}) collective-permute-start(bf16[128,2048]{1,0:T(8,128)(2,1)S(1)} %get-tuple-element.70), channel_id=1, source_target_pairs={{0,1},{1,0},{2,3},{3,2},{4,5},{5,4},{6,7},{7,6},{8,9},{9,8},{10,11... | collective-permute-start | bytes 1572872 | tf_op jit(solution)/shard_map/ppermute | solution.py:44
  129.2 20.4 %collective-permute-done.19.refs_1_ = bf16[128,2048]{1,0:T(8,128)(2,1)S(1)} collective-permute-done((bf16[128,2048]{1,0:T(8,128)(2,1)S(1)}, bf16[128,2048]{1,0:T(8,128)(2,1)S(1)}, u32[]{:S(2)}, u32[]{:S(2)}) %collective-permute-start.19) | collective-permute-done | bytes 524320 | tf_op jit(solution)/shard_map/ppermute | solution.py:44
  149.7 5.1 %collective-permute-start.21 = (bf16[64,2048]{1,0:T(8,128)(2,1)S(1)}, bf16[64,2048]{1,0:T(8,128)(2,1)S(1)}, u32[]{:S(2)}, u32[]{:S(2)}) collective-permute-start(bf16[64,2048]{1,0:T(8,128)(2,1)S(1)} %add_convert_fusion), channel_id=1, source_target_pairs={{0,4},{4,0},{8,12},{12,8},{16,20},{20,16},{24,28},{28,24},{1,5},{5... | collective-permute-start | bytes 786440 | tf_op jit(solution)/shard_map/ppermute | solution.py:44
  154.8 1.7 %shard_map.103 = (f32[512,1024]{1,0:T(8,128)}, f32[512,256]{1,0:T(8,128)}) custom-call(bf16[512,1280]{1,0:T(8,128)(2,1)S(1)} %get-tuple-element.73.refs_0_, bf16[512,1280]{1,0:T(8,128)(2,1)S(1)} %collective-permute-done.23.refs_1_, bf16[512,1280]{1,0:T(8,128)(2,1)S(1)} %collective-permute-done.25.refs_2_), custom_call_target="tpu_custom_call" | custom-call | bytes 6553600 | tf_op jit(solution)/shard_map/pallas_call | solution.py:407
  156.6 2.2 %shard_map.104 = bf16[64,4096]{1,0:T(8,128)(2,1)} custom-call(s32[3]{0:T(128)S(1)} %pad_add_fusion.place.refs_0_, bf16[64,4096]{1,0:T(8,128)(2,1)S(1)} %copy-done.1, bf16[1,4096]{1,0:T(2,128)(2,1)S(1)} %reshape.9.gain, bf16[64,4096]{1,0:T(8,128)(2,1)S(1)} %copy-done.3, bf16[64,2048]{1,0:T(8,128)(2,1)S(1)} %collective-permute-done.21.handed, ...), custom_call_target="tpu_custom_call" | custom-call | bytes 3940352 | tf_op jit(solution)/shard_map/pallas_call | solution.py:23
  (66 shorter events, 25.1 us)
Async XLA Ops:
  3.5 1.2 copy-start.4
  4.5 6.4 %collective-permute-start = (bf16[128,2048]{1,0:T(8,128)(2,1)S(1)}, bf16[128,2048]{1,0:T(8,128)(2,1)S(1)}, u32[]{:S(2)}, u32[]{:S(2)}) collective-permute-start(bf16[128,2048]{1,0:T(8,128)(2,1)S(1)} %get-tuple-element.44), channel_id=1, source_target_pairs={{0,4},{4,0},{8,12},{12,8},{16,20},{20,16},{24,28},{28,24},{1,5},{5... | collective-permute-start | bytes 1572872 | tf_op jit(solution)/shard_map/ppermute | solution.py:44
  4.7 1.2 copy-start.5
  7.1 54.2 %collective-permute-start.6 = (bf16[512,2304]{1,0:T(8,128)(2,1)S(1)}, bf16[512,2304]{1,0:T(8,128)(2,1)}, u32[]{:S(2)}, u32[]{:S(2)}) collective-permute-start(bf16[512,2304]{1,0:T(8,128)(2,1)S(1)} %shard_map.95.refs_6_.refs_0_), channel_id=1, source_target_pairs={{0,16},{4,20},{8,24},{12,28},{16,0},{20,4},{24,8},{28,12},{1,17},{... | collective-permute-start | bytes 7077896 | tf_op jit(solution)/shard_map/ppermute | solution.py:44
  9.7 52.4 %collective-permute-start.5 = (bf16[512,2304]{1,0:T(8,128)(2,1)S(1)}, bf16[512,2304]{1,0:T(8,128)(2,1)}, u32[]{:S(2)}, u32[]{:S(2)}) collective-permute-start(bf16[512,2304]{1,0:T(8,128)(2,1)S(1)} %shard_map.95.refs_6_.refs_0_), channel_id=1, source_target_pairs={{0,8},{4,12},{8,0},{12,4},{16,24},{20,28},{24,16},{28,20},{1,9},{5... | collective-permute-start | bytes 7077896 | tf_op jit(solution)/shard_map/ppermute | solution.py:44
  11.0 14.7 %collective-permute-start.8 = (bf16[128,2048]{1,0:T(8,128)(2,1)S(1)}, bf16[128,2048]{1,0:T(8,128)(2,1)}, u32[]{:S(2)}, u32[]{:S(2)}) collective-permute-start(bf16[128,2048]{1,0:T(8,128)(2,1)S(1)} %pad_maximum_fusion.3.refs_0_), channel_id=1, source_target_pairs={{1,0},{2,1},{3,2},{5,4},{6,5},{7,6},{9,8},{10,9},{11,10},{13,12},{... | collective-permute-start | bytes 1572872 | tf_op jit(solution)/shard_map/ppermute | solution.py:71
  12.3 17.4 %collective-permute-start.7 = (bf16[128,2048]{1,0:T(8,128)(2,1)S(1)}, bf16[128,2048]{1,0:T(8,128)(2,1)S(1)}, u32[]{:S(2)}, u32[]{:S(2)}) collective-permute-start(bf16[128,2048]{1,0:T(8,128)(2,1)S(1)} %pad_maximum_fusion.3.refs_0_), channel_id=1, source_target_pairs={{0,1},{1,2},{2,3},{4,5},{5,6},{6,7},{8,9},{9,10},{10,11},{12,13},{... | collective-permute-start | bytes 1572872 | tf_op jit(solution)/shard_map/ppermute | solution.py:71
  16.4 20.5 %collective-permute-start.2 = (bf16[128,2048]{1,0:T(8,128)(2,1)S(1)}, bf16[128,2048]{1,0:T(8,128)(2,1)}, u32[]{:S(2)}, u32[]{:S(2)}) collective-permute-start(bf16[128,2048]{1,0:T(8,128)(2,1)S(1)} %pad_maximum_fusion.2.refs_0_), channel_id=1, source_target_pairs={{1,0},{2,1},{3,2},{5,4},{6,5},{7,6},{9,8},{10,9},{11,10},{13,12},{... | collective-permute-start | bytes 1572872 | tf_op jit(solution)/shard_map/ppermute | solution.py:71
  25.7 12.5 %collective-permute-start.1 = (bf16[128,2048]{1,0:T(8,128)(2,1)S(1)}, bf16[128,2048]{1,0:T(8,128)(2,1)}, u32[]{:S(2)}, u32[]{:S(2)}) collective-permute-start(bf16[128,2048]{1,0:T(8,128)(2,1)S(1)} %pad_maximum_fusion.2.refs_0_), channel_id=1, source_target_pairs={{0,1},{1,2},{2,3},{4,5},{5,6},{6,7},{8,9},{9,10},{10,11},{12,13},{... | collective-permute-start | bytes 1572872 | tf_op jit(solution)/shard_map/ppermute | solution.py:71
  29.7 10.0 %collective-permute-start.9 = (bf16[128,2048]{1,0:T(8,128)(2,1)S(1)}, bf16[128,2048]{1,0:T(8,128)(2,1)}, u32[]{:S(2)}, u32[]{:S(2)}) collective-permute-start(bf16[128,2048]{1,0:T(8,128)(2,1)S(1)} %collective-permute-done.7.refs_1_), channel_id=1, source_target_pairs={{1,2},{2,3},{5,6},{6,7},{9,10},{10,11},{13,14},{14,15},{17,18},{18... | collective-permute-start | bytes 1572872 | tf_op jit(solution)/shard_map/ppermute | solution.py:71
  36.9 14.0 %collective-permute-start.10 = (bf16[128,2048]{1,0:T(8,128)(2,1)}, bf16[128,2048]{1,0:T(8,128)(2,1)}, u32[]{:S(2)}, u32[]{:S(2)}) collective-permute-start(bf16[128,2048]{1,0:T(8,128)(2,1)} %collective-permute-done.8.refs_2_), channel_id=1, source_target_pairs={{1,0},{2,1},{5,4},{6,5},{9,8},{10,9},{13,12},{14,13},{17,16},{18,1... | collective-permute-start | bytes 1572872 | tf_op jit(solution)/shard_map/ppermute | solution.py:71
  38.2 28.2 %collective-permute-start.3 = (bf16[128,2048]{1,0:T(8,128)(2,1)}, bf16[128,2048]{1,0:T(8,128)(2,1)}, u32[]{:S(2)}, u32[]{:S(2)}) collective-permute-start(bf16[128,2048]{1,0:T(8,128)(2,1)} %collective-permute-done.1.refs_1_), channel_id=1, source_target_pairs={{1,2},{2,3},{5,6},{6,7},{9,10},{10,11},{13,14},{14,15},{17,18},{18... | collective-permute-start | bytes 1572872 | tf_op jit(solution)/shard_map/ppermute | solution.py:71
  39.7 26.8 %collective-permute-start.4 = (bf16[128,2048]{1,0:T(8,128)(2,1)}, bf16[128,2048]{1,0:T(8,128)(2,1)}, u32[]{:S(2)}, u32[]{:S(2)}) collective-permute-start(bf16[128,2048]{1,0:T(8,128)(2,1)} %collective-permute-done.2.refs_2_), channel_id=1, source_target_pairs={{1,0},{2,1},{5,4},{6,5},{9,8},{10,9},{13,12},{14,13},{17,16},{18,1... | collective-permute-start | bytes 1572872 | tf_op jit(solution)/shard_map/ppermute | solution.py:71
  52.0 17.1 %collective-permute-start.12 = (bf16[128,2048]{1,0:T(8,128)(2,1)S(1)}, bf16[128,2048]{1,0:T(8,128)(2,1)S(1)}, u32[]{:S(2)}, u32[]{:S(2)}) collective-permute-start(bf16[128,2048]{1,0:T(8,128)(2,1)S(1)} %broadcast_select_fusion), channel_id=1, source_target_pairs={{1,0},{2,3},{5,4},{6,7},{9,8},{10,11},{13,12},{14,15},{17,16},{18,... | collective-permute-start | bytes 1572872 | tf_op jit(solution)/shard_map/ppermute | solution.py:71
  64.8 4.2 %copy-start.7 = (bf16[128,2048]{1,0:T(8,128)(2,1)S(1)}, bf16[128,2048]{1,0:T(8,128)(2,1)}, u32[]{:S(2)}) copy-start(bf16[128,2048]{1,0:T(8,128)(2,1)} %copy-done.6) | copy-start | bytes 1572868
  64.8 26.2 %collective-permute-start.14 = (bf16[256,2304]{1,0:T(8,128)(2,1)S(1)}, bf16[256,2304]{1,0:T(8,128)(2,1)S(1)}, u32[]{:S(2)}, u32[]{:S(2)}) collective-permute-start(bf16[256,2304]{1,0:T(8,128)(2,1)S(1)} %slice.44), channel_id=1, source_target_pairs={{0,8},{4,12},{8,0},{12,4},{16,24},{20,28},{24,16},{28,20},{1,9},{5... | collective-permute-start | bytes 3538952 | tf_op jit(solution)/shard_map/ppermute | solution.py:44
  66.1 25.8 %collective-permute-start.13 = (bf16[256,2304]{1,0:T(8,128)(2,1)S(1)}, bf16[256,2304]{1,0:T(8,128)(2,1)S(1)}, u32[]{:S(2)}, u32[]{:S(2)}) collective-permute-start(bf16[256,2304]{1,0:T(8,128)(2,1)S(1)} %slice.43), channel_id=1, source_target_pairs={{0,16},{4,20},{8,24},{12,28},{16,0},{20,4},{24,8},{28,12},{1,17},{... | collective-permute-start | bytes 3538952 | tf_op jit(solution)/shard_map/ppermute | solution.py:44
  67.5 15.9 %collective-permute-start.11 = (bf16[128,2048]{1,0:T(8,128)(2,1)S(1)}, bf16[128,2048]{1,0:T(8,128)(2,1)S(1)}, u32[]{:S(2)}, u32[]{:S(2)}) collective-permute-start(bf16[128,2048]{1,0:T(8,128)(2,1)S(1)} %broadcast_select_fusion.1), channel_id=1, source_target_pairs={{1,0},{2,3},{5,4},{6,7},{9,8},{10,11},{13,12},{14,15},{17,16},{18,... | collective-permute-start | bytes 1572872 | tf_op jit(solution)/shard_map/ppermute | solution.py:71
  91.9 6.5 %copy-start.9 = (s32[1,4]{1,0:T(1,128)S(1)}, s32[1,4]{1,0:T(1,128)}, u32[]{:S(2)}) copy-start(s32[1,4]{1,0:T(1,128)} %refs_1_.1) | copy-start | bytes 52
  93.3 5.1 %collective-permute-start.15 = (bf16[256,2304]{1,0:T(8,128)(2,1)S(1)}, bf16[256,2304]{1,0:T(8,128)(2,1)S(1)}, u32[]{:S(2)}, u32[]{:S(2)}) collective-permute-start(bf16[256,2304]{1,0:T(8,128)(2,1)S(1)} %get-tuple-element.64), channel_id=1, source_target_pairs={{0,4},{4,0},{8,12},{12,8},{16,20},{20,16},{24,28},{28,24},{1,5},{5... | collective-permute-start | bytes 3538952 | tf_op jit(solution)/shard_map/ppermute | solution.py:44
  102.4 2.2 %collective-permute-start.16 = (bf16[256,1280]{1,0:T(8,128)(2,1)S(1)}, bf16[256,1280]{1,0:T(8,128)(2,1)S(1)}, u32[]{:S(2)}, u32[]{:S(2)}) collective-permute-start(bf16[256,1280]{1,0:T(8,128)(2,1)S(1)} %shard_map.99.own), channel_id=1, source_target_pairs={{0,4},{4,0},{8,12},{12,8},{16,20},{20,16},{24,28},{28,24},{1,5},{5... | collective-permute-start | bytes 1966088 | tf_op jit(solution)/shard_map/ppermute | solution.py:44
  105.6 16.0 %collective-permute-start.24 = (bf16[256,1280]{1,0:T(8,128)(2,1)S(1)}, bf16[256,1280]{1,0:T(8,128)(2,1)S(1)}, u32[]{:S(2)}, u32[]{:S(2)}) collective-permute-start(bf16[256,1280]{1,0:T(8,128)(2,1)S(1)} %get-tuple-element.83), channel_id=1, source_target_pairs={{0,8},{4,12},{8,0},{12,4},{16,24},{20,28},{24,16},{28,20},{1,9},{5... | collective-permute-start | bytes 1966088 | tf_op jit(solution)/shard_map/ppermute | solution.py:44
  105.9 15.7 %collective-permute-start.22 = (bf16[256,1280]{1,0:T(8,128)(2,1)S(1)}, bf16[256,1280]{1,0:T(8,128)(2,1)S(1)}, u32[]{:S(2)}, u32[]{:S(2)}) collective-permute-start(bf16[256,1280]{1,0:T(8,128)(2,1)S(1)} %get-tuple-element.84), channel_id=1, source_target_pairs={{0,16},{4,20},{8,24},{12,28},{16,0},{20,4},{24,8},{28,12},{1,17},{... | collective-permute-start | bytes 1966088 | tf_op jit(solution)/shard_map/ppermute | solution.py:44
  111.0 13.4 %collective-permute-start.18 = (bf16[128,2048]{1,0:T(8,128)(2,1)S(1)}, bf16[128,2048]{1,0:T(8,128)(2,1)S(1)}, u32[]{:S(2)}, u32[]{:S(2)}) collective-permute-start(bf16[128,2048]{1,0:T(8,128)(2,1)S(1)} %get-tuple-element.67), channel_id=1, source_target_pairs={{3,2},{0,1},{7,6},{4,5},{11,10},{8,9},{15,14},{12,13},{19,18},{16,... | collective-permute-start | bytes 1572872 | tf_op jit(solution)/shard_map/ppermute | solution.py:71
  114.2 10.2 %collective-permute-start.17 = (bf16[128,2048]{1,0:T(8,128)(2,1)S(1)}, bf16[128,2048]{1,0:T(8,128)(2,1)S(1)}, u32[]{:S(2)}, u32[]{:S(2)}) collective-permute-start(bf16[128,2048]{1,0:T(8,128)(2,1)S(1)} %get-tuple-element.67), channel_id=1, source_target_pairs={{1,2},{2,1},{5,6},{6,5},{9,10},{10,9},{13,14},{14,13},{17,18},{18,... | collective-permute-start | bytes 1572872 | tf_op jit(solution)/shard_map/ppermute | solution.py:71
  121.9 32.9 %collective-permute-start.25 = (bf16[512,1280]{1,0:T(8,128)(2,1)S(1)}, bf16[512,1280]{1,0:T(8,128)(2,1)S(1)}, u32[]{:S(2)}, u32[]{:S(2)}) collective-permute-start(bf16[512,1280]{1,0:T(8,128)(2,1)S(1)} %pad_maximum_fusion.1), channel_id=1, source_target_pairs={{0,16},{4,20},{8,24},{12,28},{16,0},{20,4},{24,8},{28,12},{1,17},{... | collective-permute-start | bytes 3932168 | tf_op jit(solution)/shard_map/ppermute | solution.py:44
  122.4 32.4 %collective-permute-start.23 = (bf16[512,1280]{1,0:T(8,128)(2,1)S(1)}, bf16[512,1280]{1,0:T(8,128)(2,1)S(1)}, u32[]{:S(2)}, u32[]{:S(2)}) collective-permute-start(bf16[512,1280]{1,0:T(8,128)(2,1)S(1)} %pad_maximum_fusion), channel_id=1, source_target_pairs={{0,8},{4,12},{8,0},{12,4},{16,24},{20,28},{24,16},{28,20},{1,9},{5... | collective-permute-start | bytes 3932168 | tf_op jit(solution)/shard_map/ppermute | solution.py:44
  124.5 25.1 %collective-permute-start.19 = (bf16[128,2048]{1,0:T(8,128)(2,1)S(1)}, bf16[128,2048]{1,0:T(8,128)(2,1)S(1)}, u32[]{:S(2)}, u32[]{:S(2)}) collective-permute-start(bf16[128,2048]{1,0:T(8,128)(2,1)S(1)} %get-tuple-element.70), channel_id=1, source_target_pairs={{0,1},{1,0},{2,3},{3,2},{4,5},{5,4},{6,7},{7,6},{8,9},{9,8},{10,11... | collective-permute-start | bytes 1572872 | tf_op jit(solution)/shard_map/ppermute | solution.py:44
  128.1 21.5 %collective-permute-start.20 = (bf16[128,2048]{1,0:T(8,128)(2,1)S(1)}, bf16[128,2048]{1,0:T(8,128)(2,1)S(1)}, u32[]{:S(2)}, u32[]{:S(2)}) collective-permute-start(bf16[128,2048]{1,0:T(8,128)(2,1)S(1)} %add.18), channel_id=1, source_target_pairs={{0,2},{1,3},{2,0},{3,1},{4,6},{5,7},{6,4},{7,5},{8,10},{9,11},{10,... | collective-permute-start | bytes 1572872 | tf_op jit(solution)/shard_map/ppermute | solution.py:44
  149.7 6.8 %collective-permute-start.21 = (bf16[64,2048]{1,0:T(8,128)(2,1)S(1)}, bf16[64,2048]{1,0:T(8,128)(2,1)S(1)}, u32[]{:S(2)}, u32[]{:S(2)}) collective-permute-start(bf16[64,2048]{1,0:T(8,128)(2,1)S(1)} %add_convert_fusion), channel_id=1, source_target_pairs={{0,4},{4,0},{8,12},{12,8},{16,20},{20,16},{24,28},{28,24},{1,5},{5... | collective-permute-start | bytes 786440 | tf_op jit(solution)/shard_map/ppermute | solution.py:44
  154.8 1.7 %copy-start.1 = (bf16[64,4096]{1,0:T(8,128)(2,1)S(1)}, bf16[64,4096]{1,0:T(8,128)(2,1)}, u32[]{:S(2)}) copy-start(bf16[64,4096]{1,0:T(8,128)(2,1)} %tokens.3) | copy-start | bytes 1572868
  154.8 1.7 %copy-start.3 = (bf16[64,4096]{1,0:T(8,128)(2,1)S(1)}, bf16[64,4096]{1,0:T(8,128)(2,1)}, u32[]{:S(2)}) copy-start(bf16[64,4096]{1,0:T(8,128)(2,1)} %grad_out.3) | copy-start | bytes 1572868
  (4 other events, 3.8 us)

commit v15 on v11

--- a/solution.py
+++ b/solution.py
@@ -388,7 +388,7 @@
 
 def finish(parts, query_width, share):
     block, width = parts[0].shape
-    step = min(block, 128)
+    step = min(block, 256)
 
     def spec(columns):
         return pl.BlockSpec((step, columns), lambda i: (i, 0))

time: 160 us -> 160 us (level)
  no operation moved by 1% of the time
where the time goes in v15:
time: 160 us; the launch traced here: 159 us
  waiting for transfers between devices  76.6 us (48%)
  starting transfers between devices  43.8 us (27%)
  Pallas kernels  25.8 us (16%)
  local copies, waits for them, and re-layouts  8.76 us (5%)
  other arithmetic  3 us (2%)
    ppermute x12, waiting for transfers between devices, along(): return lax.ppermute(value, 'tensor', pairs)  47.5 us
    ppermute x14, waiting for transfers between devices, swap(): return lax.ppermute(value, axis, pairs)  29 us
    ppermute x12, starting transfers between devices, along(): return lax.ppermute(value, 'tensor', pairs)  23 us
    ppermute x14, starting transfers between devices, swap(): return lax.ppermute(value, axis, pairs)  20.8 us
    pallas_call x8, Pallas kernels, call(): pl.pallas_call(kernel, out_shape=outs, in_specs=[SCALARS] * len(scalars)...  19.4 us
    unnamed x20, local copies, waits for them, and re-layouts  5.24 us
    pallas_call x1, Pallas kernels, row_terms(): pl.pallas_call(functools.partial(row_kernel, len(weights)), grid=(1,), ou...  4.69 us
  transfers between devices with their start and end apart: 26, of which 14 were waited for; matrix products, arithmetic and copies ran while one was open for 4% of the time, Pallas kernels for 10%

profile of v15, /device:TPU:1, one launch (start us, length us, event | category | flops | bytes accessed | tf_op | source)
XLA Modules:
  0.0 158.9 jit_solution(17155462608724943494)
XLA Ops:
  7.1 2.6 %collective-permute-start.11 = (bf16[512,2304]{1,0:T(8,128)(2,1)S(1)}, bf16[512,2304]{1,0:T(8,128)(2,1)}, u32[]{:S(2)}, u32[]{:S(2)}) collective-permute-start(bf16[512,2304]{1,0:T(8,128)(2,1)S(1)} %shard_map.95.refs_12_.refs_0_), channel_id=1, source_target_pairs={{0,8},{4,12},{8,0},{12,4},{16,24},{20,28},{24,16},{28,20},{1,9},{5... | collective-permute-start | bytes 7077896 | tf_op jit(solution)/shard_map/ppermute | solution.py:44
  11.0 3.2 %collective-permute-start.6 = (bf16[128,2048]{1,0:T(8,128)(2,1)S(1)}, bf16[128,2048]{1,0:T(8,128)(2,1)S(1)}, u32[]{:S(2)}, u32[]{:S(2)}) collective-permute-start(bf16[128,2048]{1,0:T(8,128)(2,1)S(1)} %pad_maximum_fusion.3.refs_6_), channel_id=1, source_target_pairs={{0,1},{1,2},{2,3},{4,5},{5,6},{6,7},{8,9},{9,10},{10,11},{12,13},{... | collective-permute-start | bytes 1572872 | tf_op jit(solution)/shard_map/ppermute | solution.py:69
  14.2 1.3 collective-permute-start.7
  15.6 4.8 %collective-permute-start.1 = (bf16[128,2048]{1,0:T(8,128)(2,1)S(1)}, bf16[128,2048]{1,0:T(8,128)(2,1)}, u32[]{:S(2)}, u32[]{:S(2)}) collective-permute-start(bf16[128,2048]{1,0:T(8,128)(2,1)S(1)} %pad_maximum_fusion.2.refs_0_), channel_id=1, source_target_pairs={{0,1},{1,2},{2,3},{4,5},{5,6},{6,7},{8,9},{9,10},{10,11},{12,13},{... | collective-permute-start | bytes 1572872 | tf_op jit(solution)/shard_map/ppermute | solution.py:69
  20.4 4.2 %collective-permute-done.6.refs_7_ = bf16[128,2048]{1,0:T(8,128)(2,1)S(1)} collective-permute-done((bf16[128,2048]{1,0:T(8,128)(2,1)S(1)}, bf16[128,2048]{1,0:T(8,128)(2,1)S(1)}, u32[]{:S(2)}, u32[]{:S(2)}) %collective-permute-start.6) | collective-permute-done | bytes 524320 | tf_op jit(solution)/shard_map/ppermute | solution.py:69
  25.9 2.6 %collective-permute-done.7.refs_8_ = bf16[128,2048]{1,0:T(8,128)(2,1)} collective-permute-done((bf16[128,2048]{1,0:T(8,128)(2,1)S(1)}, bf16[128,2048]{1,0:T(8,128)(2,1)}, u32[]{:S(2)}, u32[]{:S(2)}) %collective-permute-start.7) | collective-permute-done | bytes 524320 | tf_op jit(solution)/shard_map/ppermute | solution.py:69
  28.6 1.5 collective-permute-start.8
  30.9 5.0 %collective-permute-done.1.refs_1_ = bf16[128,2048]{1,0:T(8,128)(2,1)} collective-permute-done((bf16[128,2048]{1,0:T(8,128)(2,1)S(1)}, bf16[128,2048]{1,0:T(8,128)(2,1)}, u32[]{:S(2)}, u32[]{:S(2)}) %collective-permute-start.1) | collective-permute-done | bytes 524320 | tf_op jit(solution)/shard_map/ppermute | solution.py:69
  38.4 1.5 collective-permute-start.3
  41.1 9.6 %collective-permute-done.9.refs_10_ = bf16[128,2048]{1,0:T(8,128)(2,1)} collective-permute-done((bf16[128,2048]{1,0:T(8,128)(2,1)}, bf16[128,2048]{1,0:T(8,128)(2,1)}, u32[]{:S(2)}, u32[]{:S(2)}) %collective-permute-start.9) | collective-permute-done | bytes 524320 | tf_op jit(solution)/shard_map/ppermute | solution.py:69
  53.1 8.8 %collective-permute-done.4.refs_4_ = bf16[128,2048]{1,0:T(8,128)(2,1)} collective-permute-done((bf16[128,2048]{1,0:T(8,128)(2,1)}, bf16[128,2048]{1,0:T(8,128)(2,1)}, u32[]{:S(2)}, u32[]{:S(2)}) %collective-permute-start.4) | collective-permute-done | bytes 524320 | tf_op jit(solution)/shard_map/ppermute | solution.py:69
  62.1 1.3 slice.44
  63.4 1.3 collective-permute-start.13
  64.7 1.3 slice.45
  67.6 1.5 collective-permute-start.5
  69.1 4.0 %collective-permute-done.10.refs_11_ = bf16[128,2048]{1,0:T(8,128)(2,1)S(1)} collective-permute-done((bf16[128,2048]{1,0:T(8,128)(2,1)S(1)}, bf16[128,2048]{1,0:T(8,128)(2,1)S(1)}, u32[]{:S(2)}, u32[]{:S(2)}) %collective-permute-start.10) | collective-permute-done | bytes 524320 | tf_op jit(solution)/shard_map/ppermute | solution.py:69
  73.1 11.2 %collective-permute-done.5.refs_5_ = bf16[128,2048]{1,0:T(8,128)(2,1)S(1)} collective-permute-done((bf16[128,2048]{1,0:T(8,128)(2,1)S(1)}, bf16[128,2048]{1,0:T(8,128)(2,1)S(1)}, u32[]{:S(2)}, u32[]{:S(2)}) %collective-permute-start.5) | collective-permute-done | bytes 524320 | tf_op jit(solution)/shard_map/ppermute | solution.py:69
  84.3 7.5 %shard_map.96 = (f32[512,2304]{1,0:T(8,128)S(1)}, bf16[512,2048]{1,0:T(8,128)(2,1)S(1)}, bf16[512,2048]{1,0:T(8,128)(2,1)S(1)}) custom-call(s32[3]{0:T(128)S(1)} %pad_add_fusion.place.refs_0_, bf16[128,2048]{1,0:T(8,128)(2,1)S(1)} %pad_maximum_fusion.2.refs_0_, bf16[128,2048]{1,0:T(8,128)(2,1)} %collective-permute-done.1.refs_1_, ...), custom_call_target="tpu_custom_call" | custom-call | flops 3623878656 | bytes 22282240 | tf_op jit(solution)/shard_map/pallas_call | solution.py:23
  91.9 1.4 shard_map.97
  93.3 2.7 %collective-permute-start.15 = (bf16[256,2304]{1,0:T(8,128)(2,1)S(1)}, bf16[256,2304]{1,0:T(8,128)(2,1)S(1)}, u32[]{:S(2)}, u32[]{:S(2)}) collective-permute-start(bf16[256,2304]{1,0:T(8,128)(2,1)S(1)} %get-tuple-element.62), channel_id=1, source_target_pairs={{0,4},{4,0},{8,12},{12,8},{16,20},{20,16},{24,28},{28,24},{1,5},{5... | collective-permute-start | bytes 3538952 | tf_op jit(solution)/shard_map/ppermute | solution.py:44
  96.0 2.5 %collective-permute-done.15.refs_3_ = bf16[256,2304]{1,0:T(8,128)(2,1)S(1)} collective-permute-done((bf16[256,2304]{1,0:T(8,128)(2,1)S(1)}, bf16[256,2304]{1,0:T(8,128)(2,1)S(1)}, u32[]{:S(2)}, u32[]{:S(2)}) %collective-permute-start.15) | collective-permute-done | bytes 1179680 | tf_op jit(solution)/shard_map/ppermute | solution.py:44
  98.5 4.0 %shard_map.98.own = bf16[256,1280]{1,0:T(8,128)(2,1)S(1)} custom-call(s32[3]{0:T(128)S(1)} %pad_add_fusion.place.refs_0_, s32[1,4]{1,0:T(1,128)S(1)} %copy-done.7, f32[256,2304]{1,0:T(8,128)S(1)} %get-tuple-element.61.refs_2_, bf16[256,2304]{1,0:T(8,128)(2,1)S(1)} %collective-permute-done.15.refs_3_), custom_call_target="tpu_custom_call" | custom-call | flops 671088640 | bytes 4194304 | tf_op jit(solution)/shard_map/pallas_call | solution.py:23
  103.0 1.7 %collective-permute-done.16.other = bf16[256,1280]{1,0:T(8,128)(2,1)S(1)} collective-permute-done((bf16[256,1280]{1,0:T(8,128)(2,1)S(1)}, bf16[256,1280]{1,0:T(8,128)(2,1)S(1)}, u32[]{:S(2)}, u32[]{:S(2)}) %collective-permute-start.16) | collective-permute-done | bytes 655392 | tf_op jit(solution)/shard_map/ppermute | solution.py:44
  106.4 4.7 %shard_map.99 = (bf16[128,2048]{1,0:T(8,128)(2,1)S(1)}, bf16[128,2048]{1,0:T(8,128)(2,1)S(1)}, bf16[128,2048]{1,0:T(8,128)(2,1)S(1)}, bf16[128,2048]{1,0:T(8,128)(2,1)S(1)}) custom-call(bf16[256,1280]{1,0:T(8,128)(2,1)S(1)} %shard_map.98.own, bf16[256,1280]{1,0:T(8,128)(2,1)S(1)} %collective-permute-done.16.other, ...), custom_call_target="tpu_custom_call" | custom-call | flops 2684354560 | bytes 8650752 | tf_op jit(solution)/shard_map/pallas_call | solution.py:365
  111.1 3.2 %collective-permute-start.17 = (bf16[128,2048]{1,0:T(8,128)(2,1)S(1)}, bf16[128,2048]{1,0:T(8,128)(2,1)S(1)}, u32[]{:S(2)}, u32[]{:S(2)}) collective-permute-start(bf16[128,2048]{1,0:T(8,128)(2,1)S(1)} %get-tuple-element.65), channel_id=1, source_target_pairs={{3,2},{0,1},{7,6},{4,5},{11,10},{8,9},{15,14},{12,13},{19,18},{16,... | collective-permute-start | bytes 1572872 | tf_op jit(solution)/shard_map/ppermute | solution.py:69
  115.2 2.3 %shard_map.100 = (bf16[512,1280]{1,0:T(8,128)(2,1)S(1)}, bf16[512,1280]{1,0:T(8,128)(2,1)S(1)}, bf16[512,1280]{1,0:T(8,128)(2,1)S(1)}) custom-call(bf16[512,2048]{1,0:T(8,128)(2,1)S(1)} %get-tuple-element.60.normed.pair, bf16[256,1280]{1,0:T(8,128)(2,1)S(1)} %shard_map.98.own, bf16[256,1280]{1,0:T(8,128)(2,1)S(1)} %collective-permute-done.16.other), custom_call_target="tpu_custom_call" | custom-call | flops 2013265920 | bytes 7340032 | tf_op jit(solution)/shard_map/pallas_call | solution.py:23
  117.4 4.3 %collective-permute-done.22 = bf16[256,1280]{1,0:T(8,128)(2,1)S(1)} collective-permute-done((bf16[256,1280]{1,0:T(8,128)(2,1)S(1)}, bf16[256,1280]{1,0:T(8,128)(2,1)S(1)}, u32[]{:S(2)}, u32[]{:S(2)}) %collective-permute-start.22) | collective-permute-done | bytes 655392 | tf_op jit(solution)/shard_map/ppermute | solution.py:44
  124.6 3.6 %collective-permute-start.19 = (bf16[128,2048]{1,0:T(8,128)(2,1)S(1)}, bf16[128,2048]{1,0:T(8,128)(2,1)S(1)}, u32[]{:S(2)}, u32[]{:S(2)}) collective-permute-start(bf16[128,2048]{1,0:T(8,128)(2,1)S(1)} %get-tuple-element.68), channel_id=1, source_target_pairs={{0,1},{1,0},{2,3},{3,2},{4,5},{5,4},{6,7},{7,6},{8,9},{9,8},{10,11... | collective-permute-start | bytes 1572872 | tf_op jit(solution)/shard_map/ppermute | solution.py:44
  129.2 20.4 %collective-permute-done.19.refs_1_ = bf16[128,2048]{1,0:T(8,128)(2,1)S(1)} collective-permute-done((bf16[128,2048]{1,0:T(8,128)(2,1)S(1)}, bf16[128,2048]{1,0:T(8,128)(2,1)S(1)}, u32[]{:S(2)}, u32[]{:S(2)}) %collective-permute-start.19) | collective-permute-done | bytes 524320 | tf_op jit(solution)/shard_map/ppermute | solution.py:44
  149.8 5.1 %collective-permute-start.21 = (bf16[64,2048]{1,0:T(8,128)(2,1)S(1)}, bf16[64,2048]{1,0:T(8,128)(2,1)S(1)}, u32[]{:S(2)}, u32[]{:S(2)}) collective-permute-start(bf16[64,2048]{1,0:T(8,128)(2,1)S(1)} %add_convert_fusion), channel_id=1, source_target_pairs={{0,4},{4,0},{8,12},{12,8},{16,20},{20,16},{24,28},{28,24},{1,5},{5... | collective-permute-start | bytes 786440 | tf_op jit(solution)/shard_map/ppermute | solution.py:44
  154.9 1.7 %shard_map.102 = (f32[512,1024]{1,0:T(8,128)}, f32[512,256]{1,0:T(8,128)}) custom-call(bf16[512,1280]{1,0:T(8,128)(2,1)S(1)} %get-tuple-element.71.refs_0_, bf16[512,1280]{1,0:T(8,128)(2,1)S(1)} %collective-permute-done.23.refs_1_, bf16[512,1280]{1,0:T(8,128)(2,1)S(1)} %collective-permute-done.25.refs_2_), custom_call_target="tpu_custom_call" | custom-call | bytes 6553600 | tf_op jit(solution)/shard_map/pallas_call | solution.py:396
  156.7 2.2 %shard_map.103 = bf16[64,4096]{1,0:T(8,128)(2,1)} custom-call(s32[3]{0:T(128)S(1)} %pad_add_fusion.place.refs_0_, bf16[64,4096]{1,0:T(8,128)(2,1)S(1)} %copy-done.1, bf16[1,4096]{1,0:T(2,128)(2,1)S(1)} %reshape.9.gain, bf16[64,4096]{1,0:T(8,128)(2,1)S(1)} %copy-done.3, bf16[64,2048]{1,0:T(8,128)(2,1)S(1)} %collective-permute-done.21.handed, ...), custom_call_target="tpu_custom_call" | custom-call | bytes 3940352 | tf_op jit(solution)/shard_map/pallas_call | solution.py:23
  (65 shorter events, 24.7 us)
Async XLA Ops:
  3.5 1.2 copy-start.4
  4.5 6.4 %collective-permute-start = (bf16[128,2048]{1,0:T(8,128)(2,1)S(1)}, bf16[128,2048]{1,0:T(8,128)(2,1)S(1)}, u32[]{:S(2)}, u32[]{:S(2)}) collective-permute-start(bf16[128,2048]{1,0:T(8,128)(2,1)S(1)} %get-tuple-element.43), channel_id=1, source_target_pairs={{0,4},{4,0},{8,12},{12,8},{16,20},{20,16},{24,28},{28,24},{1,5},{5... | collective-permute-start | bytes 1572872 | tf_op jit(solution)/shard_map/ppermute | solution.py:44
  4.7 1.2 copy-start.5
  7.1 54.9 %collective-permute-start.11 = (bf16[512,2304]{1,0:T(8,128)(2,1)S(1)}, bf16[512,2304]{1,0:T(8,128)(2,1)}, u32[]{:S(2)}, u32[]{:S(2)}) collective-permute-start(bf16[512,2304]{1,0:T(8,128)(2,1)S(1)} %shard_map.95.refs_12_.refs_0_), channel_id=1, source_target_pairs={{0,8},{4,12},{8,0},{12,4},{16,24},{20,28},{24,16},{28,20},{1,9},{5... | collective-permute-start | bytes 7077896 | tf_op jit(solution)/shard_map/ppermute | solution.py:44
  9.6 52.4 %collective-permute-start.12 = (bf16[512,2304]{1,0:T(8,128)(2,1)S(1)}, bf16[512,2304]{1,0:T(8,128)(2,1)}, u32[]{:S(2)}, u32[]{:S(2)}) collective-permute-start(bf16[512,2304]{1,0:T(8,128)(2,1)S(1)} %shard_map.95.refs_12_.refs_0_), channel_id=1, source_target_pairs={{0,16},{4,20},{8,24},{12,28},{16,0},{20,4},{24,8},{28,12},{1,17},{... | collective-permute-start | bytes 7077896 | tf_op jit(solution)/shard_map/ppermute | solution.py:44
  11.0 13.7 %collective-permute-start.6 = (bf16[128,2048]{1,0:T(8,128)(2,1)S(1)}, bf16[128,2048]{1,0:T(8,128)(2,1)S(1)}, u32[]{:S(2)}, u32[]{:S(2)}) collective-permute-start(bf16[128,2048]{1,0:T(8,128)(2,1)S(1)} %pad_maximum_fusion.3.refs_6_), channel_id=1, source_target_pairs={{0,1},{1,2},{2,3},{4,5},{5,6},{6,7},{8,9},{9,10},{10,11},{12,13},{... | collective-permute-start | bytes 1572872 | tf_op jit(solution)/shard_map/ppermute | solution.py:69
  14.2 14.4 %collective-permute-start.7 = (bf16[128,2048]{1,0:T(8,128)(2,1)S(1)}, bf16[128,2048]{1,0:T(8,128)(2,1)}, u32[]{:S(2)}, u32[]{:S(2)}) collective-permute-start(bf16[128,2048]{1,0:T(8,128)(2,1)S(1)} %pad_maximum_fusion.3.refs_6_), channel_id=1, source_target_pairs={{1,0},{2,1},{3,2},{5,4},{6,5},{7,6},{9,8},{10,9},{11,10},{13,12},{... | collective-permute-start | bytes 1572872 | tf_op jit(solution)/shard_map/ppermute | solution.py:69
  15.6 20.3 %collective-permute-start.1 = (bf16[128,2048]{1,0:T(8,128)(2,1)S(1)}, bf16[128,2048]{1,0:T(8,128)(2,1)}, u32[]{:S(2)}, u32[]{:S(2)}) collective-permute-start(bf16[128,2048]{1,0:T(8,128)(2,1)S(1)} %pad_maximum_fusion.2.refs_0_), channel_id=1, source_target_pairs={{0,1},{1,2},{2,3},{4,5},{5,6},{6,7},{8,9},{9,10},{10,11},{12,13},{... | collective-permute-start | bytes 1572872 | tf_op jit(solution)/shard_map/ppermute | solution.py:69
  24.6 13.7 %collective-permute-start.2 = (bf16[128,2048]{1,0:T(8,128)(2,1)S(1)}, bf16[128,2048]{1,0:T(8,128)(2,1)}, u32[]{:S(2)}, u32[]{:S(2)}) collective-permute-start(bf16[128,2048]{1,0:T(8,128)(2,1)S(1)} %pad_maximum_fusion.2.refs_0_), channel_id=1, source_target_pairs={{1,0},{2,1},{3,2},{5,4},{6,5},{7,6},{9,8},{10,9},{11,10},{13,12},{... | collective-permute-start | bytes 1572872 | tf_op jit(solution)/shard_map/ppermute | solution.py:69
  28.6 11.2 %collective-permute-start.8 = (bf16[128,2048]{1,0:T(8,128)(2,1)S(1)}, bf16[128,2048]{1,0:T(8,128)(2,1)}, u32[]{:S(2)}, u32[]{:S(2)}) collective-permute-start(bf16[128,2048]{1,0:T(8,128)(2,1)S(1)} %collective-permute-done.6.refs_7_), channel_id=1, source_target_pairs={{1,2},{2,3},{5,6},{6,7},{9,10},{10,11},{13,14},{14,15},{17,18},{18... | collective-permute-start | bytes 1572872 | tf_op jit(solution)/shard_map/ppermute | solution.py:69
  35.9 14.8 %collective-permute-start.9 = (bf16[128,2048]{1,0:T(8,128)(2,1)}, bf16[128,2048]{1,0:T(8,128)(2,1)}, u32[]{:S(2)}, u32[]{:S(2)}) collective-permute-start(bf16[128,2048]{1,0:T(8,128)(2,1)} %collective-permute-done.7.refs_8_), channel_id=1, source_target_pairs={{1,0},{2,1},{5,4},{6,5},{9,8},{10,9},{13,12},{14,13},{17,16},{18,1... | collective-permute-start | bytes 1572872 | tf_op jit(solution)/shard_map/ppermute | solution.py:69
  38.4 14.8 %collective-permute-start.3 = (bf16[128,2048]{1,0:T(8,128)(2,1)}, bf16[128,2048]{1,0:T(8,128)(2,1)}, u32[]{:S(2)}, u32[]{:S(2)}) collective-permute-start(bf16[128,2048]{1,0:T(8,128)(2,1)} %collective-permute-done.1.refs_1_), channel_id=1, source_target_pairs={{1,2},{2,3},{5,6},{6,7},{9,10},{10,11},{13,14},{14,15},{17,18},{18... | collective-permute-start | bytes 1572872 | tf_op jit(solution)/shard_map/ppermute | solution.py:69
  39.8 22.1 %collective-permute-start.4 = (bf16[128,2048]{1,0:T(8,128)(2,1)}, bf16[128,2048]{1,0:T(8,128)(2,1)}, u32[]{:S(2)}, u32[]{:S(2)}) collective-permute-start(bf16[128,2048]{1,0:T(8,128)(2,1)} %collective-permute-done.2.refs_2_), channel_id=1, source_target_pairs={{1,0},{2,1},{5,4},{6,5},{9,8},{10,9},{13,12},{14,13},{17,16},{18,1... | collective-permute-start | bytes 1572872 | tf_op jit(solution)/shard_map/ppermute | solution.py:69
  51.8 21.3 %collective-permute-start.10 = (bf16[128,2048]{1,0:T(8,128)(2,1)S(1)}, bf16[128,2048]{1,0:T(8,128)(2,1)S(1)}, u32[]{:S(2)}, u32[]{:S(2)}) collective-permute-start(bf16[128,2048]{1,0:T(8,128)(2,1)S(1)} %broadcast_select_fusion), channel_id=1, source_target_pairs={{1,0},{2,3},{5,4},{6,7},{9,8},{10,11},{13,12},{14,15},{17,16},{18,... | collective-permute-start | bytes 1572872 | tf_op jit(solution)/shard_map/ppermute | solution.py:69
  63.4 28.4 %collective-permute-start.13 = (bf16[256,2304]{1,0:T(8,128)(2,1)S(1)}, bf16[256,2304]{1,0:T(8,128)(2,1)S(1)}, u32[]{:S(2)}, u32[]{:S(2)}) collective-permute-start(bf16[256,2304]{1,0:T(8,128)(2,1)S(1)} %slice.44), channel_id=1, source_target_pairs={{0,16},{4,20},{8,24},{12,28},{16,0},{20,4},{24,8},{28,12},{1,17},{... | collective-permute-start | bytes 3538952 | tf_op jit(solution)/shard_map/ppermute | solution.py:44
  66.1 18.2 %copy-start.9 = (bf16[128,2048]{1,0:T(8,128)(2,1)S(1)}, bf16[128,2048]{1,0:T(8,128)(2,1)}, u32[]{:S(2)}) copy-start(bf16[128,2048]{1,0:T(8,128)(2,1)} %copy-done.8) | copy-start | bytes 1572868
  66.1 25.8 %collective-permute-start.14 = (bf16[256,2304]{1,0:T(8,128)(2,1)S(1)}, bf16[256,2304]{1,0:T(8,128)(2,1)S(1)}, u32[]{:S(2)}, u32[]{:S(2)}) collective-permute-start(bf16[256,2304]{1,0:T(8,128)(2,1)S(1)} %slice.45), channel_id=1, source_target_pairs={{0,8},{4,12},{8,0},{12,4},{16,24},{20,28},{24,16},{28,20},{1,9},{5... | collective-permute-start | bytes 3538952 | tf_op jit(solution)/shard_map/ppermute | solution.py:44
  67.6 16.7 %collective-permute-start.5 = (bf16[128,2048]{1,0:T(8,128)(2,1)S(1)}, bf16[128,2048]{1,0:T(8,128)(2,1)S(1)}, u32[]{:S(2)}, u32[]{:S(2)}) collective-permute-start(bf16[128,2048]{1,0:T(8,128)(2,1)S(1)} %broadcast_select_fusion.1), channel_id=1, source_target_pairs={{1,0},{2,3},{5,4},{6,7},{9,8},{10,11},{13,12},{14,15},{17,16},{18,... | collective-permute-start | bytes 1572872 | tf_op jit(solution)/shard_map/ppermute | solution.py:69
  91.8 6.7 %copy-start.7 = (s32[1,4]{1,0:T(1,128)S(1)}, s32[1,4]{1,0:T(1,128)}, u32[]{:S(2)}) copy-start(s32[1,4]{1,0:T(1,128)} %refs_1_.1) | copy-start | bytes 52
  93.3 5.2 %collective-permute-start.15 = (bf16[256,2304]{1,0:T(8,128)(2,1)S(1)}, bf16[256,2304]{1,0:T(8,128)(2,1)S(1)}, u32[]{:S(2)}, u32[]{:S(2)}) collective-permute-start(bf16[256,2304]{1,0:T(8,128)(2,1)S(1)} %get-tuple-element.62), channel_id=1, source_target_pairs={{0,4},{4,0},{8,12},{12,8},{16,20},{20,16},{24,28},{28,24},{1,5},{5... | collective-permute-start | bytes 3538952 | tf_op jit(solution)/shard_map/ppermute | solution.py:44
  102.5 2.2 %collective-permute-start.16 = (bf16[256,1280]{1,0:T(8,128)(2,1)S(1)}, bf16[256,1280]{1,0:T(8,128)(2,1)S(1)}, u32[]{:S(2)}, u32[]{:S(2)}) collective-permute-start(bf16[256,1280]{1,0:T(8,128)(2,1)S(1)} %shard_map.98.own), channel_id=1, source_target_pairs={{0,4},{4,0},{8,12},{12,8},{16,20},{20,16},{24,28},{28,24},{1,5},{5... | collective-permute-start | bytes 1966088 | tf_op jit(solution)/shard_map/ppermute | solution.py:44
  105.7 16.0 %collective-permute-start.22 = (bf16[256,1280]{1,0:T(8,128)(2,1)S(1)}, bf16[256,1280]{1,0:T(8,128)(2,1)S(1)}, u32[]{:S(2)}, u32[]{:S(2)}) collective-permute-start(bf16[256,1280]{1,0:T(8,128)(2,1)S(1)} %get-tuple-element.82), channel_id=1, source_target_pairs={{0,16},{4,20},{8,24},{12,28},{16,0},{20,4},{24,8},{28,12},{1,17},{... | collective-permute-start | bytes 1966088 | tf_op jit(solution)/shard_map/ppermute | solution.py:44
  106.0 15.7 %collective-permute-start.24 = (bf16[256,1280]{1,0:T(8,128)(2,1)S(1)}, bf16[256,1280]{1,0:T(8,128)(2,1)S(1)}, u32[]{:S(2)}, u32[]{:S(2)}) collective-permute-start(bf16[256,1280]{1,0:T(8,128)(2,1)S(1)} %get-tuple-element.81), channel_id=1, source_target_pairs={{0,8},{4,12},{8,0},{12,4},{16,24},{20,28},{24,16},{28,20},{1,9},{5... | collective-permute-start | bytes 1966088 | tf_op jit(solution)/shard_map/ppermute | solution.py:44
  111.1 13.4 %collective-permute-start.17 = (bf16[128,2048]{1,0:T(8,128)(2,1)S(1)}, bf16[128,2048]{1,0:T(8,128)(2,1)S(1)}, u32[]{:S(2)}, u32[]{:S(2)}) collective-permute-start(bf16[128,2048]{1,0:T(8,128)(2,1)S(1)} %get-tuple-element.65), channel_id=1, source_target_pairs={{3,2},{0,1},{7,6},{4,5},{11,10},{8,9},{15,14},{12,13},{19,18},{16,... | collective-permute-start | bytes 1572872 | tf_op jit(solution)/shard_map/ppermute | solution.py:69
  114.2 10.2 %collective-permute-start.18 = (bf16[128,2048]{1,0:T(8,128)(2,1)S(1)}, bf16[128,2048]{1,0:T(8,128)(2,1)S(1)}, u32[]{:S(2)}, u32[]{:S(2)}) collective-permute-start(bf16[128,2048]{1,0:T(8,128)(2,1)S(1)} %get-tuple-element.65), channel_id=1, source_target_pairs={{1,2},{2,1},{5,6},{6,5},{9,10},{10,9},{13,14},{14,13},{17,18},{18,... | collective-permute-start | bytes 1572872 | tf_op jit(solution)/shard_map/ppermute | solution.py:69
  122.0 32.9 %collective-permute-start.25 = (bf16[512,1280]{1,0:T(8,128)(2,1)S(1)}, bf16[512,1280]{1,0:T(8,128)(2,1)S(1)}, u32[]{:S(2)}, u32[]{:S(2)}) collective-permute-start(bf16[512,1280]{1,0:T(8,128)(2,1)S(1)} %pad_maximum_fusion.1), channel_id=1, source_target_pairs={{0,16},{4,20},{8,24},{12,28},{16,0},{20,4},{24,8},{28,12},{1,17},{... | collective-permute-start | bytes 3932168 | tf_op jit(solution)/shard_map/ppermute | solution.py:44
  123.3 31.6 %collective-permute-start.23 = (bf16[512,1280]{1,0:T(8,128)(2,1)S(1)}, bf16[512,1280]{1,0:T(8,128)(2,1)S(1)}, u32[]{:S(2)}, u32[]{:S(2)}) collective-permute-start(bf16[512,1280]{1,0:T(8,128)(2,1)S(1)} %pad_maximum_fusion), channel_id=1, source_target_pairs={{0,8},{4,12},{8,0},{12,4},{16,24},{20,28},{24,16},{28,20},{1,9},{5... | collective-permute-start | bytes 3932168 | tf_op jit(solution)/shard_map/ppermute | solution.py:44
  124.6 25.0 %collective-permute-start.19 = (bf16[128,2048]{1,0:T(8,128)(2,1)S(1)}, bf16[128,2048]{1,0:T(8,128)(2,1)S(1)}, u32[]{:S(2)}, u32[]{:S(2)}) collective-permute-start(bf16[128,2048]{1,0:T(8,128)(2,1)S(1)} %get-tuple-element.68), channel_id=1, source_target_pairs={{0,1},{1,0},{2,3},{3,2},{4,5},{5,4},{6,7},{7,6},{8,9},{9,8},{10,11... | collective-permute-start | bytes 1572872 | tf_op jit(solution)/shard_map/ppermute | solution.py:44
  128.2 21.5 %collective-permute-start.20 = (bf16[128,2048]{1,0:T(8,128)(2,1)S(1)}, bf16[128,2048]{1,0:T(8,128)(2,1)S(1)}, u32[]{:S(2)}, u32[]{:S(2)}) collective-permute-start(bf16[128,2048]{1,0:T(8,128)(2,1)S(1)} %add.18), channel_id=1, source_target_pairs={{0,2},{1,3},{2,0},{3,1},{4,6},{5,7},{6,4},{7,5},{8,10},{9,11},{10,... | collective-permute-start | bytes 1572872 | tf_op jit(solution)/shard_map/ppermute | solution.py:44
  149.8 6.8 %collective-permute-start.21 = (bf16[64,2048]{1,0:T(8,128)(2,1)S(1)}, bf16[64,2048]{1,0:T(8,128)(2,1)S(1)}, u32[]{:S(2)}, u32[]{:S(2)}) collective-permute-start(bf16[64,2048]{1,0:T(8,128)(2,1)S(1)} %add_convert_fusion), channel_id=1, source_target_pairs={{0,4},{4,0},{8,12},{12,8},{16,20},{20,16},{24,28},{28,24},{1,5},{5... | collective-permute-start | bytes 786440 | tf_op jit(solution)/shard_map/ppermute | solution.py:44
  154.9 1.7 %copy-start.1 = (bf16[64,4096]{1,0:T(8,128)(2,1)S(1)}, bf16[64,4096]{1,0:T(8,128)(2,1)}, u32[]{:S(2)}) copy-start(bf16[64,4096]{1,0:T(8,128)(2,1)} %tokens.3) | copy-start | bytes 1572868
  154.9 1.7 %copy-start.3 = (bf16[64,4096]{1,0:T(8,128)(2,1)S(1)}, bf16[64,4096]{1,0:T(8,128)(2,1)}, u32[]{:S(2)}) copy-start(bf16[64,4096]{1,0:T(8,128)(2,1)} %grad_out.3) | copy-start | bytes 1572868
  (4 other events, 3.8 us)
